TPU v7x, 32 devices: a whole 2x2x4 slice. The times are simulated.
32 devices in a mesh: dp: 2 (over core), ctx: 16 (over z, y, x).
Axes of the slice: x: 2, y: 2, z: 4, core: 2. Of those that a mesh axis runs over, the one named last changes fastest.
Arguments:
- features: bfloat16 [2, 4096, 2560], P('dp', 'ctx'), may hold values from -6 to 6
- write_keys: bfloat16 [2, 4096, 128], P('dp', 'ctx'), may hold values from -0.75 to 0.75
- read_queries: bfloat16 [2, 4096, 128], P('dp', 'ctx'), may hold values from -0.75 to 0.75
- step_logits: float32 [2, 40, 4096], P('dp', None, 'ctx'), may hold values from -6 to 6
- step_bias: float32 [40], replicated, may hold values from -1 to 1
- decay_log: float32 [40], replicated, may hold values from -16 to -2
- skip_gain: float32 [40], replicated, may hold values from 0.5 to 1.5
- doc_starts: int32 [2, 4], P('dp'), may hold values from 0 to 4095, as said below
- out_grad: bfloat16 [2, 4096, 2560], P('dp', 'ctx'), may hold values from -20 to 20
Outputs:
- mixed: bfloat16 [2, 4096, 2560], P('dp', 'ctx')
- feature_grad: bfloat16 [2, 4096, 2560], P('dp', 'ctx')
- write_grad: bfloat16 [2, 4096, 128], P('dp', 'ctx')
- read_grad: bfloat16 [2, 4096, 128], P('dp', 'ctx')
- step_grad: float32 [2, 40, 4096], P('dp', None, 'ctx')
- bias_grad: float32 [40], replicated
- decay_grad: float32 [40], replicated
- skip_grad: float32 [40], replicated
Inputs may be any that keep to these rules, and one draw needn't show every extreme that they name: `doc_starts`: each row is ascending with distinct entries, begins with 0 and ends with 4095; row b holds the first positions of the documents packed into sequence b.
All inputs are finite; a program needn't handle non-finite values.
Results may differ from a plain program's by a relative error of at most 0.002.
Values sent between devices are 32-bit elements; how exact they have to be, the bound alone decides.
No kernel may reach another device: no remote copies, remote signals or barrier semaphores. Data moves between devices by JAX's collectives and lax.ppermute only.
A program may use at most 128 MiB of HBM per device.

v0:
```python
import jax
import jax.numpy as jnp
from jax import lax
from jax.sharding import PartitionSpec as P

GROUP_HEADS = 2


EXACT = lax.Precision.HIGHEST


def swapped(value, axis, distance):
    mask = 2**distance
    pairs = [(source, source ^ mask) for source in range(lax.axis_size(axis))]
    return lax.ppermute(value, axis, pairs)


def widen(values, repeat_by):
    return jnp.repeat(values, repeat_by, axis=-1)


def step_decays(logit_block, step_bias, decay_log):
    stride = jax.nn.softplus(logit_block + step_bias[:, None])
    decay_rate = -jnp.exp(decay_log)
    cumulative = jnp.cumsum(stride * decay_rate[:, None], axis=1)
    return (stride, cumulative)


def segments(doc_starts, start_pos, length):
    positions = start_pos + jnp.arange(length, dtype=jnp.int32)
    segment = jnp.sum((doc_starts[None, :] <= positions[:, None]).astype(jnp.int32), axis=1)
    entry_segment = jnp.sum((doc_starts <= start_pos - 1).astype(jnp.int32))
    return (segment, entry_segment)


def block_state(feature_block, write_block, logit_block, step_bias, decay_log, own_last, linked):
    stride, cumulative = step_decays(logit_block, step_bias, decay_log)
    weights = own_last[None, :] * jnp.exp(cumulative[:, -1:] - cumulative) * stride
    head_size = feature_block.shape[1] // stride.shape[0]
    scaled = feature_block * widen(weights.T, head_size)
    state_end = jnp.dot(write_block.T, scaled, precision=EXACT, preferred_element_type=jnp.float32)
    totals = jnp.exp(cumulative[:, -1]) * linked
    return (state_end, totals)


def intra_group(cum_group, stride_group, feature_group, scores, same_doc):
    gaps = cum_group[:, :, None] - cum_group[:, None, :]
    decays = jnp.exp(jnp.where(same_doc[None], gaps, -jnp.inf))
    mixing = decays * scores[None] * stride_group[:, None, :]
    head_count = cum_group.shape[0]
    per_head = feature_group.reshape(feature_group.shape[0], head_count, -1)
    result = jnp.einsum("htu,uhp->thp", mixing, per_head, precision=EXACT)
    return result.reshape(feature_group.shape[0], -1)


def block_main(
    feature_block, write_block, read_block, logit_block, step_bias, decay_log, skip_gain, segment
):
    stride, cumulative = step_decays(logit_block, step_bias, decay_log)
    length = feature_block.shape[0]
    head_count = stride.shape[0]
    head_size = feature_block.shape[1] // head_count
    groups = head_count // GROUP_HEADS
    ordinal = jnp.arange(length, dtype=jnp.int32)
    same_doc = (segment[:, None] == segment[None, :]) & (ordinal[:, None] >= ordinal[None, :])
    scores = jnp.dot(read_block, write_block.T, precision=EXACT, preferred_element_type=jnp.float32)
    cum_stack = cumulative.reshape(groups, GROUP_HEADS, length)
    stride_stack = stride.reshape(groups, GROUP_HEADS, length)
    feature_stack = feature_block.reshape(length, groups, GROUP_HEADS * head_size).transpose(
        1, 0, 2
    )

    def one_group(packed):
        return intra_group(packed[0], packed[1], packed[2], scores, same_doc)

    pieces = lax.map(jax.checkpoint(one_group), (cum_stack, stride_stack, feature_stack))
    inside = pieces.transpose(1, 0, 2).reshape(length, -1)
    return inside + feature_block * widen(skip_gain, head_size)


def block_carry(read_block, logit_block, step_bias, decay_log, keep_in, state_in):
    stride, cumulative = step_decays(logit_block, step_bias, decay_log)
    factor = keep_in[:, None] * jnp.exp(cumulative.T)
    head_size = state_in.shape[1] // factor.shape[1]
    return jnp.dot(
        read_block, state_in, precision=EXACT, preferred_element_type=jnp.float32
    ) * widen(factor, head_size)


def link_states(earlier, latter):
    head_size = latter[1].shape[1] // latter[0].shape[0]
    return (earlier[0] * latter[0], earlier[1] * widen(latter[0], head_size)[None, :] + latter[1])


def select_pair(condition, first, second):
    return jax.tree.map(lambda left, right: jnp.where(condition, left, right), first, second)


def local(
    features,
    write_keys,
    read_queries,
    step_logits,
    step_bias,
    decay_log,
    skip_gain,
    doc_starts,
    out_grad,
):
    length = features.shape[1]
    position = lax.axis_index("ctx")
    bit_count = lax.axis_size("ctx").bit_length() - 1
    start_pos = position * length
    segment, entry_segment = segments(doc_starts[0], start_pos, length)
    keep_in = (segment == entry_segment).astype(jnp.float32)
    own_last = (segment == segment[-1]).astype(jnp.float32)
    linked = (segment[-1] == entry_segment).astype(jnp.float32)
    feature_full = features[0].astype(jnp.float32)
    write_full = write_keys[0].astype(jnp.float32)
    read_full = read_queries[0].astype(jnp.float32)
    logit_full = step_logits[0]

    def state_fn(feat_in, write_in, logit_in, bias_in, decay_in):
        return block_state(feat_in, write_in, logit_in, bias_in, decay_in, own_last, linked)

    (state_end, totals), state_back = jax.vjp(
        state_fn, feature_full, write_full, logit_full, step_bias, decay_log
    )
    head_count = totals.shape[0]

    def main_fn(feat_in, write_in, read_in, logit_in, bias_in, decay_in, skip_in):
        return block_main(feat_in, write_in, read_in, logit_in, bias_in, decay_in, skip_in, segment)

    def carry_fn(read_in, logit_in, bias_in, decay_in, state_arg):
        return block_carry(read_in, logit_in, bias_in, decay_in, keep_in, state_arg)

    identity = (jnp.ones_like(totals), jnp.zeros_like(state_end))
    forward_prefix = identity
    forward_total = (totals, state_end)
    for bit in range(bit_count):
        other = swapped((forward_total[0], forward_total[1]), "ctx", bit)
        partner_first = position >> bit & 1 == 1
        forward_prefix = select_pair(
            partner_first, link_states(other, forward_prefix), forward_prefix
        )
        forward_total = select_pair(
            partner_first, link_states(other, forward_total), link_states(forward_total, other)
        )
    state_in = forward_prefix[1]
    cotangent = out_grad[0].astype(jnp.float32)

    def whole_fn(feat_in, write_in, read_in, logit_in, bias_in, decay_in, skip_in, state_arg):
        return main_fn(feat_in, write_in, read_in, logit_in, bias_in, decay_in, skip_in) + carry_fn(
            read_in, logit_in, bias_in, decay_in, state_arg
        )

    mixed_out, whole_back = jax.vjp(
        whole_fn,
        feature_full,
        write_full,
        read_full,
        logit_full,
        step_bias,
        decay_log,
        skip_gain,
        state_in,
    )
    feat_main, write_main, read_main, logit_main, bias_main, decay_main, skip_total, state_grad = (
        whole_back(cotangent)
    )
    backward_prefix = identity
    backward_total = (totals, state_grad)
    for bit in range(bit_count):
        other = swapped((backward_total[0], backward_total[1]), "ctx", bit)
        partner_first = position >> bit & 1 == 0
        backward_prefix = select_pair(
            partner_first, link_states(other, backward_prefix), backward_prefix
        )
        backward_total = select_pair(
            partner_first, link_states(other, backward_total), link_states(backward_total, other)
        )
    adjoint = backward_prefix[1]
    total_grad = jnp.sum(
        (adjoint * state_in).reshape(adjoint.shape[0], head_count, -1), axis=(0, 2)
    )
    feat_state, write_state, logit_state, bias_state, decay_state = state_back(
        (adjoint, total_grad)
    )
    bias_sum, decay_sum, skip_sum = lax.psum(
        (bias_main + bias_state, decay_main + decay_state, skip_total), ("dp", "ctx")
    )
    return (
        mixed_out.astype(jnp.bfloat16)[None],
        (feat_main + feat_state).astype(jnp.bfloat16)[None],
        (write_main + write_state).astype(jnp.bfloat16)[None],
        read_main.astype(jnp.bfloat16)[None],
        (logit_main + logit_state)[None],
        bias_sum,
        decay_sum,
        skip_sum,
    )


def solution(mesh):
    in_specs = (
        P("dp", "ctx", None),
        P("dp", "ctx", None),
        P("dp", "ctx", None),
        P("dp", None, "ctx"),
        P(),
        P(),
        P(),
        P("dp", None),
        P("dp", "ctx", None),
    )
    out_specs = (
        P("dp", "ctx", None),
        P("dp", "ctx", None),
        P("dp", "ctx", None),
        P("dp", "ctx", None),
        P("dp", None, "ctx"),
        P(),
        P(),
        P(),
    )
    return jax.shard_map(local, mesh=mesh, in_specs=in_specs, out_specs=out_specs, check_vma=False)
```

profile of v0, /device:TPU:0, one launch (start us, length us, event | category | flops | bytes accessed | tf_op | source)
XLA Modules:
  0.0 518.1 jit_solution(17836829672805646578)
XLA Ops:
  14.0 2.4 convolution_bitcast_fusion.3
  16.4 2.9 collective-permute-start
  19.4 2.4 copy.112
  24.9 2.4 convolution_bitcast_fusion.2
  28.6 2.1 collective-permute-start.1
  30.8 45.7 %collective-permute-done.1 = f32[40]{0:T(128)S(1)} collective-permute-done((f32[40]{0:T(128)S(1)}, f32[40]{0:T(128)S(1)}, u32[]{:S(2)}, u32[]{:S(2)}) %collective-permute-start.1) | collective-permute-done | bytes 192 | tf_op jit(solution)/shard_map/ppermute | solution.py:15
  76.7 4.3 add_select_fusion.11
  87.3 52.0 %collective-permute-done.3 = f32[40]{0:T(128)S(1)} collective-permute-done((f32[40]{0:T(128)S(1)}, f32[40]{0:T(128)S(1)}, u32[]{:S(2)}, u32[]{:S(2)}) %collective-permute-start.3) | collective-permute-done | bytes 192 | tf_op jit(solution)/shard_map/ppermute | solution.py:15
  139.5 4.2 add_select_fusion.10
  148.8 160.9 %while.34 = (s32[]{:T(128)}, f32[256,256]{1,0:T(8,128)S(1)}, f32[20,2,256]{2,1,0:T(2,128)}, f32[20,2,256]{2,1,0:T(2,128)}, f32[20,256,128]{1,2,0:T(8,128)}, /*in...) while((s32[]{:T(128)}, f32[256,256]{1,0:T(8,128)S(1)}, ...), condition=%wide.region_11.13_spmd.clone, body=%wide.region_6.12_spmd.clone.sunk | while | flops 203816448 | bytes 4162763 | solution.py:76
  316.1 4.3 add_select_fusion.9
  320.4 2.5 collective-permute-start.10
  325.1 61.5 %while.33 = (s32[]{:T(128)}, f32[20,256,128]{1,2,0:T(8,128)}, f32[20,256,128]{1,2,0:T(8,128)S(1)}, f32[20,2,256]{2,1,0:T(2,128)}, f32[1,256,256]{2,1,0:T(8,128)}...) while((s32[]{:T(128)}, f32[20,256,128]{1,2,0:T(8,128)}, ...), condition=%wide.region_4.6_spmd.clone, body=%wide.region_3.5_spmd.clone.sunk | while | flops 101187584 | bytes 1127005 | solution.py:76
  388.3 2.7 reduce-window.34
  395.7 10.1 %collective-permute-done.10 = f32[128,2560]{0,1:T(8,128)} collective-permute-done((f32[128,2560]{0,1:T(8,128)}, f32[128,2560]{0,1:T(8,128)}, u32[]{:S(2)}, u32[]{:S(2)}) %collective-permute-start.10) | collective-permute-done | bytes 1310752 | tf_op jit(solution)/shard_map/ppermute | solution.py:15
  405.9 27.3 %collective-permute-done.6 = f32[128,2560]{0,1:T(8,128)} collective-permute-done((f32[128,2560]{0,1:T(8,128)}, f32[128,2560]{0,1:T(8,128)}, u32[]{:S(2)}, u32[]{:S(2)}) %collective-permute-start.6) | collective-permute-done | bytes 1310752 | tf_op jit(solution)/shard_map/ppermute | solution.py:15
  433.1 7.5 %multiply_reduce_fusion.2 = (f32[2560]{0:T(1024)}, f32[128,2560]{0,1:T(8,128)S(1)}, f32[128,2560]{0,1:T(8,128)S(1)}) fusion(f32[128,2560]{0,1:T(8,128)} %collective-permute-done.7, pred[]{:T(512)S(6)} %eq.85, f32[128,2560]{0,1:T(8,128)} %collective-permute-done.8, f32[2560]{0:T(1024)S(1)} %mul.572, pred[]{:T(512)S(6)} %eq.84, ...), kind=kLoop, calls=%fused_computation.71 | loop fusion | flops 7206400 | bytes 13178888 | tf_op jit(solution)/shard_map/reduce_sum | solution.py:183
  443.3 6.6 %bitcast_multiply_fusion.7 = (f32[256,2560]{0,1:T(8,128)}, bf16[256,2560]{0,1:T(8,128)(2,1)}, f32[2560]{0:T(1024)S(1)}, bf16[256,2560]{0,1:T(8,128)(2,1)}, f32[2...) fusion(bf16[1,256,2560]{1,2,0:T(8,128)(2,1)S(1)} %copy-done.2, f32[256,40]{0,1:T(8,128)S(1)} %copy-done.19, ...), kind=kOutput, calls=%fused_computation.63 | convolution fusion | flops 1018426880 | bytes 25071616 | tf_op jit(solution)/shard_map/transpose(jvp())/dot_general | solution.py:41
  449.9 2.2 reduce_sum.240
  454.2 2.5 reduce-window.36
  458.4 2.5 reduce-window.30
  466.8 6.8 %fusion.38 = bf16[1,256,128]{2,1,0:T(8,128)(2,1)} fusion(f32[256,128]{1,0:T(8,128)S(1)} %copy-done.17, f32[256,2560]{0,1:T(8,128)} %get-tuple-element.510, f32[128,2560]{0,1:T(8,128)S(1)} %copy-done.7), kind=kOutput, calls=%fused_computation.84 | convolution fusion | flops 1006698496 | bytes 4128768 | tf_op jit(solution)/shard_map/transpose(jvp())/dot_general | solution.py:85
  473.6 5.0 fusion.39
  478.5 39.5 %all-reduce.2 = (f32[40]{0:T(128)}, f32[40]{0:T(128)}, f32[40]{0:T(128)}) all-reduce(f32[40]{0:T(128)S(1)} %get-tuple-element.530, f32[40]{0:T(128)S(1)} %get-tuple-element.529, f32[40]{0:T(128)S(1)} %reduce_sum.252), channel_id=1, replica_groups=mesh['dp'=2,'ctx'=16] {'dp','ctx'}, use_global_device_ids=true, to_apply=%region_26.28 | all-reduce | flops 120 | bytes 960 | tf_op jit(solution)/shard_map/psum | solution.py:189
  (500 shorter events, 277.4 us)
Async XLA Ops:
  0.6 13.4 %copy-start = (bf16[1,256,128]{2,1,0:T(8,128)(2,1)S(1)}, bf16[1,256,128]{2,1,0:T(8,128)(2,1)}, u32[]{:S(2)}) copy-start(bf16[1,256,128]{2,1,0:T(8,128)(2,1)} %param.15) | copy-start | bytes 196612
  0.6 10.1 %copy-start.14 = (bf16[1,256,2560]{2,1,0:T(8,128)(2,1)S(1)}, bf16[1,256,2560]{2,1,0:T(8,128)(2,1)}, u32[]{:S(2)}) copy-start(bf16[1,256,2560]{2,1,0:T(8,128)(2,1)} %param.14) | copy-start | bytes 3932164
  3.9 79.0 %copy-start.22 = (f32[40,2]{0,1:T(2,128)}, f32[40,2]{0,1:T(2,128)S(1)}, u32[]{:S(2)}) copy-start(f32[40,2]{0,1:T(2,128)S(1)} %slice.33) | copy-start | bytes 964
  4.1 8.0 %copy-start.31 = (f32[40]{0:T(128)}, f32[40]{0:T(128)S(1)}, u32[]{:S(2)}) copy-start(f32[40]{0:T(128)S(1)} %slice_bitcast_fusion) | copy-start | bytes 484
  9.9 9.5 %copy-start.27 = (f32[256]{0:T(256)}, f32[256]{0:T(256)S(1)}, u32[]{:S(2)}) copy-start(f32[256]{0:T(256)S(1)} %get-tuple-element.528) | copy-start | bytes 3076
  16.4 60.3 %collective-permute-start = (f32[128,2560]{0,1:T(8,128)}, f32[128,2560]{0,1:T(8,128)}, u32[]{:S(2)}, u32[]{:S(2)}) collective-permute-start(f32[128,2560]{0,1:T(8,128)} %convolution_bitcast_fusion.3), channel_id=1, source_target_pairs={{0,1},{1,0},{2,3},{3,2},{4,5},{5,4},{6,7},{7,6},{8,9},{9,8},{10,11... | collective-permute-start | bytes 3932168 | tf_op jit(solution)/shard_map/ppermute | solution.py:15
  27.2 49.4 %collective-permute-start.7 = (f32[128,2560]{0,1:T(8,128)}, f32[128,2560]{0,1:T(8,128)}, u32[]{:S(2)}, u32[]{:S(2)}) collective-permute-start(f32[128,2560]{0,1:T(8,128)} %convolution_bitcast_fusion.2), channel_id=1, source_target_pairs={{0,1},{1,0},{2,3},{3,2},{4,5},{5,4},{6,7},{7,6},{8,9},{9,8},{10,11... | collective-permute-start | bytes 3932168 | tf_op jit(solution)/shard_map/ppermute | solution.py:15
  28.6 47.9 %collective-permute-start.1 = (f32[40]{0:T(128)S(1)}, f32[40]{0:T(128)S(1)}, u32[]{:S(2)}, u32[]{:S(2)}) collective-permute-start(f32[40]{0:T(128)S(1)} %exponential_multiply_fusion), channel_id=1, source_target_pairs={{0,1},{1,0},{2,3},{3,2},{4,5},{5,4},{6,7},{7,6},{8,9},{9,8},{10,11... | collective-permute-start | bytes 488 | tf_op jit(solution)/shard_map/ppermute | solution.py:15
  76.5 8.2 %copy-start.33 = (f32[40]{0:T(128)}, f32[40]{0:T(128)S(1)}, u32[]{:S(2)}) copy-start(f32[40]{0:T(128)S(1)} %collective-permute-done.1) | copy-start | bytes 484
  80.9 58.5 %collective-permute-start.2 = (f32[128,2560]{0,1:T(8,128)}, f32[128,2560]{0,1:T(8,128)}, u32[]{:S(2)}, u32[]{:S(2)}) collective-permute-start(f32[128,2560]{0,1:T(8,128)} %get-tuple-element.522), channel_id=1, source_target_pairs={{0,2},{1,3},{2,0},{3,1},{4,6},{5,7},{6,4},{7,5},{8,10},{9,11},{10,... | collective-permute-start | bytes 3932168 | tf_op jit(solution)/shard_map/ppermute | solution.py:15
  82.7 56.7 %collective-permute-start.8 = (f32[128,2560]{0,1:T(8,128)}, f32[128,2560]{0,1:T(8,128)}, u32[]{:S(2)}, u32[]{:S(2)}) collective-permute-start(f32[128,2560]{0,1:T(8,128)} %get-tuple-element.523), channel_id=1, source_target_pairs={{0,2},{1,3},{2,0},{3,1},{4,6},{5,7},{6,4},{7,5},{8,10},{9,11},{10,... | collective-permute-start | bytes 3932168 | tf_op jit(solution)/shard_map/ppermute | solution.py:15
  84.7 59.0 %copy-start.35 = (f32[40]{0:T(128)}, f32[40]{0:T(128)S(1)}, u32[]{:S(2)}) copy-start(f32[40]{0:T(128)S(1)} %fusion.87) | copy-start | bytes 484
  84.7 54.6 %collective-permute-start.3 = (f32[40]{0:T(128)S(1)}, f32[40]{0:T(128)S(1)}, u32[]{:S(2)}, u32[]{:S(2)}) collective-permute-start(f32[40]{0:T(128)S(1)} %fusion.87), channel_id=1, source_target_pairs={{0,2},{1,3},{2,0},{3,1},{4,6},{5,7},{6,4},{7,5},{8,10},{9,11},{10,... | collective-permute-start | bytes 488 | tf_op jit(solution)/shard_map/ppermute | solution.py:15
  143.7 172.4 %collective-permute-start.4 = (f32[128,2560]{0,1:T(8,128)}, f32[128,2560]{0,1:T(8,128)}, u32[]{:S(2)}, u32[]{:S(2)}) collective-permute-start(f32[128,2560]{0,1:T(8,128)} %get-tuple-element.520), channel_id=1, source_target_pairs={{0,4},{1,5},{2,6},{3,7},{4,0},{5,1},{6,2},{7,3},{8,12},{9,13},{10,... | collective-permute-start | bytes 3932168 | tf_op jit(solution)/shard_map/ppermute | solution.py:15
  145.3 170.8 %collective-permute-start.9 = (f32[128,2560]{0,1:T(8,128)}, f32[128,2560]{0,1:T(8,128)}, u32[]{:S(2)}, u32[]{:S(2)}) collective-permute-start(f32[128,2560]{0,1:T(8,128)} %get-tuple-element.521), channel_id=1, source_target_pairs={{0,4},{1,5},{2,6},{3,7},{4,0},{5,1},{6,2},{7,3},{8,12},{9,13},{10,... | collective-permute-start | bytes 3932168 | tf_op jit(solution)/shard_map/ppermute | solution.py:15
  311.9 3.5 collective-permute-start.5
  320.4 85.5 %collective-permute-start.10 = (f32[128,2560]{0,1:T(8,128)}, f32[128,2560]{0,1:T(8,128)}, u32[]{:S(2)}, u32[]{:S(2)}) collective-permute-start(f32[128,2560]{0,1:T(8,128)} %get-tuple-element.519), channel_id=1, source_target_pairs={{0,8},{1,9},{2,10},{3,11},{4,12},{5,13},{6,14},{7,15},{8,0},{9,1},... | collective-permute-start | bytes 3932168 | tf_op jit(solution)/shard_map/ppermute | solution.py:15
  322.9 110.3 %collective-permute-start.6 = (f32[128,2560]{0,1:T(8,128)}, f32[128,2560]{0,1:T(8,128)}, u32[]{:S(2)}, u32[]{:S(2)}) collective-permute-start(f32[128,2560]{0,1:T(8,128)} %get-tuple-element.518), channel_id=1, source_target_pairs={{0,8},{1,9},{2,10},{3,11},{4,12},{5,13},{6,14},{7,15},{8,0},{9,1},... | collective-permute-start | bytes 3932168 | tf_op jit(solution)/shard_map/ppermute | solution.py:15
  386.6 7.9 %copy-start.16 = (bf16[1,256,128]{2,1,0:T(8,128)(2,1)S(1)}, bf16[1,256,128]{2,1,0:T(8,128)(2,1)}, u32[]{:S(2)}) copy-start(bf16[1,256,128]{2,1,0:T(8,128)(2,1)} %param.16) | copy-start | bytes 196612
  386.6 8.2 %copy-start.34 = (f32[40]{0:T(128)S(1)}, f32[40]{0:T(128)}, u32[]{:S(2)}) copy-start(f32[40]{0:T(128)} %copy-done.33) | copy-start | bytes 484
  386.6 8.3 %copy-start.37 = (f32[40]{0:T(128)S(1)}, f32[40]{0:T(128)}, u32[]{:S(2)}) copy-start(f32[40]{0:T(128)} %copy-done.36) | copy-start | bytes 484
  386.6 8.3 %copy-start.39 = (f32[40]{0:T(128)S(1)}, f32[40]{0:T(128)}, u32[]{:S(2)}) copy-start(f32[40]{0:T(128)} %copy-done.38) | copy-start | bytes 484
  433.1 9.0 %copy-start.9 = (f32[20,256,128]{1,2,0:T(8,128)S(1)}, f32[20,256,128]{1,2,0:T(8,128)}, u32[]{:S(2)}) copy-start(f32[20,256,128]{1,2,0:T(8,128)} %get-tuple-element.301) | copy-start | bytes 7864324
  433.1 9.0 %copy-start.10 = (f32[20,256,128]{1,2,0:T(8,128)S(1)}, f32[20,256,128]{1,2,0:T(8,128)}, u32[]{:S(2)}) copy-start(f32[20,256,128]{1,2,0:T(8,128)} %get-tuple-element.300) | copy-start | bytes 7864324
  (47 other events, 169.1 us)
where the time goes:
time: 522 us; the launch traced here: 518 us
  waiting for transfers between devices  137 us (26%)
  local copies, waits for them, and re-layouts  127 us (24%)
  matrix products  121 us (23%)
  other arithmetic  75.8 us (15%)
  blocking collectives  39.5 us (8%)
  starting transfers between devices  15.4 us (3%)
    ppermute x11, waiting for transfers between devices, swapped(): return lax.ppermute(value, axis, pairs)  137 us
    dot_general x60, matrix products, intra_group(): result = jnp.einsum('htu,uhp->thp', mixing, per_head, precision=EXACT)  94.2 us
    dynamic_update_slice x60, local copies, waits for them, and re-layouts, block_main(): lax.map(jax.checkpoint(one_group), (cum_stack, stride_stack, feature_stack))  51.9 us
    psum x1, blocking collectives, local(): lax.psum((bias_main + bias_state, decay_main + decay_state, skip_total),...  39.5 us
    squeeze x40, local copies, waits for them, and re-layouts, block_main(): lax.map(jax.checkpoint(one_group), (cum_stack, stride_stack, feature_stack))  33.1 us
    and x21, other arithmetic, block_main(): (segment[:, None] == segment[None, :]) & (ordinal[:, None] >= ordinal[Non...  17.4 us
    ppermute x11, starting transfers between devices, swapped(): return lax.ppermute(value, axis, pairs)  15.4 us
    dot_general x3, matrix products, block_state(): jnp.dot(write_block.T, scaled, precision=EXACT, preferred_element_type=jn...  13.9 us
  transfers between devices with their start and end apart: 11, of which 5 were waited for; matrix products, arithmetic and copies ran while one was open for 48% of the time, Pallas kernels for 0%

commit v1 on v0

v1 whole, which is shorter than its diff:
```python
import functools

import jax
import jax.numpy as jnp
from jax import lax
from jax.experimental import pallas as pl
from jax.experimental.pallas import tpu as pltpu
from jax.sharding import PartitionSpec as P

F32 = jnp.float32
BF16 = jnp.bfloat16
PLANE = 4
LANES = 128
LOG2E = 1.4426950408889634
FAR = -1e30
VMEM_BYTES = 56 * 1024 * 1024
VMEM = pl.BlockSpec(memory_space=pltpu.VMEM)
SMEM = pl.BlockSpec(memory_space=pltpu.SMEM)


def iota(shape, axis):
    return lax.broadcasted_iota(jnp.int32, shape, axis)


def matmul(left, right):
    return lax.dot_general(left, right, (((1,), (0,)), ((), ())), preferred_element_type=F32)


def matmul_nt(left, right):
    return lax.dot_general(left, right, (((1,), (1,)), ((), ())), preferred_element_type=F32)


def split2(value):
    high = value.astype(BF16)
    return high, (value - high.astype(F32)).astype(BF16)


def split3(value):
    high = value.astype(BF16)
    rest = value - high.astype(F32)
    middle = rest.astype(BF16)
    return high, middle, (rest - middle.astype(F32)).astype(BF16)


def column(row):
    count = row.shape[1]
    eye = iota((count, count), 0) == iota((count, count), 1)
    return jnp.sum(jnp.where(eye, row, 0.0), axis=1, keepdims=True)


def stacked_columns(rows):
    parts = [part.astype(F32) for part in split3(rows)]
    spare = LANES - 3 * rows.shape[0]
    if spare:
        parts.append(jnp.zeros((spare, rows.shape[1]), F32))
    return jnp.concatenate(parts, axis=0).T.astype(BF16)


def head_of(shape, axis, head_dim):
    return lax.div(iota(shape, axis), head_dim)


def spread_matrix(heads, first, width, head_dim):
    lane = iota((LANES, width), 0)
    head = head_of((LANES, width), 1, head_dim) + first
    hit = (lane == head) | (lane == head + heads) | (lane == head + 2 * heads)
    return jnp.where(hit, 1.0, 0.0).astype(BF16)


def gather_matrix(first, width, head_dim):
    head = head_of((width, LANES), 0, head_dim) + first
    return jnp.where(iota((width, LANES), 1) == head, 1.0, 0.0).astype(BF16)


def softplus(value):
    return jnp.maximum(value, 0.0) + jnp.log1p(jnp.exp(-jnp.abs(value)))


def document_at(starts_ref, position):
    total = jnp.zeros_like(position)
    for entry in range(starts_ref.shape[1]):
        total = total + (starts_ref[0, entry] <= position).astype(jnp.int32)
    return total


def place():
    index = lax.axis_index("ctx")
    return index, lax.rem(index, PLANE)


def states_kernel(
    head_dim, starts, logits, bias, decay, features, cotangent, writes, reads,
    send0, send1, send2, send3, weight_cols, factor_cols, cum_cols, cum_rows, stride_out, log_out,
):
    index, own = place()
    heads, length = logits.shape
    state = writes.shape[1]
    width = features.shape[1] // PLANE
    first = index * length
    stride = softplus(logits[...] + column(bias[...]))
    log_decay = stride * column(-jnp.exp(decay[...]))
    upto = jnp.where(iota((length, length), 0) <= iota((length, length), 1), 1.0, 0.0).astype(BF16)
    parts = matmul(jnp.concatenate(split3(log_decay), axis=0), upto)
    cum = parts[:heads] + parts[heads : 2 * heads] + parts[2 * heads :]
    segment = document_at(starts, first + iota((1, length), 1))
    entry = document_at(starts, jnp.full((1, 1), first - 1, jnp.int32))
    leave = document_at(starts, jnp.full((1, 1), first + length - 1, jnp.int32))
    own_last = jnp.where(segment == leave, 1.0, 0.0)
    keep_in = jnp.where(segment == entry, 1.0, 0.0)
    weight = own_last * jnp.exp(cum[:, length - 1 :] - cum) * stride
    factor = keep_in * jnp.exp(cum)
    weight_stack = stacked_columns(weight)
    factor_stack = stacked_columns(factor)
    weight_cols[...] = weight_stack
    factor_cols[...] = factor_stack
    write_t = writes[...].astype(F32).T.astype(BF16)
    read_t = reads[...].astype(F32).T.astype(BF16)
    for distance, send in enumerate((send0, send1, send2, send3)):
        quarter = own ^ distance
        cols = pl.ds(pl.multiple_of(quarter * width, LANES), width)
        spread = spread_matrix(heads, quarter * (heads // PLANE), width, head_dim)
        high, low = split2(features[:, cols].astype(F32) * matmul(weight_stack, spread))
        send[0:state] = matmul(write_t, high) + matmul(write_t, low)
        wide = matmul(factor_stack, spread)
        high, low = split2(cotangent[:, cols].astype(F32) * wide)
        send[state : 2 * state] = matmul(read_t, high) + matmul(read_t, low)
        send[2 * state :] = jnp.broadcast_to(wide[length - 1 :], (8, width))
    cum_cols[...] = stacked_columns(cum * LOG2E)
    cum_rows[...] = cum * LOG2E - jnp.log2(stride)
    stride_out[...] = stride
    log_out[...] = log_decay


def inner_kernel(
    head_dim, starts, cum_cols, cum_rows, features, cotangent, writes, reads,
    inside, feature_part, write_part, read_part, skip_part, scores_ref, mask_ref, grad_ref,
):
    index, _ = place()
    length = features.shape[0]
    heads = cum_rows.shape[0]
    pair = 2 * head_dim
    first = index * length
    segment_row = document_at(starts, first + iota((1, length), 1))
    segment_col = document_at(starts, first + iota((length, 1), 0))
    allowed = (segment_row == segment_col) & (iota((length, length), 0) >= iota((length, length), 1))
    mask_ref[...] = jnp.where(allowed, 0.0, FAR)
    scores_ref[...] = matmul_nt(reads[...], writes[...])
    grad_ref[...] = jnp.zeros_like(grad_ref)

    def one_pair(at, carry):
        cols = pl.ds(pl.multiple_of(at * pair, LANES), pair)
        feature = features[:, cols]
        grad = cotangent[:, cols]
        grad_f32 = grad.astype(F32)
        grad_t = grad_f32.T.astype(BF16)
        skip_part[:, cols] = jnp.sum(grad_f32 * feature.astype(F32), axis=0, keepdims=True)
        second = iota((length, pair), 1) >= head_dim
        values, back = [], []
        for side in range(2):
            head = at * 2 + side
            lane = iota((LANES, LANES), 0)
            pick = (lane == head) | (lane == head + heads) | (lane == head + 2 * heads)
            upper = matmul(cum_cols[...], jnp.where(pick, 1.0, 0.0).astype(BF16))
            upper = jnp.concatenate([upper] * (length // LANES), axis=1)
            weight = jnp.exp2(upper - cum_rows[pl.ds(head, 1), :] + mask_ref[...])
            high, low = split2(weight * scores_ref[...])
            values.append(matmul(high, feature) + matmul(low, feature))
            rows = grad_t[side * head_dim : (side + 1) * head_dim]
            back.append(matmul(rows, high) + matmul(rows, low))
            only = jnp.where(second == (side == 1), grad_f32, 0.0).astype(BF16)
            grad_ref[...] += matmul_nt(only, feature) * weight
        inside[:, cols] = jnp.where(second, values[1], values[0])
        feature_part[:, cols] = jnp.concatenate(back, axis=0).T
        return carry

    lax.fori_loop(0, heads // 2, one_pair, 0)
    score_grad = grad_ref[...]
    high, low = split2(score_grad)
    read_part[...] = matmul(high, writes[...]) + matmul(low, writes[...])
    high, low = split2(score_grad.T)
    write_part[...] = matmul(high, reads[...]) + matmul(low, reads[...])


def plane_kernel(state, part0, part1, part2, part3, up, down):
    _, own = place()
    parts = (part0, part1, part2, part3)
    for at in range(PLANE):

        @pl.when(own == at)
        def _(at=at):
            block = [parts[j ^ at] for j in range(PLANE)]
            keeps = [ref[2 * state : 2 * state + 1] for ref in block]
            total = block[0][0:state]
            for j in range(1, PLANE):
                total = total * keeps[j] + block[j][0:state]
            up[0:state] = total
            total = block[PLANE - 1][state : 2 * state]
            for j in reversed(range(PLANE - 1)):
                total = total * keeps[j] + block[j][state : 2 * state]
            down[0:state] = total
            keep = jnp.broadcast_to(
                keeps[0] * keeps[1] * keeps[2] * keeps[3], (8, up.shape[1])
            )
            up[state:] = keep
            down[state:] = keep


def arrived(state, came):
    total, keep = came[0][0:state], came[0][state : state + 1]
    for ref in came[1:]:
        total = total + keep * ref[0:state]
        keep = keep * ref[state : state + 1]
    return total, keep


def link_kernel(state, count, up, down, *refs):
    ups, downs, (up_out, down_out) = refs[:count], refs[count : 2 * count], refs[2 * count :]
    for own, came, out in ((up, ups, up_out), (down, downs, down_out)):
        total, keep = arrived(state, came)
        out[0:state] = own[0:state] + own[state : state + 1] * total
        out[state:] = own[state:] * keep


def spread_kernel(state, count, *refs):
    parts = refs[:PLANE]
    ups = refs[PLANE : PLANE + count]
    downs = refs[PLANE + count : PLANE + 2 * count]
    outs = refs[PLANE + 2 * count :]
    _, own = place()
    entering, returning = arrived(state, ups)[0], arrived(state, downs)[0]
    for at in range(PLANE):

        @pl.when(own == at)
        def _(at=at):
            block = [parts[j ^ at] for j in range(PLANE)]
            keeps = [ref[2 * state : 2 * state + 1] for ref in block]
            total = entering
            for j in range(PLANE):
                outs[j ^ at][0:state] = total
                if j < PLANE - 1:
                    total = total * keeps[j] + block[j][0:state]
            total = returning
            for j in reversed(range(PLANE)):
                outs[j ^ at][state:] = total
                if j > 0:
                    total = total * keeps[j] + block[j][state : 2 * state]


def finish_kernel(
    head_dim, own_ref, logits, bias, decay, skip, weight_cols, factor_cols, stride_ref, log_ref,
    features, cotangent, writes, reads, inside, feature_part, write_part, read_part, skip_part,
    part0, part1, part2, part3, have0, have1, have2, have3,
    mixed, feature_grad, write_grad, read_grad, step_grad, sums, row_acc, col_acc, last_acc, read_acc, write_acc, skip_acc,
):
    heads, length = logits.shape
    state = writes.shape[1]
    width = features.shape[1]
    step = pl.program_id(0)
    quarter = own_ref[0] ^ step
    first = quarter * (heads // PLANE)

    @pl.when(step == 0)
    def _():
        for ref in (row_acc, col_acc, last_acc, read_acc, write_acc, skip_acc):
            ref[...] = jnp.zeros_like(ref)

    spread = spread_matrix(heads, first, width, head_dim)
    gather = gather_matrix(first, width, head_dim)
    skip_stack = stacked_columns(jnp.broadcast_to(column(skip[...]), (heads, LANES)))
    skip_wide = matmul(skip_stack[0:16], spread)[0:1]
    factor = matmul(factor_cols[...], spread)
    weight = matmul(weight_cols[...], spread)
    feature = features[...].astype(F32)
    grad = cotangent[...].astype(F32)
    writes2 = jnp.concatenate([writes[...]] * 2, axis=1)
    reads2 = jnp.concatenate([reads[...]] * 2, axis=1)

    def add_heads(ref, value):
        high, low = split2(value)
        ref[...] += matmul(high, gather) + matmul(low, gather)

    for distance, (part, have) in enumerate(
        zip((part0, part1, part2, part3), (have0, have1, have2, have3))
    ):

        @pl.when(step == distance)
        def _(part=part, have=have):
            entering = have[0:state]
            stack = jnp.concatenate(split2(entering), axis=0)
            total = inside[...] + factor * matmul(reads2, stack)
            mixed[...] = (total + skip_wide * feature).astype(BF16)
            add_heads(row_acc, grad * total)
            high, low = split2(factor * grad)
            read_acc[...] += matmul_nt(high, stack) + matmul_nt(low, stack)
            returning = have[state:]
            keep = part[2 * state : 2 * state + 1]
            leaving = keep * entering + part[0:state]
            add_heads(last_acc, jnp.sum((returning * leaving).reshape(state // 8, 8, width), axis=0))
            stack = jnp.concatenate(split2(returning), axis=0)
            total = feature_part[...] + weight * matmul(writes2, stack)
            feature_grad[...] = (total + skip_wide * grad).astype(BF16)
            add_heads(col_acc, feature * total)
            high, low = split2(weight * feature)
            write_acc[...] += matmul_nt(high, stack) + matmul_nt(low, stack)

    add_heads(skip_acc, jnp.broadcast_to(skip_part[...], (8, width)))

    @pl.when(step == PLANE - 1)
    def _():
        read_grad[...] = (read_part[...] + read_acc[:, :state] + read_acc[:, state:]).astype(BF16)
        write_grad[...] = (write_part[...] + write_acc[:, :state] + write_acc[:, state:]).astype(BF16)
        rows = row_acc[...].T[:heads]
        cols = col_acc[...].T[:heads]
        last = column(jnp.sum(last_acc[...], axis=0, keepdims=True))[:heads]
        stride = stride_ref[...]
        gap_grad = rows - cols + jnp.where(iota((heads, length), 1) == length - 1, last, 0.0)
        onward = jnp.where(iota((length, length), 0) >= iota((length, length), 1), 1.0, 0.0).astype(BF16)
        parts = matmul(jnp.concatenate(split3(gap_grad), axis=0), onward)
        log_grad = parts[:heads] + parts[heads : 2 * heads] + parts[2 * heads :]
        rate = column(-jnp.exp(decay[...]))
        slope = 1.0 / (1.0 + jnp.exp(-(logits[...] + column(bias[...]))))
        step_value = (cols / stride + rate * log_grad) * slope
        step_grad[...] = step_value
        bias_sum = jnp.sum(step_value, axis=1, keepdims=True)
        decay_sum = jnp.sum(log_grad * log_ref[...], axis=1, keepdims=True)
        lane = iota((heads, LANES), 1)
        table = jnp.where(lane == 0, bias_sum, jnp.where(lane == 1, decay_sum, 0.0))
        table = jnp.concatenate([table, jnp.zeros((LANES - heads, LANES), F32)], axis=0).T[0:8]
        sums[...] = jnp.where(iota((8, LANES), 0) == 2, skip_acc[...], table)


def params(**more):
    return pltpu.CompilerParams(vmem_limit_bytes=VMEM_BYTES, **more)


def cost(flops, size):
    return pl.CostEstimate(flops=flops, bytes_accessed=size, transcendentals=0)


def struct(shape, dtype=F32):
    return jax.ShapeDtypeStruct(shape, dtype)


def local(
    features, write_keys, read_queries, step_logits, step_bias, decay_log, skip_gain, doc_starts, out_grad
):
    features, writes, reads, logits, cotangent = (
        features[0], write_keys[0], read_queries[0], step_logits[0], out_grad[0]
    )
    length, wide = features.shape
    heads = logits.shape[0]
    state = writes.shape[1]
    head_dim = wide // heads
    width = wide // PLANE
    bias, decay, skip = step_bias[None], decay_log[None], skip_gain[None]
    blocks = lax.axis_size("ctx")

    def exchange(value, distance):
        return lax.ppermute(value, "ctx", [(k, k ^ distance) for k in range(blocks)])

    def shift(value, distance):
        pairs = [(k, k + distance) for k in range(blocks) if 0 <= k + distance < blocks]
        return lax.ppermute(value, "ctx", pairs)

    stack = struct((length, LANES), BF16)
    small = struct((heads, length))
    message = struct((2 * state + 8, width))
    *sent, weight_cols, factor_cols, cum_cols, cum_rows, stride, log_decay = pl.pallas_call(
        functools.partial(states_kernel, head_dim),
        out_shape=[message] * PLANE + [stack] * 3 + [small] * 3,
        in_specs=[SMEM] + [VMEM] * 7,
        out_specs=[VMEM] * (PLANE + 6),
        compiler_params=params(),
        cost_estimate=cost(4 * 10**9, 6 * 10**6),
        name="states",
    )(doc_starts, logits, bias, decay, features, cotangent, writes, reads)
    parts = [sent[0]] + [exchange(sent[d], d) for d in range(1, PLANE)]

    inside, feature_part, write_part, read_part, skip_part = pl.pallas_call(
        functools.partial(inner_kernel, head_dim),
        out_shape=[
            struct((length, wide)),
            struct((length, wide)),
            struct((length, state)),
            struct((length, state)),
            struct((1, wide)),
        ],
        in_specs=[SMEM] + [VMEM] * 6,
        out_specs=[VMEM] * 5,
        scratch_shapes=[pltpu.VMEM((length, length), F32)] * 3,
        compiler_params=params(),
        cost_estimate=cost(2 * 10**10, 10**7),
        name="inner",
    )(doc_starts, cum_cols, cum_rows, features, cotangent, writes, reads)

    sums_shape = struct((state + 8, width))
    up, down = pl.pallas_call(
        functools.partial(plane_kernel, state),
        out_shape=[sums_shape] * 2,
        in_specs=[VMEM] * PLANE,
        out_specs=[VMEM] * 2,
        compiler_params=params(),
        cost_estimate=cost(10**6, 4 * 10**6),
        name="plane",
    )(*parts)
    planes = blocks // PLANE
    ups, downs = [], []
    near_up, near_down = up, down
    reach = 1
    while reach < planes:
        ups.append(shift(near_up, PLANE * reach))
        downs.append(shift(near_down, -PLANE * reach))
        reach *= 2
        if reach < planes:
            near_up, near_down = pl.pallas_call(
                functools.partial(link_kernel, state, len(ups)),
                out_shape=[sums_shape] * 2,
                in_specs=[VMEM] * (2 + 2 * len(ups)),
                out_specs=[VMEM] * 2,
                compiler_params=params(),
                cost_estimate=cost(10**6, 2 * 10**6),
                name="link",
            )(up, down, *ups, *downs)
    haves = pl.pallas_call(
        functools.partial(spread_kernel, state, len(ups)),
        out_shape=[struct((2 * state, width))] * PLANE,
        in_specs=[VMEM] * (PLANE + 2 * len(ups)),
        out_specs=[VMEM] * PLANE,
        compiler_params=params(),
        cost_estimate=cost(10**6, 6 * 10**6),
        name="spread",
    )(*parts, *ups, *downs)
    haves = [haves[0]] + [exchange(haves[d], d) for d in range(1, PLANE)]

    def whole(shape):
        return pl.BlockSpec(shape, lambda step, own: (0,) * len(shape))

    by_quarter = pl.BlockSpec((length, width), lambda step, own: (0, own[0] ^ step))
    row_quarter = pl.BlockSpec((1, width), lambda step, own: (0, own[0] ^ step))
    row_small = whole((1, heads))
    tokens = whole((length, state))
    own = jnp.reshape(lax.rem(lax.axis_index("ctx"), PLANE), (1,))
    mixed, feature_grad, write_grad, read_grad, step_grad, sums = pl.pallas_call(
        functools.partial(finish_kernel, head_dim),
        out_shape=[
            struct((length, wide), BF16),
            struct((length, wide), BF16),
            struct((length, state), BF16),
            struct((length, state), BF16),
            small,
            struct((8, LANES)),
        ],
        grid_spec=pltpu.PrefetchScalarGridSpec(
            num_scalar_prefetch=1,
            grid=(PLANE,),
            in_specs=[whole((heads, length))]
            + [row_small] * 3
            + [whole((length, LANES))] * 2
            + [whole((heads, length))] * 2
            + [by_quarter] * 2
            + [tokens] * 2
            + [by_quarter] * 2
            + [tokens] * 2
            + [row_quarter]
            + [whole((2 * state + 8, width))] * PLANE
            + [whole((2 * state, width))] * PLANE,
            out_specs=[
                by_quarter,
                by_quarter,
                tokens,
                tokens,
                whole((heads, length)),
                whole((8, LANES)),
            ],
            scratch_shapes=[
                pltpu.VMEM((length, LANES), F32),
                pltpu.VMEM((length, LANES), F32),
                pltpu.VMEM((8, LANES), F32),
                pltpu.VMEM((length, 2 * state), F32),
                pltpu.VMEM((length, 2 * state), F32),
                pltpu.VMEM((8, LANES), F32),
            ],
        ),
        compiler_params=params(dimension_semantics=("arbitrary",)),
        cost_estimate=cost(10**10, 2 * 10**7),
        name="finish",
    )(
        own, logits, bias, decay, skip, weight_cols, factor_cols, stride, log_decay, features, cotangent,
        writes, reads, inside, feature_part, write_part, read_part, skip_part, *sent, *haves,
    )
    for distance in [2**bit for bit in range(blocks.bit_length() - 1)]:
        sums = sums + exchange(sums, distance)
    members = lax.axis_size("dp")
    for distance in [2**bit for bit in range(members.bit_length() - 1)]:
        sums = sums + lax.ppermute(sums, "dp", [(k, k ^ distance) for k in range(members)])
    return (
        mixed[None],
        feature_grad[None],
        write_grad[None],
        read_grad[None],
        step_grad[None],
        sums[0, :heads],
        sums[1, :heads],
        sums[2, :heads],
    )


def solution(mesh):
    by_tokens = P("dp", "ctx", None)
    by_heads = P("dp", None, "ctx")
    in_specs = (by_tokens, by_tokens, by_tokens, by_heads, P(), P(), P(), P("dp", None), by_tokens)
    out_specs = (by_tokens, by_tokens, by_tokens, by_tokens, by_heads, P(), P(), P())
    return jax.shard_map(local, mesh=mesh, in_specs=in_specs, out_specs=out_specs, check_vma=False)
```

time: 522 us -> 154 us (0.30)
  local copies, waits for them, and re-layouts: 127 us -> 4.13 us
  matrix products: 121 us -> 0 us
  other arithmetic: 75.8 us -> 0.7 us
  waiting for transfers between devices: 137 us -> 79.6 us
  Pallas kernels: 0 us -> 49.4 us
  blocking collectives: 39.5 us -> 0 us
    dot_general x69 -> x0, matrix products: 121 us -> none  [the longest x60 94.2 us: intra_group(): result = jnp.einsum('htu,uhp->thp', mixing, per_head, precision=EXACT)]
    ppermute x11 -> x15, waiting for transfers between devices: 137 us -> 79.6 us  [the longest x10 54 us: exchange(): lax.ppermute(value, 'ctx', [(k, k ^ distance) for k in range(blocks)])]
    dynamic_update_slice x60 -> x0, local copies, waits for them, and re-layouts: 51.9 us -> none  [block_main(): lax.map(jax.checkpoint(one_group), (cum_stack, stride_stack, feature_stack))]
    pallas_call x0 -> x6, Pallas kernels: none -> 49.4 us  [the longest x1 19.8 us: local(): pl.pallas_call(functools.partial(inner_kernel, head_dim), out_shape=[stru...]
    psum x1 -> x0, blocking collectives: 39.5 us -> none  [local(): lax.psum((bias_main + bias_state, decay_main + decay_state, skip_total),...]
    squeeze x40 -> x1, local copies, waits for them, and re-layouts: 33.1 us -> 0.52 us  [local(): sums[2, :heads]]
    and x21 -> x0, other arithmetic: 17.4 us -> none  [block_main(): (segment[:, None] == segment[None, :]) & (ordinal[:, None] >= ordinal[Non...]
    mul x33 -> x0, local copies, waits for them, and re-layouts: 14.6 us -> none  [the longest x20 13.6 us: intra_group(): mixing = decays * scores[None] * stride_group[:, None, :]]
  transfers between devices with their start and end apart: 11 -> 15, of which waited for: 5 -> 12; matrix products, arithmetic and copies ran while one was open for 48% -> 0% of each run, Pallas kernels for 0% -> 13%
where the time goes in v1:
time: 154 us
  waiting for transfers between devices  79.6 us (52%)
  Pallas kernels  49.4 us (32%)
  starting transfers between devices  19.2 us (12%)
  local copies, waits for them, and re-layouts  4.13 us (3%)
    ppermute x10, waiting for transfers between devices, exchange(): lax.ppermute(value, 'ctx', [(k, k ^ distance) for k in range(blocks)])  54 us
    ppermute x4, waiting for transfers between devices, shift(): return lax.ppermute(value, 'ctx', pairs)  24.5 us
    pallas_call x1, Pallas kernels, local(): pl.pallas_call(functools.partial(inner_kernel, head_dim), out_shape=[stru...  19.8 us
    pallas_call x1, Pallas kernels, local(): pl.pallas_call(functools.partial(finish_kernel, head_dim), out_shape=[str...  14.5 us
    ppermute x4, starting transfers between devices, shift(): return lax.ppermute(value, 'ctx', pairs)  10.6 us
    ppermute x10, starting transfers between devices, exchange(): lax.ppermute(value, 'ctx', [(k, k ^ distance) for k in range(blocks)])  8.67 us
    pallas_call x1, Pallas kernels, local(): pl.pallas_call(functools.partial(states_kernel, head_dim), out_shape=[mes...  6.05 us
    pallas_call x1, Pallas kernels, local(): pl.pallas_call(functools.partial(spread_kernel, state, len(ups)), out_sha...  4.19 us
  transfers between devices with their start and end apart: 15, of which 12 were waited for; matrix products, arithmetic and copies ran while one was open for 0% of the time, Pallas kernels for 13%

profile of v1, /device:TPU:0, one launch (start us, length us, event | category | flops | bytes accessed | tf_op | source)
XLA Modules:
  0.0 153.8 jit_solution(3343906087959422768)
XLA Ops:
  0.6 6.0 %states.1 = (f32[264,640]{1,0:T(8,128)}, f32[264,640]{1,0:T(8,128)}, f32[264,640]{1,0:T(8,128)}, f32[264,640]{1,0:T(8,128)}, bf16[256,128]{1,0:T(8,128)(2,1)}, /...) custom-call(s32[1,4]{1,0:T(1,128)} %starts.3, ...), custom_call_target="tpu_custom_call" | custom-call | flops 4000000000 | bytes 6000000 | tf_op jit(solution)/shard_map/states/pallas_call | solution.py:368
  6.7 3.0 %collective-permute-start = (f32[264,640]{1,0:T(8,128)}, f32[264,640]{1,0:T(8,128)S(1)}, u32[]{:S(2)}, u32[]{:S(2)}) collective-permute-start(f32[264,640]{1,0:T(8,128)} %get-tuple-element.49.part1), channel_id=1, source_target_pairs={{0,1},{1,0},{2,3},{3,2},{4,5},{5,4},{6,7},{7,6},{8,9},{9,8},{10,11... | collective-permute-start | bytes 2027528 | tf_op jit(solution)/shard_map/ppermute | solution.py:359
  9.7 1.5 collective-permute-start.1
  11.2 14.7 %collective-permute-done.part1.refs_1_ = f32[264,640]{1,0:T(8,128)S(1)} collective-permute-done((f32[264,640]{1,0:T(8,128)}, f32[264,640]{1,0:T(8,128)S(1)}, u32[]{:S(2)}, u32[]{:S(2)}) %collective-permute-start) | collective-permute-done | bytes 675872 | tf_op jit(solution)/shard_map/ppermute | solution.py:359
  25.9 15.1 %collective-permute-done.1.part2.refs_2_ = f32[264,640]{1,0:T(8,128)S(1)} collective-permute-done((f32[264,640]{1,0:T(8,128)}, f32[264,640]{1,0:T(8,128)S(1)}, u32[]{:S(2)}, u32[]{:S(2)}) %collective-permute-start.1) | collective-permute-done | bytes 675872 | tf_op jit(solution)/shard_map/ppermute | solution.py:359
  42.1 2.7 %plane.1 = (f32[136,640]{1,0:T(8,128)}, f32[136,640]{1,0:T(8,128)}) custom-call(f32[264,640]{1,0:T(8,128)} %get-tuple-element.48.part0.refs_0_, f32[264,640]{1,0:T(8,128)} %copy-done, f32[264,640]{1,0:T(8,128)} %copy-done.1, f32[264,640]{1,0:T(8,128)} %copy-done.2), custom_call_target="tpu_custom_call" | custom-call | flops 1000000 | bytes 4000000 | tf_op jit(solution)/shard_map/plane/pallas_call | solution.py:397
  44.8 3.5 %collective-permute-start.3 = (f32[136,640]{1,0:T(8,128)}, f32[136,640]{1,0:T(8,128)S(1)}, u32[]{:S(2)}, u32[]{:S(2)}) collective-permute-start(f32[136,640]{1,0:T(8,128)} %get-tuple-element.52.up), channel_id=1, source_target_pairs={{0,4},{1,5},{2,6},{3,7},{4,8},{5,9},{6,10},{7,11},{8,12},{9,13},{1... | collective-permute-start | bytes 1044488 | tf_op jit(solution)/shard_map/ppermute | solution.py:363
  48.3 1.3 collective-permute-start.4
  49.6 5.1 %collective-permute-done.3.refs_0_.refs_4_ = f32[136,640]{1,0:T(8,128)S(1)} collective-permute-done((f32[136,640]{1,0:T(8,128)}, f32[136,640]{1,0:T(8,128)S(1)}, u32[]{:S(2)}, u32[]{:S(2)}) %collective-permute-start.3) | collective-permute-done | bytes 348192 | tf_op jit(solution)/shard_map/ppermute | solution.py:363
  54.7 4.0 %collective-permute-done.4.refs_1_.refs_6_ = f32[136,640]{1,0:T(8,128)S(1)} collective-permute-done((f32[136,640]{1,0:T(8,128)}, f32[136,640]{1,0:T(8,128)S(1)}, u32[]{:S(2)}, u32[]{:S(2)}) %collective-permute-start.4) | collective-permute-done | bytes 348192 | tf_op jit(solution)/shard_map/ppermute | solution.py:363
  59.4 2.2 %link.1 = (f32[136,640]{1,0:T(8,128)}, f32[136,640]{1,0:T(8,128)}) custom-call(f32[136,640]{1,0:T(8,128)} %get-tuple-element.52.up, f32[136,640]{1,0:T(8,128)} %get-tuple-element.53.down, f32[136,640]{1,0:T(8,128)} %copy-done.3, f32[136,640]{1,0:T(8,128)} %copy-done.4), custom_call_target="tpu_custom_call" | custom-call | flops 1000000 | bytes 2000000 | tf_op jit(solution)/shard_map/link/pallas_call | solution.py:415
  61.6 4.5 %collective-permute-start.5 = (f32[136,640]{1,0:T(8,128)}, f32[136,640]{1,0:T(8,128)S(1)}, u32[]{:S(2)}, u32[]{:S(2)}) collective-permute-start(f32[136,640]{1,0:T(8,128)} %get-tuple-element.54), channel_id=1, source_target_pairs={{0,8},{1,9},{2,10},{3,11},{4,12},{5,13},{6,14},{7,15},{16,24},{17,... | collective-permute-start | bytes 1044488 | tf_op jit(solution)/shard_map/ppermute | solution.py:363
  67.4 3.9 %collective-permute-done.5.refs_5_ = f32[136,640]{1,0:T(8,128)S(1)} collective-permute-done((f32[136,640]{1,0:T(8,128)}, f32[136,640]{1,0:T(8,128)S(1)}, u32[]{:S(2)}, u32[]{:S(2)}) %collective-permute-start.5) | collective-permute-done | bytes 348192 | tf_op jit(solution)/shard_map/ppermute | solution.py:363
  71.4 11.4 %collective-permute-done.6.refs_7_ = f32[136,640]{1,0:T(8,128)S(1)} collective-permute-done((f32[136,640]{1,0:T(8,128)}, f32[136,640]{1,0:T(8,128)S(1)}, u32[]{:S(2)}, u32[]{:S(2)}) %collective-permute-start.6) | collective-permute-done | bytes 348192 | tf_op jit(solution)/shard_map/ppermute | solution.py:363
  83.5 4.2 %spread.1 = (f32[256,640]{1,0:T(8,128)}, f32[256,640]{1,0:T(8,128)}, f32[256,640]{1,0:T(8,128)}, f32[256,640]{1,0:T(8,128)}) custom-call(f32[264,640]{1,0:T(8,128)} %get-tuple-element.48.part0.refs_0_, f32[264,640]{1,0:T(8,128)} %copy-done, f32[264,640]{1,0:T(8,128)} %copy-done.1, f32[264,640]{1,0:T(8,128)} %copy-done.2, f32[136,640]{1,0:T(8,128)} %copy-done.3, ...), custom_call_target="tpu_custom_call" | custom-call | flops 1000000 | bytes 6000000 | tf_op jit(solution)/shard_map/spread/pallas_call | solution.py:424
  87.7 1.9 %collective-permute-start.7 = (f32[256,640]{1,0:T(8,128)}, f32[256,640]{1,0:T(8,128)S(1)}, u32[]{:S(2)}, u32[]{:S(2)}) collective-permute-start(f32[256,640]{1,0:T(8,128)} %get-tuple-element.57), channel_id=1, source_target_pairs={{0,1},{1,0},{2,3},{3,2},{4,5},{5,4},{6,7},{7,6},{8,9},{9,8},{10,11... | collective-permute-start | bytes 1966088 | tf_op jit(solution)/shard_map/ppermute | solution.py:359
  89.6 1.6 %collective-permute-start.9 = (f32[256,640]{1,0:T(8,128)}, f32[256,640]{1,0:T(8,128)S(1)}, u32[]{:S(2)}, u32[]{:S(2)}) collective-permute-start(f32[256,640]{1,0:T(8,128)} %get-tuple-element.59), channel_id=1, source_target_pairs={{0,3},{1,2},{2,1},{3,0},{4,7},{5,6},{6,5},{7,4},{8,11},{9,10},{10,... | collective-permute-start | bytes 1966088 | tf_op jit(solution)/shard_map/ppermute | solution.py:359
  91.2 19.8 %inner.1 = (f32[256,2560]{1,0:T(8,128)}, f32[256,2560]{1,0:T(8,128)}, f32[256,128]{1,0:T(8,128)}, f32[256,128]{1,0:T(8,128)}, f32[1,2560]{1,0:T(1,128)}) custom-call(s32[1,4]{1,0:T(1,128)} %starts.3, bf16[256,128]{1,0:T(8,128)(2,1)} %get-tuple-element.41.cum_cols, f32[40,256]{1,0:T(8,128)} %get-tuple-element.42.cum_rows, bf16[256,2560]{1,0:T(8,128)(2,1)} %bitcast.21, ...), custom_call_target="tpu_custom_call" | custom-call | flops 20000000000 | bytes 10000000 | tf_op jit(solution)/shard_map/inner/pallas_call | solution.py:379
  111.0 9.2 %collective-permute-done.8.have2 = f32[256,640]{1,0:T(8,128)S(1)} collective-permute-done((f32[256,640]{1,0:T(8,128)}, f32[256,640]{1,0:T(8,128)S(1)}, u32[]{:S(2)}, u32[]{:S(2)}) %collective-permute-start.8) | collective-permute-done | bytes 655392 | tf_op jit(solution)/shard_map/ppermute | solution.py:359
  121.3 14.5 %finish.1 = (bf16[256,2560]{1,0:T(8,128)(2,1)}, bf16[256,2560]{1,0:T(8,128)(2,1)}, bf16[256,128]{1,0:T(8,128)(2,1)}, bf16[256,128]{1,0:T(8,128)(2,1)}, f32[40,256]{1,0:T(8,128)}, /*index=5*/f32[8,128]{1,0:T(8,128)}) custom-call(s32[1]{0:T(128)} %bitcast.own_ref, f32[40,256]{1,0:T(8,128)} %bitcast.33, f32[1,40]{1,0:T(1,128)} %bitcast.35, f32[1,40]{1,0:T(1,128)} %bitcast.37, ...), custom_call_target="tpu_custom_call" | custom-call | flops 10000000000 | bytes 20000000 | tf_op jit(solution)/shard_map/finish/pallas_call | solution.py:443
  136.1 3.5 %collective-permute-done.10 = f32[8,128]{1,0:T(8,128)S(1)} collective-permute-done((f32[8,128]{1,0:T(8,128)}, f32[8,128]{1,0:T(8,128)S(1)}, u32[]{:S(2)}, u32[]{:S(2)}) %collective-permute-start.10) | collective-permute-done | bytes 4128 | tf_op jit(solution)/shard_map/ppermute | solution.py:359
  140.6 3.3 %collective-permute-done.11 = f32[8,128]{1,0:T(8,128)S(1)} collective-permute-done((f32[8,128]{1,0:T(8,128)S(1)}, f32[8,128]{1,0:T(8,128)S(1)}, u32[]{:S(2)}, u32[]{:S(2)}) %collective-permute-start.11) | collective-permute-done | bytes 4128 | tf_op jit(solution)/shard_map/ppermute | solution.py:359
  144.0 3.6 %collective-permute-done.12 = f32[8,128]{1,0:T(8,128)S(1)} collective-permute-done((f32[8,128]{1,0:T(8,128)S(1)}, f32[8,128]{1,0:T(8,128)S(1)}, u32[]{:S(2)}, u32[]{:S(2)}) %collective-permute-start.12) | collective-permute-done | bytes 4128 | tf_op jit(solution)/shard_map/ppermute | solution.py:359
  147.6 4.5 %collective-permute-done.13 = f32[8,128]{1,0:T(8,128)S(1)} collective-permute-done((f32[8,128]{1,0:T(8,128)S(1)}, f32[8,128]{1,0:T(8,128)S(1)}, u32[]{:S(2)}, u32[]{:S(2)}) %collective-permute-start.13) | collective-permute-done | bytes 4128 | tf_op jit(solution)/shard_map/ppermute | solution.py:359
  (38 shorter events, 8.0 us)
Async XLA Ops:
  6.7 19.2 %collective-permute-start = (f32[264,640]{1,0:T(8,128)}, f32[264,640]{1,0:T(8,128)S(1)}, u32[]{:S(2)}, u32[]{:S(2)}) collective-permute-start(f32[264,640]{1,0:T(8,128)} %get-tuple-element.49.part1), channel_id=1, source_target_pairs={{0,1},{1,0},{2,3},{3,2},{4,5},{5,4},{6,7},{7,6},{8,9},{9,8},{10,11... | collective-permute-start | bytes 2027528 | tf_op jit(solution)/shard_map/ppermute | solution.py:359
  9.7 31.3 %collective-permute-start.1 = (f32[264,640]{1,0:T(8,128)}, f32[264,640]{1,0:T(8,128)S(1)}, u32[]{:S(2)}, u32[]{:S(2)}) collective-permute-start(f32[264,640]{1,0:T(8,128)} %get-tuple-element.50.part2), channel_id=1, source_target_pairs={{0,2},{1,3},{2,0},{3,1},{4,6},{5,7},{6,4},{7,5},{8,10},{9,11},{10,... | collective-permute-start | bytes 2027528 | tf_op jit(solution)/shard_map/ppermute | solution.py:359
  11.2 29.8 %collective-permute-start.2 = (f32[264,640]{1,0:T(8,128)}, f32[264,640]{1,0:T(8,128)S(1)}, u32[]{:S(2)}, u32[]{:S(2)}) collective-permute-start(f32[264,640]{1,0:T(8,128)} %get-tuple-element.51.part3), channel_id=1, source_target_pairs={{0,3},{1,2},{2,1},{3,0},{4,7},{5,6},{6,5},{7,4},{8,11},{9,10},{10,... | collective-permute-start | bytes 2027528 | tf_op jit(solution)/shard_map/ppermute | solution.py:359
  25.9 15.1 %copy-start = (f32[264,640]{1,0:T(8,128)}, f32[264,640]{1,0:T(8,128)S(1)}, u32[]{:S(2)}) copy-start(f32[264,640]{1,0:T(8,128)S(1)} %collective-permute-done.part1.refs_1_) | copy-start | bytes 2027524
  41.0 0.8 copy-start.1
  41.0 1.1 copy-start.2
  44.8 9.9 %collective-permute-start.3 = (f32[136,640]{1,0:T(8,128)}, f32[136,640]{1,0:T(8,128)S(1)}, u32[]{:S(2)}, u32[]{:S(2)}) collective-permute-start(f32[136,640]{1,0:T(8,128)} %get-tuple-element.52.up), channel_id=1, source_target_pairs={{0,4},{1,5},{2,6},{3,7},{4,8},{5,9},{6,10},{7,11},{8,12},{9,13},{1... | collective-permute-start | bytes 1044488 | tf_op jit(solution)/shard_map/ppermute | solution.py:363
  48.3 10.4 %collective-permute-start.4 = (f32[136,640]{1,0:T(8,128)}, f32[136,640]{1,0:T(8,128)S(1)}, u32[]{:S(2)}, u32[]{:S(2)}) collective-permute-start(f32[136,640]{1,0:T(8,128)} %get-tuple-element.53.down), channel_id=1, source_target_pairs={{4,0},{5,1},{6,2},{7,3},{8,4},{9,5},{10,6},{11,7},{12,8},{13,9},{1... | collective-permute-start | bytes 1044488 | tf_op jit(solution)/shard_map/ppermute | solution.py:363
  54.7 4.0 %copy-start.3 = (f32[136,640]{1,0:T(8,128)}, f32[136,640]{1,0:T(8,128)S(1)}, u32[]{:S(2)}) copy-start(f32[136,640]{1,0:T(8,128)S(1)} %collective-permute-done.3.refs_0_.refs_4_) | copy-start | bytes 1044484
  61.6 9.7 %collective-permute-start.5 = (f32[136,640]{1,0:T(8,128)}, f32[136,640]{1,0:T(8,128)S(1)}, u32[]{:S(2)}, u32[]{:S(2)}) collective-permute-start(f32[136,640]{1,0:T(8,128)} %get-tuple-element.54), channel_id=1, source_target_pairs={{0,8},{1,9},{2,10},{3,11},{4,12},{5,13},{6,14},{7,15},{16,24},{17,... | collective-permute-start | bytes 1044488 | tf_op jit(solution)/shard_map/ppermute | solution.py:363
  66.1 16.7 %collective-permute-start.6 = (f32[136,640]{1,0:T(8,128)}, f32[136,640]{1,0:T(8,128)S(1)}, u32[]{:S(2)}, u32[]{:S(2)}) collective-permute-start(f32[136,640]{1,0:T(8,128)} %get-tuple-element.55), channel_id=1, source_target_pairs={{8,0},{9,1},{10,2},{11,3},{12,4},{13,5},{14,6},{15,7},{24,16},{25,... | collective-permute-start | bytes 1044488 | tf_op jit(solution)/shard_map/ppermute | solution.py:363
  71.4 11.4 %copy-start.5 = (f32[136,640]{1,0:T(8,128)}, f32[136,640]{1,0:T(8,128)S(1)}, u32[]{:S(2)}) copy-start(f32[136,640]{1,0:T(8,128)S(1)} %collective-permute-done.5.refs_5_) | copy-start | bytes 1044484
  82.8 0.7 copy-start.6
  87.7 23.3 %collective-permute-start.7 = (f32[256,640]{1,0:T(8,128)}, f32[256,640]{1,0:T(8,128)S(1)}, u32[]{:S(2)}, u32[]{:S(2)}) collective-permute-start(f32[256,640]{1,0:T(8,128)} %get-tuple-element.57), channel_id=1, source_target_pairs={{0,1},{1,0},{2,3},{3,2},{4,5},{5,4},{6,7},{7,6},{8,9},{9,8},{10,11... | collective-permute-start | bytes 1966088 | tf_op jit(solution)/shard_map/ppermute | solution.py:359
  89.6 30.6 %collective-permute-start.8 = (f32[256,640]{1,0:T(8,128)}, f32[256,640]{1,0:T(8,128)S(1)}, u32[]{:S(2)}, u32[]{:S(2)}) collective-permute-start(f32[256,640]{1,0:T(8,128)} %get-tuple-element.58), channel_id=1, source_target_pairs={{0,2},{1,3},{2,0},{3,1},{4,6},{5,7},{6,4},{7,5},{8,10},{9,11},{10,... | collective-permute-start | bytes 1966088 | tf_op jit(solution)/shard_map/ppermute | solution.py:359
  89.6 30.6 %collective-permute-start.9 = (f32[256,640]{1,0:T(8,128)}, f32[256,640]{1,0:T(8,128)S(1)}, u32[]{:S(2)}, u32[]{:S(2)}) collective-permute-start(f32[256,640]{1,0:T(8,128)} %get-tuple-element.59), channel_id=1, source_target_pairs={{0,3},{1,2},{2,1},{3,0},{4,7},{5,6},{6,5},{7,4},{8,11},{9,10},{10,... | collective-permute-start | bytes 1966088 | tf_op jit(solution)/shard_map/ppermute | solution.py:359
  111.0 9.2 %copy-start.7 = (f32[256,640]{1,0:T(8,128)}, f32[256,640]{1,0:T(8,128)S(1)}, u32[]{:S(2)}) copy-start(f32[256,640]{1,0:T(8,128)S(1)} %collective-permute-done.7.have1) | copy-start | bytes 1966084
  120.2 0.8 copy-start.8
  120.2 1.1 copy-start.9
  135.8 3.9 %collective-permute-start.10 = (f32[8,128]{1,0:T(8,128)}, f32[8,128]{1,0:T(8,128)S(1)}, u32[]{:S(2)}, u32[]{:S(2)}) collective-permute-start(f32[8,128]{1,0:T(8,128)} %get-tuple-element.65), channel_id=1, source_target_pairs={{0,1},{1,0},{2,3},{3,2},{4,5},{5,4},{6,7},{7,6},{8,9},{9,8},{10,11... | collective-permute-start | bytes 12296 | tf_op jit(solution)/shard_map/ppermute | solution.py:359
  140.4 3.6 %collective-permute-start.11 = (f32[8,128]{1,0:T(8,128)S(1)}, f32[8,128]{1,0:T(8,128)S(1)}, u32[]{:S(2)}, u32[]{:S(2)}) collective-permute-start(f32[8,128]{1,0:T(8,128)S(1)} %add.15), channel_id=1, source_target_pairs={{0,2},{1,3},{2,0},{3,1},{4,6},{5,7},{6,4},{7,5},{8,10},{9,11},{10,... | collective-permute-start | bytes 12296 | tf_op jit(solution)/shard_map/ppermute | solution.py:359
  144.0 3.6 %collective-permute-start.12 = (f32[8,128]{1,0:T(8,128)S(1)}, f32[8,128]{1,0:T(8,128)S(1)}, u32[]{:S(2)}, u32[]{:S(2)}) collective-permute-start(f32[8,128]{1,0:T(8,128)S(1)} %add.16), channel_id=1, source_target_pairs={{0,4},{1,5},{2,6},{3,7},{4,0},{5,1},{6,2},{7,3},{8,12},{9,13},{10,... | collective-permute-start | bytes 12296 | tf_op jit(solution)/shard_map/ppermute | solution.py:359
  147.6 4.5 %collective-permute-start.13 = (f32[8,128]{1,0:T(8,128)S(1)}, f32[8,128]{1,0:T(8,128)S(1)}, u32[]{:S(2)}, u32[]{:S(2)}) collective-permute-start(f32[8,128]{1,0:T(8,128)S(1)} %add.17), channel_id=1, source_target_pairs={{0,8},{1,9},{2,10},{3,11},{4,12},{5,13},{6,14},{7,15},{8,0},{9,1},... | collective-permute-start | bytes 12296 | tf_op jit(solution)/shard_map/ppermute | solution.py:359
  152.1 1.2 collective-permute-start.14
  (1 other events, 0.7 us)

commit v2 on v0

v2 whole, which is shorter than its diff:
```python
import functools

import jax
import jax.numpy as jnp
import numpy as np
from jax import lax
from jax.experimental import pallas as pl
from jax.experimental.pallas import tpu as pltpu
from jax.sharding import PartitionSpec as P

F32 = jnp.float32
BF16 = jnp.bfloat16
QUARTERS = 4
HALVES = 2
GROUP = QUARTERS * HALVES
LANES = 128
LOG2E = 1.4426950408889634
FAR = -1e30
VMEM = pl.BlockSpec(memory_space=pltpu.VMEM)
SMEM = pl.BlockSpec(memory_space=pltpu.SMEM)
ANY = pl.BlockSpec(memory_space=pl.ANY)


def iota(shape, axis):
    return lax.broadcasted_iota(jnp.int32, shape, axis)


def matmul(left, right):
    return lax.dot_general(left, right, (((1,), (0,)), ((), ())), preferred_element_type=F32)


def matmul_nt(left, right):
    return lax.dot_general(left, right, (((1,), (1,)), ((), ())), preferred_element_type=F32)


def split2(value):
    high = value.astype(BF16)
    return high, (value - high.astype(F32)).astype(BF16)


def split3(value):
    high = value.astype(BF16)
    rest = value - high.astype(F32)
    middle = rest.astype(BF16)
    return high, middle, (rest - middle.astype(F32)).astype(BF16)


def column(row):
    count = row.shape[1]
    eye = iota((count, count), 0) == iota((count, count), 1)
    return jnp.sum(jnp.where(eye, row, 0.0), axis=1, keepdims=True)


def stacked_columns(rows):
    parts = [part.astype(F32) for part in split3(rows)]
    spare = LANES - 3 * rows.shape[0]
    if spare:
        parts.append(jnp.zeros((spare, rows.shape[1]), F32))
    return jnp.concatenate(parts, axis=0).T.astype(BF16)


def spread_table(heads, head_dim):
    table = np.zeros((LANES, heads * head_dim), np.float32)
    for head in range(heads):
        for part in range(3):
            table[part * heads + head, head * head_dim : (head + 1) * head_dim] = 1.0
    return jnp.asarray(table, BF16)


def softplus(value):
    return jnp.maximum(value, 0.0) + jnp.log1p(jnp.exp(-jnp.abs(value)))


def document_at(starts_ref, position):
    total = jnp.zeros_like(position)
    for entry in range(starts_ref.shape[1]):
        total = total + (starts_ref[0, entry] <= position).astype(jnp.int32)
    return total


def group_place():
    return lax.rem(lax.axis_index("ctx"), GROUP)


def share_out(own, quarter_of_state, sends, scratch, part):
    mine = lax.div(own, QUARTERS)
    for distance in range(QUARTERS):
        scratch[...] = quarter_of_state(lax.rem(own ^ distance, QUARTERS))
        for half in range(HALVES):
            rows = pl.ds(pl.multiple_of((mine ^ half) * part, part), part)
            sends[half * QUARTERS + distance][0:part] = scratch[rows]


def states_kernel(starts, logits, bias, decay, spread_ref, features, writes, *refs):
    sends = refs[:GROUP]
    weight_cols, factor_cols, cum_cols, cum_rows, stride_out, log_out, scratch = refs[GROUP:]
    heads, length = logits.shape
    state = writes.shape[1]
    width = features.shape[1] // QUARTERS
    part = state // HALVES
    first = lax.axis_index("ctx") * length
    own = group_place()
    stride = softplus(logits[...] + column(bias[...]))
    log_decay = stride * column(-jnp.exp(decay[...]))
    upto = jnp.where(iota((length, length), 0) <= iota((length, length), 1), 1.0, 0.0).astype(BF16)
    parts = matmul(jnp.concatenate(split3(log_decay), axis=0), upto)
    cum = parts[:heads] + parts[heads : 2 * heads] + parts[2 * heads :]
    segment = document_at(starts, first + iota((1, length), 1))
    entry = document_at(starts, jnp.full((1, 1), first - 1, jnp.int32))
    leave = document_at(starts, jnp.full((1, 1), first + length - 1, jnp.int32))
    own_last = jnp.where(segment == leave, 1.0, 0.0)
    keep_in = jnp.where(segment == entry, 1.0, 0.0)
    weight_stack = stacked_columns(own_last * jnp.exp(cum[:, length - 1 :] - cum) * stride)
    factor_stack = stacked_columns(keep_in * jnp.exp(cum))
    write_t = writes[...].astype(F32).T.astype(BF16)

    def quarter_of_state(quarter):
        cols = pl.ds(pl.multiple_of(quarter * width, LANES), width)
        high, low = split2(features[:, cols].astype(F32) * matmul(weight_stack, spread_ref[:, cols]))
        return matmul(write_t, high) + matmul(write_t, low)

    share_out(own, quarter_of_state, sends, scratch, part)
    for distance in range(QUARTERS):
        cols = pl.ds(pl.multiple_of(lax.rem(own ^ distance, QUARTERS) * width, LANES), width)
        keep = matmul(factor_stack[length - 16 :], spread_ref[:, cols])[15:16]
        for half in range(HALVES):
            sends[half * QUARTERS + distance][part:] = jnp.broadcast_to(keep, (8, width))
    weight_cols[...] = weight_stack
    factor_cols[...] = factor_stack
    cum_cols[...] = stacked_columns(cum * LOG2E)
    cum_rows[...] = cum * LOG2E - jnp.log2(stride)
    stride_out[...] = stride
    log_out[...] = log_decay


def back_states_kernel(factor_cols, spread_ref, cotangent, reads, *refs):
    scratch = refs[-1]
    state = reads.shape[1]
    width = cotangent.shape[1] // QUARTERS
    read_t = reads[...].astype(F32).T.astype(BF16)

    def quarter_of_state(quarter):
        cols = pl.ds(pl.multiple_of(quarter * width, LANES), width)
        high, low = split2(cotangent[:, cols].astype(F32) * matmul(factor_cols[...], spread_ref[:, cols]))
        return matmul(read_t, high) + matmul(read_t, low)

    share_out(group_place(), quarter_of_state, refs[:GROUP], scratch, state // HALVES)


def inner_kernel(offset, last, starts, cum_cols, cum_rows, features, cotangent, writes, reads, *refs):
    if last:
        refs = refs[:1] + refs[5:]
    else:
        refs = refs[1:]
    if last:
        before, inside, feature_part, skip_part, write_part, read_part = refs[:6]
    else:
        inside, feature_part, skip_part, grad_out = refs[:4]
    scores_ref, mask_ref, grad_ref = refs[-3:]
    length, width = features.shape
    heads = cum_rows.shape[0]
    here = heads // QUARTERS
    head_dim = width // here
    pair = 2 * head_dim
    step = pl.program_id(0)

    @pl.when(step == 0)
    def _():
        first = lax.axis_index("ctx") * length
        segment_row = document_at(starts, first + iota((1, length), 1))
        segment_col = document_at(starts, first + iota((length, 1), 0))
        causal = iota((length, length), 0) >= iota((length, length), 1)
        mask_ref[...] = jnp.where((segment_row == segment_col) & causal, 0.0, FAR)
        scores_ref[...] = matmul_nt(reads[...], writes[...])
        grad_ref[...] = before[...] if last else jnp.zeros_like(grad_ref)

    def one_pair(at, carry):
        cols = pl.ds(pl.multiple_of(at * pair, LANES), pair)
        feature = features[:, cols]
        grad = cotangent[:, cols]
        grad_f32 = grad.astype(F32)
        grad_t = grad_f32.T.astype(BF16)
        skip_part[:, cols] = jnp.sum(grad_f32 * feature.astype(F32), axis=0, keepdims=True)
        head = (offset + step) * here + at * 2
        lane = iota((LANES, 2 * LANES), 0)
        wanted = head + lax.div(iota((LANES, 2 * LANES), 1), LANES)
        pick = (lane == wanted) | (lane == wanted + heads) | (lane == wanted + 2 * heads)
        upper = matmul(cum_cols[...], jnp.where(pick, 1.0, 0.0).astype(BF16))
        second = iota((LANES, pair), 1) >= head_dim
        back = [None, None]
        for block in range(length // LANES):
            rows = slice(block * LANES, (block + 1) * LANES)
            reach = (block + 1) * LANES
            values = []
            for side in range(2):
                high_row = jnp.concatenate([upper[rows, side * LANES : (side + 1) * LANES]] * (block + 1), axis=1)
                low_row = cum_rows[pl.ds(head + side, 1), :][:, 0:reach]
                weight = jnp.exp2(high_row - low_row + mask_ref[rows, 0:reach])
                high, low = split2(weight * scores_ref[rows, 0:reach])
                values.append(matmul(high, feature[0:reach]) + matmul(low, feature[0:reach]))
                grad_rows = grad_t[side * head_dim : (side + 1) * head_dim, rows]
                found = matmul(grad_rows, high) + matmul(grad_rows, low)
                if block:
                    found = jnp.concatenate([found[:, : reach - LANES] + back[side], found[:, reach - LANES :]], axis=1)
                back[side] = found
                only = jnp.where(second == (side == 1), grad_f32[rows], 0.0).astype(BF16)
                grad_ref[rows, 0:reach] += matmul_nt(only, feature[0:reach]) * weight
            inside[rows, cols] = jnp.where(second, values[1], values[0])
        feature_part[:, cols] = jnp.concatenate(back, axis=0).T
        return carry

    lax.fori_loop(0, here // 2, one_pair, 0)

    @pl.when(step == pl.num_programs(0) - 1)
    def _():
        score_grad = grad_ref[...]
        if last:
            high, low = split2(score_grad)
            read_part[...] = matmul(high, writes[...]) + matmul(low, writes[...])
            high, low = split2(score_grad.T)
            write_part[...] = matmul(high, reads[...]) + matmul(low, reads[...])
        else:
            grad_out[...] = score_grad


def in_order(refs, scratch):
    own = group_place()
    for distance, ref in enumerate(refs):
        scratch[own ^ distance] = ref[...]


def group_kernel(part, *refs):
    up, keeps, came = refs[-3:]
    in_order(refs[:GROUP], came)
    total = came[0, 0:part]
    keep = came[0, part:]
    for j in range(1, GROUP):
        total = total * came[j, part : part + 1] + came[j, 0:part]
        keep = keep * came[j, part:]
    up[0:part] = total
    up[part:] = keep
    for j in range(GROUP):
        keeps[j : j + 1] = came[j, part : part + 1]


def back_group_kernel(part, *refs):
    keeps, up = refs[GROUP : GROUP + 2]
    down, came = refs[-2:]
    in_order(refs[:GROUP], came)
    total = came[GROUP - 1]
    for j in reversed(range(GROUP - 1)):
        total = total * keeps[j : j + 1] + came[j]
    down[0:part] = total
    down[part:] = up[part:]


def arrived(part, came):
    total, keep = came[0][0:part], came[0][part : part + 1]
    for ref in came[1:]:
        total = total + keep * ref[0:part]
        keep = keep * ref[part : part + 1]
    return total, keep


def link_kernel(part, own, *refs):
    total, keep = arrived(part, refs[:-1])
    refs[-1][0:part] = own[0:part] + own[part : part + 1] * total
    refs[-1][part:] = own[part:] * keep


def give_out(outs, scratch):
    own = group_place()
    for distance, out in enumerate(outs):
        out[...] = scratch[own ^ distance]


def spread_kernel(part, count, *refs):
    came, out = refs[-2:]
    in_order(refs[:GROUP], came)
    total = arrived(part, refs[GROUP : GROUP + count])[0]
    for j in range(GROUP):
        out[j] = total
        if j < GROUP - 1:
            total = total * came[j, part : part + 1] + came[j, 0:part]
    give_out(refs[-2 - GROUP : -2], out)


def back_spread_kernel(part, count, *refs):
    keeps = refs[GROUP]
    came, out = refs[-2:]
    in_order(refs[:GROUP], came)
    total = arrived(part, refs[GROUP + 1 : GROUP + 1 + count])[0]
    for j in reversed(range(GROUP)):
        out[j] = total
        if j > 0:
            total = total * keeps[j : j + 1] + came[j]
    give_out(refs[-2 - GROUP : -2], out)


def head_sums(ref, value, spread):
    high, low = split2(value)
    ref[...] += matmul_nt(high, spread) + matmul_nt(low, spread)


def wide_skip(skip, heads, spread):
    stack = stacked_columns(jnp.broadcast_to(column(skip[...]), (heads, LANES)))
    return matmul(stack[0:16], spread)[0:1]


def quarter_rows(scratch):
    step = pl.program_id(0)
    return jnp.concatenate([scratch[half * QUARTERS + step] for half in range(HALVES)], axis=0)


def finish_kernel(skip, factor_cols, spread_ref, features, cotangent, reads, inside, read_part, *refs):
    haves = refs[:GROUP]
    mixed, read_grad, rows, kept, read_acc, have = refs[GROUP + 1 :]
    length, state = reads.shape
    heads = skip.shape[1]
    step = pl.program_id(0)

    @pl.when(step == 0)
    def _():
        rows[...] = jnp.zeros_like(rows)
        read_acc[...] = jnp.zeros_like(read_acc)
        in_order(haves, have)

    spread = spread_ref[...]
    factor = matmul(factor_cols[...], spread)
    grad = cotangent[...].astype(F32)
    entering = quarter_rows(have)
    kept[...] = entering * factor[length - 1 :]
    stack = jnp.concatenate(split2(entering), axis=0)
    reads2 = jnp.concatenate([reads[...]] * 2, axis=1)
    total = inside[...] + factor * matmul(reads2, stack)
    mixed[...] = (total + wide_skip(skip, heads, spread) * features[...].astype(F32)).astype(BF16)
    head_sums(rows, grad * total, spread)
    high, low = split2(factor * grad)
    read_acc[...] += matmul_nt(high, stack) + matmul_nt(low, stack)

    @pl.when(step == QUARTERS - 1)
    def _():
        read_grad[...] = (read_part[...] + read_acc[:, :state] + read_acc[:, state:]).astype(BF16)


def back_finish_kernel(
    logits, bias, decay, skip, weight_cols, stride_ref, log_ref, spread_ref,
    features, cotangent, writes, feature_part, skip_part, row_ref, kept, *refs,
):
    haves = refs[:GROUP]
    feature_grad, step_grad, sums, col_acc, last_acc, skip_acc, have = refs[GROUP:]
    heads, length = logits.shape
    state = writes.shape[1]
    width = features.shape[1]
    step = pl.program_id(0)

    @pl.when(step == 0)
    def _():
        for ref in (col_acc, last_acc, skip_acc):
            ref[...] = jnp.zeros_like(ref)
        in_order(haves, have)

    spread = spread_ref[...]
    weight = matmul(weight_cols[...], spread)
    feature = features[...].astype(F32)
    returning = quarter_rows(have)
    stack = jnp.concatenate(split2(returning), axis=0)
    writes2 = jnp.concatenate([writes[...]] * 2, axis=1)
    carried = weight * matmul(writes2, stack)
    total = feature_part[...] + carried
    feature_grad[...] = (total + wide_skip(skip, heads, spread) * cotangent[...].astype(F32)).astype(BF16)
    head_sums(col_acc, feature * total, spread)
    leaving = jnp.sum((returning * kept[...]).reshape(state // 8, 8, width), axis=0)
    leaving = leaving + jnp.sum((feature * carried).reshape(length // 8, 8, width), axis=0)
    head_sums(last_acc, leaving, spread)
    head_sums(skip_acc, jnp.broadcast_to(skip_part[...], (8, width)), spread)

    @pl.when(step == QUARTERS - 1)
    def _():
        rows = row_ref[...].T[:heads]
        cols = col_acc[...].T[:heads]
        last = column(jnp.sum(last_acc[...], axis=0, keepdims=True))[:heads]
        stride = stride_ref[...]
        gap_grad = rows - cols + jnp.where(iota((heads, length), 1) == length - 1, last, 0.0)
        onward = jnp.where(iota((length, length), 0) >= iota((length, length), 1), 1.0, 0.0).astype(BF16)
        parts = matmul(jnp.concatenate(split3(gap_grad), axis=0), onward)
        log_grad = parts[:heads] + parts[heads : 2 * heads] + parts[2 * heads :]
        rate = column(-jnp.exp(decay[...]))
        slope = 1.0 / (1.0 + jnp.exp(-(logits[...] + column(bias[...]))))
        step_value = (cols / stride + rate * log_grad) * slope
        step_grad[...] = step_value
        bias_sum = jnp.sum(step_value, axis=1, keepdims=True)
        decay_sum = jnp.sum(log_grad * log_ref[...], axis=1, keepdims=True)
        skip_sum = column(skip_acc[0:1])[:heads]
        spare = jnp.zeros((LANES - 3 * heads, 1), F32)
        table = jnp.concatenate([bias_sum, decay_sum, skip_sum, spare], axis=0)
        eye = iota((LANES, LANES), 0) == iota((LANES, LANES), 1)
        table = jnp.sum(jnp.where(eye, table, 0.0), axis=0, keepdims=True)
        sums[...] = jnp.broadcast_to(table[None], sums.shape)


def write_kernel(weight_cols, spread_ref, features, write_part, *refs):
    write_grad, write_acc, have = refs[GROUP + 1 :]
    state = write_part.shape[1]
    step = pl.program_id(0)

    @pl.when(step == 0)
    def _():
        write_acc[...] = jnp.zeros_like(write_acc)
        in_order(refs[:GROUP], have)

    weight = matmul(weight_cols[...], spread_ref[...])
    stack = jnp.concatenate(split2(quarter_rows(have)), axis=0)
    high, low = split2(weight * features[...].astype(F32))
    write_acc[...] += matmul_nt(high, stack) + matmul_nt(low, stack)

    @pl.when(step == QUARTERS - 1)
    def _():
        write_grad[...] = (write_part[...] + write_acc[:, :state] + write_acc[:, state:]).astype(BF16)


def call(kernel, name, outs, in_specs, work, mib, **more):
    return pl.pallas_call(
        kernel,
        out_shape=outs,
        in_specs=in_specs,
        out_specs=more.pop("out_specs", [VMEM] * len(outs)),
        compiler_params=pltpu.CompilerParams(vmem_limit_bytes=mib * 2**20),
        cost_estimate=pl.CostEstimate(flops=work * 10**9, bytes_accessed=10**6, transcendentals=0),
        name=name,
        **more,
    )


def struct(shape, dtype=F32):
    return jax.ShapeDtypeStruct(shape, dtype)


def local(
    features, write_keys, read_queries, step_logits, step_bias, decay_log, skip_gain, doc_starts, out_grad
):
    features, writes, reads, logits, cotangent = (
        features[0], write_keys[0], read_queries[0], step_logits[0], out_grad[0]
    )
    length, wide = features.shape
    heads = logits.shape[0]
    state = writes.shape[1]
    head_dim = wide // heads
    width = wide // QUARTERS
    part = state // HALVES
    bias, decay, skip = step_bias[None], decay_log[None], skip_gain[None]
    blocks, members = lax.axis_size("ctx"), lax.axis_size("dp")
    spread = spread_table(heads, head_dim)

    def swap(values):
        pairs = [[(k, k ^ d) for k in range(blocks)] for d in range(GROUP)]
        return [values[0]] + [lax.ppermute(values[d], "ctx", pairs[d]) for d in range(1, GROUP)]

    def shift(value, distance):
        pairs = [(k, k + distance) for k in range(blocks) if 0 <= k + distance < blocks]
        return lax.ppermute(value, "ctx", pairs)

    def scan(own, sign):
        came, near, reach = [], own, 1
        while reach < blocks // GROUP:
            came.append(shift(near, sign * GROUP * reach))
            reach *= 2
            if reach < blocks // GROUP:
                near = call(
                    functools.partial(link_kernel, part), "link", [group_sum], [VMEM] * (1 + len(came)), 1, 8
                )(own, *came)[0]
        return came

    def all_of(*shape):
        return pl.BlockSpec(shape, lambda step: (0,) * len(shape))

    def quarter_of(rows, offset=0):
        return pl.BlockSpec((rows, width), lambda step: (0, step + offset))

    stack = struct((length, LANES), BF16)
    small = struct((heads, length))
    result = struct((length, wide), BF16)
    tokens_result = struct((length, state), BF16)
    group_sum = struct((part + 8, width))
    share = struct((part, width))
    tokens = all_of(length, state)
    columns = all_of(length, LANES)
    by_heads = all_of(heads, length)
    row = all_of(1, heads)
    whole_share = all_of(part, width)
    by_quarter = quarter_of(length)
    spread_quarter = quarter_of(LANES)
    shares = pltpu.VMEM((GROUP, part, width), F32)
    long_shares = pltpu.VMEM((GROUP, part + 8, width), F32)

    out = call(
        states_kernel,
        "states",
        [group_sum] * GROUP + [stack] * 3 + [small] * 3,
        [SMEM] + [VMEM] * 6,
        3,
        24,
        scratch_shapes=[pltpu.VMEM((state, width), F32)],
    )(doc_starts, logits, bias, decay, spread, features, writes)
    send, (weight_cols, factor_cols, cum_cols, cum_rows, stride, log_decay) = out[:GROUP], out[GROUP:]
    came = swap(send)
    back_send = call(
        back_states_kernel,
        "back_states",
        [share] * GROUP,
        [VMEM] * 4,
        3,
        24,
        scratch_shapes=[pltpu.VMEM((state, width), F32)],
    )(factor_cols, spread, cotangent, reads)
    back_came = swap(back_send)

    half = QUARTERS // 2
    started = struct((length, wide)), struct((length, wide)), struct((1, wide))
    square = all_of(length, length)
    inner_args = (doc_starts, cum_cols, cum_rows, features, cotangent, writes, reads)
    score_scratch = [pltpu.VMEM((length, length), F32)] * 3

    def inner_specs(offset):
        mine = quarter_of(length, offset)
        return [SMEM, columns, by_heads, mine, mine, tokens, tokens], [mine, mine, quarter_of(1, offset)]

    specs, out_specs = inner_specs(0)
    *begun, score_grad = call(
        functools.partial(inner_kernel, 0, False),
        "inner_first",
        [*started, struct((length, length))],
        specs + [ANY],
        10,
        24,
        grid=(half,),
        out_specs=out_specs + [square],
        scratch_shapes=score_scratch,
    )(*inner_args, back_send[0])
    up, keeps = call(
        functools.partial(group_kernel, part),
        "group",
        [group_sum, struct((GROUP, width))],
        [VMEM] * GROUP + [ANY],
        2,
        8,
        scratch_shapes=[long_shares],
    )(*came, score_grad)
    ups = scan(up, 1)
    specs, out_specs = inner_specs(half)
    inside, feature_part, skip_part, write_part, read_part = call(
        functools.partial(inner_kernel, half, True),
        "inner_second",
        [*started, struct((length, state)), struct((length, state))],
        specs + [square] + [ANY] * 4,
        10,
        24,
        grid=(half,),
        out_specs=out_specs + [tokens, tokens],
        scratch_shapes=score_scratch,
        input_output_aliases={8: 0, 9: 1, 10: 2},
    )(*inner_args, score_grad, *begun, up)
    (down,) = call(
        functools.partial(back_group_kernel, part),
        "back_group",
        [group_sum],
        [VMEM] * (GROUP + 2) + [ANY],
        2,
        8,
        scratch_shapes=[shares],
    )(*back_came, keeps, up, write_part)
    downs = scan(down, -1)
    give = call(
        functools.partial(spread_kernel, part, len(ups)),
        "spread",
        [share] * GROUP,
        [VMEM] * (GROUP + len(ups)) + [ANY],
        2,
        12,
        scratch_shapes=[long_shares, shares],
    )(*came, *ups, down)
    have = swap(give)
    back_give = call(
        functools.partial(back_spread_kernel, part, len(downs)),
        "back_spread",
        [share] * GROUP,
        [VMEM] * (GROUP + 1 + len(downs)) + [ANY],
        2,
        12,
        scratch_shapes=[shares, shares],
    )(*back_came, keeps, *downs, give[0])
    back_have = swap(back_give)

    mixed, read_grad, rows, kept = call(
        finish_kernel,
        "finish",
        [result, tokens_result, struct((length, LANES)), struct((state, wide))],
        [row, columns, spread_quarter, by_quarter, by_quarter, tokens, by_quarter, tokens]
        + [whole_share] * GROUP
        + [ANY],
        8,
        24,
        grid=(QUARTERS,),
        out_specs=[by_quarter, tokens, columns, quarter_of(state)],
        scratch_shapes=[pltpu.VMEM((length, 2 * state), F32), shares],
    )(skip, factor_cols, spread, features, cotangent, reads, inside, read_part, *have, back_give[0])
    devices = blocks * members
    feature_grad, step_grad, sums = call(
        back_finish_kernel,
        "back_finish",
        [result, small, struct((devices, 1, LANES))],
        [by_heads, row, row, row, columns, by_heads, by_heads, spread_quarter]
        + [by_quarter, by_quarter, tokens, by_quarter]
        + [quarter_of(1), columns, quarter_of(state)]
        + [whole_share] * GROUP,
        8,
        24,
        grid=(QUARTERS,),
        out_specs=[by_quarter, by_heads, all_of(devices, 1, LANES)],
        scratch_shapes=[
            pltpu.VMEM((length, LANES), F32),
            pltpu.VMEM((8, LANES), F32),
            pltpu.VMEM((8, LANES), F32),
            shares,
        ],
    )(
        logits, bias, decay, skip, weight_cols, stride, log_decay, spread, features, cotangent, writes,
        feature_part, skip_part, rows, kept, *back_have,
    )
    (write_grad,) = call(
        write_kernel,
        "write_grad",
        [tokens_result],
        [columns, spread_quarter, by_quarter, tokens] + [whole_share] * GROUP + [ANY],
        4,
        24,
        grid=(QUARTERS,),
        out_specs=[tokens],
        scratch_shapes=[pltpu.VMEM((length, 2 * state), F32), shares],
    )(weight_cols, spread, features, write_part, *back_have, step_grad)
    sums = jnp.sum(lax.all_to_all(sums, ("dp", "ctx"), 0, 0), axis=(0, 1))
    return (
        mixed[None],
        feature_grad[None],
        write_grad[None],
        read_grad[None],
        step_grad[None],
        sums[:heads],
        sums[heads : 2 * heads],
        sums[2 * heads : 3 * heads],
    )


def solution(mesh):
    by_tokens = P("dp", "ctx", None)
    by_heads = P("dp", None, "ctx")
    in_specs = (by_tokens, by_tokens, by_tokens, by_heads, P(), P(), P(), P("dp", None), by_tokens)
    out_specs = (by_tokens, by_tokens, by_tokens, by_tokens, by_heads, P(), P(), P())
    return jax.shard_map(local, mesh=mesh, in_specs=in_specs, out_specs=out_specs, check_vma=False)
```

time: 522 us -> 114 us (0.22)
  waiting for transfers between devices: 137 us -> 11.3 us
  matrix products: 121 us -> 0 us
  local copies, waits for them, and re-layouts: 127 us -> 7.39 us
  other arithmetic: 75.8 us -> 0.05 us
  starting transfers between devices: 15.4 us -> 58.2 us
  blocking collectives: 39.5 us -> 0 us
  Pallas kernels: 0 us -> 35.3 us
    ppermute x11 -> x30, waiting for transfers between devices: 137 us -> 8.6 us  [the longest x28 7.07 us: swap(): lax.ppermute(values[d], 'ctx', pairs[d])]
    dot_general x69 -> x0, matrix products: 121 us -> none  [the longest x60 94.2 us: intra_group(): result = jnp.einsum('htu,uhp->thp', mixing, per_head, precision=EXACT)]
    dynamic_update_slice x60 -> x0, local copies, waits for them, and re-layouts: 51.9 us -> none  [block_main(): lax.map(jax.checkpoint(one_group), (cum_stack, stride_stack, feature_stack))]
    psum x1 -> x0, blocking collectives: 39.5 us -> none  [local(): lax.psum((bias_main + bias_state, decay_main + decay_state, skip_total),...]
    ppermute x11 -> x30, starting transfers between devices: 15.4 us -> 53.2 us  [the longest x28 47.3 us: swap(): lax.ppermute(values[d], 'ctx', pairs[d])]
    pallas_call x0 -> x11, Pallas kernels: none -> 35.3 us  [the longest x1 7.36 us: local(): call(functools.partial(inner_kernel, half, True), 'inner_second', [*start...]
    squeeze x40 -> x0, local copies, waits for them, and re-layouts: 33.1 us -> none  [block_main(): lax.map(jax.checkpoint(one_group), (cum_stack, stride_stack, feature_stack))]
    and x21 -> x0, other arithmetic: 17.4 us -> none  [block_main(): (segment[:, None] == segment[None, :]) & (ordinal[:, None] >= ordinal[Non...]
  transfers between devices with their start and end apart: 11 -> 31, of which waited for: 5 -> 6; matrix products, arithmetic and copies ran while one was open for 48% -> 0% of each run, Pallas kernels for 0% -> 24%
where the time goes in v2:
time: 114 us; the launch traced here: 113 us
  starting transfers between devices  58.2 us (51%)
  Pallas kernels  35.3 us (31%)
  waiting for transfers between devices  11.3 us (10%)
  local copies, waits for them, and re-layouts  7.39 us (6%)
    ppermute x28, starting transfers between devices, swap(): lax.ppermute(values[d], 'ctx', pairs[d])  47.3 us
    pallas_call x1, Pallas kernels, local(): call(functools.partial(inner_kernel, half, True), 'inner_second', [*start...  7.36 us
    pallas_call x1, Pallas kernels, local(): call(functools.partial(inner_kernel, 0, False), 'inner_first', [*started,...  7.08 us
    ppermute x28, waiting for transfers between devices, swap(): lax.ppermute(values[d], 'ctx', pairs[d])  7.07 us
    unnamed x36, local copies, waits for them, and re-layouts  6.79 us
    pallas_call x1, Pallas kernels, local(): call(finish_kernel, 'finish', [result, tokens_result, struct((length, LAN...  6.12 us
    pallas_call x1, Pallas kernels, local(): call(back_finish_kernel, 'back_finish', [result, small, struct((devices,...  6.02 us
    ppermute x2, starting transfers between devices, shift(): return lax.ppermute(value, 'ctx', pairs)  5.86 us
  transfers between devices with their start and end apart: 31, of which 6 were waited for; matrix products, arithmetic and copies ran while one was open for 0% of the time, Pallas kernels for 24%

profile of v2, /device:TPU:0, one launch (start us, length us, event | category | flops | bytes accessed | tf_op | source)
XLA Modules:
  0.0 113.2 jit_solution(1087999943074611305)
XLA Ops:
  6.6 2.5 %states.1 = (f32[72,640]{1,0:T(8,128)S(1)}, f32[72,640]{1,0:T(8,128)S(1)}, f32[72,640]{1,0:T(8,128)S(1)}, f32[72,640]{1,0:T(8,128)S(1)}, f32[72,640]{1,0:T(8,128...) custom-call(s32[1,4]{1,0:T(1,128)S(1)} %copy-done.8, ...), custom_call_target="tpu_custom_call" | custom-call | flops 3000000000 | bytes 1000000 | tf_op jit(solution)/shard_map/states/pallas_call | solution.py:496
  9.1 3.0 %collective-permute-start = (f32[72,640]{1,0:T(8,128)S(1)}, f32[72,640]{1,0:T(8,128)S(1)}, u32[]{:S(2)}, u32[]{:S(2)}) collective-permute-start(f32[72,640]{1,0:T(8,128)S(1)} %get-tuple-element.73), channel_id=1, source_target_pairs={{0,1},{1,0},{2,3},{3,2},{4,5},{5,4},{6,7},{7,6},{8,9},{9,8},{10,11... | collective-permute-start | bytes 552968 | tf_op jit(solution)/shard_map/ppermute | solution.py:457
  13.7 2.0 %collective-permute-start.3 = (f32[72,640]{1,0:T(8,128)S(1)}, f32[72,640]{1,0:T(8,128)S(1)}, u32[]{:S(2)}, u32[]{:S(2)}) collective-permute-start(f32[72,640]{1,0:T(8,128)S(1)} %get-tuple-element.76), channel_id=1, source_target_pairs={{0,4},{1,5},{2,6},{3,7},{4,0},{5,1},{6,2},{7,3},{8,12},{9,13},{10,... | collective-permute-start | bytes 552968 | tf_op jit(solution)/shard_map/ppermute | solution.py:457
  18.7 2.6 %collective-permute-start.5 = (f32[72,640]{1,0:T(8,128)S(1)}, f32[72,640]{1,0:T(8,128)S(1)}, u32[]{:S(2)}, u32[]{:S(2)}) collective-permute-start(f32[72,640]{1,0:T(8,128)S(1)} %get-tuple-element.78), channel_id=1, source_target_pairs={{0,6},{1,7},{2,4},{3,5},{4,2},{5,3},{6,0},{7,1},{8,14},{9,15},{10,... | collective-permute-start | bytes 552968 | tf_op jit(solution)/shard_map/ppermute | solution.py:457
  22.3 7.1 %inner_first.1 = (f32[256,2560]{1,0:T(8,128)S(1)}, f32[256,2560]{1,0:T(8,128)S(1)}, f32[1,2560]{1,0:T(1,128)S(1)}, f32[256,256]{1,0:T(8,128)S(1)}) custom-call(s32[1,4]{1,0:T(1,128)S(1)} %copy-done.9, bf16[256,128]{1,0:T(8,128)(2,1)S(1)} %get-tuple-element.65.cum_cols, f32[40,256]{1,0:T(8,128)S(1)} %get-tuple-element.66.cum_rows, ...), custom_call_target="tpu_custom_call" | custom-call | flops 10000000000 | bytes 1000000 | tf_op jit(solution)/shard_map/inner_first/pallas_call | solution.py:529
  29.4 2.8 %collective-permute-start.8 = (f32[64,640]{1,0:T(8,128)S(1)}, f32[64,640]{1,0:T(8,128)S(1)}, u32[]{:S(2)}, u32[]{:S(2)}) collective-permute-start(f32[64,640]{1,0:T(8,128)S(1)} %get-tuple-element.83), channel_id=1, source_target_pairs={{0,1},{1,0},{2,3},{3,2},{4,5},{5,4},{6,7},{7,6},{8,9},{9,8},{10,11... | collective-permute-start | bytes 491528 | tf_op jit(solution)/shard_map/ppermute | solution.py:457
  34.8 2.3 %collective-permute-start.12 = (f32[64,640]{1,0:T(8,128)S(1)}, f32[64,640]{1,0:T(8,128)S(1)}, u32[]{:S(2)}, u32[]{:S(2)}) collective-permute-start(f32[64,640]{1,0:T(8,128)S(1)} %get-tuple-element.87), channel_id=1, source_target_pairs={{0,5},{1,4},{2,7},{3,6},{4,1},{5,0},{6,3},{7,2},{8,13},{9,12},{10,... | collective-permute-start | bytes 491528 | tf_op jit(solution)/shard_map/ppermute | solution.py:457
  39.0 2.2 %collective-permute-start.13 = (f32[64,640]{1,0:T(8,128)S(1)}, f32[64,640]{1,0:T(8,128)S(1)}, u32[]{:S(2)}, u32[]{:S(2)}) collective-permute-start(f32[64,640]{1,0:T(8,128)S(1)} %get-tuple-element.88), channel_id=1, source_target_pairs={{0,6},{1,7},{2,4},{3,5},{4,2},{5,3},{6,0},{7,1},{8,14},{9,15},{10,... | collective-permute-start | bytes 491528 | tf_op jit(solution)/shard_map/ppermute | solution.py:457
  42.4 7.4 %inner_second.1 = (f32[256,2560]{1,0:T(8,128)S(1)}, f32[256,2560]{1,0:T(8,128)S(1)}, f32[1,2560]{1,0:T(1,128)S(1)}, f32[256,128]{1,0:T(8,128)S(1)}, f32[256,128]{1,0:T(8,128)S(1)}) custom-call(s32[1,4]{1,0:T(1,128)S(1)} %copy-done.9, bf16[256,128]{1,0:T(8,128)(2,1)S(1)} %get-tuple-element.65.cum_cols, ...), custom_call_target="tpu_custom_call", output_to_operand_aliasing={{0}: (8, {}), {1}: (9, {}), {2}: (10, {})} | custom-call | flops 10000000000 | bytes 1000000 | tf_op jit(solution)/shard_map/inner_second/pallas_call | solution.py:551
  49.8 4.6 %collective-permute-start.7 = (f32[72,640]{1,0:T(8,128)S(1)}, f32[72,640]{1,0:T(8,128)S(1)}, u32[]{:S(2)}, u32[]{:S(2)}) collective-permute-start(f32[72,640]{1,0:T(8,128)S(1)} %get-tuple-element.80.refs_4_.refs_9_), channel_id=1, source_target_pairs={{0,8},{1,9},{2,10},{3,11},{4,12},{5,13},{6,14},{7,15},{16,24},{17,... | collective-permute-start | bytes 552968 | tf_op jit(solution)/shard_map/ppermute | solution.py:461
  59.6 1.8 %collective-permute-start.17 = (f32[64,640]{1,0:T(8,128)S(1)}, f32[64,640]{1,0:T(8,128)S(1)}, u32[]{:S(2)}, u32[]{:S(2)}) collective-permute-start(f32[64,640]{1,0:T(8,128)S(1)} %get-tuple-element.95), channel_id=1, source_target_pairs={{0,3},{1,2},{2,1},{3,0},{4,7},{5,6},{6,5},{7,4},{8,11},{9,10},{10,... | collective-permute-start | bytes 491528 | tf_op jit(solution)/shard_map/ppermute | solution.py:457
  61.3 3.2 %collective-permute-start.18 = (f32[64,640]{1,0:T(8,128)S(1)}, f32[64,640]{1,0:T(8,128)S(1)}, u32[]{:S(2)}, u32[]{:S(2)}) collective-permute-start(f32[64,640]{1,0:T(8,128)S(1)} %get-tuple-element.96), channel_id=1, source_target_pairs={{0,4},{1,5},{2,6},{3,7},{4,0},{5,1},{6,2},{7,3},{8,12},{9,13},{10,... | collective-permute-start | bytes 491528 | tf_op jit(solution)/shard_map/ppermute | solution.py:457
  64.6 2.1 %collective-permute-start.19 = (f32[64,640]{1,0:T(8,128)S(1)}, f32[64,640]{1,0:T(8,128)S(1)}, u32[]{:S(2)}, u32[]{:S(2)}) collective-permute-start(f32[64,640]{1,0:T(8,128)S(1)} %get-tuple-element.97), channel_id=1, source_target_pairs={{0,5},{1,4},{2,7},{3,6},{4,1},{5,0},{6,3},{7,2},{8,13},{9,12},{10,... | collective-permute-start | bytes 491528 | tf_op jit(solution)/shard_map/ppermute | solution.py:457
  67.8 7.1 %collective-permute-start.21 = (f32[64,640]{1,0:T(8,128)S(1)}, f32[64,640]{1,0:T(8,128)S(1)}, u32[]{:S(2)}, u32[]{:S(2)}) collective-permute-start(f32[64,640]{1,0:T(8,128)S(1)} %get-tuple-element.99), channel_id=1, source_target_pairs={{0,7},{1,6},{2,5},{3,4},{4,3},{5,2},{6,1},{7,0},{8,15},{9,14},{10,... | collective-permute-start | bytes 491528 | tf_op jit(solution)/shard_map/ppermute | solution.py:457
  74.9 1.8 %collective-permute-start.24 = (f32[64,640]{1,0:T(8,128)S(1)}, f32[64,640]{1,0:T(8,128)S(1)}, u32[]{:S(2)}, u32[]{:S(2)}) collective-permute-start(f32[64,640]{1,0:T(8,128)S(1)} %get-tuple-element.110), channel_id=1, source_target_pairs={{0,2},{1,3},{2,0},{3,1},{4,6},{5,7},{6,4},{7,5},{8,10},{9,11},{10,... | collective-permute-start | bytes 491528 | tf_op jit(solution)/shard_map/ppermute | solution.py:457
  76.7 1.7 %collective-permute-start.25 = (f32[64,640]{1,0:T(8,128)S(1)}, f32[64,640]{1,0:T(8,128)S(1)}, u32[]{:S(2)}, u32[]{:S(2)}) collective-permute-start(f32[64,640]{1,0:T(8,128)S(1)} %get-tuple-element.111), channel_id=1, source_target_pairs={{0,3},{1,2},{2,1},{3,0},{4,7},{5,6},{6,5},{7,4},{8,11},{9,10},{10,... | collective-permute-start | bytes 491528 | tf_op jit(solution)/shard_map/ppermute | solution.py:457
  79.1 1.8 %collective-permute-done.21.refs_7_ = f32[64,640]{1,0:T(8,128)S(1)} collective-permute-done((f32[64,640]{1,0:T(8,128)S(1)}, f32[64,640]{1,0:T(8,128)S(1)}, u32[]{:S(2)}, u32[]{:S(2)}) %collective-permute-start.21) | collective-permute-done | bytes 163872 | tf_op jit(solution)/shard_map/ppermute | solution.py:457
  80.9 2.7 %collective-permute-start.27 = (f32[64,640]{1,0:T(8,128)S(1)}, f32[64,640]{1,0:T(8,128)S(1)}, u32[]{:S(2)}, u32[]{:S(2)}) collective-permute-start(f32[64,640]{1,0:T(8,128)S(1)} %get-tuple-element.113), channel_id=1, source_target_pairs={{0,5},{1,4},{2,7},{3,6},{4,1},{5,0},{6,3},{7,2},{8,13},{9,12},{10,... | collective-permute-start | bytes 491528 | tf_op jit(solution)/shard_map/ppermute | solution.py:457
  84.2 2.4 %collective-permute-done.24.refs_2_ = f32[64,640]{1,0:T(8,128)S(1)} collective-permute-done((f32[64,640]{1,0:T(8,128)S(1)}, f32[64,640]{1,0:T(8,128)S(1)}, u32[]{:S(2)}, u32[]{:S(2)}) %collective-permute-start.24) | collective-permute-done | bytes 163872 | tf_op jit(solution)/shard_map/ppermute | solution.py:457
  88.1 6.1 %finish.1 = (bf16[256,2560]{1,0:T(8,128)(2,1)}, bf16[256,128]{1,0:T(8,128)(2,1)}, f32[256,128]{1,0:T(8,128)S(1)}, f32[128,2560]{1,0:T(8,128)S(1)}) custom-call(f32[1,40]{1,0:T(1,128)S(1)} %bitcast.34, bf16[256,128]{1,0:T(8,128)(2,1)S(1)} %get-tuple-element.64.factor_cols, bf16[128,2560]{1,0:T(8,128)(2,1)S(1)} %copy-done.16, bf16[256,2560]{1,0:T(8,128)(2,1)S(1)} %bitcast.21, ...), custom_call_target="tpu_custom_call" | custom-call | flops 8000000000 | bytes 1000000 | tf_op jit(solution)/shard_map/finish/pallas_call | solution.py:594
  94.3 6.0 %back_finish.1 = (bf16[256,2560]{1,0:T(8,128)(2,1)}, f32[40,256]{1,0:T(8,128)}, f32[32,1,128]{2,1,0:T(1,128)}) custom-call(f32[40,256]{1,0:T(8,128)S(1)} %bitcast.33, f32[1,40]{1,0:T(1,128)S(1)} %bitcast.37, f32[1,40]{1,0:T(1,128)S(1)} %bitcast.39, f32[1,40]{1,0:T(1,128)S(1)} %bitcast.35, bf16[256,128]{1,0:T(8,128)(2,1)S(1)} %get-tuple-element.102.weight_cols, ...), custom_call_target="tpu_custom_call" | custom-call | flops 8000000000 | bytes 1000000 | tf_op jit(solution)/shard_map/back_finish/pallas_call | solution.py:608
  100.3 5.1 %all-to-all-start = ((f32[32,1,128]{2,1,0:T(1,128)}), f32[32,1,128]{2,1,0:T(1,128)S(1)}, u32[]{:S(2)}, u32[]{:S(2)}) async-start(f32[32,1,128]{2,1,0:T(1,128)} %get-tuple-element.119), calls=%async_computation | async-start | bytes 32768 | tf_op jit(solution)/shard_map/all_to_all | solution.py:641
  106.2 3.6 %write_grad.1 = bf16[256,128]{1,0:T(8,128)(2,1)} custom-call(bf16[256,128]{1,0:T(8,128)(2,1)S(1)} %get-tuple-element.102.weight_cols, bf16[128,2560]{1,0:T(8,128)(2,1)S(1)} %copy-done.16, bf16[256,2560]{1,0:T(8,128)(2,1)S(1)} %bitcast.23, f32[256,128]{1,0:T(8,128)S(1)} %get-tuple-element.91.refs_10_.write_part, ...), custom_call_target="tpu_custom_call" | custom-call | flops 4000000000 | bytes 1000000 | tf_op jit(solution)/shard_map/write_grad/pallas_call | solution.py:630
  109.8 2.7 %all-to-all-done = f32[32,1,128]{2,1,0:T(1,128)S(1)} async-done(((f32[32,1,128]{2,1,0:T(1,128)}), f32[32,1,128]{2,1,0:T(1,128)S(1)}, u32[]{:S(2)}, u32[]{:S(2)}) %all-to-all-start) | async-done | bytes 16416 | tf_op jit(solution)/shard_map/all_to_all | solution.py:641
  (87 shorter events, 27.7 us)
Async XLA Ops:
  13.7 15.8 %collective-permute-start.2 = (f32[72,640]{1,0:T(8,128)S(1)}, f32[72,640]{1,0:T(8,128)S(1)}, u32[]{:S(2)}, u32[]{:S(2)}) collective-permute-start(f32[72,640]{1,0:T(8,128)S(1)} %get-tuple-element.75), channel_id=1, source_target_pairs={{0,3},{1,2},{2,1},{3,0},{4,7},{5,6},{6,5},{7,4},{8,11},{9,10},{10,... | collective-permute-start | bytes 552968 | tf_op jit(solution)/shard_map/ppermute | solution.py:457
  13.7 18.5 %collective-permute-start.3 = (f32[72,640]{1,0:T(8,128)S(1)}, f32[72,640]{1,0:T(8,128)S(1)}, u32[]{:S(2)}, u32[]{:S(2)}) collective-permute-start(f32[72,640]{1,0:T(8,128)S(1)} %get-tuple-element.76), channel_id=1, source_target_pairs={{0,4},{1,5},{2,6},{3,7},{4,0},{5,1},{6,2},{7,3},{8,12},{9,13},{10,... | collective-permute-start | bytes 552968 | tf_op jit(solution)/shard_map/ppermute | solution.py:457
  15.7 16.5 %collective-permute-start.4 = (f32[72,640]{1,0:T(8,128)S(1)}, f32[72,640]{1,0:T(8,128)S(1)}, u32[]{:S(2)}, u32[]{:S(2)}) collective-permute-start(f32[72,640]{1,0:T(8,128)S(1)} %get-tuple-element.77), channel_id=1, source_target_pairs={{0,5},{1,4},{2,7},{3,6},{4,1},{5,0},{6,3},{7,2},{8,13},{9,12},{10,... | collective-permute-start | bytes 552968 | tf_op jit(solution)/shard_map/ppermute | solution.py:457
  18.7 15.1 %collective-permute-start.5 = (f32[72,640]{1,0:T(8,128)S(1)}, f32[72,640]{1,0:T(8,128)S(1)}, u32[]{:S(2)}, u32[]{:S(2)}) collective-permute-start(f32[72,640]{1,0:T(8,128)S(1)} %get-tuple-element.78), channel_id=1, source_target_pairs={{0,6},{1,7},{2,4},{3,5},{4,2},{5,3},{6,0},{7,1},{8,14},{9,15},{10,... | collective-permute-start | bytes 552968 | tf_op jit(solution)/shard_map/ppermute | solution.py:457
  21.3 13.5 %collective-permute-start.6 = (f32[72,640]{1,0:T(8,128)S(1)}, f32[72,640]{1,0:T(8,128)S(1)}, u32[]{:S(2)}, u32[]{:S(2)}) collective-permute-start(f32[72,640]{1,0:T(8,128)S(1)} %get-tuple-element.79), channel_id=1, source_target_pairs={{0,7},{1,6},{2,5},{3,4},{4,3},{5,2},{6,1},{7,0},{8,15},{9,14},{10,... | collective-permute-start | bytes 552968 | tf_op jit(solution)/shard_map/ppermute | solution.py:457
  29.4 9.5 %collective-permute-start.8 = (f32[64,640]{1,0:T(8,128)S(1)}, f32[64,640]{1,0:T(8,128)S(1)}, u32[]{:S(2)}, u32[]{:S(2)}) collective-permute-start(f32[64,640]{1,0:T(8,128)S(1)} %get-tuple-element.83), channel_id=1, source_target_pairs={{0,1},{1,0},{2,3},{3,2},{4,5},{5,4},{6,7},{7,6},{8,9},{9,8},{10,11... | collective-permute-start | bytes 491528 | tf_op jit(solution)/shard_map/ppermute | solution.py:457
  32.2 10.2 %collective-permute-start.9 = (f32[64,640]{1,0:T(8,128)S(1)}, f32[64,640]{1,0:T(8,128)S(1)}, u32[]{:S(2)}, u32[]{:S(2)}) collective-permute-start(f32[64,640]{1,0:T(8,128)S(1)} %get-tuple-element.84), channel_id=1, source_target_pairs={{0,2},{1,3},{2,0},{3,1},{4,6},{5,7},{6,4},{7,5},{8,10},{9,11},{10,... | collective-permute-start | bytes 491528 | tf_op jit(solution)/shard_map/ppermute | solution.py:457
  32.2 17.6 %collective-permute-start.10 = (f32[64,640]{1,0:T(8,128)S(1)}, f32[64,640]{1,0:T(8,128)S(1)}, u32[]{:S(2)}, u32[]{:S(2)}) collective-permute-start(f32[64,640]{1,0:T(8,128)S(1)} %get-tuple-element.85), channel_id=1, source_target_pairs={{0,3},{1,2},{2,1},{3,0},{4,7},{5,6},{6,5},{7,4},{8,11},{9,10},{10,... | collective-permute-start | bytes 491528 | tf_op jit(solution)/shard_map/ppermute | solution.py:457
  33.7 20.7 %collective-permute-start.11 = (f32[64,640]{1,0:T(8,128)S(1)}, f32[64,640]{1,0:T(8,128)S(1)}, u32[]{:S(2)}, u32[]{:S(2)}) collective-permute-start(f32[64,640]{1,0:T(8,128)S(1)} %get-tuple-element.86), channel_id=1, source_target_pairs={{0,4},{1,5},{2,6},{3,7},{4,0},{5,1},{6,2},{7,3},{8,12},{9,13},{10,... | collective-permute-start | bytes 491528 | tf_op jit(solution)/shard_map/ppermute | solution.py:457
  34.8 19.6 %collective-permute-start.12 = (f32[64,640]{1,0:T(8,128)S(1)}, f32[64,640]{1,0:T(8,128)S(1)}, u32[]{:S(2)}, u32[]{:S(2)}) collective-permute-start(f32[64,640]{1,0:T(8,128)S(1)} %get-tuple-element.87), channel_id=1, source_target_pairs={{0,5},{1,4},{2,7},{3,6},{4,1},{5,0},{6,3},{7,2},{8,13},{9,12},{10,... | collective-permute-start | bytes 491528 | tf_op jit(solution)/shard_map/ppermute | solution.py:457
  39.0 15.4 %collective-permute-start.13 = (f32[64,640]{1,0:T(8,128)S(1)}, f32[64,640]{1,0:T(8,128)S(1)}, u32[]{:S(2)}, u32[]{:S(2)}) collective-permute-start(f32[64,640]{1,0:T(8,128)S(1)} %get-tuple-element.88), channel_id=1, source_target_pairs={{0,6},{1,7},{2,4},{3,5},{4,2},{5,3},{6,0},{7,1},{8,14},{9,15},{10,... | collective-permute-start | bytes 491528 | tf_op jit(solution)/shard_map/ppermute | solution.py:457
  42.4 12.0 %collective-permute-start.14 = (f32[64,640]{1,0:T(8,128)S(1)}, f32[64,640]{1,0:T(8,128)S(1)}, u32[]{:S(2)}, u32[]{:S(2)}) collective-permute-start(f32[64,640]{1,0:T(8,128)S(1)} %get-tuple-element.89), channel_id=1, source_target_pairs={{0,7},{1,6},{2,5},{3,4},{4,3},{5,2},{6,1},{7,0},{8,15},{9,14},{10,... | collective-permute-start | bytes 491528 | tf_op jit(solution)/shard_map/ppermute | solution.py:457
  54.6 9.9 %collective-permute-start.22 = (f32[72,640]{1,0:T(8,128)S(1)}, f32[72,640]{1,0:T(8,128)S(1)}, u32[]{:S(2)}, u32[]{:S(2)}) collective-permute-start(f32[72,640]{1,0:T(8,128)S(1)} %back_group.1.refs_9_), channel_id=1, source_target_pairs={{8,0},{9,1},{10,2},{11,3},{12,4},{13,5},{14,6},{15,7},{24,16},{25,... | collective-permute-start | bytes 552968 | tf_op jit(solution)/shard_map/ppermute | solution.py:461
  59.6 15.4 %collective-permute-start.17 = (f32[64,640]{1,0:T(8,128)S(1)}, f32[64,640]{1,0:T(8,128)S(1)}, u32[]{:S(2)}, u32[]{:S(2)}) collective-permute-start(f32[64,640]{1,0:T(8,128)S(1)} %get-tuple-element.95), channel_id=1, source_target_pairs={{0,3},{1,2},{2,1},{3,0},{4,7},{5,6},{6,5},{7,4},{8,11},{9,10},{10,... | collective-permute-start | bytes 491528 | tf_op jit(solution)/shard_map/ppermute | solution.py:457
  61.3 13.6 %collective-permute-start.18 = (f32[64,640]{1,0:T(8,128)S(1)}, f32[64,640]{1,0:T(8,128)S(1)}, u32[]{:S(2)}, u32[]{:S(2)}) collective-permute-start(f32[64,640]{1,0:T(8,128)S(1)} %get-tuple-element.96), channel_id=1, source_target_pairs={{0,4},{1,5},{2,6},{3,7},{4,0},{5,1},{6,2},{7,3},{8,12},{9,13},{10,... | collective-permute-start | bytes 491528 | tf_op jit(solution)/shard_map/ppermute | solution.py:457
  64.6 12.2 %collective-permute-start.19 = (f32[64,640]{1,0:T(8,128)S(1)}, f32[64,640]{1,0:T(8,128)S(1)}, u32[]{:S(2)}, u32[]{:S(2)}) collective-permute-start(f32[64,640]{1,0:T(8,128)S(1)} %get-tuple-element.97), channel_id=1, source_target_pairs={{0,5},{1,4},{2,7},{3,6},{4,1},{5,0},{6,3},{7,2},{8,13},{9,12},{10,... | collective-permute-start | bytes 491528 | tf_op jit(solution)/shard_map/ppermute | solution.py:457
  67.0 11.4 %collective-permute-start.20 = (f32[64,640]{1,0:T(8,128)S(1)}, f32[64,640]{1,0:T(8,128)S(1)}, u32[]{:S(2)}, u32[]{:S(2)}) collective-permute-start(f32[64,640]{1,0:T(8,128)S(1)} %get-tuple-element.98), channel_id=1, source_target_pairs={{0,6},{1,7},{2,4},{3,5},{4,2},{5,3},{6,0},{7,1},{8,14},{9,15},{10,... | collective-permute-start | bytes 491528 | tf_op jit(solution)/shard_map/ppermute | solution.py:457
  67.8 13.1 %collective-permute-start.21 = (f32[64,640]{1,0:T(8,128)S(1)}, f32[64,640]{1,0:T(8,128)S(1)}, u32[]{:S(2)}, u32[]{:S(2)}) collective-permute-start(f32[64,640]{1,0:T(8,128)S(1)} %get-tuple-element.99), channel_id=1, source_target_pairs={{0,7},{1,6},{2,5},{3,4},{4,3},{5,2},{6,1},{7,0},{8,15},{9,14},{10,... | collective-permute-start | bytes 491528 | tf_op jit(solution)/shard_map/ppermute | solution.py:457
  74.9 11.6 %collective-permute-start.24 = (f32[64,640]{1,0:T(8,128)S(1)}, f32[64,640]{1,0:T(8,128)S(1)}, u32[]{:S(2)}, u32[]{:S(2)}) collective-permute-start(f32[64,640]{1,0:T(8,128)S(1)} %get-tuple-element.110), channel_id=1, source_target_pairs={{0,2},{1,3},{2,0},{3,1},{4,6},{5,7},{6,4},{7,5},{8,10},{9,11},{10,... | collective-permute-start | bytes 491528 | tf_op jit(solution)/shard_map/ppermute | solution.py:457
  76.7 17.5 %collective-permute-start.25 = (f32[64,640]{1,0:T(8,128)S(1)}, f32[64,640]{1,0:T(8,128)S(1)}, u32[]{:S(2)}, u32[]{:S(2)}) collective-permute-start(f32[64,640]{1,0:T(8,128)S(1)} %get-tuple-element.111), channel_id=1, source_target_pairs={{0,3},{1,2},{2,1},{3,0},{4,7},{5,6},{6,5},{7,4},{8,11},{9,10},{10,... | collective-permute-start | bytes 491528 | tf_op jit(solution)/shard_map/ppermute | solution.py:457
  78.4 15.8 %collective-permute-start.26 = (f32[64,640]{1,0:T(8,128)S(1)}, f32[64,640]{1,0:T(8,128)S(1)}, u32[]{:S(2)}, u32[]{:S(2)}) collective-permute-start(f32[64,640]{1,0:T(8,128)S(1)} %get-tuple-element.112), channel_id=1, source_target_pairs={{0,4},{1,5},{2,6},{3,7},{4,0},{5,1},{6,2},{7,3},{8,12},{9,13},{10,... | collective-permute-start | bytes 491528 | tf_op jit(solution)/shard_map/ppermute | solution.py:457
  80.9 13.4 %collective-permute-start.27 = (f32[64,640]{1,0:T(8,128)S(1)}, f32[64,640]{1,0:T(8,128)S(1)}, u32[]{:S(2)}, u32[]{:S(2)}) collective-permute-start(f32[64,640]{1,0:T(8,128)S(1)} %get-tuple-element.113), channel_id=1, source_target_pairs={{0,5},{1,4},{2,7},{3,6},{4,1},{5,0},{6,3},{7,2},{8,13},{9,12},{10,... | collective-permute-start | bytes 491528 | tf_op jit(solution)/shard_map/ppermute | solution.py:457
  83.6 10.7 %collective-permute-start.28 = (f32[64,640]{1,0:T(8,128)S(1)}, f32[64,640]{1,0:T(8,128)S(1)}, u32[]{:S(2)}, u32[]{:S(2)}) collective-permute-start(f32[64,640]{1,0:T(8,128)S(1)} %get-tuple-element.114), channel_id=1, source_target_pairs={{0,6},{1,7},{2,4},{3,5},{4,2},{5,3},{6,0},{7,1},{8,14},{9,15},{10,... | collective-permute-start | bytes 491528 | tf_op jit(solution)/shard_map/ppermute | solution.py:457
  100.3 12.2 %all-to-all-start = ((f32[32,1,128]{2,1,0:T(1,128)}), f32[32,1,128]{2,1,0:T(1,128)S(1)}, u32[]{:S(2)}, u32[]{:S(2)}) async-start(f32[32,1,128]{2,1,0:T(1,128)} %get-tuple-element.119), calls=%async_computation | async-start | bytes 32768 | tf_op jit(solution)/shard_map/all_to_all | solution.py:641
  (25 other events, 154.8 us)

commit v3 on v2

--- a/solution.py
+++ b/solution.py
@@ -133,18 +133,17 @@
     log_out[...] = log_decay
 
 
-def back_states_kernel(factor_cols, spread_ref, cotangent, reads, *refs):
-    scratch = refs[-1]
+def back_states_kernel(factor_cols, spread_ref, cotangent, reads, send):
     state = reads.shape[1]
     width = cotangent.shape[1] // QUARTERS
+    part = state // HALVES
     read_t = reads[...].astype(F32).T.astype(BF16)
-
-    def quarter_of_state(quarter):
-        cols = pl.ds(pl.multiple_of(quarter * width, LANES), width)
+    for quarter in range(QUARTERS):
+        cols = slice(quarter * width, (quarter + 1) * width)
         high, low = split2(cotangent[:, cols].astype(F32) * matmul(factor_cols[...], spread_ref[:, cols]))
-        return matmul(read_t, high) + matmul(read_t, low)
-
-    share_out(group_place(), quarter_of_state, refs[:GROUP], scratch, state // HALVES)
+        total = matmul(read_t, high) + matmul(read_t, low)
+        for half in range(HALVES):
+            send[half * QUARTERS + quarter] = total[half * part : (half + 1) * part]
 
 
 def inner_kernel(offset, last, starts, cum_cols, cum_rows, features, cotangent, writes, reads, *refs):
@@ -243,10 +242,7 @@
         keeps[j : j + 1] = came[j, part : part + 1]
 
 
-def back_group_kernel(part, *refs):
-    keeps, up = refs[GROUP : GROUP + 2]
-    down, came = refs[-2:]
-    in_order(refs[:GROUP], came)
+def back_group_kernel(part, came, keeps, up, _, down):
     total = came[GROUP - 1]
     for j in reversed(range(GROUP - 1)):
         total = total * keeps[j : j + 1] + came[j]
@@ -285,16 +281,13 @@
     give_out(refs[-2 - GROUP : -2], out)
 
 
-def back_spread_kernel(part, count, *refs):
-    keeps = refs[GROUP]
-    came, out = refs[-2:]
-    in_order(refs[:GROUP], came)
-    total = arrived(part, refs[GROUP + 1 : GROUP + 1 + count])[0]
+def back_spread_kernel(part, count, came, keeps, *refs):
+    out = refs[-1]
+    total = arrived(part, refs[:count])[0]
     for j in reversed(range(GROUP)):
         out[j] = total
         if j > 0:
             total = total * keeps[j : j + 1] + came[j]
-    give_out(refs[-2 - GROUP : -2], out)
 
 
 def head_sums(ref, value, spread):
@@ -344,11 +337,10 @@
 
 
 def back_finish_kernel(
-    logits, bias, decay, skip, weight_cols, stride_ref, log_ref, spread_ref,
-    features, cotangent, writes, feature_part, skip_part, row_ref, kept, *refs,
+    logits, bias, decay, weight_cols, stride_ref, log_ref, spread_ref,
+    features, writes, feature_part, skip_part, row_ref, kept, have,
+    step_grad, sums, col_acc, last_acc, skip_acc,
 ):
-    haves = refs[:GROUP]
-    feature_grad, step_grad, sums, col_acc, last_acc, skip_acc, have = refs[GROUP:]
     heads, length = logits.shape
     state = writes.shape[1]
     width = features.shape[1]
@@ -358,7 +350,6 @@
     def _():
         for ref in (col_acc, last_acc, skip_acc):
             ref[...] = jnp.zeros_like(ref)
-        in_order(haves, have)
 
     spread = spread_ref[...]
     weight = matmul(weight_cols[...], spread)
@@ -368,7 +359,6 @@
     writes2 = jnp.concatenate([writes[...]] * 2, axis=1)
     carried = weight * matmul(writes2, stack)
     total = feature_part[...] + carried
-    feature_grad[...] = (total + wide_skip(skip, heads, spread) * cotangent[...].astype(F32)).astype(BF16)
     head_sums(col_acc, feature * total, spread)
     leaving = jnp.sum((returning * kept[...]).reshape(state // 8, 8, width), axis=0)
     leaving = leaving + jnp.sum((feature * carried).reshape(length // 8, 8, width), axis=0)
@@ -399,18 +389,24 @@
         sums[...] = jnp.broadcast_to(table[None], sums.shape)
 
 
-def write_kernel(weight_cols, spread_ref, features, write_part, *refs):
-    write_grad, write_acc, have = refs[GROUP + 1 :]
+def write_kernel(
+    skip, weight_cols, spread_ref, features, cotangent, writes, feature_part, write_part, have, _,
+    feature_grad, write_grad, write_acc,
+):
     state = write_part.shape[1]
     step = pl.program_id(0)
 
     @pl.when(step == 0)
     def _():
         write_acc[...] = jnp.zeros_like(write_acc)
-        in_order(refs[:GROUP], have)
-
-    weight = matmul(weight_cols[...], spread_ref[...])
+
+    spread = spread_ref[...]
+    weight = matmul(weight_cols[...], spread)
     stack = jnp.concatenate(split2(quarter_rows(have)), axis=0)
+    writes2 = jnp.concatenate([writes[...]] * 2, axis=1)
+    total = feature_part[...] + weight * matmul(writes2, stack)
+    skips = wide_skip(skip, skip.shape[1], spread) * cotangent[...].astype(F32)
+    feature_grad[...] = (total + skips).astype(BF16)
     high, low = split2(weight * features[...].astype(F32))
     write_acc[...] += matmul_nt(high, stack) + matmul_nt(low, stack)
 
@@ -453,8 +449,14 @@
     spread = spread_table(heads, head_dim)
 
     def swap(values):
-        pairs = [[(k, k ^ d) for k in range(blocks)] for d in range(GROUP)]
-        return [values[0]] + [lax.ppermute(values[d], "ctx", pairs[d]) for d in range(1, GROUP)]
+        came = dict.fromkeys(range(GROUP), values[0])
+        for d in (1, 2, 4, 7, 3, 5, 6):
+            came[d] = lax.ppermute(values[d], "ctx", [(k, k ^ d) for k in range(blocks)])
+        return [came[d] for d in range(GROUP)]
+
+    def swap_stacked(value):
+        groups = [list(range(k, k + GROUP)) for k in range(0, blocks, GROUP)]
+        return lax.all_to_all(value, "ctx", 0, 0, axis_index_groups=groups)
 
     def shift(value, distance):
         pairs = [(k, k + distance) for k in range(blocks) if 0 <= k + distance < blocks]
@@ -491,6 +493,8 @@
     by_quarter = quarter_of(length)
     spread_quarter = quarter_of(LANES)
     shares = pltpu.VMEM((GROUP, part, width), F32)
+    shares_out = struct((GROUP, part, width))
+    whole_shares = all_of(GROUP, part, width)
     long_shares = pltpu.VMEM((GROUP, part + 8, width), F32)
 
     out = call(
@@ -499,21 +503,15 @@
         [group_sum] * GROUP + [stack] * 3 + [small] * 3,
         [SMEM] + [VMEM] * 6,
         3,
-        24,
+        60,
         scratch_shapes=[pltpu.VMEM((state, width), F32)],
     )(doc_starts, logits, bias, decay, spread, features, writes)
     send, (weight_cols, factor_cols, cum_cols, cum_rows, stride, log_decay) = out[:GROUP], out[GROUP:]
     came = swap(send)
-    back_send = call(
-        back_states_kernel,
-        "back_states",
-        [share] * GROUP,
-        [VMEM] * 4,
-        3,
-        24,
-        scratch_shapes=[pltpu.VMEM((state, width), F32)],
-    )(factor_cols, spread, cotangent, reads)
-    back_came = swap(back_send)
+    (back_send,) = call(back_states_kernel, "back_states", [shares_out], [VMEM] * 4, 3, 24)(
+        factor_cols, spread, cotangent, reads
+    )
+    back_came = swap_stacked(back_send)
 
     half = QUARTERS // 2
     started = struct((length, wide)), struct((length, wide)), struct((1, wide))
@@ -536,7 +534,7 @@
         grid=(half,),
         out_specs=out_specs + [square],
         scratch_shapes=score_scratch,
-    )(*inner_args, back_send[0])
+    )(*inner_args, back_send)
     up, keeps = call(
         functools.partial(group_kernel, part),
         "group",
@@ -564,11 +562,10 @@
         functools.partial(back_group_kernel, part),
         "back_group",
         [group_sum],
-        [VMEM] * (GROUP + 2) + [ANY],
+        [VMEM] * 3 + [ANY],
         2,
         8,
-        scratch_shapes=[shares],
-    )(*back_came, keeps, up, write_part)
+    )(back_came, keeps, up, write_part)
     downs = scan(down, -1)
     give = call(
         functools.partial(spread_kernel, part, len(ups)),
@@ -580,16 +577,15 @@
         scratch_shapes=[long_shares, shares],
     )(*came, *ups, down)
     have = swap(give)
-    back_give = call(
+    (back_give,) = call(
         functools.partial(back_spread_kernel, part, len(downs)),
         "back_spread",
-        [share] * GROUP,
-        [VMEM] * (GROUP + 1 + len(downs)) + [ANY],
+        [shares_out],
+        [VMEM] * (2 + len(downs)) + [ANY],
         2,
         12,
-        scratch_shapes=[shares, shares],
-    )(*back_came, keeps, *downs, give[0])
-    back_have = swap(back_give)
+    )(back_came, keeps, *downs, give[0])
+    back_have = swap_stacked(back_give)
 
     mixed, read_grad, rows, kept = call(
         finish_kernel,
@@ -603,41 +599,35 @@
         grid=(QUARTERS,),
         out_specs=[by_quarter, tokens, columns, quarter_of(state)],
         scratch_shapes=[pltpu.VMEM((length, 2 * state), F32), shares],
-    )(skip, factor_cols, spread, features, cotangent, reads, inside, read_part, *have, back_give[0])
+    )(skip, factor_cols, spread, features, cotangent, reads, inside, read_part, *have, back_give)
     devices = blocks * members
-    feature_grad, step_grad, sums = call(
+    step_grad, sums = call(
         back_finish_kernel,
         "back_finish",
-        [result, small, struct((devices, 1, LANES))],
-        [by_heads, row, row, row, columns, by_heads, by_heads, spread_quarter]
-        + [by_quarter, by_quarter, tokens, by_quarter]
-        + [quarter_of(1), columns, quarter_of(state)]
-        + [whole_share] * GROUP,
+        [small, struct((devices, 1, LANES))],
+        [by_heads, row, row, columns, by_heads, by_heads, spread_quarter]
+        + [by_quarter, tokens, by_quarter]
+        + [quarter_of(1), columns, quarter_of(state), whole_shares],
         8,
         24,
         grid=(QUARTERS,),
-        out_specs=[by_quarter, by_heads, all_of(devices, 1, LANES)],
-        scratch_shapes=[
-            pltpu.VMEM((length, LANES), F32),
-            pltpu.VMEM((8, LANES), F32),
-            pltpu.VMEM((8, LANES), F32),
-            shares,
-        ],
+        out_specs=[by_heads, all_of(devices, 1, LANES)],
+        scratch_shapes=[pltpu.VMEM((length, LANES), F32), pltpu.VMEM((8, LANES), F32), pltpu.VMEM((8, LANES), F32)],
     )(
-        logits, bias, decay, skip, weight_cols, stride, log_decay, spread, features, cotangent, writes,
-        feature_part, skip_part, rows, kept, *back_have,
+        logits, bias, decay, weight_cols, stride, log_decay, spread, features, writes,
+        feature_part, skip_part, rows, kept, back_have,
     )
-    (write_grad,) = call(
+    feature_grad, write_grad = call(
         write_kernel,
         "write_grad",
-        [tokens_result],
-        [columns, spread_quarter, by_quarter, tokens] + [whole_share] * GROUP + [ANY],
-        4,
+        [result, tokens_result],
+        [row, columns, spread_quarter, by_quarter, by_quarter, tokens, by_quarter, tokens, whole_shares, ANY],
+        6,
         24,
         grid=(QUARTERS,),
-        out_specs=[tokens],
-        scratch_shapes=[pltpu.VMEM((length, 2 * state), F32), shares],
-    )(weight_cols, spread, features, write_part, *back_have, step_grad)
+        out_specs=[by_quarter, tokens],
+        scratch_shapes=[pltpu.VMEM((length, 2 * state), F32)],
+    )(skip, weight_cols, spread, features, cotangent, writes, feature_part, write_part, back_have, step_grad)
     sums = jnp.sum(lax.all_to_all(sums, ("dp", "ctx"), 0, 0), axis=(0, 1))
     return (
         mixed[None],

time: 114 us -> 169 us (1.48)
  waiting for transfers between devices: 11.3 us -> 45.7 us
  local copies, waits for them, and re-layouts: 7.39 us -> 38.1 us
  starting transfers between devices: 58.2 us -> 41.2 us
  Pallas kernels: 35.3 us -> 41.4 us
    ppermute x28 -> x14, waiting for transfers between devices: 7.07 us -> 41.7 us  [swap(): lax.ppermute(values[d], 'ctx', [(k, k ^ d) for k in range(blocks)])]
    unnamed x36 -> x132, local copies, waits for them, and re-layouts: 6.79 us -> 37.5 us
    ppermute x28 -> x14, starting transfers between devices: 47.3 us -> 22.2 us  [swap(): lax.ppermute(values[d], 'ctx', [(k, k ^ d) for k in range(blocks)])]
    all_to_all x0 -> x2, starting transfers between devices: none -> 10 us  [swap_stacked(): return lax.all_to_all(value, 'ctx', 0, 0, axis_index_groups=groups)]
    all_to_all x1, waiting for transfers between devices: 2.73 us -> 0.01 us  [local(): sums = jnp.sum(lax.all_to_all(sums, ('dp', 'ctx'), 0, 0), axis=(0, 1))]
    all_to_all x1, starting transfers between devices: 5.08 us -> 2.5 us  [local(): sums = jnp.sum(lax.all_to_all(sums, ('dp', 'ctx'), 0, 0), axis=(0, 1))]
    ppermute x2, waiting for transfers between devices: 1.53 us -> 4.09 us  [shift(): return lax.ppermute(value, 'ctx', pairs)]
    pallas_call x1, Pallas kernels: 2.5 us -> 4.8 us  [local(): call(states_kernel, 'states', [group_sum] * GROUP + [stack] * 3 + [small]...]
  transfers between devices with their start and end apart: 31 -> 19, of which waited for: 6 -> 6; matrix products, arithmetic and copies ran while one was open for 0% -> 0% of each run, Pallas kernels for 24% -> 17%
where the time goes in v3:
time: 169 us; the launch traced here: 168 us
  waiting for transfers between devices  45.7 us (27%)
  Pallas kernels  41.4 us (24%)
  starting transfers between devices  41.2 us (24%)
  local copies, waits for them, and re-layouts  38.1 us (23%)
    ppermute x14, waiting for transfers between devices, swap(): lax.ppermute(values[d], 'ctx', [(k, k ^ d) for k in range(blocks)])  41.7 us
    unnamed x132, local copies, waits for them, and re-layouts  37.5 us
    ppermute x14, starting transfers between devices, swap(): lax.ppermute(values[d], 'ctx', [(k, k ^ d) for k in range(blocks)])  22.2 us
    all_to_all x2, starting transfers between devices, swap_stacked(): return lax.all_to_all(value, 'ctx', 0, 0, axis_index_groups=groups)  10 us
    pallas_call x1, Pallas kernels, local(): call(functools.partial(inner_kernel, half, True), 'inner_second', [*start...  7.36 us
    pallas_call x1, Pallas kernels, local(): call(functools.partial(inner_kernel, 0, False), 'inner_first', [*started,...  7.08 us
    ppermute x2, starting transfers between devices, shift(): return lax.ppermute(value, 'ctx', pairs)  6.47 us
    pallas_call x1, Pallas kernels, local(): call(finish_kernel, 'finish', [result, tokens_result, struct((length, LAN...  6.11 us
  transfers between devices with their start and end apart: 19, of which 6 were waited for; matrix products, arithmetic and copies ran while one was open for 0% of the time, Pallas kernels for 17%

profile of v3, /device:TPU:0, one launch (start us, length us, event | category | flops | bytes accessed | tf_op | source)
XLA Modules:
  0.0 167.5 jit_solution(16753677783642013571)
XLA Ops:
  0.7 4.8 %states.1 = (f32[72,640]{1,0:T(8,128)}, f32[72,640]{1,0:T(8,128)}, f32[72,640]{1,0:T(8,128)}, f32[72,640]{1,0:T(8,128)}, f32[72,640]{1,0:T(8,128)}, /*index=5*/f...) custom-call(s32[1,4]{1,0:T(1,128)} %starts.5, ...), custom_call_target="tpu_custom_call" | custom-call | flops 3000000000 | bytes 1000000 | tf_op jit(solution)/shard_map/states/pallas_call | solution.py:500
  6.3 2.5 %back_states.1.refs_0_ = f32[8,64,640]{2,1,0:T(8,128)} custom-call(bf16[256,128]{1,0:T(8,128)(2,1)S(1)} %copy-done.49, bf16[128,2560]{1,0:T(8,128)(2,1)S(1)} %copy-done.31, bf16[256,2560]{1,0:T(8,128)(2,1)S(1)} %bitcast.19, bf16[256,128]{1,0:T(8,128)(2,1)S(1)} %bitcast.24), custom_call_target="tpu_custom_call" | custom-call | flops 3000000000 | bytes 1000000 | tf_op jit(solution)/shard_map/back_states/pallas_call | solution.py:511
  8.9 6.3 %all-to-all-start = ((f32[8,64,640]{2,1,0:T(8,128)}), f32[8,64,640]{2,1,0:T(8,128)S(1)}, u32[]{:S(2)}, u32[]{:S(2)}) async-start(f32[8,64,640]{2,1,0:T(8,128)} %back_states.1.refs_0_), calls=%async_computation | async-start | bytes 2621440 | tf_op jit(solution)/shard_map/all_to_all | solution.py:459
  15.2 2.0 %collective-permute-start = (f32[72,640]{1,0:T(8,128)}, f32[72,640]{1,0:T(8,128)S(1)}, u32[]{:S(2)}, u32[]{:S(2)}) collective-permute-start(f32[72,640]{1,0:T(8,128)} %get-tuple-element.57), channel_id=1, source_target_pairs={{0,1},{1,0},{2,3},{3,2},{4,5},{5,4},{6,7},{7,6},{8,9},{9,8},{10,11... | collective-permute-start | bytes 552968 | tf_op jit(solution)/shard_map/ppermute | solution.py:454
  18.7 2.0 %collective-permute-start.3 = (f32[72,640]{1,0:T(8,128)}, f32[72,640]{1,0:T(8,128)S(1)}, u32[]{:S(2)}, u32[]{:S(2)}) collective-permute-start(f32[72,640]{1,0:T(8,128)} %get-tuple-element.60), channel_id=1, source_target_pairs={{0,4},{1,5},{2,6},{3,7},{4,0},{5,1},{6,2},{7,3},{8,12},{9,13},{10,... | collective-permute-start | bytes 552968 | tf_op jit(solution)/shard_map/ppermute | solution.py:454
  22.2 17.4 %collective-permute-done.refs_1_ = f32[72,640]{1,0:T(8,128)S(1)} collective-permute-done((f32[72,640]{1,0:T(8,128)}, f32[72,640]{1,0:T(8,128)S(1)}, u32[]{:S(2)}, u32[]{:S(2)}) %collective-permute-start) | collective-permute-done | bytes 184352 | tf_op jit(solution)/shard_map/ppermute | solution.py:454
  41.2 3.2 %collective-permute-start.6 = (f32[72,640]{1,0:T(8,128)}, f32[72,640]{1,0:T(8,128)S(1)}, u32[]{:S(2)}, u32[]{:S(2)}) collective-permute-start(f32[72,640]{1,0:T(8,128)} %get-tuple-element.63), channel_id=1, source_target_pairs={{0,7},{1,6},{2,5},{3,4},{4,3},{5,2},{6,1},{7,0},{8,15},{9,14},{10,... | collective-permute-start | bytes 552968 | tf_op jit(solution)/shard_map/ppermute | solution.py:454
  48.9 7.1 %inner_first.1 = (f32[256,2560]{1,0:T(8,128)S(1)}, f32[256,2560]{1,0:T(8,128)S(1)}, f32[1,2560]{1,0:T(1,128)S(1)}, f32[256,256]{1,0:T(8,128)S(1)}) custom-call(s32[1,4]{1,0:T(1,128)S(1)} %copy-done.27, bf16[256,128]{1,0:T(8,128)(2,1)S(1)} %copy-done.55, f32[40,256]{1,0:T(8,128)S(1)} %copy-done.58, bf16[256,2560]{1,0:T(8,128)(2,1)S(1)} %bitcast.14, ...), custom_call_target="tpu_custom_call" | custom-call | flops 10000000000 | bytes 1000000 | tf_op jit(solution)/shard_map/inner_first/pallas_call | solution.py:527
  57.6 5.2 %collective-permute-start.7 = (f32[72,640]{1,0:T(8,128)}, f32[72,640]{1,0:T(8,128)}, u32[]{:S(2)}, u32[]{:S(2)}) collective-permute-start(f32[72,640]{1,0:T(8,128)} %get-tuple-element.64.refs_4_.up), channel_id=1, source_target_pairs={{0,8},{1,9},{2,10},{3,11},{4,12},{5,13},{6,14},{7,15},{16,24},{17,... | collective-permute-start | bytes 552968 | tf_op jit(solution)/shard_map/ppermute | solution.py:463
  62.8 7.4 %inner_second.1 = (f32[256,2560]{1,0:T(8,128)S(1)}, f32[256,2560]{1,0:T(8,128)S(1)}, f32[1,2560]{1,0:T(1,128)S(1)}, f32[256,128]{1,0:T(8,128)S(1)}, f32[256,128]{1,0:T(8,128)S(1)}) custom-call(s32[1,4]{1,0:T(1,128)S(1)} %copy-done.27, bf16[256,128]{1,0:T(8,128)(2,1)S(1)} %copy-done.55, ...), custom_call_target="tpu_custom_call", output_to_operand_aliasing={{0}: (8, {}), {1}: (9, {}), {2}: (10, {})} | custom-call | flops 10000000000 | bytes 1000000 | tf_op jit(solution)/shard_map/inner_second/pallas_call | solution.py:549
  85.0 4.1 %collective-permute-done.15.refs_0_ = f32[72,640]{1,0:T(8,128)S(1)} collective-permute-done((f32[72,640]{1,0:T(8,128)S(1)}, f32[72,640]{1,0:T(8,128)S(1)}, u32[]{:S(2)}, u32[]{:S(2)}) %collective-permute-start.15) | collective-permute-done | bytes 184352 | tf_op jit(solution)/shard_map/ppermute | solution.py:463
  91.0 3.7 %all-to-all-start.1 = ((f32[8,64,640]{2,1,0:T(8,128)}), f32[8,64,640]{2,1,0:T(8,128)S(1)}, u32[]{:S(2)}, u32[]{:S(2)}) async-start(f32[8,64,640]{2,1,0:T(8,128)} %back_spread.1.refs_8_), calls=%async_computation.1 | async-start | bytes 2621440 | tf_op jit(solution)/shard_map/all_to_all | solution.py:459
  94.7 1.9 %collective-permute-start.8 = (f32[64,640]{1,0:T(8,128)}, f32[64,640]{1,0:T(8,128)S(1)}, u32[]{:S(2)}, u32[]{:S(2)}) collective-permute-start(f32[64,640]{1,0:T(8,128)} %copy-done.20), channel_id=1, source_target_pairs={{0,1},{1,0},{2,3},{3,2},{4,5},{5,4},{6,7},{7,6},{8,9},{9,8},{10,11... | collective-permute-start | bytes 491528 | tf_op jit(solution)/shard_map/ppermute | solution.py:454
  98.3 1.9 %collective-permute-start.11 = (f32[64,640]{1,0:T(8,128)S(1)}, f32[64,640]{1,0:T(8,128)S(1)}, u32[]{:S(2)}, u32[]{:S(2)}) collective-permute-start(f32[64,640]{1,0:T(8,128)S(1)} %copy-done.16), channel_id=1, source_target_pairs={{0,4},{1,5},{2,6},{3,7},{4,0},{5,1},{6,2},{7,3},{8,12},{9,13},{10,... | collective-permute-start | bytes 491528 | tf_op jit(solution)/shard_map/ppermute | solution.py:454
  101.6 17.3 %collective-permute-done.8.refs_1_ = f32[64,640]{1,0:T(8,128)S(1)} collective-permute-done((f32[64,640]{1,0:T(8,128)}, f32[64,640]{1,0:T(8,128)S(1)}, u32[]{:S(2)}, u32[]{:S(2)}) %collective-permute-start.8) | collective-permute-done | bytes 163872 | tf_op jit(solution)/shard_map/ppermute | solution.py:454
  120.1 2.4 %collective-permute-start.14 = (f32[64,640]{1,0:T(8,128)S(1)}, f32[64,640]{1,0:T(8,128)S(1)}, u32[]{:S(2)}, u32[]{:S(2)}) collective-permute-start(f32[64,640]{1,0:T(8,128)S(1)} %copy-done.10), channel_id=1, source_target_pairs={{0,7},{1,6},{2,5},{3,4},{4,3},{5,2},{6,1},{7,0},{8,15},{9,14},{10,... | collective-permute-start | bytes 491528 | tf_op jit(solution)/shard_map/ppermute | solution.py:454
  122.5 1.8 %collective-permute-done.10.refs_3_ = f32[64,640]{1,0:T(8,128)S(1)} collective-permute-done((f32[64,640]{1,0:T(8,128)S(1)}, f32[64,640]{1,0:T(8,128)S(1)}, u32[]{:S(2)}, u32[]{:S(2)}) %collective-permute-start.10) | collective-permute-done | bytes 163872 | tf_op jit(solution)/shard_map/ppermute | solution.py:454
  124.3 2.5 %collective-permute-done.13.refs_6_ = f32[64,640]{1,0:T(8,128)S(1)} collective-permute-done((f32[64,640]{1,0:T(8,128)S(1)}, f32[64,640]{1,0:T(8,128)S(1)}, u32[]{:S(2)}, u32[]{:S(2)}) %collective-permute-start.13) | collective-permute-done | bytes 163872 | tf_op jit(solution)/shard_map/ppermute | solution.py:454
  126.8 2.7 %collective-permute-done.14.refs_7_ = f32[64,640]{1,0:T(8,128)S(1)} collective-permute-done((f32[64,640]{1,0:T(8,128)S(1)}, f32[64,640]{1,0:T(8,128)S(1)}, u32[]{:S(2)}, u32[]{:S(2)}) %collective-permute-start.14) | collective-permute-done | bytes 163872 | tf_op jit(solution)/shard_map/ppermute | solution.py:454
  132.8 1.7 %copy-done.41 = f32[256,2560]{1,0:T(8,128)S(1)} copy-done((f32[256,2560]{1,0:T(8,128)S(1)}, f32[256,2560]{1,0:T(8,128)}, u32[]{:S(2)}) %copy-start.41) | copy-done | bytes 2621464
  136.3 6.1 %finish.1 = (bf16[256,2560]{1,0:T(8,128)(2,1)}, bf16[256,128]{1,0:T(8,128)(2,1)}, f32[256,128]{1,0:T(8,128)S(1)}, f32[128,2560]{1,0:T(8,128)S(1)}) custom-call(f32[1,40]{1,0:T(1,128)S(1)} %bitcast.39, bf16[256,128]{1,0:T(8,128)(2,1)S(1)} %copy-done.50, bf16[128,2560]{1,0:T(8,128)(2,1)S(1)} %copy-done.32, bf16[256,2560]{1,0:T(8,128)(2,1)S(1)} %bitcast.16, ...), custom_call_target="tpu_custom_call" | custom-call | flops 8000000000 | bytes 1000000 | tf_op jit(solution)/shard_map/finish/pallas_call | solution.py:590
  150.4 5.0 %back_finish.1 = (f32[40,256]{1,0:T(8,128)}, f32[32,1,128]{2,1,0:T(1,128)}) custom-call(f32[40,256]{1,0:T(8,128)S(1)} %bitcast.34, f32[1,40]{1,0:T(1,128)S(1)} %bitcast.36, f32[1,40]{1,0:T(1,128)S(1)} %bitcast.38, bf16[256,128]{1,0:T(8,128)(2,1)S(1)} %copy-done.54, f32[40,256]{1,0:T(8,128)S(1)} %copy-done.56, f32[40,256]{1,0:T(8,128)S(1)} %copy-done.57, ...), custom_call_target="tpu_custom_call" | custom-call | flops 8000000000 | bytes 1000000 | tf_op jit(solution)/shard_map/back_finish/pallas_call | solution.py:604
  155.4 2.5 %all-to-all-start.2 = ((f32[32,1,128]{2,1,0:T(1,128)}), f32[32,1,128]{2,1,0:T(1,128)S(1)}, u32[]{:S(2)}, u32[]{:S(2)}) async-start(f32[32,1,128]{2,1,0:T(1,128)} %get-tuple-element.89), calls=%async_computation.2 | async-start | bytes 32768 | tf_op jit(solution)/shard_map/all_to_all | solution.py:631
  162.7 4.2 %write_grad.1 = (bf16[256,2560]{1,0:T(8,128)(2,1)}, bf16[256,128]{1,0:T(8,128)(2,1)}) custom-call(f32[1,40]{1,0:T(1,128)S(1)} %bitcast.40, bf16[256,128]{1,0:T(8,128)(2,1)S(1)} %copy-done.54, bf16[128,2560]{1,0:T(8,128)(2,1)S(1)} %copy-done.33, bf16[256,2560]{1,0:T(8,128)(2,1)S(1)} %bitcast.18, bf16[256,2560]{1,0:T(8,128)(2,1)S(1)} %bitcast.23, ...), custom_call_target="tpu_custom_call" | custom-call | flops 6000000000 | bytes 1000000 | tf_op jit(solution)/shard_map/write_grad/pallas_call | solution.py:620
  (159 shorter events, 50.9 us)
Async XLA Ops:
  8.9 35.4 %copy-start = (bf16[1,256,2560]{2,1,0:T(8,128)(2,1)S(1)}, bf16[1,256,2560]{2,1,0:T(8,128)(2,1)}, u32[]{:S(2)}) copy-start(bf16[1,256,2560]{2,1,0:T(8,128)(2,1)} %param.10) | copy-start | bytes 3932164
  8.9 35.4 %copy-start.27 = (s32[1,4]{1,0:T(1,128)S(1)}, s32[1,4]{1,0:T(1,128)}, u32[]{:S(2)}) copy-start(s32[1,4]{1,0:T(1,128)} %starts.5) | copy-start | bytes 52
  8.9 66.2 %all-to-all-start = ((f32[8,64,640]{2,1,0:T(8,128)}), f32[8,64,640]{2,1,0:T(8,128)S(1)}, u32[]{:S(2)}, u32[]{:S(2)}) async-start(f32[8,64,640]{2,1,0:T(8,128)} %back_states.1.refs_0_), calls=%async_computation | async-start | bytes 2621440 | tf_op jit(solution)/shard_map/all_to_all | solution.py:459
  15.2 24.4 %collective-permute-start = (f32[72,640]{1,0:T(8,128)}, f32[72,640]{1,0:T(8,128)S(1)}, u32[]{:S(2)}, u32[]{:S(2)}) collective-permute-start(f32[72,640]{1,0:T(8,128)} %get-tuple-element.57), channel_id=1, source_target_pairs={{0,1},{1,0},{2,3},{3,2},{4,5},{5,4},{6,7},{7,6},{8,9},{9,8},{10,11... | collective-permute-start | bytes 552968 | tf_op jit(solution)/shard_map/ppermute | solution.py:454
  17.2 23.9 %collective-permute-start.1 = (f32[72,640]{1,0:T(8,128)}, f32[72,640]{1,0:T(8,128)S(1)}, u32[]{:S(2)}, u32[]{:S(2)}) collective-permute-start(f32[72,640]{1,0:T(8,128)} %get-tuple-element.58), channel_id=1, source_target_pairs={{0,2},{1,3},{2,0},{3,1},{4,6},{5,7},{6,4},{7,5},{8,10},{9,11},{10,... | collective-permute-start | bytes 552968 | tf_op jit(solution)/shard_map/ppermute | solution.py:454
  18.7 37.3 %collective-permute-start.2 = (f32[72,640]{1,0:T(8,128)}, f32[72,640]{1,0:T(8,128)S(1)}, u32[]{:S(2)}, u32[]{:S(2)}) collective-permute-start(f32[72,640]{1,0:T(8,128)} %get-tuple-element.59), channel_id=1, source_target_pairs={{0,3},{1,2},{2,1},{3,0},{4,7},{5,6},{6,5},{7,4},{8,11},{9,10},{10,... | collective-permute-start | bytes 552968 | tf_op jit(solution)/shard_map/ppermute | solution.py:454
  18.7 37.3 %collective-permute-start.3 = (f32[72,640]{1,0:T(8,128)}, f32[72,640]{1,0:T(8,128)S(1)}, u32[]{:S(2)}, u32[]{:S(2)}) collective-permute-start(f32[72,640]{1,0:T(8,128)} %get-tuple-element.60), channel_id=1, source_target_pairs={{0,4},{1,5},{2,6},{3,7},{4,0},{5,1},{6,2},{7,3},{8,12},{9,13},{10,... | collective-permute-start | bytes 552968 | tf_op jit(solution)/shard_map/ppermute | solution.py:454
  20.7 35.3 %collective-permute-start.4 = (f32[72,640]{1,0:T(8,128)}, f32[72,640]{1,0:T(8,128)S(1)}, u32[]{:S(2)}, u32[]{:S(2)}) collective-permute-start(f32[72,640]{1,0:T(8,128)} %get-tuple-element.61), channel_id=1, source_target_pairs={{0,5},{1,4},{2,7},{3,6},{4,1},{5,0},{6,3},{7,2},{8,13},{9,12},{10,... | collective-permute-start | bytes 552968 | tf_op jit(solution)/shard_map/ppermute | solution.py:454
  39.6 16.5 %collective-permute-start.5 = (f32[72,640]{1,0:T(8,128)}, f32[72,640]{1,0:T(8,128)S(1)}, u32[]{:S(2)}, u32[]{:S(2)}) collective-permute-start(f32[72,640]{1,0:T(8,128)} %get-tuple-element.62), channel_id=1, source_target_pairs={{0,6},{1,7},{2,4},{3,5},{4,2},{5,3},{6,0},{7,1},{8,14},{9,15},{10,... | collective-permute-start | bytes 552968 | tf_op jit(solution)/shard_map/ppermute | solution.py:454
  41.2 14.9 %collective-permute-start.6 = (f32[72,640]{1,0:T(8,128)}, f32[72,640]{1,0:T(8,128)S(1)}, u32[]{:S(2)}, u32[]{:S(2)}) collective-permute-start(f32[72,640]{1,0:T(8,128)} %get-tuple-element.63), channel_id=1, source_target_pairs={{0,7},{1,6},{2,5},{3,4},{4,3},{5,2},{6,1},{7,0},{8,15},{9,14},{10,... | collective-permute-start | bytes 552968 | tf_op jit(solution)/shard_map/ppermute | solution.py:454
  57.6 21.5 %collective-permute-start.7 = (f32[72,640]{1,0:T(8,128)}, f32[72,640]{1,0:T(8,128)}, u32[]{:S(2)}, u32[]{:S(2)}) collective-permute-start(f32[72,640]{1,0:T(8,128)} %get-tuple-element.64.refs_4_.up), channel_id=1, source_target_pairs={{0,8},{1,9},{2,10},{3,11},{4,12},{5,13},{6,14},{7,15},{16,24},{17,... | collective-permute-start | bytes 552968 | tf_op jit(solution)/shard_map/ppermute | solution.py:463
  77.8 11.3 %collective-permute-start.15 = (f32[72,640]{1,0:T(8,128)S(1)}, f32[72,640]{1,0:T(8,128)S(1)}, u32[]{:S(2)}, u32[]{:S(2)}) collective-permute-start(f32[72,640]{1,0:T(8,128)S(1)} %back_group.1.refs_9_), channel_id=1, source_target_pairs={{8,0},{9,1},{10,2},{11,3},{12,4},{13,5},{14,6},{15,7},{24,16},{25,... | collective-permute-start | bytes 552968 | tf_op jit(solution)/shard_map/ppermute | solution.py:463
  91.0 29.1 %copy-start.10 = (f32[64,640]{1,0:T(8,128)S(1)}, f32[64,640]{1,0:T(8,128)}, u32[]{:S(2)}) copy-start(f32[64,640]{1,0:T(8,128)} %copy-done.9) | copy-start | bytes 491524
  91.0 38.5 %copy-start.23 = (bf16[1,256,128]{2,1,0:T(8,128)(2,1)S(1)}, bf16[1,256,128]{2,1,0:T(8,128)(2,1)}, u32[]{:S(2)}) copy-start(bf16[1,256,128]{2,1,0:T(8,128)(2,1)} %param.12) | copy-start | bytes 196612
  91.0 38.5 %copy-start.30 = (f32[40]{0:T(128)S(1)}, f32[40]{0:T(128)}, u32[]{:S(2)}) copy-start(f32[40]{0:T(128)} %param.16) | copy-start | bytes 484
  91.0 53.1 %all-to-all-start.1 = ((f32[8,64,640]{2,1,0:T(8,128)}), f32[8,64,640]{2,1,0:T(8,128)S(1)}, u32[]{:S(2)}, u32[]{:S(2)}) async-start(f32[8,64,640]{2,1,0:T(8,128)} %back_spread.1.refs_8_), calls=%async_computation.1 | async-start | bytes 2621440 | tf_op jit(solution)/shard_map/all_to_all | solution.py:459
  94.7 24.2 %collective-permute-start.8 = (f32[64,640]{1,0:T(8,128)}, f32[64,640]{1,0:T(8,128)S(1)}, u32[]{:S(2)}, u32[]{:S(2)}) collective-permute-start(f32[64,640]{1,0:T(8,128)} %copy-done.20), channel_id=1, source_target_pairs={{0,1},{1,0},{2,3},{3,2},{4,5},{5,4},{6,7},{7,6},{8,9},{9,8},{10,11... | collective-permute-start | bytes 491528 | tf_op jit(solution)/shard_map/ppermute | solution.py:454
  96.6 23.5 %collective-permute-start.9 = (f32[64,640]{1,0:T(8,128)}, f32[64,640]{1,0:T(8,128)S(1)}, u32[]{:S(2)}, u32[]{:S(2)}) collective-permute-start(f32[64,640]{1,0:T(8,128)} %copy-done.19), channel_id=1, source_target_pairs={{0,2},{1,3},{2,0},{3,1},{4,6},{5,7},{6,4},{7,5},{8,10},{9,11},{10,... | collective-permute-start | bytes 491528 | tf_op jit(solution)/shard_map/ppermute | solution.py:454
  98.1 26.2 %collective-permute-start.10 = (f32[64,640]{1,0:T(8,128)S(1)}, f32[64,640]{1,0:T(8,128)S(1)}, u32[]{:S(2)}, u32[]{:S(2)}) collective-permute-start(f32[64,640]{1,0:T(8,128)S(1)} %copy-done.18), channel_id=1, source_target_pairs={{0,3},{1,2},{2,1},{3,0},{4,7},{5,6},{6,5},{7,4},{8,11},{9,10},{10,... | collective-permute-start | bytes 491528 | tf_op jit(solution)/shard_map/ppermute | solution.py:454
  98.3 26.0 %collective-permute-start.11 = (f32[64,640]{1,0:T(8,128)S(1)}, f32[64,640]{1,0:T(8,128)S(1)}, u32[]{:S(2)}, u32[]{:S(2)}) collective-permute-start(f32[64,640]{1,0:T(8,128)S(1)} %copy-done.16), channel_id=1, source_target_pairs={{0,4},{1,5},{2,6},{3,7},{4,0},{5,1},{6,2},{7,3},{8,12},{9,13},{10,... | collective-permute-start | bytes 491528 | tf_op jit(solution)/shard_map/ppermute | solution.py:454
  100.2 24.2 %collective-permute-start.12 = (f32[64,640]{1,0:T(8,128)S(1)}, f32[64,640]{1,0:T(8,128)S(1)}, u32[]{:S(2)}, u32[]{:S(2)}) collective-permute-start(f32[64,640]{1,0:T(8,128)S(1)} %copy-done.14), channel_id=1, source_target_pairs={{0,5},{1,4},{2,7},{3,6},{4,1},{5,0},{6,3},{7,2},{8,13},{9,12},{10,... | collective-permute-start | bytes 491528 | tf_op jit(solution)/shard_map/ppermute | solution.py:454
  118.9 7.9 %collective-permute-start.13 = (f32[64,640]{1,0:T(8,128)S(1)}, f32[64,640]{1,0:T(8,128)S(1)}, u32[]{:S(2)}, u32[]{:S(2)}) collective-permute-start(f32[64,640]{1,0:T(8,128)S(1)} %copy-done.12), channel_id=1, source_target_pairs={{0,6},{1,7},{2,4},{3,5},{4,2},{5,3},{6,0},{7,1},{8,14},{9,15},{10,... | collective-permute-start | bytes 491528 | tf_op jit(solution)/shard_map/ppermute | solution.py:454
  120.1 9.3 %collective-permute-start.14 = (f32[64,640]{1,0:T(8,128)S(1)}, f32[64,640]{1,0:T(8,128)S(1)}, u32[]{:S(2)}, u32[]{:S(2)}) collective-permute-start(f32[64,640]{1,0:T(8,128)S(1)} %copy-done.10), channel_id=1, source_target_pairs={{0,7},{1,6},{2,5},{3,4},{4,3},{5,2},{6,1},{7,0},{8,15},{9,14},{10,... | collective-permute-start | bytes 491528 | tf_op jit(solution)/shard_map/ppermute | solution.py:454
  155.4 11.5 %all-to-all-start.2 = ((f32[32,1,128]{2,1,0:T(1,128)}), f32[32,1,128]{2,1,0:T(1,128)S(1)}, u32[]{:S(2)}, u32[]{:S(2)}) async-start(f32[32,1,128]{2,1,0:T(1,128)} %get-tuple-element.89), calls=%async_computation.2 | async-start | bytes 32768 | tf_op jit(solution)/shard_map/all_to_all | solution.py:631
  (61 other events, 185.2 us)

commit v4 on v2

--- a/solution.py
+++ b/solution.py
@@ -13,6 +13,7 @@
 QUARTERS = 4
 HALVES = 2
 GROUP = QUARTERS * HALVES
+EARLY, LATE = (1, 2, 4, 7), (3, 5, 6)
 LANES = 128
 LOG2E = 1.4426950408889634
 FAR = -1e30
@@ -82,18 +83,20 @@
     return lax.rem(lax.axis_index("ctx"), GROUP)
 
 
-def share_out(own, quarter_of_state, sends, scratch, part):
+def share_out(own, quarter_of_state, places, scratch):
     mine = lax.div(own, QUARTERS)
+    part = scratch.shape[0] // HALVES
     for distance in range(QUARTERS):
         scratch[...] = quarter_of_state(lax.rem(own ^ distance, QUARTERS))
         for half in range(HALVES):
             rows = pl.ds(pl.multiple_of((mine ^ half) * part, part), part)
-            sends[half * QUARTERS + distance][0:part] = scratch[rows]
-
-
-def states_kernel(starts, logits, bias, decay, spread_ref, features, writes, *refs):
+            places[half * QUARTERS + distance][...] = scratch[rows]
+
+
+def states_kernel(starts, logits, bias, decay, spread_ref, features, writes, cotangent, reads, *refs):
     sends = refs[:GROUP]
-    weight_cols, factor_cols, cum_cols, cum_rows, stride_out, log_out, scratch = refs[GROUP:]
+    late = refs[GROUP : GROUP + len(LATE)]
+    weight_cols, factor_cols, cum_cols, cum_rows, stride_out, log_out, scratch = refs[GROUP + len(LATE) :]
     heads, length = logits.shape
     state = writes.shape[1]
     width = features.shape[1] // QUARTERS
@@ -119,32 +122,31 @@
         high, low = split2(features[:, cols].astype(F32) * matmul(weight_stack, spread_ref[:, cols]))
         return matmul(write_t, high) + matmul(write_t, low)
 
-    share_out(own, quarter_of_state, sends, scratch, part)
-    for distance in range(QUARTERS):
-        cols = pl.ds(pl.multiple_of(lax.rem(own ^ distance, QUARTERS) * width, LANES), width)
-        keep = matmul(factor_stack[length - 16 :], spread_ref[:, cols])[15:16]
-        for half in range(HALVES):
-            sends[half * QUARTERS + distance][part:] = jnp.broadcast_to(keep, (8, width))
+    share_out(own, quarter_of_state, [send.at[0:part] for send in sends], scratch)
+    read_t = reads[...].astype(F32).T.astype(BF16)
+
+    keeps = []
+
+    def back_quarter(quarter):
+        cols = pl.ds(pl.multiple_of(quarter * width, LANES), width)
+        wide = matmul(factor_stack, spread_ref[:, cols])
+        keeps.append(jnp.broadcast_to(wide[length - 1 :], (8, width)))
+        high, low = split2(cotangent[:, cols].astype(F32) * wide)
+        return matmul(read_t, high) + matmul(read_t, low)
+
+    places = [
+        late[LATE.index(distance)] if distance in LATE else send.at[part + 8 :]
+        for distance, send in enumerate(sends)
+    ]
+    share_out(own, back_quarter, places, scratch)
+    for distance, send in enumerate(sends):
+        send[part : part + 8] = keeps[distance % QUARTERS]
     weight_cols[...] = weight_stack
     factor_cols[...] = factor_stack
     cum_cols[...] = stacked_columns(cum * LOG2E)
     cum_rows[...] = cum * LOG2E - jnp.log2(stride)
     stride_out[...] = stride
     log_out[...] = log_decay
-
-
-def back_states_kernel(factor_cols, spread_ref, cotangent, reads, *refs):
-    scratch = refs[-1]
-    state = reads.shape[1]
-    width = cotangent.shape[1] // QUARTERS
-    read_t = reads[...].astype(F32).T.astype(BF16)
-
-    def quarter_of_state(quarter):
-        cols = pl.ds(pl.multiple_of(quarter * width, LANES), width)
-        high, low = split2(cotangent[:, cols].astype(F32) * matmul(factor_cols[...], spread_ref[:, cols]))
-        return matmul(read_t, high) + matmul(read_t, low)
-
-    share_out(group_place(), quarter_of_state, refs[:GROUP], scratch, state // HALVES)
 
 
 def inner_kernel(offset, last, starts, cum_cols, cum_rows, features, cotangent, writes, reads, *refs):
@@ -223,10 +225,18 @@
             grad_out[...] = score_grad
 
 
-def in_order(refs, scratch):
+def in_order(refs, scratch, back=False):
     own = group_place()
+    rows = scratch.shape[1]
     for distance, ref in enumerate(refs):
-        scratch[own ^ distance] = ref[...]
+        first = ref.shape[0] - rows if back else 0
+        scratch[own ^ distance] = ref[first : first + rows]
+
+
+def hold_kernel(*refs):
+    count = len(LATE)
+    for value, out in zip(refs[:count], refs[count + 1 :]):
+        out[...] = value[...]
 
 
 def group_kernel(part, *refs):
@@ -246,7 +256,7 @@
 def back_group_kernel(part, *refs):
     keeps, up = refs[GROUP : GROUP + 2]
     down, came = refs[-2:]
-    in_order(refs[:GROUP], came)
+    in_order(refs[:GROUP], came, back=True)
     total = came[GROUP - 1]
     for j in reversed(range(GROUP - 1)):
         total = total * keeps[j : j + 1] + came[j]
@@ -288,7 +298,7 @@
 def back_spread_kernel(part, count, *refs):
     keeps = refs[GROUP]
     came, out = refs[-2:]
-    in_order(refs[:GROUP], came)
+    in_order(refs[:GROUP], came, back=True)
     total = arrived(part, refs[GROUP + 1 : GROUP + 1 + count])[0]
     for j in reversed(range(GROUP)):
         out[j] = total
@@ -344,11 +354,11 @@
 
 
 def back_finish_kernel(
-    logits, bias, decay, skip, weight_cols, stride_ref, log_ref, spread_ref,
-    features, cotangent, writes, feature_part, skip_part, row_ref, kept, *refs,
+    logits, bias, decay, weight_cols, stride_ref, log_ref, spread_ref,
+    features, writes, feature_part, skip_part, row_ref, kept, *refs,
 ):
     haves = refs[:GROUP]
-    feature_grad, step_grad, sums, col_acc, last_acc, skip_acc, have = refs[GROUP:]
+    step_grad, sums, col_acc, last_acc, skip_acc, have = refs[GROUP:]
     heads, length = logits.shape
     state = writes.shape[1]
     width = features.shape[1]
@@ -368,7 +378,6 @@
     writes2 = jnp.concatenate([writes[...]] * 2, axis=1)
     carried = weight * matmul(writes2, stack)
     total = feature_part[...] + carried
-    feature_grad[...] = (total + wide_skip(skip, heads, spread) * cotangent[...].astype(F32)).astype(BF16)
     head_sums(col_acc, feature * total, spread)
     leaving = jnp.sum((returning * kept[...]).reshape(state // 8, 8, width), axis=0)
     leaving = leaving + jnp.sum((feature * carried).reshape(length // 8, 8, width), axis=0)
@@ -399,8 +408,10 @@
         sums[...] = jnp.broadcast_to(table[None], sums.shape)
 
 
-def write_kernel(weight_cols, spread_ref, features, write_part, *refs):
-    write_grad, write_acc, have = refs[GROUP + 1 :]
+def write_kernel(
+    skip, weight_cols, spread_ref, features, cotangent, writes, feature_part, write_part, *refs,
+):
+    feature_grad, write_grad, write_acc, have = refs[GROUP + 1 :]
     state = write_part.shape[1]
     step = pl.program_id(0)
 
@@ -409,8 +420,13 @@
         write_acc[...] = jnp.zeros_like(write_acc)
         in_order(refs[:GROUP], have)
 
-    weight = matmul(weight_cols[...], spread_ref[...])
+    spread = spread_ref[...]
+    weight = matmul(weight_cols[...], spread)
     stack = jnp.concatenate(split2(quarter_rows(have)), axis=0)
+    writes2 = jnp.concatenate([writes[...]] * 2, axis=1)
+    total = feature_part[...] + weight * matmul(writes2, stack)
+    skips = wide_skip(skip, skip.shape[1], spread) * cotangent[...].astype(F32)
+    feature_grad[...] = (total + skips).astype(BF16)
     high, low = split2(weight * features[...].astype(F32))
     write_acc[...] += matmul_nt(high, stack) + matmul_nt(low, stack)
 
@@ -452,9 +468,12 @@
     blocks, members = lax.axis_size("ctx"), lax.axis_size("dp")
     spread = spread_table(heads, head_dim)
 
+    def exchange(value, distance):
+        return lax.ppermute(value, "ctx", [(k, k ^ distance) for k in range(blocks)])
+
     def swap(values):
-        pairs = [[(k, k ^ d) for k in range(blocks)] for d in range(GROUP)]
-        return [values[0]] + [lax.ppermute(values[d], "ctx", pairs[d]) for d in range(1, GROUP)]
+        came = {d: exchange(values[d], d) for d in EARLY + LATE}
+        return [came.get(d, values[0]) for d in range(GROUP)]
 
     def shift(value, distance):
         pairs = [(k, k + distance) for k in range(blocks) if 0 <= k + distance < blocks]
@@ -493,27 +512,19 @@
     shares = pltpu.VMEM((GROUP, part, width), F32)
     long_shares = pltpu.VMEM((GROUP, part + 8, width), F32)
 
+    both = struct((2 * part + 8, width))
     out = call(
         states_kernel,
         "states",
-        [group_sum] * GROUP + [stack] * 3 + [small] * 3,
-        [SMEM] + [VMEM] * 6,
-        3,
-        24,
+        [group_sum if d in LATE else both for d in range(GROUP)] + [share] * len(LATE) + [stack] * 3 + [small] * 3,
+        [SMEM] + [VMEM] * 8,
+        4,
+        60,
         scratch_shapes=[pltpu.VMEM((state, width), F32)],
-    )(doc_starts, logits, bias, decay, spread, features, writes)
-    send, (weight_cols, factor_cols, cum_cols, cum_rows, stride, log_decay) = out[:GROUP], out[GROUP:]
+    )(doc_starts, logits, bias, decay, spread, features, writes, cotangent, reads)
+    send, late_send = out[:GROUP], out[GROUP : GROUP + len(LATE)]
+    weight_cols, factor_cols, cum_cols, cum_rows, stride, log_decay = out[GROUP + len(LATE) :]
     came = swap(send)
-    back_send = call(
-        back_states_kernel,
-        "back_states",
-        [share] * GROUP,
-        [VMEM] * 4,
-        3,
-        24,
-        scratch_shapes=[pltpu.VMEM((state, width), F32)],
-    )(factor_cols, spread, cotangent, reads)
-    back_came = swap(back_send)
 
     half = QUARTERS // 2
     started = struct((length, wide)), struct((length, wide)), struct((1, wide))
@@ -531,22 +542,12 @@
         "inner_first",
         [*started, struct((length, length))],
         specs + [ANY],
-        10,
+        1,
         24,
         grid=(half,),
         out_specs=out_specs + [square],
         scratch_shapes=score_scratch,
-    )(*inner_args, back_send[0])
-    up, keeps = call(
-        functools.partial(group_kernel, part),
-        "group",
-        [group_sum, struct((GROUP, width))],
-        [VMEM] * GROUP + [ANY],
-        2,
-        8,
-        scratch_shapes=[long_shares],
-    )(*came, score_grad)
-    ups = scan(up, 1)
+    )(*inner_args, cum_rows)
     specs, out_specs = inner_specs(half)
     inside, feature_part, skip_part, write_part, read_part = call(
         functools.partial(inner_kernel, half, True),
@@ -559,7 +560,30 @@
         out_specs=out_specs + [tokens, tokens],
         scratch_shapes=score_scratch,
         input_output_aliases={8: 0, 9: 1, 10: 2},
-    )(*inner_args, score_grad, *begun, up)
+    )(*inner_args, score_grad, *begun, cum_rows)
+    up, keeps = call(
+        functools.partial(group_kernel, part),
+        "group",
+        [group_sum, struct((GROUP, width))],
+        [VMEM] * GROUP + [ANY],
+        2,
+        8,
+        scratch_shapes=[long_shares],
+    )(*came, write_part)
+    ups = scan(up, 1)
+    held = call(hold_kernel, "hold", [share] * len(LATE), [VMEM] * len(LATE) + [ANY], 1, 8)(*late_send, up)
+    late_came = [exchange(value, d) for value, d in zip(held, LATE)]
+    back_came = [late_came[LATE.index(d)] if d in LATE else came[d] for d in range(GROUP)]
+
+    give = call(
+        functools.partial(spread_kernel, part, len(ups)),
+        "spread",
+        [share] * GROUP,
+        [VMEM] * (GROUP + len(ups)) + [ANY],
+        2,
+        12,
+        scratch_shapes=[long_shares, shares],
+    )(*came, *ups, up)
     (down,) = call(
         functools.partial(back_group_kernel, part),
         "back_group",
@@ -568,17 +592,8 @@
         2,
         8,
         scratch_shapes=[shares],
-    )(*back_came, keeps, up, write_part)
+    )(*back_came, keeps, up, give[0])
     downs = scan(down, -1)
-    give = call(
-        functools.partial(spread_kernel, part, len(ups)),
-        "spread",
-        [share] * GROUP,
-        [VMEM] * (GROUP + len(ups)) + [ANY],
-        2,
-        12,
-        scratch_shapes=[long_shares, shares],
-    )(*came, *ups, down)
     have = swap(give)
     back_give = call(
         functools.partial(back_spread_kernel, part, len(downs)),
@@ -605,18 +620,18 @@
         scratch_shapes=[pltpu.VMEM((length, 2 * state), F32), shares],
     )(skip, factor_cols, spread, features, cotangent, reads, inside, read_part, *have, back_give[0])
     devices = blocks * members
-    feature_grad, step_grad, sums = call(
+    step_grad, sums = call(
         back_finish_kernel,
         "back_finish",
-        [result, small, struct((devices, 1, LANES))],
-        [by_heads, row, row, row, columns, by_heads, by_heads, spread_quarter]
-        + [by_quarter, by_quarter, tokens, by_quarter]
+        [small, struct((devices, 1, LANES))],
+        [by_heads, row, row, columns, by_heads, by_heads, spread_quarter]
+        + [by_quarter, tokens, by_quarter]
         + [quarter_of(1), columns, quarter_of(state)]
         + [whole_share] * GROUP,
         8,
         24,
         grid=(QUARTERS,),
-        out_specs=[by_quarter, by_heads, all_of(devices, 1, LANES)],
+        out_specs=[by_heads, all_of(devices, 1, LANES)],
         scratch_shapes=[
             pltpu.VMEM((length, LANES), F32),
             pltpu.VMEM((8, LANES), F32),
@@ -624,20 +639,22 @@
             shares,
         ],
     )(
-        logits, bias, decay, skip, weight_cols, stride, log_decay, spread, features, cotangent, writes,
+        logits, bias, decay, weight_cols, stride, log_decay, spread, features, writes,
         feature_part, skip_part, rows, kept, *back_have,
     )
-    (write_grad,) = call(
+    feature_grad, write_grad = call(
         write_kernel,
         "write_grad",
-        [tokens_result],
-        [columns, spread_quarter, by_quarter, tokens] + [whole_share] * GROUP + [ANY],
-        4,
+        [result, tokens_result],
+        [row, columns, spread_quarter, by_quarter, by_quarter, tokens, by_quarter, tokens]
+        + [whole_share] * GROUP
+        + [ANY],
+        6,
         24,
         grid=(QUARTERS,),
-        out_specs=[tokens],
+        out_specs=[by_quarter, tokens],
         scratch_shapes=[pltpu.VMEM((length, 2 * state), F32), shares],
-    )(weight_cols, spread, features, write_part, *back_have, step_grad)
+    )(skip, weight_cols, spread, features, cotangent, writes, feature_part, write_part, *back_have, step_grad)
     sums = jnp.sum(lax.all_to_all(sums, ("dp", "ctx"), 0, 0), axis=(0, 1))
     return (
         mixed[None],

time: 114 us -> 118 us (1.035)
  starting transfers between devices: 58.2 us -> 50.3 us
  waiting for transfers between devices: 11.3 us -> 18.1 us
  local copies, waits for them, and re-layouts: 7.39 us -> 10.4 us
  Pallas kernels: 35.3 us -> 37.6 us
    ppermute x28 -> x24, waiting for transfers between devices: 7.07 us -> 15.2 us  [exchange(): lax.ppermute(value, 'ctx', [(k, k ^ distance) for k in range(blocks)])]
    ppermute x28 -> x24, starting transfers between devices: 47.3 us -> 41.9 us  [exchange(): lax.ppermute(value, 'ctx', [(k, k ^ distance) for k in range(blocks)])]
    unnamed x36 -> x74, local copies, waits for them, and re-layouts: 6.79 us -> 9.82 us
    all_to_all x1, waiting for transfers between devices: 2.73 us -> 0.01 us  [local(): sums = jnp.sum(lax.all_to_all(sums, ('dp', 'ctx'), 0, 0), axis=(0, 1))]
    all_to_all x1, starting transfers between devices: 5.08 us -> 2.51 us  [local(): sums = jnp.sum(lax.all_to_all(sums, ('dp', 'ctx'), 0, 0), axis=(0, 1))]
    pallas_call x4, Pallas kernels: 13.7 us -> 16 us  [the longest x1 6.46 us: local(): call(states_kernel, 'states', [group_sum if d in LATE else both for d in...]
    ppermute x2, waiting for transfers between devices: 1.53 us -> 2.91 us  [shift(): return lax.ppermute(value, 'ctx', pairs)]
  transfers between devices with their start and end apart: 31 -> 27, of which waited for: 6 -> 10; matrix products, arithmetic and copies ran while one was open for 0% -> 0% of each run, Pallas kernels for 24% -> 22%
where the time goes in v4:
time: 118 us
  starting transfers between devices  50.3 us (43%)
  Pallas kernels  37.6 us (32%)
  waiting for transfers between devices  18.1 us (15%)
  local copies, waits for them, and re-layouts  10.4 us (9%)
    ppermute x24, starting transfers between devices, exchange(): lax.ppermute(value, 'ctx', [(k, k ^ distance) for k in range(blocks)])  41.9 us
    ppermute x24, waiting for transfers between devices, exchange(): lax.ppermute(value, 'ctx', [(k, k ^ distance) for k in range(blocks)])  15.2 us
    unnamed x74, local copies, waits for them, and re-layouts  9.82 us
    pallas_call x1, Pallas kernels, local(): call(functools.partial(inner_kernel, half, True), 'inner_second', [*start...  7.39 us
    pallas_call x1, Pallas kernels, local(): call(functools.partial(inner_kernel, 0, False), 'inner_first', [*started,...  7.11 us
    pallas_call x1, Pallas kernels, local(): call(states_kernel, 'states', [group_sum if d in LATE else both for d in...  6.46 us
    pallas_call x1, Pallas kernels, local(): call(finish_kernel, 'finish', [result, tokens_result, struct((length, LAN...  6.11 us
    ppermute x2, starting transfers between devices, shift(): return lax.ppermute(value, 'ctx', pairs)  5.9 us
  transfers between devices with their start and end apart: 27, of which 10 were waited for; matrix products, arithmetic and copies ran while one was open for 0% of the time, Pallas kernels for 22%

profile of v4, /device:TPU:0, one launch (start us, length us, event | category | flops | bytes accessed | tf_op | source)
XLA Modules:
  0.0 117.6 jit_solution(724847369563643625)
XLA Ops:
  0.7 6.5 %states.1 = (f32[136,640]{1,0:T(8,128)}, f32[136,640]{1,0:T(8,128)}, f32[136,640]{1,0:T(8,128)}, f32[72,640]{1,0:T(8,128)}, f32[136,640]{1,0:T(8,128)}, /*index=...) custom-call(s32[1,4]{1,0:T(1,128)} %starts.5, ...), custom_call_target="tpu_custom_call" | custom-call | flops 4000000000 | bytes 1000000 | tf_op jit(solution)/shard_map/states/pallas_call | solution.py:516
  7.1 4.0 %collective-permute-start.2 = (f32[72,640]{1,0:T(8,128)}, f32[72,640]{1,0:T(8,128)S(1)}, u32[]{:S(2)}, u32[]{:S(2)}) collective-permute-start(f32[72,640]{1,0:T(8,128)} %get-tuple-element.75), channel_id=1, source_target_pairs={{0,3},{1,2},{2,1},{3,0},{4,7},{5,6},{6,5},{7,4},{8,11},{9,10},{10,... | collective-permute-start | bytes 552968 | tf_op jit(solution)/shard_map/ppermute | solution.py:472
  12.7 1.9 %collective-permute-start = (f32[136,640]{1,0:T(8,128)}, f32[136,640]{1,0:T(8,128)S(1)}, u32[]{:S(2)}, u32[]{:S(2)}) collective-permute-start(f32[136,640]{1,0:T(8,128)} %get-tuple-element.73), channel_id=1, source_target_pairs={{0,1},{1,0},{2,3},{3,2},{4,5},{5,4},{6,7},{7,6},{8,9},{9,8},{10,11... | collective-permute-start | bytes 1044488 | tf_op jit(solution)/shard_map/ppermute | solution.py:472
  17.7 7.1 %inner_first.1 = (f32[256,2560]{1,0:T(8,128)S(1)}, f32[256,2560]{1,0:T(8,128)S(1)}, f32[1,2560]{1,0:T(1,128)S(1)}, f32[256,256]{1,0:T(8,128)S(1)}) custom-call(s32[1,4]{1,0:T(1,128)S(1)} %copy-done.9, bf16[256,128]{1,0:T(8,128)(2,1)S(1)} %copy-done.18, f32[40,256]{1,0:T(8,128)S(1)} %copy-done.20, bf16[256,2560]{1,0:T(8,128)(2,1)S(1)} %bitcast.14, ...), custom_call_target="tpu_custom_call" | custom-call | flops 1000000000 | bytes 1000000 | tf_op jit(solution)/shard_map/inner_first/pallas_call | solution.py:540
  24.9 1.6 %collective-permute-start.3 = (f32[136,640]{1,0:T(8,128)S(1)}, f32[136,640]{1,0:T(8,128)S(1)}, u32[]{:S(2)}, u32[]{:S(2)}) collective-permute-start(f32[136,640]{1,0:T(8,128)S(1)} %copy-done.36), channel_id=1, source_target_pairs={{0,4},{1,5},{2,6},{3,7},{4,0},{5,1},{6,2},{7,3},{8,12},{9,13},{10,... | collective-permute-start | bytes 1044488 | tf_op jit(solution)/shard_map/ppermute | solution.py:472
  26.5 7.4 %inner_second.1 = (f32[256,2560]{1,0:T(8,128)S(1)}, f32[256,2560]{1,0:T(8,128)S(1)}, f32[1,2560]{1,0:T(1,128)S(1)}, f32[256,128]{1,0:T(8,128)S(1)}, f32[256,128]{1,0:T(8,128)S(1)}) custom-call(s32[1,4]{1,0:T(1,128)S(1)} %copy-done.9, bf16[256,128]{1,0:T(8,128)(2,1)S(1)} %copy-done.19, ...), custom_call_target="tpu_custom_call", output_to_operand_aliasing={{0}: (8, {}), {1}: (9, {}), {2}: (10, {})} | custom-call | flops 10000000000 | bytes 1000000 | tf_op jit(solution)/shard_map/inner_second/pallas_call | solution.py:552
  34.0 2.0 %collective-permute-done.3.refs_4_ = f32[136,640]{1,0:T(8,128)S(1)} collective-permute-done((f32[136,640]{1,0:T(8,128)S(1)}, f32[136,640]{1,0:T(8,128)S(1)}, u32[]{:S(2)}, u32[]{:S(2)}) %collective-permute-start.3) | collective-permute-done | bytes 348192 | tf_op jit(solution)/shard_map/ppermute | solution.py:472
  36.0 4.7 %collective-permute-done.6.refs_7_ = f32[136,640]{1,0:T(8,128)S(1)} collective-permute-done((f32[136,640]{1,0:T(8,128)S(1)}, f32[136,640]{1,0:T(8,128)S(1)}, u32[]{:S(2)}, u32[]{:S(2)}) %collective-permute-start.6) | collective-permute-done | bytes 348192 | tf_op jit(solution)/shard_map/ppermute | solution.py:472
  41.0 4.6 %collective-permute-start.7 = (f32[72,640]{1,0:T(8,128)S(1)}, f32[72,640]{1,0:T(8,128)S(1)}, u32[]{:S(2)}, u32[]{:S(2)}) collective-permute-start(f32[72,640]{1,0:T(8,128)S(1)} %get-tuple-element.81.refs_9_.refs_3_), channel_id=1, source_target_pairs={{0,8},{1,9},{2,10},{3,11},{4,12},{5,13},{6,14},{7,15},{16,24},{17,... | collective-permute-start | bytes 552968 | tf_op jit(solution)/shard_map/ppermute | solution.py:480
  45.6 2.5 %collective-permute-start.15 = (f32[64,640]{1,0:T(8,128)S(1)}, f32[64,640]{1,0:T(8,128)S(1)}, u32[]{:S(2)}, u32[]{:S(2)}) collective-permute-start(f32[64,640]{1,0:T(8,128)S(1)} %get-tuple-element.93), channel_id=1, source_target_pairs={{0,3},{1,2},{2,1},{3,0},{4,7},{5,6},{6,5},{7,4},{8,11},{9,10},{10,... | collective-permute-start | bytes 491528 | tf_op jit(solution)/shard_map/ppermute | solution.py:472
  50.7 2.7 %collective-permute-done.15.refs_3_ = f32[64,640]{1,0:T(8,128)S(1)} collective-permute-done((f32[64,640]{1,0:T(8,128)S(1)}, f32[64,640]{1,0:T(8,128)S(1)}, u32[]{:S(2)}, u32[]{:S(2)}) %collective-permute-start.15) | collective-permute-done | bytes 163872 | tf_op jit(solution)/shard_map/ppermute | solution.py:472
  61.0 2.2 %collective-permute-start.11 = (f32[64,640]{1,0:T(8,128)S(1)}, f32[64,640]{1,0:T(8,128)S(1)}, u32[]{:S(2)}, u32[]{:S(2)}) collective-permute-start(f32[64,640]{1,0:T(8,128)S(1)} %get-tuple-element.86), channel_id=1, source_target_pairs={{0,4},{1,5},{2,6},{3,7},{4,0},{5,1},{6,2},{7,3},{8,12},{9,13},{10,... | collective-permute-start | bytes 491528 | tf_op jit(solution)/shard_map/ppermute | solution.py:472
  63.2 2.6 %collective-permute-done.18.refs_9_ = f32[72,640]{1,0:T(8,128)S(1)} collective-permute-done((f32[72,640]{1,0:T(8,128)S(1)}, f32[72,640]{1,0:T(8,128)S(1)}, u32[]{:S(2)}, u32[]{:S(2)}) %collective-permute-start.18) | collective-permute-done | bytes 184352 | tf_op jit(solution)/shard_map/ppermute | solution.py:480
  65.8 3.8 %collective-permute-start.12 = (f32[64,640]{1,0:T(8,128)S(1)}, f32[64,640]{1,0:T(8,128)S(1)}, u32[]{:S(2)}, u32[]{:S(2)}) collective-permute-start(f32[64,640]{1,0:T(8,128)S(1)} %get-tuple-element.87), channel_id=1, source_target_pairs={{0,5},{1,4},{2,7},{3,6},{4,1},{5,0},{6,3},{7,2},{8,13},{9,12},{10,... | collective-permute-start | bytes 491528 | tf_op jit(solution)/shard_map/ppermute | solution.py:472
  70.0 2.8 %collective-permute-start.14 = (f32[64,640]{1,0:T(8,128)S(1)}, f32[64,640]{1,0:T(8,128)S(1)}, u32[]{:S(2)}, u32[]{:S(2)}) collective-permute-start(f32[64,640]{1,0:T(8,128)S(1)} %get-tuple-element.89), channel_id=1, source_target_pairs={{0,7},{1,6},{2,5},{3,4},{4,3},{5,2},{6,1},{7,0},{8,15},{9,14},{10,... | collective-permute-start | bytes 491528 | tf_op jit(solution)/shard_map/ppermute | solution.py:472
  76.4 2.2 %collective-permute-done.13.refs_6_ = f32[64,640]{1,0:T(8,128)S(1)} collective-permute-done((f32[64,640]{1,0:T(8,128)S(1)}, f32[64,640]{1,0:T(8,128)S(1)}, u32[]{:S(2)}, u32[]{:S(2)}) %collective-permute-start.13) | collective-permute-done | bytes 163872 | tf_op jit(solution)/shard_map/ppermute | solution.py:472
  78.6 1.9 %collective-permute-start.22 = (f32[64,640]{1,0:T(8,128)S(1)}, f32[64,640]{1,0:T(8,128)S(1)}, u32[]{:S(2)}, u32[]{:S(2)}) collective-permute-start(f32[64,640]{1,0:T(8,128)S(1)} %get-tuple-element.104), channel_id=1, source_target_pairs={{0,4},{1,5},{2,6},{3,7},{4,0},{5,1},{6,2},{7,3},{8,12},{9,13},{10,... | collective-permute-start | bytes 491528 | tf_op jit(solution)/shard_map/ppermute | solution.py:472
  81.4 4.6 %collective-permute-start.23 = (f32[64,640]{1,0:T(8,128)S(1)}, f32[64,640]{1,0:T(8,128)S(1)}, u32[]{:S(2)}, u32[]{:S(2)}) collective-permute-start(f32[64,640]{1,0:T(8,128)S(1)} %get-tuple-element.105), channel_id=1, source_target_pairs={{0,5},{1,4},{2,7},{3,6},{4,1},{5,0},{6,3},{7,2},{8,13},{9,12},{10,... | collective-permute-start | bytes 491528 | tf_op jit(solution)/shard_map/ppermute | solution.py:472
  86.1 4.4 %collective-permute-start.25 = (f32[64,640]{1,0:T(8,128)S(1)}, f32[64,640]{1,0:T(8,128)S(1)}, u32[]{:S(2)}, u32[]{:S(2)}) collective-permute-start(f32[64,640]{1,0:T(8,128)S(1)} %get-tuple-element.107), channel_id=1, source_target_pairs={{0,7},{1,6},{2,5},{3,4},{4,3},{5,2},{6,1},{7,0},{8,15},{9,14},{10,... | collective-permute-start | bytes 491528 | tf_op jit(solution)/shard_map/ppermute | solution.py:472
  90.6 6.1 %finish.1 = (bf16[256,2560]{1,0:T(8,128)(2,1)}, bf16[256,128]{1,0:T(8,128)(2,1)}, f32[256,128]{1,0:T(8,128)S(1)}, f32[128,2560]{1,0:T(8,128)S(1)}) custom-call(f32[1,40]{1,0:T(1,128)S(1)} %bitcast.39, bf16[256,128]{1,0:T(8,128)(2,1)S(1)} %copy-done.32, bf16[128,2560]{1,0:T(8,128)(2,1)S(1)} %copy-done.13, bf16[256,2560]{1,0:T(8,128)(2,1)S(1)} %bitcast.16, ...), custom_call_target="tpu_custom_call" | custom-call | flops 8000000000 | bytes 1000000 | tf_op jit(solution)/shard_map/finish/pallas_call | solution.py:609
  96.8 5.2 %back_finish.1 = (f32[40,256]{1,0:T(8,128)}, f32[32,1,128]{2,1,0:T(1,128)}) custom-call(f32[40,256]{1,0:T(8,128)S(1)} %bitcast.34, f32[1,40]{1,0:T(1,128)S(1)} %bitcast.36, f32[1,40]{1,0:T(1,128)S(1)} %bitcast.38, bf16[256,128]{1,0:T(8,128)(2,1)S(1)} %copy-done.30, f32[40,256]{1,0:T(8,128)S(1)} %copy-done.33, f32[40,256]{1,0:T(8,128)S(1)} %copy-done.34, ...), custom_call_target="tpu_custom_call" | custom-call | flops 8000000000 | bytes 1000000 | tf_op jit(solution)/shard_map/back_finish/pallas_call | solution.py:623
  102.0 2.5 %all-to-all-start = ((f32[32,1,128]{2,1,0:T(1,128)}), f32[32,1,128]{2,1,0:T(1,128)S(1)}, u32[]{:S(2)}, u32[]{:S(2)}) async-start(f32[32,1,128]{2,1,0:T(1,128)} %get-tuple-element.117), calls=%async_computation | async-start | bytes 32768 | tf_op jit(solution)/shard_map/all_to_all | solution.py:658
  108.2 1.7 %copy-done.17 = f32[256,2560]{1,0:T(8,128)S(1)} copy-done((f32[256,2560]{1,0:T(8,128)S(1)}, f32[256,2560]{1,0:T(8,128)}, u32[]{:S(2)}) %copy-start.17) | copy-done | bytes 2621464
  112.6 4.3 %write_grad.1 = (bf16[256,2560]{1,0:T(8,128)(2,1)}, bf16[256,128]{1,0:T(8,128)(2,1)}) custom-call(f32[1,40]{1,0:T(1,128)S(1)} %bitcast.40, bf16[256,128]{1,0:T(8,128)(2,1)S(1)} %copy-done.31, bf16[128,2560]{1,0:T(8,128)(2,1)S(1)} %copy-done.14, bf16[256,2560]{1,0:T(8,128)(2,1)S(1)} %bitcast.18, bf16[256,2560]{1,0:T(8,128)(2,1)S(1)} %bitcast.23, ...), custom_call_target="tpu_custom_call" | custom-call | flops 6000000000 | bytes 1000000 | tf_op jit(solution)/shard_map/write_grad/pallas_call | solution.py:645
  (117 shorter events, 27.1 us)
Async XLA Ops:
  7.1 17.7 %collective-permute-start.2 = (f32[72,640]{1,0:T(8,128)}, f32[72,640]{1,0:T(8,128)S(1)}, u32[]{:S(2)}, u32[]{:S(2)}) collective-permute-start(f32[72,640]{1,0:T(8,128)} %get-tuple-element.75), channel_id=1, source_target_pairs={{0,3},{1,2},{2,1},{3,0},{4,7},{5,6},{6,5},{7,4},{8,11},{9,10},{10,... | collective-permute-start | bytes 552968 | tf_op jit(solution)/shard_map/ppermute | solution.py:472
  11.1 15.4 %collective-permute-start.4 = (f32[72,640]{1,0:T(8,128)}, f32[72,640]{1,0:T(8,128)S(1)}, u32[]{:S(2)}, u32[]{:S(2)}) collective-permute-start(f32[72,640]{1,0:T(8,128)} %get-tuple-element.77), channel_id=1, source_target_pairs={{0,5},{1,4},{2,7},{3,6},{4,1},{5,0},{6,3},{7,2},{8,13},{9,12},{10,... | collective-permute-start | bytes 552968 | tf_op jit(solution)/shard_map/ppermute | solution.py:472
  12.7 21.3 %collective-permute-start.5 = (f32[72,640]{1,0:T(8,128)}, f32[72,640]{1,0:T(8,128)S(1)}, u32[]{:S(2)}, u32[]{:S(2)}) collective-permute-start(f32[72,640]{1,0:T(8,128)} %get-tuple-element.78), channel_id=1, source_target_pairs={{0,6},{1,7},{2,4},{3,5},{4,2},{5,3},{6,0},{7,1},{8,14},{9,15},{10,... | collective-permute-start | bytes 552968 | tf_op jit(solution)/shard_map/ppermute | solution.py:472
  12.7 21.3 %collective-permute-start = (f32[136,640]{1,0:T(8,128)}, f32[136,640]{1,0:T(8,128)S(1)}, u32[]{:S(2)}, u32[]{:S(2)}) collective-permute-start(f32[136,640]{1,0:T(8,128)} %get-tuple-element.73), channel_id=1, source_target_pairs={{0,1},{1,0},{2,3},{3,2},{4,5},{5,4},{6,7},{7,6},{8,9},{9,8},{10,11... | collective-permute-start | bytes 1044488 | tf_op jit(solution)/shard_map/ppermute | solution.py:472
  14.6 19.4 %collective-permute-start.1 = (f32[136,640]{1,0:T(8,128)}, f32[136,640]{1,0:T(8,128)S(1)}, u32[]{:S(2)}, u32[]{:S(2)}) collective-permute-start(f32[136,640]{1,0:T(8,128)} %get-tuple-element.74), channel_id=1, source_target_pairs={{0,2},{1,3},{2,0},{3,1},{4,6},{5,7},{6,4},{7,5},{8,10},{9,11},{10,... | collective-permute-start | bytes 1044488 | tf_op jit(solution)/shard_map/ppermute | solution.py:472
  24.9 11.2 %collective-permute-start.3 = (f32[136,640]{1,0:T(8,128)S(1)}, f32[136,640]{1,0:T(8,128)S(1)}, u32[]{:S(2)}, u32[]{:S(2)}) collective-permute-start(f32[136,640]{1,0:T(8,128)S(1)} %copy-done.36), channel_id=1, source_target_pairs={{0,4},{1,5},{2,6},{3,7},{4,0},{5,1},{6,2},{7,3},{8,12},{9,13},{10,... | collective-permute-start | bytes 1044488 | tf_op jit(solution)/shard_map/ppermute | solution.py:472
  26.5 14.2 %collective-permute-start.6 = (f32[136,640]{1,0:T(8,128)S(1)}, f32[136,640]{1,0:T(8,128)S(1)}, u32[]{:S(2)}, u32[]{:S(2)}) collective-permute-start(f32[136,640]{1,0:T(8,128)S(1)} %copy-done.35), channel_id=1, source_target_pairs={{0,7},{1,6},{2,5},{3,4},{4,3},{5,2},{6,1},{7,0},{8,15},{9,14},{10,... | collective-permute-start | bytes 1044488 | tf_op jit(solution)/shard_map/ppermute | solution.py:472
  41.0 9.5 %collective-permute-start.7 = (f32[72,640]{1,0:T(8,128)S(1)}, f32[72,640]{1,0:T(8,128)S(1)}, u32[]{:S(2)}, u32[]{:S(2)}) collective-permute-start(f32[72,640]{1,0:T(8,128)S(1)} %get-tuple-element.81.refs_9_.refs_3_), channel_id=1, source_target_pairs={{0,8},{1,9},{2,10},{3,11},{4,12},{5,13},{6,14},{7,15},{16,24},{17,... | collective-permute-start | bytes 552968 | tf_op jit(solution)/shard_map/ppermute | solution.py:480
  56.1 9.7 %collective-permute-start.18 = (f32[72,640]{1,0:T(8,128)S(1)}, f32[72,640]{1,0:T(8,128)S(1)}, u32[]{:S(2)}, u32[]{:S(2)}) collective-permute-start(f32[72,640]{1,0:T(8,128)S(1)} %back_group.1), channel_id=1, source_target_pairs={{8,0},{9,1},{10,2},{11,3},{12,4},{13,5},{14,6},{15,7},{24,16},{25,... | collective-permute-start | bytes 552968 | tf_op jit(solution)/shard_map/ppermute | solution.py:480
  57.4 12.5 %collective-permute-start.8 = (f32[64,640]{1,0:T(8,128)S(1)}, f32[64,640]{1,0:T(8,128)S(1)}, u32[]{:S(2)}, u32[]{:S(2)}) collective-permute-start(f32[64,640]{1,0:T(8,128)S(1)} %get-tuple-element.83), channel_id=1, source_target_pairs={{0,1},{1,0},{2,3},{3,2},{4,5},{5,4},{6,7},{7,6},{8,9},{9,8},{10,11... | collective-permute-start | bytes 491528 | tf_op jit(solution)/shard_map/ppermute | solution.py:472
  59.0 11.0 %collective-permute-start.9 = (f32[64,640]{1,0:T(8,128)S(1)}, f32[64,640]{1,0:T(8,128)S(1)}, u32[]{:S(2)}, u32[]{:S(2)}) collective-permute-start(f32[64,640]{1,0:T(8,128)S(1)} %get-tuple-element.84), channel_id=1, source_target_pairs={{0,2},{1,3},{2,0},{3,1},{4,6},{5,7},{6,4},{7,5},{8,10},{9,11},{10,... | collective-permute-start | bytes 491528 | tf_op jit(solution)/shard_map/ppermute | solution.py:472
  60.5 12.4 %collective-permute-start.10 = (f32[64,640]{1,0:T(8,128)S(1)}, f32[64,640]{1,0:T(8,128)S(1)}, u32[]{:S(2)}, u32[]{:S(2)}) collective-permute-start(f32[64,640]{1,0:T(8,128)S(1)} %get-tuple-element.85), channel_id=1, source_target_pairs={{0,3},{1,2},{2,1},{3,0},{4,7},{5,6},{6,5},{7,4},{8,11},{9,10},{10,... | collective-permute-start | bytes 491528 | tf_op jit(solution)/shard_map/ppermute | solution.py:472
  61.0 13.4 %collective-permute-start.11 = (f32[64,640]{1,0:T(8,128)S(1)}, f32[64,640]{1,0:T(8,128)S(1)}, u32[]{:S(2)}, u32[]{:S(2)}) collective-permute-start(f32[64,640]{1,0:T(8,128)S(1)} %get-tuple-element.86), channel_id=1, source_target_pairs={{0,4},{1,5},{2,6},{3,7},{4,0},{5,1},{6,2},{7,3},{8,12},{9,13},{10,... | collective-permute-start | bytes 491528 | tf_op jit(solution)/shard_map/ppermute | solution.py:472
  65.8 9.9 %collective-permute-start.12 = (f32[64,640]{1,0:T(8,128)S(1)}, f32[64,640]{1,0:T(8,128)S(1)}, u32[]{:S(2)}, u32[]{:S(2)}) collective-permute-start(f32[64,640]{1,0:T(8,128)S(1)} %get-tuple-element.87), channel_id=1, source_target_pairs={{0,5},{1,4},{2,7},{3,6},{4,1},{5,0},{6,3},{7,2},{8,13},{9,12},{10,... | collective-permute-start | bytes 491528 | tf_op jit(solution)/shard_map/ppermute | solution.py:472
  69.9 8.7 %collective-permute-start.13 = (f32[64,640]{1,0:T(8,128)S(1)}, f32[64,640]{1,0:T(8,128)S(1)}, u32[]{:S(2)}, u32[]{:S(2)}) collective-permute-start(f32[64,640]{1,0:T(8,128)S(1)} %get-tuple-element.88), channel_id=1, source_target_pairs={{0,6},{1,7},{2,4},{3,5},{4,2},{5,3},{6,0},{7,1},{8,14},{9,15},{10,... | collective-permute-start | bytes 491528 | tf_op jit(solution)/shard_map/ppermute | solution.py:472
  70.0 11.3 %collective-permute-start.14 = (f32[64,640]{1,0:T(8,128)S(1)}, f32[64,640]{1,0:T(8,128)S(1)}, u32[]{:S(2)}, u32[]{:S(2)}) collective-permute-start(f32[64,640]{1,0:T(8,128)S(1)} %get-tuple-element.89), channel_id=1, source_target_pairs={{0,7},{1,6},{2,5},{3,4},{4,3},{5,2},{6,1},{7,0},{8,15},{9,14},{10,... | collective-permute-start | bytes 491528 | tf_op jit(solution)/shard_map/ppermute | solution.py:472
  72.9 13.1 %collective-permute-start.19 = (f32[64,640]{1,0:T(8,128)S(1)}, f32[64,640]{1,0:T(8,128)S(1)}, u32[]{:S(2)}, u32[]{:S(2)}) collective-permute-start(f32[64,640]{1,0:T(8,128)S(1)} %get-tuple-element.101), channel_id=1, source_target_pairs={{0,1},{1,0},{2,3},{3,2},{4,5},{5,4},{6,7},{7,6},{8,9},{9,8},{10,11... | collective-permute-start | bytes 491528 | tf_op jit(solution)/shard_map/ppermute | solution.py:472
  74.4 11.7 %collective-permute-start.20 = (f32[64,640]{1,0:T(8,128)S(1)}, f32[64,640]{1,0:T(8,128)S(1)}, u32[]{:S(2)}, u32[]{:S(2)}) collective-permute-start(f32[64,640]{1,0:T(8,128)S(1)} %get-tuple-element.102), channel_id=1, source_target_pairs={{0,2},{1,3},{2,0},{3,1},{4,6},{5,7},{6,4},{7,5},{8,10},{9,11},{10,... | collective-permute-start | bytes 491528 | tf_op jit(solution)/shard_map/ppermute | solution.py:472
  75.7 20.9 %collective-permute-start.21 = (f32[64,640]{1,0:T(8,128)S(1)}, f32[64,640]{1,0:T(8,128)S(1)}, u32[]{:S(2)}, u32[]{:S(2)}) collective-permute-start(f32[64,640]{1,0:T(8,128)S(1)} %get-tuple-element.103), channel_id=1, source_target_pairs={{0,3},{1,2},{2,1},{3,0},{4,7},{5,6},{6,5},{7,4},{8,11},{9,10},{10,... | collective-permute-start | bytes 491528 | tf_op jit(solution)/shard_map/ppermute | solution.py:472
  78.6 18.1 %collective-permute-start.22 = (f32[64,640]{1,0:T(8,128)S(1)}, f32[64,640]{1,0:T(8,128)S(1)}, u32[]{:S(2)}, u32[]{:S(2)}) collective-permute-start(f32[64,640]{1,0:T(8,128)S(1)} %get-tuple-element.104), channel_id=1, source_target_pairs={{0,4},{1,5},{2,6},{3,7},{4,0},{5,1},{6,2},{7,3},{8,12},{9,13},{10,... | collective-permute-start | bytes 491528 | tf_op jit(solution)/shard_map/ppermute | solution.py:472
  81.4 15.3 %collective-permute-start.23 = (f32[64,640]{1,0:T(8,128)S(1)}, f32[64,640]{1,0:T(8,128)S(1)}, u32[]{:S(2)}, u32[]{:S(2)}) collective-permute-start(f32[64,640]{1,0:T(8,128)S(1)} %get-tuple-element.105), channel_id=1, source_target_pairs={{0,5},{1,4},{2,7},{3,6},{4,1},{5,0},{6,3},{7,2},{8,13},{9,12},{10,... | collective-permute-start | bytes 491528 | tf_op jit(solution)/shard_map/ppermute | solution.py:472
  85.9 10.7 %collective-permute-start.24 = (f32[64,640]{1,0:T(8,128)S(1)}, f32[64,640]{1,0:T(8,128)S(1)}, u32[]{:S(2)}, u32[]{:S(2)}) collective-permute-start(f32[64,640]{1,0:T(8,128)S(1)} %get-tuple-element.106), channel_id=1, source_target_pairs={{0,6},{1,7},{2,4},{3,5},{4,2},{5,3},{6,0},{7,1},{8,14},{9,15},{10,... | collective-permute-start | bytes 491528 | tf_op jit(solution)/shard_map/ppermute | solution.py:472
  86.1 10.6 %collective-permute-start.25 = (f32[64,640]{1,0:T(8,128)S(1)}, f32[64,640]{1,0:T(8,128)S(1)}, u32[]{:S(2)}, u32[]{:S(2)}) collective-permute-start(f32[64,640]{1,0:T(8,128)S(1)} %get-tuple-element.107), channel_id=1, source_target_pairs={{0,7},{1,6},{2,5},{3,4},{4,3},{5,2},{6,1},{7,0},{8,15},{9,14},{10,... | collective-permute-start | bytes 491528 | tf_op jit(solution)/shard_map/ppermute | solution.py:472
  102.0 15.0 %all-to-all-start = ((f32[32,1,128]{2,1,0:T(1,128)}), f32[32,1,128]{2,1,0:T(1,128)S(1)}, u32[]{:S(2)}, u32[]{:S(2)}) async-start(f32[32,1,128]{2,1,0:T(1,128)} %get-tuple-element.117), calls=%async_computation | async-start | bytes 32768 | tf_op jit(solution)/shard_map/all_to_all | solution.py:658
  (40 other events, 388.1 us)

commit v5 on v4

--- a/solution.py
+++ b/solution.py
@@ -13,7 +13,7 @@
 QUARTERS = 4
 HALVES = 2
 GROUP = QUARTERS * HALVES
-EARLY, LATE = (1, 2, 4, 7), (3, 5, 6)
+DISTANCES = (1, 2, 4, 7, 3, 5, 6)
 LANES = 128
 LOG2E = 1.4426950408889634
 FAR = -1e30
@@ -95,8 +95,7 @@
 
 def states_kernel(starts, logits, bias, decay, spread_ref, features, writes, cotangent, reads, *refs):
     sends = refs[:GROUP]
-    late = refs[GROUP : GROUP + len(LATE)]
-    weight_cols, factor_cols, cum_cols, cum_rows, stride_out, log_out, scratch = refs[GROUP + len(LATE) :]
+    weight_cols, factor_cols, cum_cols, cum_rows, stride_out, log_out, scratch = refs[GROUP:]
     heads, length = logits.shape
     state = writes.shape[1]
     width = features.shape[1] // QUARTERS
@@ -134,11 +133,7 @@
         high, low = split2(cotangent[:, cols].astype(F32) * wide)
         return matmul(read_t, high) + matmul(read_t, low)
 
-    places = [
-        late[LATE.index(distance)] if distance in LATE else send.at[part + 8 :]
-        for distance, send in enumerate(sends)
-    ]
-    share_out(own, back_quarter, places, scratch)
+    share_out(own, back_quarter, [send.at[part + 8 :] for send in sends], scratch)
     for distance, send in enumerate(sends):
         send[part : part + 8] = keeps[distance % QUARTERS]
     weight_cols[...] = weight_stack
@@ -233,12 +228,6 @@
         scratch[own ^ distance] = ref[first : first + rows]
 
 
-def hold_kernel(*refs):
-    count = len(LATE)
-    for value, out in zip(refs[:count], refs[count + 1 :]):
-        out[...] = value[...]
-
-
 def group_kernel(part, *refs):
     up, keeps, came = refs[-3:]
     in_order(refs[:GROUP], came)
@@ -472,7 +461,7 @@
         return lax.ppermute(value, "ctx", [(k, k ^ distance) for k in range(blocks)])
 
     def swap(values):
-        came = {d: exchange(values[d], d) for d in EARLY + LATE}
+        came = {d: exchange(values[d], d) for d in DISTANCES}
         return [came.get(d, values[0]) for d in range(GROUP)]
 
     def shift(value, distance):
@@ -516,15 +505,14 @@
     out = call(
         states_kernel,
         "states",
-        [group_sum if d in LATE else both for d in range(GROUP)] + [share] * len(LATE) + [stack] * 3 + [small] * 3,
+        [both] * GROUP + [stack] * 3 + [small] * 3,
         [SMEM] + [VMEM] * 8,
         4,
         60,
         scratch_shapes=[pltpu.VMEM((state, width), F32)],
     )(doc_starts, logits, bias, decay, spread, features, writes, cotangent, reads)
-    send, late_send = out[:GROUP], out[GROUP : GROUP + len(LATE)]
-    weight_cols, factor_cols, cum_cols, cum_rows, stride, log_decay = out[GROUP + len(LATE) :]
-    came = swap(send)
+    came = swap(out[:GROUP])
+    weight_cols, factor_cols, cum_cols, cum_rows, stride, log_decay = out[GROUP:]
 
     half = QUARTERS // 2
     started = struct((length, wide)), struct((length, wide)), struct((1, wide))
@@ -571,10 +559,16 @@
         scratch_shapes=[long_shares],
     )(*came, write_part)
     ups = scan(up, 1)
-    held = call(hold_kernel, "hold", [share] * len(LATE), [VMEM] * len(LATE) + [ANY], 1, 8)(*late_send, up)
-    late_came = [exchange(value, d) for value, d in zip(held, LATE)]
-    back_came = [late_came[LATE.index(d)] if d in LATE else came[d] for d in range(GROUP)]
-
+    (down,) = call(
+        functools.partial(back_group_kernel, part),
+        "back_group",
+        [group_sum],
+        [VMEM] * (GROUP + 2),
+        2,
+        8,
+        scratch_shapes=[shares],
+    )(*came, keeps, up)
+    downs = scan(down, -1)
     give = call(
         functools.partial(spread_kernel, part, len(ups)),
         "spread",
@@ -583,17 +577,7 @@
         2,
         12,
         scratch_shapes=[long_shares, shares],
-    )(*came, *ups, up)
-    (down,) = call(
-        functools.partial(back_group_kernel, part),
-        "back_group",
-        [group_sum],
-        [VMEM] * (GROUP + 2) + [ANY],
-        2,
-        8,
-        scratch_shapes=[shares],
-    )(*back_came, keeps, up, give[0])
-    downs = scan(down, -1)
+    )(*came, *ups, down)
     have = swap(give)
     back_give = call(
         functools.partial(back_spread_kernel, part, len(downs)),
@@ -603,7 +587,7 @@
         2,
         12,
         scratch_shapes=[shares, shares],
-    )(*back_came, keeps, *downs, give[0])
+    )(*came, keeps, *downs, give[0])
     back_have = swap(back_give)
 
     mixed, read_grad, rows, kept = call(
@@ -650,7 +634,7 @@
         + [whole_share] * GROUP
         + [ANY],
         6,
-        24,
+        60,
         grid=(QUARTERS,),
         out_specs=[by_quarter, tokens],
         scratch_shapes=[pltpu.VMEM((length, 2 * state), F32), shares],

time: 118 us -> 112 us (0.949)
  local copies, waits for them, and re-layouts: 10.4 us -> 2.32 us
  starting transfers between devices: 50.3 us -> 44.3 us
  waiting for transfers between devices: 18.1 us -> 23.7 us
  Pallas kernels: 37.6 us -> 39.7 us
    unnamed x74 -> x58, local copies, waits for them, and re-layouts: 9.82 us -> 1.73 us
    ppermute x24 -> x21, starting transfers between devices: 41.9 us -> 34.3 us  [exchange(): lax.ppermute(value, 'ctx', [(k, k ^ distance) for k in range(blocks)])]
    ppermute x24 -> x21, waiting for transfers between devices: 15.2 us -> 21.6 us  [exchange(): lax.ppermute(value, 'ctx', [(k, k ^ distance) for k in range(blocks)])]
    pallas_call x1, Pallas kernels: 4.33 us -> 6.62 us  [local(): call(write_kernel, 'write_grad', [result, tokens_result], [row, columns,...]
    all_to_all x1, starting transfers between devices: 2.51 us -> 4.28 us  [local(): sums = jnp.sum(lax.all_to_all(sums, ('dp', 'ctx'), 0, 0), axis=(0, 1))]
    ppermute x2, waiting for transfers between devices: 2.91 us -> 1.57 us  [shift(): return lax.ppermute(value, 'ctx', pairs)]
    pallas_call x2 -> x1, Pallas kernels: 6.5 us -> 6.39 us  [local(): call(states_kernel, 'states', [both] * GROUP + [stack] * 3 + [small] * 3,...]
  transfers between devices with their start and end apart: 27 -> 24, of which waited for: 10 -> 10; matrix products, arithmetic and copies ran while one was open for 0% -> 0% of each run, Pallas kernels for 22% -> 25%
where the time goes in v5:
time: 112 us; the launch traced here: 111 us
  starting transfers between devices  44.3 us (40%)
  Pallas kernels  39.7 us (35%)
  waiting for transfers between devices  23.7 us (21%)
  local copies, waits for them, and re-layouts  2.32 us (2%)
    ppermute x21, starting transfers between devices, exchange(): lax.ppermute(value, 'ctx', [(k, k ^ distance) for k in range(blocks)])  34.3 us
    ppermute x21, waiting for transfers between devices, exchange(): lax.ppermute(value, 'ctx', [(k, k ^ distance) for k in range(blocks)])  21.6 us
    pallas_call x1, Pallas kernels, local(): call(functools.partial(inner_kernel, half, True), 'inner_second', [*start...  7.37 us
    pallas_call x1, Pallas kernels, local(): call(functools.partial(inner_kernel, 0, False), 'inner_first', [*started,...  7.08 us
    pallas_call x1, Pallas kernels, local(): call(write_kernel, 'write_grad', [result, tokens_result], [row, columns,...  6.62 us
    pallas_call x1, Pallas kernels, local(): call(states_kernel, 'states', [both] * GROUP + [stack] * 3 + [small] * 3,...  6.39 us
    pallas_call x1, Pallas kernels, local(): call(finish_kernel, 'finish', [result, tokens_result, struct((length, LAN...  6.1 us
    ppermute x2, starting transfers between devices, shift(): return lax.ppermute(value, 'ctx', pairs)  5.81 us
  transfers between devices with their start and end apart: 24, of which 10 were waited for; matrix products, arithmetic and copies ran while one was open for 0% of the time, Pallas kernels for 25%

profile of v5, /device:TPU:0, one launch (start us, length us, event | category | flops | bytes accessed | tf_op | source)
XLA Modules:
  0.0 111.2 jit_solution(12041140966649684719)
XLA Ops:
  0.7 6.4 %states.1 = (f32[136,640]{1,0:T(8,128)}, f32[136,640]{1,0:T(8,128)}, f32[136,640]{1,0:T(8,128)}, f32[136,640]{1,0:T(8,128)}, f32[136,640]{1,0:T(8,128)}, /*index...) custom-call(s32[1,4]{1,0:T(1,128)} %starts.5, ...), custom_call_target="tpu_custom_call" | custom-call | flops 4000000000 | bytes 1000000 | tf_op jit(solution)/shard_map/states/pallas_call | solution.py:505
  7.1 3.0 %collective-permute-start = (f32[136,640]{1,0:T(8,128)}, f32[136,640]{1,0:T(8,128)S(1)}, u32[]{:S(2)}, u32[]{:S(2)}) collective-permute-start(f32[136,640]{1,0:T(8,128)} %get-tuple-element.67), channel_id=1, source_target_pairs={{0,1},{1,0},{2,3},{3,2},{4,5},{5,4},{6,7},{7,6},{8,9},{9,8},{10,11... | collective-permute-start | bytes 1044488 | tf_op jit(solution)/shard_map/ppermute | solution.py:461
  10.1 1.5 %collective-permute-start.1 = (f32[136,640]{1,0:T(8,128)}, f32[136,640]{1,0:T(8,128)S(1)}, u32[]{:S(2)}, u32[]{:S(2)}) collective-permute-start(f32[136,640]{1,0:T(8,128)} %get-tuple-element.68), channel_id=1, source_target_pairs={{0,2},{1,3},{2,0},{3,1},{4,6},{5,7},{6,4},{7,5},{8,10},{9,11},{10,... | collective-permute-start | bytes 1044488 | tf_op jit(solution)/shard_map/ppermute | solution.py:461
  11.6 2.0 %collective-permute-start.3 = (f32[136,640]{1,0:T(8,128)}, f32[136,640]{1,0:T(8,128)S(1)}, u32[]{:S(2)}, u32[]{:S(2)}) collective-permute-start(f32[136,640]{1,0:T(8,128)} %get-tuple-element.70), channel_id=1, source_target_pairs={{0,4},{1,5},{2,6},{3,7},{4,0},{5,1},{6,2},{7,3},{8,12},{9,13},{10,... | collective-permute-start | bytes 1044488 | tf_op jit(solution)/shard_map/ppermute | solution.py:461
  16.7 7.1 %inner_first.1 = (f32[256,2560]{1,0:T(8,128)S(1)}, f32[256,2560]{1,0:T(8,128)S(1)}, f32[1,2560]{1,0:T(1,128)S(1)}, f32[256,256]{1,0:T(8,128)S(1)}) custom-call(s32[1,4]{1,0:T(1,128)S(1)} %copy-done.12, bf16[256,128]{1,0:T(8,128)(2,1)S(1)} %copy-done.18, f32[40,256]{1,0:T(8,128)S(1)} %copy-done.19, bf16[256,2560]{1,0:T(8,128)(2,1)S(1)} %bitcast.15, ...), custom_call_target="tpu_custom_call" | custom-call | flops 1000000000 | bytes 1000000 | tf_op jit(solution)/shard_map/inner_first/pallas_call | solution.py:528
  23.8 2.6 %collective-permute-start.5 = (f32[136,640]{1,0:T(8,128)S(1)}, f32[136,640]{1,0:T(8,128)S(1)}, u32[]{:S(2)}, u32[]{:S(2)}) collective-permute-start(f32[136,640]{1,0:T(8,128)S(1)} %copy-done.28), channel_id=1, source_target_pairs={{0,6},{1,7},{2,4},{3,5},{4,2},{5,3},{6,0},{7,1},{8,14},{9,15},{10,... | collective-permute-start | bytes 1044488 | tf_op jit(solution)/shard_map/ppermute | solution.py:461
  26.5 7.4 %inner_second.1 = (f32[256,2560]{1,0:T(8,128)S(1)}, f32[256,2560]{1,0:T(8,128)S(1)}, f32[1,2560]{1,0:T(1,128)S(1)}, f32[256,128]{1,0:T(8,128)S(1)}, f32[256,128]{1,0:T(8,128)S(1)}) custom-call(s32[1,4]{1,0:T(1,128)S(1)} %copy-done.12, bf16[256,128]{1,0:T(8,128)(2,1)S(1)} %copy-done.18, ...), custom_call_target="tpu_custom_call", output_to_operand_aliasing={{0}: (8, {}), {1}: (9, {}), {2}: (10, {})} | custom-call | flops 10000000000 | bytes 1000000 | tf_op jit(solution)/shard_map/inner_second/pallas_call | solution.py:540
  33.9 2.9 %collective-permute-done.2.refs_3_ = f32[136,640]{1,0:T(8,128)S(1)} collective-permute-done((f32[136,640]{1,0:T(8,128)}, f32[136,640]{1,0:T(8,128)S(1)}, u32[]{:S(2)}, u32[]{:S(2)}) %collective-permute-start.2) | collective-permute-done | bytes 348192 | tf_op jit(solution)/shard_map/ppermute | solution.py:461
  36.7 4.7 %collective-permute-done.5.refs_6_ = f32[136,640]{1,0:T(8,128)S(1)} collective-permute-done((f32[136,640]{1,0:T(8,128)S(1)}, f32[136,640]{1,0:T(8,128)S(1)}, u32[]{:S(2)}, u32[]{:S(2)}) %collective-permute-start.5) | collective-permute-done | bytes 348192 | tf_op jit(solution)/shard_map/ppermute | solution.py:461
  41.4 6.6 %collective-permute-done.6.refs_7_ = f32[136,640]{1,0:T(8,128)S(1)} collective-permute-done((f32[136,640]{1,0:T(8,128)S(1)}, f32[136,640]{1,0:T(8,128)S(1)}, u32[]{:S(2)}, u32[]{:S(2)}) %collective-permute-start.6) | collective-permute-done | bytes 348192 | tf_op jit(solution)/shard_map/ppermute | solution.py:461
  48.3 4.5 %collective-permute-start.7 = (f32[72,640]{1,0:T(8,128)S(1)}, f32[72,640]{1,0:T(8,128)S(1)}, u32[]{:S(2)}, u32[]{:S(2)}) collective-permute-start(f32[72,640]{1,0:T(8,128)S(1)} %get-tuple-element.75.refs_9_), channel_id=1, source_target_pairs={{0,8},{1,9},{2,10},{3,11},{4,12},{5,13},{6,14},{7,15},{16,24},{17,... | collective-permute-start | bytes 552968 | tf_op jit(solution)/shard_map/ppermute | solution.py:469
  54.3 1.6 %collective-permute-done.7.refs_8_ = f32[72,640]{1,0:T(8,128)S(1)} collective-permute-done((f32[72,640]{1,0:T(8,128)S(1)}, f32[72,640]{1,0:T(8,128)S(1)}, u32[]{:S(2)}, u32[]{:S(2)}) %collective-permute-start.7) | collective-permute-done | bytes 184352 | tf_op jit(solution)/shard_map/ppermute | solution.py:469
  57.7 2.0 %collective-permute-start.10 = (f32[64,640]{1,0:T(8,128)S(1)}, f32[64,640]{1,0:T(8,128)S(1)}, u32[]{:S(2)}, u32[]{:S(2)}) collective-permute-start(f32[64,640]{1,0:T(8,128)S(1)} %get-tuple-element.80), channel_id=1, source_target_pairs={{0,3},{1,2},{2,1},{3,0},{4,7},{5,6},{6,5},{7,4},{8,11},{9,10},{10,... | collective-permute-start | bytes 491528 | tf_op jit(solution)/shard_map/ppermute | solution.py:461
  59.7 4.4 %collective-permute-start.11 = (f32[64,640]{1,0:T(8,128)S(1)}, f32[64,640]{1,0:T(8,128)S(1)}, u32[]{:S(2)}, u32[]{:S(2)}) collective-permute-start(f32[64,640]{1,0:T(8,128)S(1)} %get-tuple-element.81), channel_id=1, source_target_pairs={{0,4},{1,5},{2,6},{3,7},{4,0},{5,1},{6,2},{7,3},{8,12},{9,13},{10,... | collective-permute-start | bytes 491528 | tf_op jit(solution)/shard_map/ppermute | solution.py:461
  64.8 4.6 %collective-permute-start.13 = (f32[64,640]{1,0:T(8,128)S(1)}, f32[64,640]{1,0:T(8,128)S(1)}, u32[]{:S(2)}, u32[]{:S(2)}) collective-permute-start(f32[64,640]{1,0:T(8,128)S(1)} %get-tuple-element.83), channel_id=1, source_target_pairs={{0,6},{1,7},{2,4},{3,5},{4,2},{5,3},{6,0},{7,1},{8,14},{9,15},{10,... | collective-permute-start | bytes 491528 | tf_op jit(solution)/shard_map/ppermute | solution.py:461
  74.3 2.8 %collective-permute-done.13.refs_6_ = f32[64,640]{1,0:T(8,128)S(1)} collective-permute-done((f32[64,640]{1,0:T(8,128)S(1)}, f32[64,640]{1,0:T(8,128)S(1)}, u32[]{:S(2)}, u32[]{:S(2)}) %collective-permute-start.13) | collective-permute-done | bytes 163872 | tf_op jit(solution)/shard_map/ppermute | solution.py:461
  78.0 1.6 %collective-permute-done.14.refs_7_ = f32[64,640]{1,0:T(8,128)S(1)} collective-permute-done((f32[64,640]{1,0:T(8,128)S(1)}, f32[64,640]{1,0:T(8,128)S(1)}, u32[]{:S(2)}, u32[]{:S(2)}) %collective-permute-start.14) | collective-permute-done | bytes 163872 | tf_op jit(solution)/shard_map/ppermute | solution.py:461
  79.6 2.3 %collective-permute-start.20 = (f32[64,640]{1,0:T(8,128)S(1)}, f32[64,640]{1,0:T(8,128)S(1)}, u32[]{:S(2)}, u32[]{:S(2)}) collective-permute-start(f32[64,640]{1,0:T(8,128)S(1)} %get-tuple-element.93), channel_id=1, source_target_pairs={{0,5},{1,4},{2,7},{3,6},{4,1},{5,0},{6,3},{7,2},{8,13},{9,12},{10,... | collective-permute-start | bytes 491528 | tf_op jit(solution)/shard_map/ppermute | solution.py:461
  81.9 1.7 %collective-permute-start.21 = (f32[64,640]{1,0:T(8,128)S(1)}, f32[64,640]{1,0:T(8,128)S(1)}, u32[]{:S(2)}, u32[]{:S(2)}) collective-permute-start(f32[64,640]{1,0:T(8,128)S(1)} %get-tuple-element.94), channel_id=1, source_target_pairs={{0,6},{1,7},{2,4},{3,5},{4,2},{5,3},{6,0},{7,1},{8,14},{9,15},{10,... | collective-permute-start | bytes 491528 | tf_op jit(solution)/shard_map/ppermute | solution.py:461
  85.2 6.1 %finish.1 = (bf16[256,2560]{1,0:T(8,128)(2,1)}, bf16[256,128]{1,0:T(8,128)(2,1)}, f32[256,128]{1,0:T(8,128)S(1)}, f32[128,2560]{1,0:T(8,128)S(1)}) custom-call(f32[1,40]{1,0:T(1,128)S(1)} %bitcast.40, bf16[256,128]{1,0:T(8,128)(2,1)S(1)} %copy-done.24, bf16[128,2560]{1,0:T(8,128)(2,1)S(1)} %copy-done.16, bf16[256,2560]{1,0:T(8,128)(2,1)S(1)} %bitcast.17, ...), custom_call_target="tpu_custom_call" | custom-call | flops 8000000000 | bytes 1000000 | tf_op jit(solution)/shard_map/finish/pallas_call | solution.py:593
  91.9 1.9 %collective-permute-done.22.refs_7_ = f32[64,640]{1,0:T(8,128)S(1)} collective-permute-done((f32[64,640]{1,0:T(8,128)S(1)}, f32[64,640]{1,0:T(8,128)S(1)}, u32[]{:S(2)}, u32[]{:S(2)}) %collective-permute-start.22) | collective-permute-done | bytes 163872 | tf_op jit(solution)/shard_map/ppermute | solution.py:461
  93.9 5.1 %back_finish.1 = (f32[40,256]{1,0:T(8,128)}, f32[32,1,128]{2,1,0:T(1,128)}) custom-call(f32[40,256]{1,0:T(8,128)S(1)} %bitcast.34, f32[1,40]{1,0:T(1,128)S(1)} %bitcast.36, f32[1,40]{1,0:T(1,128)S(1)} %bitcast.38, bf16[256,128]{1,0:T(8,128)(2,1)S(1)} %copy-done.23, f32[40,256]{1,0:T(8,128)S(1)} %copy-done.25, f32[40,256]{1,0:T(8,128)S(1)} %copy-done.26, ...), custom_call_target="tpu_custom_call" | custom-call | flops 8000000000 | bytes 1000000 | tf_op jit(solution)/shard_map/back_finish/pallas_call | solution.py:607
  99.1 4.3 %all-to-all-start = ((f32[32,1,128]{2,1,0:T(1,128)}), f32[32,1,128]{2,1,0:T(1,128)S(1)}, u32[]{:S(2)}, u32[]{:S(2)}) async-start(f32[32,1,128]{2,1,0:T(1,128)} %get-tuple-element.105), calls=%async_computation | async-start | bytes 32768 | tf_op jit(solution)/shard_map/all_to_all | solution.py:642
  103.4 6.6 %write_grad.1 = (bf16[256,2560]{1,0:T(8,128)(2,1)}, bf16[256,128]{1,0:T(8,128)(2,1)}) custom-call(f32[1,40]{1,0:T(1,128)} %bitcast.39, bf16[256,128]{1,0:T(8,128)(2,1)} %get-tuple-element.87.weight_cols, bf16[128,2560]{1,0:T(8,128)(2,1)} %constant.4.clone.spread_ref, bf16[256,2560]{1,0:T(8,128)(2,1)} %bitcast.14, bf16[256,2560]{1,0:T(8,128)(2,1)} %bitcast.20, ...), custom_call_target="tpu_custom_call" | custom-call | flops 6000000000 | bytes 1000000 | tf_op jit(solution)/shard_map/write_grad/pallas_call | solution.py:629
  (94 shorter events, 16.4 us)
Async XLA Ops:
  7.1 16.7 %collective-permute-start = (f32[136,640]{1,0:T(8,128)}, f32[136,640]{1,0:T(8,128)S(1)}, u32[]{:S(2)}, u32[]{:S(2)}) collective-permute-start(f32[136,640]{1,0:T(8,128)} %get-tuple-element.67), channel_id=1, source_target_pairs={{0,1},{1,0},{2,3},{3,2},{4,5},{5,4},{6,7},{7,6},{8,9},{9,8},{10,11... | collective-permute-start | bytes 1044488 | tf_op jit(solution)/shard_map/ppermute | solution.py:461
  10.1 16.3 %collective-permute-start.1 = (f32[136,640]{1,0:T(8,128)}, f32[136,640]{1,0:T(8,128)S(1)}, u32[]{:S(2)}, u32[]{:S(2)}) collective-permute-start(f32[136,640]{1,0:T(8,128)} %get-tuple-element.68), channel_id=1, source_target_pairs={{0,2},{1,3},{2,0},{3,1},{4,6},{5,7},{6,4},{7,5},{8,10},{9,11},{10,... | collective-permute-start | bytes 1044488 | tf_op jit(solution)/shard_map/ppermute | solution.py:461
  11.6 25.1 %collective-permute-start.2 = (f32[136,640]{1,0:T(8,128)}, f32[136,640]{1,0:T(8,128)S(1)}, u32[]{:S(2)}, u32[]{:S(2)}) collective-permute-start(f32[136,640]{1,0:T(8,128)} %get-tuple-element.69), channel_id=1, source_target_pairs={{0,3},{1,2},{2,1},{3,0},{4,7},{5,6},{6,5},{7,4},{8,11},{9,10},{10,... | collective-permute-start | bytes 1044488 | tf_op jit(solution)/shard_map/ppermute | solution.py:461
  11.6 25.1 %collective-permute-start.3 = (f32[136,640]{1,0:T(8,128)}, f32[136,640]{1,0:T(8,128)S(1)}, u32[]{:S(2)}, u32[]{:S(2)}) collective-permute-start(f32[136,640]{1,0:T(8,128)} %get-tuple-element.70), channel_id=1, source_target_pairs={{0,4},{1,5},{2,6},{3,7},{4,0},{5,1},{6,2},{7,3},{8,12},{9,13},{10,... | collective-permute-start | bytes 1044488 | tf_op jit(solution)/shard_map/ppermute | solution.py:461
  13.6 23.1 %collective-permute-start.4 = (f32[136,640]{1,0:T(8,128)}, f32[136,640]{1,0:T(8,128)S(1)}, u32[]{:S(2)}, u32[]{:S(2)}) collective-permute-start(f32[136,640]{1,0:T(8,128)} %get-tuple-element.71), channel_id=1, source_target_pairs={{0,5},{1,4},{2,7},{3,6},{4,1},{5,0},{6,3},{7,2},{8,13},{9,12},{10,... | collective-permute-start | bytes 1044488 | tf_op jit(solution)/shard_map/ppermute | solution.py:461
  23.8 17.6 %collective-permute-start.5 = (f32[136,640]{1,0:T(8,128)S(1)}, f32[136,640]{1,0:T(8,128)S(1)}, u32[]{:S(2)}, u32[]{:S(2)}) collective-permute-start(f32[136,640]{1,0:T(8,128)S(1)} %copy-done.28), channel_id=1, source_target_pairs={{0,6},{1,7},{2,4},{3,5},{4,2},{5,3},{6,0},{7,1},{8,14},{9,15},{10,... | collective-permute-start | bytes 1044488 | tf_op jit(solution)/shard_map/ppermute | solution.py:461
  26.4 21.6 %collective-permute-start.6 = (f32[136,640]{1,0:T(8,128)S(1)}, f32[136,640]{1,0:T(8,128)S(1)}, u32[]{:S(2)}, u32[]{:S(2)}) collective-permute-start(f32[136,640]{1,0:T(8,128)S(1)} %copy-done.27), channel_id=1, source_target_pairs={{0,7},{1,6},{2,5},{3,4},{4,3},{5,2},{6,1},{7,0},{8,15},{9,14},{10,... | collective-permute-start | bytes 1044488 | tf_op jit(solution)/shard_map/ppermute | solution.py:461
  48.3 7.6 %collective-permute-start.7 = (f32[72,640]{1,0:T(8,128)S(1)}, f32[72,640]{1,0:T(8,128)S(1)}, u32[]{:S(2)}, u32[]{:S(2)}) collective-permute-start(f32[72,640]{1,0:T(8,128)S(1)} %get-tuple-element.75.refs_9_), channel_id=1, source_target_pairs={{0,8},{1,9},{2,10},{3,11},{4,12},{5,13},{6,14},{7,15},{16,24},{17,... | collective-permute-start | bytes 552968 | tf_op jit(solution)/shard_map/ppermute | solution.py:469
  53.0 11.2 %collective-permute-start.15 = (f32[72,640]{1,0:T(8,128)S(1)}, f32[72,640]{1,0:T(8,128)S(1)}, u32[]{:S(2)}, u32[]{:S(2)}) collective-permute-start(f32[72,640]{1,0:T(8,128)S(1)} %back_group.1.refs_9_), channel_id=1, source_target_pairs={{8,0},{9,1},{10,2},{11,3},{12,4},{13,5},{14,6},{15,7},{24,16},{25,... | collective-permute-start | bytes 552968 | tf_op jit(solution)/shard_map/ppermute | solution.py:469
  56.2 8.6 %collective-permute-start.8 = (f32[64,640]{1,0:T(8,128)S(1)}, f32[64,640]{1,0:T(8,128)S(1)}, u32[]{:S(2)}, u32[]{:S(2)}) collective-permute-start(f32[64,640]{1,0:T(8,128)S(1)} %get-tuple-element.78), channel_id=1, source_target_pairs={{0,1},{1,0},{2,3},{3,2},{4,5},{5,4},{6,7},{7,6},{8,9},{9,8},{10,11... | collective-permute-start | bytes 491528 | tf_op jit(solution)/shard_map/ppermute | solution.py:461
  57.2 12.2 %collective-permute-start.9 = (f32[64,640]{1,0:T(8,128)S(1)}, f32[64,640]{1,0:T(8,128)S(1)}, u32[]{:S(2)}, u32[]{:S(2)}) collective-permute-start(f32[64,640]{1,0:T(8,128)S(1)} %get-tuple-element.79), channel_id=1, source_target_pairs={{0,2},{1,3},{2,0},{3,1},{4,6},{5,7},{6,4},{7,5},{8,10},{9,11},{10,... | collective-permute-start | bytes 491528 | tf_op jit(solution)/shard_map/ppermute | solution.py:461
  57.7 11.7 %collective-permute-start.10 = (f32[64,640]{1,0:T(8,128)S(1)}, f32[64,640]{1,0:T(8,128)S(1)}, u32[]{:S(2)}, u32[]{:S(2)}) collective-permute-start(f32[64,640]{1,0:T(8,128)S(1)} %get-tuple-element.80), channel_id=1, source_target_pairs={{0,3},{1,2},{2,1},{3,0},{4,7},{5,6},{6,5},{7,4},{8,11},{9,10},{10,... | collective-permute-start | bytes 491528 | tf_op jit(solution)/shard_map/ppermute | solution.py:461
  59.7 11.1 %collective-permute-start.11 = (f32[64,640]{1,0:T(8,128)S(1)}, f32[64,640]{1,0:T(8,128)S(1)}, u32[]{:S(2)}, u32[]{:S(2)}) collective-permute-start(f32[64,640]{1,0:T(8,128)S(1)} %get-tuple-element.81), channel_id=1, source_target_pairs={{0,4},{1,5},{2,6},{3,7},{4,0},{5,1},{6,2},{7,3},{8,12},{9,13},{10,... | collective-permute-start | bytes 491528 | tf_op jit(solution)/shard_map/ppermute | solution.py:461
  64.2 8.6 %collective-permute-start.12 = (f32[64,640]{1,0:T(8,128)S(1)}, f32[64,640]{1,0:T(8,128)S(1)}, u32[]{:S(2)}, u32[]{:S(2)}) collective-permute-start(f32[64,640]{1,0:T(8,128)S(1)} %get-tuple-element.82), channel_id=1, source_target_pairs={{0,5},{1,4},{2,7},{3,6},{4,1},{5,0},{6,3},{7,2},{8,13},{9,12},{10,... | collective-permute-start | bytes 491528 | tf_op jit(solution)/shard_map/ppermute | solution.py:461
  64.8 12.3 %collective-permute-start.13 = (f32[64,640]{1,0:T(8,128)S(1)}, f32[64,640]{1,0:T(8,128)S(1)}, u32[]{:S(2)}, u32[]{:S(2)}) collective-permute-start(f32[64,640]{1,0:T(8,128)S(1)} %get-tuple-element.83), channel_id=1, source_target_pairs={{0,6},{1,7},{2,4},{3,5},{4,2},{5,3},{6,0},{7,1},{8,14},{9,15},{10,... | collective-permute-start | bytes 491528 | tf_op jit(solution)/shard_map/ppermute | solution.py:461
  69.4 10.2 %collective-permute-start.14 = (f32[64,640]{1,0:T(8,128)S(1)}, f32[64,640]{1,0:T(8,128)S(1)}, u32[]{:S(2)}, u32[]{:S(2)}) collective-permute-start(f32[64,640]{1,0:T(8,128)S(1)} %get-tuple-element.84), channel_id=1, source_target_pairs={{0,7},{1,6},{2,5},{3,4},{4,3},{5,2},{6,1},{7,0},{8,15},{9,14},{10,... | collective-permute-start | bytes 491528 | tf_op jit(solution)/shard_map/ppermute | solution.py:461
  69.4 12.6 %collective-permute-start.16 = (f32[64,640]{1,0:T(8,128)S(1)}, f32[64,640]{1,0:T(8,128)S(1)}, u32[]{:S(2)}, u32[]{:S(2)}) collective-permute-start(f32[64,640]{1,0:T(8,128)S(1)} %get-tuple-element.89), channel_id=1, source_target_pairs={{0,1},{1,0},{2,3},{3,2},{4,5},{5,4},{6,7},{7,6},{8,9},{9,8},{10,11... | collective-permute-start | bytes 491528 | tf_op jit(solution)/shard_map/ppermute | solution.py:461
  70.8 12.8 %collective-permute-start.17 = (f32[64,640]{1,0:T(8,128)S(1)}, f32[64,640]{1,0:T(8,128)S(1)}, u32[]{:S(2)}, u32[]{:S(2)}) collective-permute-start(f32[64,640]{1,0:T(8,128)S(1)} %get-tuple-element.90), channel_id=1, source_target_pairs={{0,2},{1,3},{2,0},{3,1},{4,6},{5,7},{6,4},{7,5},{8,10},{9,11},{10,... | collective-permute-start | bytes 491528 | tf_op jit(solution)/shard_map/ppermute | solution.py:461
  72.8 18.5 %collective-permute-start.18 = (f32[64,640]{1,0:T(8,128)S(1)}, f32[64,640]{1,0:T(8,128)S(1)}, u32[]{:S(2)}, u32[]{:S(2)}) collective-permute-start(f32[64,640]{1,0:T(8,128)S(1)} %get-tuple-element.91), channel_id=1, source_target_pairs={{0,3},{1,2},{2,1},{3,0},{4,7},{5,6},{6,5},{7,4},{8,11},{9,10},{10,... | collective-permute-start | bytes 491528 | tf_op jit(solution)/shard_map/ppermute | solution.py:461
  77.0 14.2 %collective-permute-start.19 = (f32[64,640]{1,0:T(8,128)S(1)}, f32[64,640]{1,0:T(8,128)S(1)}, u32[]{:S(2)}, u32[]{:S(2)}) collective-permute-start(f32[64,640]{1,0:T(8,128)S(1)} %get-tuple-element.92), channel_id=1, source_target_pairs={{0,4},{1,5},{2,6},{3,7},{4,0},{5,1},{6,2},{7,3},{8,12},{9,13},{10,... | collective-permute-start | bytes 491528 | tf_op jit(solution)/shard_map/ppermute | solution.py:461
  79.6 11.7 %collective-permute-start.20 = (f32[64,640]{1,0:T(8,128)S(1)}, f32[64,640]{1,0:T(8,128)S(1)}, u32[]{:S(2)}, u32[]{:S(2)}) collective-permute-start(f32[64,640]{1,0:T(8,128)S(1)} %get-tuple-element.93), channel_id=1, source_target_pairs={{0,5},{1,4},{2,7},{3,6},{4,1},{5,0},{6,3},{7,2},{8,13},{9,12},{10,... | collective-permute-start | bytes 491528 | tf_op jit(solution)/shard_map/ppermute | solution.py:461
  81.9 10.0 %collective-permute-start.21 = (f32[64,640]{1,0:T(8,128)S(1)}, f32[64,640]{1,0:T(8,128)S(1)}, u32[]{:S(2)}, u32[]{:S(2)}) collective-permute-start(f32[64,640]{1,0:T(8,128)S(1)} %get-tuple-element.94), channel_id=1, source_target_pairs={{0,6},{1,7},{2,4},{3,5},{4,2},{5,3},{6,0},{7,1},{8,14},{9,15},{10,... | collective-permute-start | bytes 491528 | tf_op jit(solution)/shard_map/ppermute | solution.py:461
  83.7 10.2 %collective-permute-start.22 = (f32[64,640]{1,0:T(8,128)S(1)}, f32[64,640]{1,0:T(8,128)S(1)}, u32[]{:S(2)}, u32[]{:S(2)}) collective-permute-start(f32[64,640]{1,0:T(8,128)S(1)} %get-tuple-element.95), channel_id=1, source_target_pairs={{0,7},{1,6},{2,5},{3,4},{4,3},{5,2},{6,1},{7,0},{8,15},{9,14},{10,... | collective-permute-start | bytes 491528 | tf_op jit(solution)/shard_map/ppermute | solution.py:461
  99.1 11.4 %all-to-all-start = ((f32[32,1,128]{2,1,0:T(1,128)}), f32[32,1,128]{2,1,0:T(1,128)S(1)}, u32[]{:S(2)}, u32[]{:S(2)}) async-start(f32[32,1,128]{2,1,0:T(1,128)} %get-tuple-element.105), calls=%async_computation | async-start | bytes 32768 | tf_op jit(solution)/shard_map/all_to_all | solution.py:642
  (29 other events, 388.2 us)

commit v6 on v5

--- a/solution.py
+++ b/solution.py
@@ -13,13 +13,14 @@
 QUARTERS = 4
 HALVES = 2
 GROUP = QUARTERS * HALVES
-DISTANCES = (1, 2, 4, 7, 3, 5, 6)
+DISTANCES = (4, 2, 1, 7, 3, 5, 6)
 LANES = 128
 LOG2E = 1.4426950408889634
 FAR = -1e30
 VMEM = pl.BlockSpec(memory_space=pltpu.VMEM)
 SMEM = pl.BlockSpec(memory_space=pltpu.SMEM)
 ANY = pl.BlockSpec(memory_space=pl.ANY)
+INNER_AFTER = 2
 
 
 def iota(shape, axis):
@@ -144,16 +145,12 @@
     log_out[...] = log_decay
 
 
-def inner_kernel(offset, last, starts, cum_cols, cum_rows, features, cotangent, writes, reads, *refs):
-    if last:
-        refs = refs[:1] + refs[5:]
-    else:
-        refs = refs[1:]
-    if last:
-        before, inside, feature_part, skip_part, write_part, read_part = refs[:6]
-    else:
-        inside, feature_part, skip_part, grad_out = refs[:4]
-    scores_ref, mask_ref, grad_ref = refs[-3:]
+def inner_kernel(
+    starts, cum_cols, cum_rows, features, cotangent, writes, reads, weight_cols, factor_cols, spread_ref, *refs
+):
+    refs = refs[INNER_AFTER:]
+    inside, feature_part, skip_part, write_part, read_part, write_high, write_low, read_high, read_low = refs[:9]
+    scores_ref, mask_ref, grad_ref = refs[9:]
     length, width = features.shape
     heads = cum_rows.shape[0]
     here = heads // QUARTERS
@@ -169,7 +166,10 @@
         causal = iota((length, length), 0) >= iota((length, length), 1)
         mask_ref[...] = jnp.where((segment_row == segment_col) & causal, 0.0, FAR)
         scores_ref[...] = matmul_nt(reads[...], writes[...])
-        grad_ref[...] = before[...] if last else jnp.zeros_like(grad_ref)
+        grad_ref[...] = jnp.zeros_like(grad_ref)
+
+    write_high[...], write_low[...] = split2(matmul(weight_cols[...], spread_ref[...]) * features[...].astype(F32))
+    read_high[...], read_low[...] = split2(matmul(factor_cols[...], spread_ref[...]) * cotangent[...].astype(F32))
 
     def one_pair(at, carry):
         cols = pl.ds(pl.multiple_of(at * pair, LANES), pair)
@@ -178,7 +178,7 @@
         grad_f32 = grad.astype(F32)
         grad_t = grad_f32.T.astype(BF16)
         skip_part[:, cols] = jnp.sum(grad_f32 * feature.astype(F32), axis=0, keepdims=True)
-        head = (offset + step) * here + at * 2
+        head = step * here + at * 2
         lane = iota((LANES, 2 * LANES), 0)
         wanted = head + lax.div(iota((LANES, 2 * LANES), 1), LANES)
         pick = (lane == wanted) | (lane == wanted + heads) | (lane == wanted + 2 * heads)
@@ -208,16 +208,13 @@
 
     lax.fori_loop(0, here // 2, one_pair, 0)
 
-    @pl.when(step == pl.num_programs(0) - 1)
+    @pl.when(step == QUARTERS - 1)
     def _():
         score_grad = grad_ref[...]
-        if last:
-            high, low = split2(score_grad)
-            read_part[...] = matmul(high, writes[...]) + matmul(low, writes[...])
-            high, low = split2(score_grad.T)
-            write_part[...] = matmul(high, reads[...]) + matmul(low, reads[...])
-        else:
-            grad_out[...] = score_grad
+        high, low = split2(score_grad)
+        read_part[...] = matmul(high, writes[...]) + matmul(low, writes[...])
+        high, low = split2(score_grad.T)
+        write_part[...] = matmul(high, reads[...]) + matmul(low, reads[...])
 
 
 def in_order(refs, scratch, back=False):
@@ -229,7 +226,7 @@
 
 
 def group_kernel(part, *refs):
-    up, keeps, came = refs[-3:]
+    up, down, keeps, came, back_came = refs[-5:]
     in_order(refs[:GROUP], came)
     total = came[0, 0:part]
     keep = came[0, part:]
@@ -240,17 +237,12 @@
     up[part:] = keep
     for j in range(GROUP):
         keeps[j : j + 1] = came[j, part : part + 1]
-
-
-def back_group_kernel(part, *refs):
-    keeps, up = refs[GROUP : GROUP + 2]
-    down, came = refs[-2:]
-    in_order(refs[:GROUP], came, back=True)
-    total = came[GROUP - 1]
+    in_order(refs[:GROUP], back_came, back=True)
+    total = back_came[GROUP - 1]
     for j in reversed(range(GROUP - 1)):
-        total = total * keeps[j : j + 1] + came[j]
+        total = total * keeps[j : j + 1] + back_came[j]
     down[0:part] = total
-    down[part:] = up[part:]
+    down[part:] = keep
 
 
 def arrived(part, came):
@@ -267,33 +259,26 @@
     refs[-1][part:] = own[part:] * keep
 
 
-def give_out(outs, scratch):
+def spread_kernel(part, count, *refs):
+    ups, downs = refs[GROUP : GROUP + count], refs[GROUP + count : GROUP + 2 * count]
+    keeps = refs[GROUP + 2 * count]
+    outs = refs[GROUP + 2 * count + 1 : -3]
+    came, back_came, give = refs[-3:]
+    in_order(refs[:GROUP], came)
+    total = arrived(part, ups)[0]
+    for j in range(GROUP):
+        give[j, 0:part] = total
+        if j < GROUP - 1:
+            total = total * keeps[j : j + 1] + came[j, 0:part]
+    in_order(refs[:GROUP], back_came, back=True)
+    total = arrived(part, downs)[0]
+    for j in reversed(range(GROUP)):
+        give[j, part:] = total
+        if j > 0:
+            total = total * keeps[j : j + 1] + back_came[j]
     own = group_place()
     for distance, out in enumerate(outs):
-        out[...] = scratch[own ^ distance]
-
-
-def spread_kernel(part, count, *refs):
-    came, out = refs[-2:]
-    in_order(refs[:GROUP], came)
-    total = arrived(part, refs[GROUP : GROUP + count])[0]
-    for j in range(GROUP):
-        out[j] = total
-        if j < GROUP - 1:
-            total = total * came[j, part : part + 1] + came[j, 0:part]
-    give_out(refs[-2 - GROUP : -2], out)
-
-
-def back_spread_kernel(part, count, *refs):
-    keeps = refs[GROUP]
-    came, out = refs[-2:]
-    in_order(refs[:GROUP], came, back=True)
-    total = arrived(part, refs[GROUP + 1 : GROUP + 1 + count])[0]
-    for j in reversed(range(GROUP)):
-        out[j] = total
-        if j > 0:
-            total = total * keeps[j : j + 1] + came[j]
-    give_out(refs[-2 - GROUP : -2], out)
+        out[...] = give[own ^ distance]
 
 
 def head_sums(ref, value, spread):
@@ -306,48 +291,17 @@
     return matmul(stack[0:16], spread)[0:1]
 
 
-def quarter_rows(scratch):
-    step = pl.program_id(0)
-    return jnp.concatenate([scratch[half * QUARTERS + step] for half in range(HALVES)], axis=0)
-
-
-def finish_kernel(skip, factor_cols, spread_ref, features, cotangent, reads, inside, read_part, *refs):
-    haves = refs[:GROUP]
-    mixed, read_grad, rows, kept, read_acc, have = refs[GROUP + 1 :]
-    length, state = reads.shape
-    heads = skip.shape[1]
-    step = pl.program_id(0)
-
-    @pl.when(step == 0)
-    def _():
-        rows[...] = jnp.zeros_like(rows)
-        read_acc[...] = jnp.zeros_like(read_acc)
-        in_order(haves, have)
-
-    spread = spread_ref[...]
-    factor = matmul(factor_cols[...], spread)
-    grad = cotangent[...].astype(F32)
-    entering = quarter_rows(have)
-    kept[...] = entering * factor[length - 1 :]
-    stack = jnp.concatenate(split2(entering), axis=0)
-    reads2 = jnp.concatenate([reads[...]] * 2, axis=1)
-    total = inside[...] + factor * matmul(reads2, stack)
-    mixed[...] = (total + wide_skip(skip, heads, spread) * features[...].astype(F32)).astype(BF16)
-    head_sums(rows, grad * total, spread)
-    high, low = split2(factor * grad)
-    read_acc[...] += matmul_nt(high, stack) + matmul_nt(low, stack)
-
-    @pl.when(step == QUARTERS - 1)
-    def _():
-        read_grad[...] = (read_part[...] + read_acc[:, :state] + read_acc[:, state:]).astype(BF16)
-
-
-def back_finish_kernel(
-    logits, bias, decay, weight_cols, stride_ref, log_ref, spread_ref,
-    features, writes, feature_part, skip_part, row_ref, kept, *refs,
+def quarter_rows(have, step, back):
+    part = have.shape[1] // 2
+    return jnp.concatenate([have[half * QUARTERS + step, back * part : (back + 1) * part] for half in range(HALVES)], axis=0)
+
+
+def finish_kernel(
+    logits, bias, decay, skip, weight_cols, factor_cols, stride_ref, log_ref, spread_ref,
+    features, cotangent, writes, reads, inside, feature_part, skip_part, *refs,
 ):
     haves = refs[:GROUP]
-    step_grad, sums, col_acc, last_acc, skip_acc, have = refs[GROUP:]
+    mixed, feature_grad, step_grad, sums, row_acc, col_acc, last_acc, skip_acc, have = refs[GROUP:]
     heads, length = logits.shape
     state = writes.shape[1]
     width = features.shape[1]
@@ -355,27 +309,34 @@
 
     @pl.when(step == 0)
     def _():
-        for ref in (col_acc, last_acc, skip_acc):
+        for ref in (row_acc, col_acc, last_acc, skip_acc):
             ref[...] = jnp.zeros_like(ref)
         in_order(haves, have)
 
     spread = spread_ref[...]
-    weight = matmul(weight_cols[...], spread)
+    skips = wide_skip(skip, heads, spread)
     feature = features[...].astype(F32)
-    returning = quarter_rows(have)
+    grad = cotangent[...].astype(F32)
+    factor = matmul(factor_cols[...], spread)
+    entering = quarter_rows(have, step, 0)
+    stack = jnp.concatenate(split2(entering), axis=0)
+    total = inside[...] + factor * matmul(jnp.concatenate([reads[...]] * 2, axis=1), stack)
+    mixed[...] = (total + skips * feature).astype(BF16)
+    head_sums(row_acc, grad * total, spread)
+    returning = quarter_rows(have, step, 1)
     stack = jnp.concatenate(split2(returning), axis=0)
-    writes2 = jnp.concatenate([writes[...]] * 2, axis=1)
-    carried = weight * matmul(writes2, stack)
+    carried = matmul(weight_cols[...], spread) * matmul(jnp.concatenate([writes[...]] * 2, axis=1), stack)
     total = feature_part[...] + carried
+    feature_grad[...] = (total + skips * grad).astype(BF16)
     head_sums(col_acc, feature * total, spread)
-    leaving = jnp.sum((returning * kept[...]).reshape(state // 8, 8, width), axis=0)
+    leaving = jnp.sum((returning * entering).reshape(state // 8, 8, width), axis=0) * factor[length - 1 :]
     leaving = leaving + jnp.sum((feature * carried).reshape(length // 8, 8, width), axis=0)
     head_sums(last_acc, leaving, spread)
     head_sums(skip_acc, jnp.broadcast_to(skip_part[...], (8, width)), spread)
 
     @pl.when(step == QUARTERS - 1)
     def _():
-        rows = row_ref[...].T[:heads]
+        rows = row_acc[...].T[:heads]
         cols = col_acc[...].T[:heads]
         last = column(jnp.sum(last_acc[...], axis=0, keepdims=True))[:heads]
         stride = stride_ref[...]
@@ -397,31 +358,25 @@
         sums[...] = jnp.broadcast_to(table[None], sums.shape)
 
 
-def write_kernel(
-    skip, weight_cols, spread_ref, features, cotangent, writes, feature_part, write_part, *refs,
-):
-    feature_grad, write_grad, write_acc, have = refs[GROUP + 1 :]
+def keys_kernel(write_part, read_part, write_high, write_low, read_high, read_low, *refs):
+    write_grad, read_grad, write_acc, read_acc, have = refs[GROUP + 1 :]
     state = write_part.shape[1]
     step = pl.program_id(0)
 
     @pl.when(step == 0)
     def _():
         write_acc[...] = jnp.zeros_like(write_acc)
+        read_acc[...] = jnp.zeros_like(read_acc)
         in_order(refs[:GROUP], have)
 
-    spread = spread_ref[...]
-    weight = matmul(weight_cols[...], spread)
-    stack = jnp.concatenate(split2(quarter_rows(have)), axis=0)
-    writes2 = jnp.concatenate([writes[...]] * 2, axis=1)
-    total = feature_part[...] + weight * matmul(writes2, stack)
-    skips = wide_skip(skip, skip.shape[1], spread) * cotangent[...].astype(F32)
-    feature_grad[...] = (total + skips).astype(BF16)
-    high, low = split2(weight * features[...].astype(F32))
-    write_acc[...] += matmul_nt(high, stack) + matmul_nt(low, stack)
+    for back, high, low, acc in ((0, read_high, read_low, read_acc), (1, write_high, write_low, write_acc)):
+        stack = jnp.concatenate(split2(quarter_rows(have, step, back)), axis=0)
+        acc[...] += matmul_nt(high[...], stack) + matmul_nt(low[...], stack)
 
     @pl.when(step == QUARTERS - 1)
     def _():
         write_grad[...] = (write_part[...] + write_acc[:, :state] + write_acc[:, state:]).astype(BF16)
+        read_grad[...] = (read_part[...] + read_acc[:, :state] + read_acc[:, state:]).astype(BF16)
 
 
 def call(kernel, name, outs, in_specs, work, mib, **more):
@@ -490,16 +445,15 @@
     result = struct((length, wide), BF16)
     tokens_result = struct((length, state), BF16)
     group_sum = struct((part + 8, width))
-    share = struct((part, width))
     tokens = all_of(length, state)
     columns = all_of(length, LANES)
     by_heads = all_of(heads, length)
     row = all_of(1, heads)
-    whole_share = all_of(part, width)
     by_quarter = quarter_of(length)
     spread_quarter = quarter_of(LANES)
     shares = pltpu.VMEM((GROUP, part, width), F32)
     long_shares = pltpu.VMEM((GROUP, part + 8, width), F32)
+    both_shares = pltpu.VMEM((GROUP, 2 * part, width), F32)
 
     both = struct((2 * part + 8, width))
     out = call(
@@ -514,131 +468,71 @@
     came = swap(out[:GROUP])
     weight_cols, factor_cols, cum_cols, cum_rows, stride, log_decay = out[GROUP:]
 
-    half = QUARTERS // 2
-    started = struct((length, wide)), struct((length, wide)), struct((1, wide))
-    square = all_of(length, length)
-    inner_args = (doc_starts, cum_cols, cum_rows, features, cotangent, writes, reads)
-    score_scratch = [pltpu.VMEM((length, length), F32)] * 3
-
-    def inner_specs(offset):
-        mine = quarter_of(length, offset)
-        return [SMEM, columns, by_heads, mine, mine, tokens, tokens], [mine, mine, quarter_of(1, offset)]
-
-    specs, out_specs = inner_specs(0)
-    *begun, score_grad = call(
-        functools.partial(inner_kernel, 0, False),
-        "inner_first",
-        [*started, struct((length, length))],
-        specs + [ANY],
-        1,
-        24,
-        grid=(half,),
-        out_specs=out_specs + [square],
-        scratch_shapes=score_scratch,
-    )(*inner_args, cum_rows)
-    specs, out_specs = inner_specs(half)
-    inside, feature_part, skip_part, write_part, read_part = call(
-        functools.partial(inner_kernel, half, True),
-        "inner_second",
-        [*started, struct((length, state)), struct((length, state))],
-        specs + [square] + [ANY] * 4,
+    wide_part, wide_piece = struct((length, wide)), struct((length, wide), BF16)
+    inside, feature_part, skip_part, write_part, read_part, *pieces = call(
+        inner_kernel,
+        "inner",
+        [wide_part] * 2 + [struct((1, wide))] + [struct((length, state))] * 2 + [wide_piece] * 4,
+        [SMEM, columns, by_heads, by_quarter, by_quarter, tokens, tokens, columns, columns, spread_quarter]
+        + [ANY] * INNER_AFTER,
         10,
         24,
-        grid=(half,),
-        out_specs=out_specs + [tokens, tokens],
-        scratch_shapes=score_scratch,
-        input_output_aliases={8: 0, 9: 1, 10: 2},
-    )(*inner_args, score_grad, *begun, cum_rows)
-    up, keeps = call(
+        grid=(QUARTERS,),
+        out_specs=[by_quarter, by_quarter, quarter_of(1), tokens, tokens] + [by_quarter] * 4,
+        scratch_shapes=[pltpu.VMEM((length, length), F32)] * 3,
+    )(
+        doc_starts, cum_cols, cum_rows, features, cotangent, writes, reads, weight_cols, factor_cols, spread,
+        *[came[d] for d in DISTANCES[:INNER_AFTER]],
+    )
+    up, down, keeps = call(
         functools.partial(group_kernel, part),
         "group",
-        [group_sum, struct((GROUP, width))],
+        [group_sum, group_sum, struct((GROUP, width))],
         [VMEM] * GROUP + [ANY],
         2,
-        8,
-        scratch_shapes=[long_shares],
+        12,
+        scratch_shapes=[long_shares, shares],
     )(*came, write_part)
-    ups = scan(up, 1)
-    (down,) = call(
-        functools.partial(back_group_kernel, part),
-        "back_group",
-        [group_sum],
-        [VMEM] * (GROUP + 2),
-        2,
-        8,
-        scratch_shapes=[shares],
-    )(*came, keeps, up)
-    downs = scan(down, -1)
+    ups, downs = scan(up, 1), scan(down, -1)
     give = call(
         functools.partial(spread_kernel, part, len(ups)),
         "spread",
-        [share] * GROUP,
-        [VMEM] * (GROUP + len(ups)) + [ANY],
+        [struct((2 * part, width))] * GROUP,
+        [VMEM] * (GROUP + 2 * len(ups) + 1),
         2,
-        12,
-        scratch_shapes=[long_shares, shares],
-    )(*came, *ups, down)
+        16,
+        scratch_shapes=[long_shares, shares, both_shares],
+    )(*came, *ups, *downs, keeps)
     have = swap(give)
-    back_give = call(
-        functools.partial(back_spread_kernel, part, len(downs)),
-        "back_spread",
-        [share] * GROUP,
-        [VMEM] * (GROUP + 1 + len(downs)) + [ANY],
-        2,
-        12,
-        scratch_shapes=[shares, shares],
-    )(*came, keeps, *downs, give[0])
-    back_have = swap(back_give)
-
-    mixed, read_grad, rows, kept = call(
+    devices = blocks * members
+    whole_shares = [all_of(2 * part, width)] * GROUP
+    mixed, feature_grad, step_grad, sums = call(
         finish_kernel,
         "finish",
-        [result, tokens_result, struct((length, LANES)), struct((state, wide))],
-        [row, columns, spread_quarter, by_quarter, by_quarter, tokens, by_quarter, tokens]
-        + [whole_share] * GROUP
-        + [ANY],
+        [result, result, small, struct((devices, 1, LANES))],
+        [by_heads, row, row, row, columns, columns, by_heads, by_heads, spread_quarter]
+        + [by_quarter, by_quarter, tokens, tokens, by_quarter, by_quarter, quarter_of(1)]
+        + whole_shares,
         8,
         24,
         grid=(QUARTERS,),
-        out_specs=[by_quarter, tokens, columns, quarter_of(state)],
-        scratch_shapes=[pltpu.VMEM((length, 2 * state), F32), shares],
-    )(skip, factor_cols, spread, features, cotangent, reads, inside, read_part, *have, back_give[0])
-    devices = blocks * members
-    step_grad, sums = call(
-        back_finish_kernel,
-        "back_finish",
-        [small, struct((devices, 1, LANES))],
-        [by_heads, row, row, columns, by_heads, by_heads, spread_quarter]
-        + [by_quarter, tokens, by_quarter]
-        + [quarter_of(1), columns, quarter_of(state)]
-        + [whole_share] * GROUP,
-        8,
-        24,
-        grid=(QUARTERS,),
-        out_specs=[by_heads, all_of(devices, 1, LANES)],
-        scratch_shapes=[
-            pltpu.VMEM((length, LANES), F32),
-            pltpu.VMEM((8, LANES), F32),
-            pltpu.VMEM((8, LANES), F32),
-            shares,
-        ],
+        out_specs=[by_quarter, by_quarter, by_heads, all_of(devices, 1, LANES)],
+        scratch_shapes=[pltpu.VMEM((length, LANES), F32)] * 2 + [pltpu.VMEM((8, LANES), F32)] * 2 + [both_shares],
     )(
-        logits, bias, decay, weight_cols, stride, log_decay, spread, features, writes,
-        feature_part, skip_part, rows, kept, *back_have,
+        logits, bias, decay, skip, weight_cols, factor_cols, stride, log_decay, spread,
+        features, cotangent, writes, reads, inside, feature_part, skip_part, *have,
     )
-    feature_grad, write_grad = call(
-        write_kernel,
-        "write_grad",
-        [result, tokens_result],
-        [row, columns, spread_quarter, by_quarter, by_quarter, tokens, by_quarter, tokens]
-        + [whole_share] * GROUP
-        + [ANY],
+    write_grad, read_grad = call(
+        keys_kernel,
+        "keys",
+        [tokens_result] * 2,
+        [tokens] * 2 + [by_quarter] * 4 + whole_shares + [ANY],
         6,
         60,
         grid=(QUARTERS,),
-        out_specs=[by_quarter, tokens],
-        scratch_shapes=[pltpu.VMEM((length, 2 * state), F32), shares],
-    )(skip, weight_cols, spread, features, cotangent, writes, feature_part, write_part, *back_have, step_grad)
+        out_specs=[tokens] * 2,
+        scratch_shapes=[pltpu.VMEM((length, 2 * state), F32)] * 2 + [both_shares],
+    )(write_part, read_part, *pieces, *have, step_grad)
     sums = jnp.sum(lax.all_to_all(sums, ("dp", "ctx"), 0, 0), axis=(0, 1))
     return (
         mixed[None],

time: 112 us -> 120 us (1.071)
  waiting for transfers between devices: 23.7 us -> 43.1 us
  starting transfers between devices: 44.3 us -> 32.9 us
  local copies, waits for them, and re-layouts: 2.32 us -> 4 us
  Pallas kernels: 39.7 us -> 38.1 us
    ppermute x21 -> x14, waiting for transfers between devices: 21.6 us -> 33.5 us  [exchange(): lax.ppermute(value, 'ctx', [(k, k ^ distance) for k in range(blocks)])]
    ppermute x21 -> x14, starting transfers between devices: 34.3 us -> 24.5 us  [exchange(): lax.ppermute(value, 'ctx', [(k, k ^ distance) for k in range(blocks)])]
    ppermute x2, waiting for transfers between devices: 1.57 us -> 9.01 us  [shift(): return lax.ppermute(value, 'ctx', pairs)]
    all_to_all x1, starting transfers between devices: 4.28 us -> 2.52 us  [local(): sums = jnp.sum(lax.all_to_all(sums, ('dp', 'ctx'), 0, 0), axis=(0, 1))]
    unnamed x58 -> x64, local copies, waits for them, and re-layouts: 1.73 us -> 3.41 us
    pallas_call x9 -> x5, Pallas kernels: 33.4 us -> 31.8 us  [the longest x1 15.9 us: local(): call(inner_kernel, 'inner', [wide_part] * 2 + [struct((1, wide))] + [stru...]
  transfers between devices with their start and end apart: 24 -> 17, of which waited for: 10 -> 10; matrix products, arithmetic and copies ran while one was open for 0% -> 0% of each run, Pallas kernels for 25% -> 19%
where the time goes in v6:
time: 120 us; the launch traced here: 119 us
  waiting for transfers between devices  43.1 us (36%)
  Pallas kernels  38.1 us (32%)
  starting transfers between devices  32.9 us (27%)
  local copies, waits for them, and re-layouts  4 us (3%)
    ppermute x14, waiting for transfers between devices, exchange(): lax.ppermute(value, 'ctx', [(k, k ^ distance) for k in range(blocks)])  33.5 us
    ppermute x14, starting transfers between devices, exchange(): lax.ppermute(value, 'ctx', [(k, k ^ distance) for k in range(blocks)])  24.5 us
    pallas_call x1, Pallas kernels, local(): call(inner_kernel, 'inner', [wide_part] * 2 + [struct((1, wide))] + [stru...  15.9 us
    ppermute x2, waiting for transfers between devices, shift(): return lax.ppermute(value, 'ctx', pairs)  9.01 us
    pallas_call x1, Pallas kernels, local(): call(finish_kernel, 'finish', [result, result, small, struct((devices, 1,...  8.37 us
    pallas_call x1, Pallas kernels, local(): call(keys_kernel, 'keys', [tokens_result] * 2, [tokens] * 2 + [by_quarter...  6.48 us
    pallas_call x1, Pallas kernels, local(): call(states_kernel, 'states', [both] * GROUP + [stack] * 3 + [small] * 3,...  6.37 us
    ppermute x2, starting transfers between devices, shift(): return lax.ppermute(value, 'ctx', pairs)  5.81 us
  transfers between devices with their start and end apart: 17, of which 10 were waited for; matrix products, arithmetic and copies ran while one was open for 0% of the time, Pallas kernels for 19%

profile of v6, /device:TPU:0, one launch (start us, length us, event | category | flops | bytes accessed | tf_op | source)
XLA Modules:
  0.0 119.2 jit_solution(2603781915374384240)
XLA Ops:
  0.7 6.4 %states.1 = (f32[136,640]{1,0:T(8,128)}, f32[136,640]{1,0:T(8,128)}, f32[136,640]{1,0:T(8,128)}, f32[136,640]{1,0:T(8,128)}, f32[136,640]{1,0:T(8,128)}, /*index...) custom-call(s32[1,4]{1,0:T(1,128)} %starts.3, ...), custom_call_target="tpu_custom_call" | custom-call | flops 4000000000 | bytes 1000000 | tf_op jit(solution)/shard_map/states/pallas_call | solution.py:459
  7.1 3.1 %collective-permute-start = (f32[136,640]{1,0:T(8,128)}, f32[136,640]{1,0:T(8,128)S(1)}, u32[]{:S(2)}, u32[]{:S(2)}) collective-permute-start(f32[136,640]{1,0:T(8,128)} %get-tuple-element.54), channel_id=1, source_target_pairs={{0,4},{1,5},{2,6},{3,7},{4,0},{5,1},{6,2},{7,3},{8,12},{9,13},{10,... | collective-permute-start | bytes 1044488 | tf_op jit(solution)/shard_map/ppermute | solution.py:416
  10.2 1.5 %collective-permute-start.1 = (f32[136,640]{1,0:T(8,128)}, f32[136,640]{1,0:T(8,128)S(1)}, u32[]{:S(2)}, u32[]{:S(2)}) collective-permute-start(f32[136,640]{1,0:T(8,128)} %get-tuple-element.55), channel_id=1, source_target_pairs={{0,2},{1,3},{2,0},{3,1},{4,6},{5,7},{6,4},{7,5},{8,10},{9,11},{10,... | collective-permute-start | bytes 1044488 | tf_op jit(solution)/shard_map/ppermute | solution.py:416
  11.7 1.5 %collective-permute-start.2 = (f32[136,640]{1,0:T(8,128)}, f32[136,640]{1,0:T(8,128)S(1)}, u32[]{:S(2)}, u32[]{:S(2)}) collective-permute-start(f32[136,640]{1,0:T(8,128)} %get-tuple-element.60), channel_id=1, source_target_pairs={{0,1},{1,0},{2,3},{3,2},{4,5},{5,4},{6,7},{7,6},{8,9},{9,8},{10,11... | collective-permute-start | bytes 1044488 | tf_op jit(solution)/shard_map/ppermute | solution.py:416
  13.7 1.4 %collective-permute-start.4 = (f32[136,640]{1,0:T(8,128)}, f32[136,640]{1,0:T(8,128)S(1)}, u32[]{:S(2)}, u32[]{:S(2)}) collective-permute-start(f32[136,640]{1,0:T(8,128)} %get-tuple-element.62), channel_id=1, source_target_pairs={{0,5},{1,4},{2,7},{3,6},{4,1},{5,0},{6,3},{7,2},{8,13},{9,12},{10,... | collective-permute-start | bytes 1044488 | tf_op jit(solution)/shard_map/ppermute | solution.py:416
  15.0 4.3 %collective-permute-done.refs_0_.refs_4_ = f32[136,640]{1,0:T(8,128)S(1)} collective-permute-done((f32[136,640]{1,0:T(8,128)}, f32[136,640]{1,0:T(8,128)S(1)}, u32[]{:S(2)}, u32[]{:S(2)}) %collective-permute-start) | collective-permute-done | bytes 348192 | tf_op jit(solution)/shard_map/ppermute | solution.py:416
  19.4 3.0 %collective-permute-start.5 = (f32[136,640]{1,0:T(8,128)}, f32[136,640]{1,0:T(8,128)S(1)}, u32[]{:S(2)}, u32[]{:S(2)}) collective-permute-start(f32[136,640]{1,0:T(8,128)} %get-tuple-element.63), channel_id=1, source_target_pairs={{0,6},{1,7},{2,4},{3,5},{4,2},{5,3},{6,0},{7,1},{8,14},{9,15},{10,... | collective-permute-start | bytes 1044488 | tf_op jit(solution)/shard_map/ppermute | solution.py:416
  22.4 1.3 %collective-permute-start.6 = (f32[136,640]{1,0:T(8,128)}, f32[136,640]{1,0:T(8,128)S(1)}, u32[]{:S(2)}, u32[]{:S(2)}) collective-permute-start(f32[136,640]{1,0:T(8,128)} %get-tuple-element.64), channel_id=1, source_target_pairs={{0,7},{1,6},{2,5},{3,4},{4,3},{5,2},{6,1},{7,0},{8,15},{9,14},{10,... | collective-permute-start | bytes 1044488 | tf_op jit(solution)/shard_map/ppermute | solution.py:416
  27.0 15.9 %inner.1 = (f32[256,2560]{1,0:T(8,128)S(1)}, f32[256,2560]{1,0:T(8,128)S(1)}, f32[1,2560]{1,0:T(1,128)S(1)}, f32[256,128]{1,0:T(8,128)S(1)}, f32[256,128]{1,0:T(...) custom-call(s32[1,4]{1,0:T(1,128)S(1)} %copy-done.12, ...), custom_call_target="tpu_custom_call" | custom-call | flops 10000000000 | bytes 1000000 | tf_op jit(solution)/shard_map/inner/pallas_call | solution.py:472
  43.0 5.6 %collective-permute-done.3.refs_3_ = f32[136,640]{1,0:T(8,128)S(1)} collective-permute-done((f32[136,640]{1,0:T(8,128)}, f32[136,640]{1,0:T(8,128)S(1)}, u32[]{:S(2)}, u32[]{:S(2)}) %collective-permute-start.3) | collective-permute-done | bytes 348192 | tf_op jit(solution)/shard_map/ppermute | solution.py:416
  49.1 4.5 %collective-permute-start.7 = (f32[72,640]{1,0:T(8,128)S(1)}, f32[72,640]{1,0:T(8,128)S(1)}, u32[]{:S(2)}, u32[]{:S(2)}) collective-permute-start(f32[72,640]{1,0:T(8,128)S(1)} %get-tuple-element.66), channel_id=1, source_target_pairs={{0,8},{1,9},{2,10},{3,11},{4,12},{5,13},{6,14},{7,15},{16,24},{17,... | collective-permute-start | bytes 552968 | tf_op jit(solution)/shard_map/ppermute | solution.py:424
  54.9 1.8 %collective-permute-done.7.refs_8_ = f32[72,640]{1,0:T(8,128)S(1)} collective-permute-done((f32[72,640]{1,0:T(8,128)S(1)}, f32[72,640]{1,0:T(8,128)S(1)}, u32[]{:S(2)}, u32[]{:S(2)}) %collective-permute-start.7) | collective-permute-done | bytes 184352 | tf_op jit(solution)/shard_map/ppermute | solution.py:424
  56.7 7.2 %collective-permute-done.8.refs_9_ = f32[72,640]{1,0:T(8,128)S(1)} collective-permute-done((f32[72,640]{1,0:T(8,128)S(1)}, f32[72,640]{1,0:T(8,128)S(1)}, u32[]{:S(2)}, u32[]{:S(2)}) %collective-permute-start.8) | collective-permute-done | bytes 184352 | tf_op jit(solution)/shard_map/ppermute | solution.py:424
  64.6 2.3 %collective-permute-start.9 = (f32[128,640]{1,0:T(8,128)S(1)}, f32[128,640]{1,0:T(8,128)S(1)}, u32[]{:S(2)}, u32[]{:S(2)}) collective-permute-start(f32[128,640]{1,0:T(8,128)S(1)} %get-tuple-element.70), channel_id=1, source_target_pairs={{0,1},{1,0},{2,3},{3,2},{4,5},{5,4},{6,7},{7,6},{8,9},{9,8},{10,11... | collective-permute-start | bytes 983048 | tf_op jit(solution)/shard_map/ppermute | solution.py:416
  66.9 1.5 %collective-permute-start.10 = (f32[128,640]{1,0:T(8,128)S(1)}, f32[128,640]{1,0:T(8,128)S(1)}, u32[]{:S(2)}, u32[]{:S(2)}) collective-permute-start(f32[128,640]{1,0:T(8,128)S(1)} %get-tuple-element.71), channel_id=1, source_target_pairs={{0,2},{1,3},{2,0},{3,1},{4,6},{5,7},{6,4},{7,5},{8,10},{9,11},{10,... | collective-permute-start | bytes 983048 | tf_op jit(solution)/shard_map/ppermute | solution.py:416
  68.4 3.4 %collective-permute-start.13 = (f32[128,640]{1,0:T(8,128)S(1)}, f32[128,640]{1,0:T(8,128)S(1)}, u32[]{:S(2)}, u32[]{:S(2)}) collective-permute-start(f32[128,640]{1,0:T(8,128)S(1)} %get-tuple-element.74), channel_id=1, source_target_pairs={{0,5},{1,4},{2,7},{3,6},{4,1},{5,0},{6,3},{7,2},{8,13},{9,12},{10,... | collective-permute-start | bytes 983048 | tf_op jit(solution)/shard_map/ppermute | solution.py:416
  71.8 4.9 %collective-permute-done.9.refs_1_ = f32[128,640]{1,0:T(8,128)S(1)} collective-permute-done((f32[128,640]{1,0:T(8,128)S(1)}, f32[128,640]{1,0:T(8,128)S(1)}, u32[]{:S(2)}, u32[]{:S(2)}) %collective-permute-start.9) | collective-permute-done | bytes 327712 | tf_op jit(solution)/shard_map/ppermute | solution.py:416
  77.1 5.0 %collective-permute-start.15 = (f32[128,640]{1,0:T(8,128)S(1)}, f32[128,640]{1,0:T(8,128)S(1)}, u32[]{:S(2)}, u32[]{:S(2)}) collective-permute-start(f32[128,640]{1,0:T(8,128)S(1)} %get-tuple-element.76), channel_id=1, source_target_pairs={{0,7},{1,6},{2,5},{3,4},{4,3},{5,2},{6,1},{7,0},{8,15},{9,14},{10,... | collective-permute-start | bytes 983048 | tf_op jit(solution)/shard_map/ppermute | solution.py:416
  82.1 7.6 %collective-permute-done.11.refs_3_ = f32[128,640]{1,0:T(8,128)S(1)} collective-permute-done((f32[128,640]{1,0:T(8,128)S(1)}, f32[128,640]{1,0:T(8,128)S(1)}, u32[]{:S(2)}, u32[]{:S(2)}) %collective-permute-start.11) | collective-permute-done | bytes 327712 | tf_op jit(solution)/shard_map/ppermute | solution.py:416
  89.6 5.0 %collective-permute-done.14.refs_6_ = f32[128,640]{1,0:T(8,128)S(1)} collective-permute-done((f32[128,640]{1,0:T(8,128)S(1)}, f32[128,640]{1,0:T(8,128)S(1)}, u32[]{:S(2)}, u32[]{:S(2)}) %collective-permute-start.14) | collective-permute-done | bytes 327712 | tf_op jit(solution)/shard_map/ppermute | solution.py:416
  94.6 5.8 %collective-permute-done.15.refs_7_ = f32[128,640]{1,0:T(8,128)S(1)} collective-permute-done((f32[128,640]{1,0:T(8,128)S(1)}, f32[128,640]{1,0:T(8,128)S(1)}, u32[]{:S(2)}, u32[]{:S(2)}) %collective-permute-start.15) | collective-permute-done | bytes 327712 | tf_op jit(solution)/shard_map/ppermute | solution.py:416
  100.5 8.4 %finish.1 = (bf16[256,2560]{1,0:T(8,128)(2,1)}, bf16[256,2560]{1,0:T(8,128)(2,1)}, f32[40,256]{1,0:T(8,128)}, f32[32,1,128]{2,1,0:T(1,128)}) custom-call(f32[40,256]{1,0:T(8,128)S(1)} %bitcast.26, f32[1,40]{1,0:T(1,128)S(1)} %bitcast.28, f32[1,40]{1,0:T(1,128)S(1)} %bitcast.30, f32[1,40]{1,0:T(1,128)S(1)} %bitcast.31, bf16[256,128]{1,0:T(8,128)(2,1)S(1)} %copy-done.26, ...), custom_call_target="tpu_custom_call" | custom-call | flops 8000000000 | bytes 1000000 | tf_op jit(solution)/shard_map/finish/pallas_call | solution.py:509
  108.9 2.5 %all-to-all-start = ((f32[32,1,128]{2,1,0:T(1,128)}), f32[32,1,128]{2,1,0:T(1,128)S(1)}, u32[]{:S(2)}, u32[]{:S(2)}) async-start(f32[32,1,128]{2,1,0:T(1,128)} %get-tuple-element.87), calls=%async_computation | async-start | bytes 32768 | tf_op jit(solution)/shard_map/all_to_all | solution.py:536
  111.4 6.5 %keys.1 = (bf16[256,128]{1,0:T(8,128)(2,1)}, bf16[256,128]{1,0:T(8,128)(2,1)}) custom-call(f32[256,128]{1,0:T(8,128)} %copy-done.24, f32[256,128]{1,0:T(8,128)} %copy-done.25, bf16[256,2560]{1,0:T(8,128)(2,1)} %copy-done.20, bf16[256,2560]{1,0:T(8,128)(2,1)} %copy-done.21, bf16[256,2560]{1,0:T(8,128)(2,1)} %copy-done.22, bf16[256,2560]{1,0:T(8,128)(2,1)} %copy-done.23, ...), custom_call_target="tpu_custom_call" | custom-call | flops 6000000000 | bytes 1000000 | tf_op jit(solution)/shard_map/keys/pallas_call | solution.py:525
  (82 shorter events, 7.9 us)
Async XLA Ops:
  7.1 12.3 %collective-permute-start = (f32[136,640]{1,0:T(8,128)}, f32[136,640]{1,0:T(8,128)S(1)}, u32[]{:S(2)}, u32[]{:S(2)}) collective-permute-start(f32[136,640]{1,0:T(8,128)} %get-tuple-element.54), channel_id=1, source_target_pairs={{0,4},{1,5},{2,6},{3,7},{4,0},{5,1},{6,2},{7,3},{8,12},{9,13},{10,... | collective-permute-start | bytes 1044488 | tf_op jit(solution)/shard_map/ppermute | solution.py:416
  10.2 12.2 %collective-permute-start.1 = (f32[136,640]{1,0:T(8,128)}, f32[136,640]{1,0:T(8,128)S(1)}, u32[]{:S(2)}, u32[]{:S(2)}) collective-permute-start(f32[136,640]{1,0:T(8,128)} %get-tuple-element.55), channel_id=1, source_target_pairs={{0,2},{1,3},{2,0},{3,1},{4,6},{5,7},{6,4},{7,5},{8,10},{9,11},{10,... | collective-permute-start | bytes 1044488 | tf_op jit(solution)/shard_map/ppermute | solution.py:416
  11.7 31.3 %collective-permute-start.2 = (f32[136,640]{1,0:T(8,128)}, f32[136,640]{1,0:T(8,128)S(1)}, u32[]{:S(2)}, u32[]{:S(2)}) collective-permute-start(f32[136,640]{1,0:T(8,128)} %get-tuple-element.60), channel_id=1, source_target_pairs={{0,1},{1,0},{2,3},{3,2},{4,5},{5,4},{6,7},{7,6},{8,9},{9,8},{10,11... | collective-permute-start | bytes 1044488 | tf_op jit(solution)/shard_map/ppermute | solution.py:416
  13.2 35.4 %collective-permute-start.3 = (f32[136,640]{1,0:T(8,128)}, f32[136,640]{1,0:T(8,128)S(1)}, u32[]{:S(2)}, u32[]{:S(2)}) collective-permute-start(f32[136,640]{1,0:T(8,128)} %get-tuple-element.61), channel_id=1, source_target_pairs={{0,3},{1,2},{2,1},{3,0},{4,7},{5,6},{6,5},{7,4},{8,11},{9,10},{10,... | collective-permute-start | bytes 1044488 | tf_op jit(solution)/shard_map/ppermute | solution.py:416
  13.7 34.9 %collective-permute-start.4 = (f32[136,640]{1,0:T(8,128)}, f32[136,640]{1,0:T(8,128)S(1)}, u32[]{:S(2)}, u32[]{:S(2)}) collective-permute-start(f32[136,640]{1,0:T(8,128)} %get-tuple-element.62), channel_id=1, source_target_pairs={{0,5},{1,4},{2,7},{3,6},{4,1},{5,0},{6,3},{7,2},{8,13},{9,12},{10,... | collective-permute-start | bytes 1044488 | tf_op jit(solution)/shard_map/ppermute | solution.py:416
  19.4 29.2 %collective-permute-start.5 = (f32[136,640]{1,0:T(8,128)}, f32[136,640]{1,0:T(8,128)S(1)}, u32[]{:S(2)}, u32[]{:S(2)}) collective-permute-start(f32[136,640]{1,0:T(8,128)} %get-tuple-element.63), channel_id=1, source_target_pairs={{0,6},{1,7},{2,4},{3,5},{4,2},{5,3},{6,0},{7,1},{8,14},{9,15},{10,... | collective-permute-start | bytes 1044488 | tf_op jit(solution)/shard_map/ppermute | solution.py:416
  22.4 26.2 %collective-permute-start.6 = (f32[136,640]{1,0:T(8,128)}, f32[136,640]{1,0:T(8,128)S(1)}, u32[]{:S(2)}, u32[]{:S(2)}) collective-permute-start(f32[136,640]{1,0:T(8,128)} %get-tuple-element.64), channel_id=1, source_target_pairs={{0,7},{1,6},{2,5},{3,4},{4,3},{5,2},{6,1},{7,0},{8,15},{9,14},{10,... | collective-permute-start | bytes 1044488 | tf_op jit(solution)/shard_map/ppermute | solution.py:416
  49.1 7.6 %collective-permute-start.7 = (f32[72,640]{1,0:T(8,128)S(1)}, f32[72,640]{1,0:T(8,128)S(1)}, u32[]{:S(2)}, u32[]{:S(2)}) collective-permute-start(f32[72,640]{1,0:T(8,128)S(1)} %get-tuple-element.66), channel_id=1, source_target_pairs={{0,8},{1,9},{2,10},{3,11},{4,12},{5,13},{6,14},{7,15},{16,24},{17,... | collective-permute-start | bytes 552968 | tf_op jit(solution)/shard_map/ppermute | solution.py:424
  53.6 10.3 %collective-permute-start.8 = (f32[72,640]{1,0:T(8,128)S(1)}, f32[72,640]{1,0:T(8,128)S(1)}, u32[]{:S(2)}, u32[]{:S(2)}) collective-permute-start(f32[72,640]{1,0:T(8,128)S(1)} %get-tuple-element.67), channel_id=1, source_target_pairs={{8,0},{9,1},{10,2},{11,3},{12,4},{13,5},{14,6},{15,7},{24,16},{25,... | collective-permute-start | bytes 552968 | tf_op jit(solution)/shard_map/ppermute | solution.py:424
  63.9 36.5 %copy-start.13 = (f32[40]{0:T(128)S(1)}, f32[40]{0:T(128)}, u32[]{:S(2)}) copy-start(f32[40]{0:T(128)} %param.14) | copy-start | bytes 484
  63.9 36.5 %copy-start.14 = (f32[40]{0:T(128)S(1)}, f32[40]{0:T(128)}, u32[]{:S(2)}) copy-start(f32[40]{0:T(128)} %param.15) | copy-start | bytes 484
  63.9 36.5 %copy-start.15 = (f32[40]{0:T(128)S(1)}, f32[40]{0:T(128)}, u32[]{:S(2)}) copy-start(f32[40]{0:T(128)} %param.16) | copy-start | bytes 484
  63.9 36.5 %copy-start.17 = (bf16[128,2560]{1,0:T(8,128)(2,1)S(1)}, bf16[128,2560]{1,0:T(8,128)(2,1)}, u32[]{:S(2)}) copy-start(bf16[128,2560]{1,0:T(8,128)(2,1)} %constant.4.clone.spread_ref) | copy-start | bytes 1966084
  63.9 36.5 %copy-start.29 = (f32[40,256]{1,0:T(8,128)S(1)}, f32[40,256]{1,0:T(8,128)}, u32[]{:S(2)}) copy-start(f32[40,256]{1,0:T(8,128)} %get-tuple-element.50.stride_ref) | copy-start | bytes 122884
  64.0 36.5 %copy-start.30 = (f32[40,256]{1,0:T(8,128)S(1)}, f32[40,256]{1,0:T(8,128)}, u32[]{:S(2)}) copy-start(f32[40,256]{1,0:T(8,128)} %get-tuple-element.51.log_ref) | copy-start | bytes 122884
  64.6 44.3 %copy-start.19 = (f32[128,640]{1,0:T(8,128)}, f32[128,640]{1,0:T(8,128)S(1)}, u32[]{:S(2)}) copy-start(f32[128,640]{1,0:T(8,128)S(1)} %get-tuple-element.69.refs_0_) | copy-start | bytes 983044
  64.6 12.1 %collective-permute-start.9 = (f32[128,640]{1,0:T(8,128)S(1)}, f32[128,640]{1,0:T(8,128)S(1)}, u32[]{:S(2)}, u32[]{:S(2)}) collective-permute-start(f32[128,640]{1,0:T(8,128)S(1)} %get-tuple-element.70), channel_id=1, source_target_pairs={{0,1},{1,0},{2,3},{3,2},{4,5},{5,4},{6,7},{7,6},{8,9},{9,8},{10,11... | collective-permute-start | bytes 983048 | tf_op jit(solution)/shard_map/ppermute | solution.py:416
  66.9 10.2 %collective-permute-start.10 = (f32[128,640]{1,0:T(8,128)S(1)}, f32[128,640]{1,0:T(8,128)S(1)}, u32[]{:S(2)}, u32[]{:S(2)}) collective-permute-start(f32[128,640]{1,0:T(8,128)S(1)} %get-tuple-element.71), channel_id=1, source_target_pairs={{0,2},{1,3},{2,0},{3,1},{4,6},{5,7},{6,4},{7,5},{8,10},{9,11},{10,... | collective-permute-start | bytes 983048 | tf_op jit(solution)/shard_map/ppermute | solution.py:416
  68.4 21.2 %collective-permute-start.11 = (f32[128,640]{1,0:T(8,128)S(1)}, f32[128,640]{1,0:T(8,128)S(1)}, u32[]{:S(2)}, u32[]{:S(2)}) collective-permute-start(f32[128,640]{1,0:T(8,128)S(1)} %get-tuple-element.72), channel_id=1, source_target_pairs={{0,3},{1,2},{2,1},{3,0},{4,7},{5,6},{6,5},{7,4},{8,11},{9,10},{10,... | collective-permute-start | bytes 983048 | tf_op jit(solution)/shard_map/ppermute | solution.py:416
  68.4 21.2 %collective-permute-start.12 = (f32[128,640]{1,0:T(8,128)S(1)}, f32[128,640]{1,0:T(8,128)S(1)}, u32[]{:S(2)}, u32[]{:S(2)}) collective-permute-start(f32[128,640]{1,0:T(8,128)S(1)} %get-tuple-element.73), channel_id=1, source_target_pairs={{0,4},{1,5},{2,6},{3,7},{4,0},{5,1},{6,2},{7,3},{8,12},{9,13},{10,... | collective-permute-start | bytes 983048 | tf_op jit(solution)/shard_map/ppermute | solution.py:416
  68.4 21.2 %collective-permute-start.13 = (f32[128,640]{1,0:T(8,128)S(1)}, f32[128,640]{1,0:T(8,128)S(1)}, u32[]{:S(2)}, u32[]{:S(2)}) collective-permute-start(f32[128,640]{1,0:T(8,128)S(1)} %get-tuple-element.74), channel_id=1, source_target_pairs={{0,5},{1,4},{2,7},{3,6},{4,1},{5,0},{6,3},{7,2},{8,13},{9,12},{10,... | collective-permute-start | bytes 983048 | tf_op jit(solution)/shard_map/ppermute | solution.py:416
  76.7 17.9 %collective-permute-start.14 = (f32[128,640]{1,0:T(8,128)S(1)}, f32[128,640]{1,0:T(8,128)S(1)}, u32[]{:S(2)}, u32[]{:S(2)}) collective-permute-start(f32[128,640]{1,0:T(8,128)S(1)} %get-tuple-element.75), channel_id=1, source_target_pairs={{0,6},{1,7},{2,4},{3,5},{4,2},{5,3},{6,0},{7,1},{8,14},{9,15},{10,... | collective-permute-start | bytes 983048 | tf_op jit(solution)/shard_map/ppermute | solution.py:416
  77.1 23.3 %collective-permute-start.15 = (f32[128,640]{1,0:T(8,128)S(1)}, f32[128,640]{1,0:T(8,128)S(1)}, u32[]{:S(2)}, u32[]{:S(2)}) collective-permute-start(f32[128,640]{1,0:T(8,128)S(1)} %get-tuple-element.76), channel_id=1, source_target_pairs={{0,7},{1,6},{2,5},{3,4},{4,3},{5,2},{6,1},{7,0},{8,15},{9,14},{10,... | collective-permute-start | bytes 983048 | tf_op jit(solution)/shard_map/ppermute | solution.py:416
  108.9 9.6 %all-to-all-start = ((f32[32,1,128]{2,1,0:T(1,128)}), f32[32,1,128]{2,1,0:T(1,128)S(1)}, u32[]{:S(2)}, u32[]{:S(2)}) async-start(f32[32,1,128]{2,1,0:T(1,128)} %get-tuple-element.87), calls=%async_computation | async-start | bytes 32768 | tf_op jit(solution)/shard_map/all_to_all | solution.py:536
  (25 other events, 380.8 us)

commit v7 on v6

--- a/solution.py
+++ b/solution.py
@@ -13,7 +13,7 @@
 QUARTERS = 4
 HALVES = 2
 GROUP = QUARTERS * HALVES
-DISTANCES = (4, 2, 1, 7, 3, 5, 6)
+DISTANCES = (1, 2, 3, 4, 5, 6, 7)
 LANES = 128
 LOG2E = 1.4426950408889634
 FAR = -1e30
@@ -226,7 +226,9 @@
 
 
 def group_kernel(part, *refs):
-    up, down, keeps, came, back_came = refs[-5:]
+    keeps, came, back_came = refs[-3:]
+    sums = refs[GROUP + 1 : -3]
+    up, down = sums[0], sums[-1]
     in_order(refs[:GROUP], came)
     total = came[0, 0:part]
     keep = came[0, part:]
@@ -238,11 +240,18 @@
     for j in range(GROUP):
         keeps[j : j + 1] = came[j, part : part + 1]
     in_order(refs[:GROUP], back_came, back=True)
-    total = back_came[GROUP - 1]
-    for j in reversed(range(GROUP - 1)):
-        total = total * keeps[j : j + 1] + back_came[j]
-    down[0:part] = total
-    down[part:] = keep
+
+    def downward():
+        total = back_came[GROUP - 1]
+        for j in reversed(range(GROUP - 1)):
+            total = total * keeps[j : j + 1] + back_came[j]
+        down[0:part] = total
+        down[part:] = keep
+
+    if len(sums) == 1:
+        pl.when(lax.axis_index("ctx") >= GROUP)(downward)
+    else:
+        downward()
 
 
 def arrived(part, came):
@@ -259,19 +268,25 @@
     refs[-1][part:] = own[part:] * keep
 
 
-def spread_kernel(part, count, *refs):
-    ups, downs = refs[GROUP : GROUP + count], refs[GROUP + count : GROUP + 2 * count]
-    keeps = refs[GROUP + 2 * count]
-    outs = refs[GROUP + 2 * count + 1 : -3]
+def spread_kernel(part, count, back_count, *refs):
+    ups, downs = refs[GROUP : GROUP + count], refs[GROUP + count : GROUP + count + back_count]
+    keeps = refs[GROUP + count + back_count]
+    outs = refs[GROUP + count + back_count + 1 : -3]
     came, back_came, give = refs[-3:]
     in_order(refs[:GROUP], came)
-    total = arrived(part, ups)[0]
+    if downs:
+        entering, returning = arrived(part, ups)[0], arrived(part, downs)[0]
+    else:
+        upper = jnp.full((1, 1), lax.axis_index("ctx")) >= GROUP
+        entering = jnp.where(upper, ups[0][0:part], 0.0)
+        returning = jnp.where(upper, 0.0, ups[0][0:part])
+    total = entering
     for j in range(GROUP):
         give[j, 0:part] = total
         if j < GROUP - 1:
             total = total * keeps[j : j + 1] + came[j, 0:part]
     in_order(refs[:GROUP], back_came, back=True)
-    total = arrived(part, downs)[0]
+    total = returning
     for j in reversed(range(GROUP)):
         give[j, part:] = total
         if j > 0:
@@ -484,21 +499,25 @@
         doc_starts, cum_cols, cum_rows, features, cotangent, writes, reads, weight_cols, factor_cols, spread,
         *[came[d] for d in DISTANCES[:INNER_AFTER]],
     )
-    up, down, keeps = call(
+    two = blocks == 2 * GROUP
+    *sums, keeps = call(
         functools.partial(group_kernel, part),
         "group",
-        [group_sum, group_sum, struct((GROUP, width))],
+        [group_sum] * (1 if two else 2) + [struct((GROUP, width))],
         [VMEM] * GROUP + [ANY],
         2,
         12,
         scratch_shapes=[long_shares, shares],
     )(*came, write_part)
-    ups, downs = scan(up, 1), scan(down, -1)
+    if two:
+        ups, downs = [exchange(sums[0], GROUP)], []
+    else:
+        ups, downs = scan(sums[0], 1), scan(sums[1], -1)
     give = call(
-        functools.partial(spread_kernel, part, len(ups)),
+        functools.partial(spread_kernel, part, len(ups), len(downs)),
         "spread",
         [struct((2 * part, width))] * GROUP,
-        [VMEM] * (GROUP + 2 * len(ups) + 1),
+        [VMEM] * (GROUP + len(ups) + len(downs) + 1),
         2,
         16,
         scratch_shapes=[long_shares, shares, both_shares],

time: 120 us -> 114 us (0.950)
  starting transfers between devices: 32.9 us -> 28.6 us
  waiting for transfers between devices: 43.1 us -> 41.9 us
    ppermute x2 -> x0, waiting for transfers between devices: 9.01 us -> none  [shift(): return lax.ppermute(value, 'ctx', pairs)]
    ppermute x14 -> x15, waiting for transfers between devices: 33.5 us -> 41.3 us  [exchange(): lax.ppermute(value, 'ctx', [(k, k ^ distance) for k in range(blocks)])]
    ppermute x2 -> x0, starting transfers between devices: 5.81 us -> none  [shift(): return lax.ppermute(value, 'ctx', pairs)]
    all_to_all x1, starting transfers between devices: 2.52 us -> 4.55 us  [local(): sums = jnp.sum(lax.all_to_all(sums, ('dp', 'ctx'), 0, 0), axis=(0, 1))]
    ppermute x14 -> x15, starting transfers between devices: 24.5 us -> 24.1 us  [exchange(): lax.ppermute(value, 'ctx', [(k, k ^ distance) for k in range(blocks)])]
  transfers between devices with their start and end apart: 17 -> 16, of which waited for: 10 -> 8; matrix products, arithmetic and copies ran while one was open for 0% -> 0% of each run, Pallas kernels for 19% -> 20%
where the time goes in v7:
time: 114 us
  waiting for transfers between devices  41.9 us (37%)
  Pallas kernels  38.1 us (33%)
  starting transfers between devices  28.6 us (25%)
  local copies, waits for them, and re-layouts  4 us (4%)
    ppermute x15, waiting for transfers between devices, exchange(): lax.ppermute(value, 'ctx', [(k, k ^ distance) for k in range(blocks)])  41.3 us
    ppermute x15, starting transfers between devices, exchange(): lax.ppermute(value, 'ctx', [(k, k ^ distance) for k in range(blocks)])  24.1 us
    pallas_call x1, Pallas kernels, local(): call(inner_kernel, 'inner', [wide_part] * 2 + [struct((1, wide))] + [stru...  15.9 us
    pallas_call x1, Pallas kernels, local(): call(finish_kernel, 'finish', [result, result, small, struct((devices, 1,...  8.37 us
    pallas_call x1, Pallas kernels, local(): call(keys_kernel, 'keys', [tokens_result] * 2, [tokens] * 2 + [by_quarter...  6.48 us
    pallas_call x1, Pallas kernels, local(): call(states_kernel, 'states', [both] * GROUP + [stack] * 3 + [small] * 3,...  6.37 us
    all_to_all x1, starting transfers between devices, local(): sums = jnp.sum(lax.all_to_all(sums, ('dp', 'ctx'), 0, 0), axis=(0, 1))  4.55 us
    unnamed x64, local copies, waits for them, and re-layouts  3.41 us
  transfers between devices with their start and end apart: 16, of which 8 were waited for; matrix products, arithmetic and copies ran while one was open for 0% of the time, Pallas kernels for 20%

profile of v7, /device:TPU:0, one launch (start us, length us, event | category | flops | bytes accessed | tf_op | source)
XLA Modules:
  0.0 113.7 jit_solution(15145856840537490836)
XLA Ops:
  0.7 6.4 %states.1 = (f32[136,640]{1,0:T(8,128)}, f32[136,640]{1,0:T(8,128)}, f32[136,640]{1,0:T(8,128)}, f32[136,640]{1,0:T(8,128)}, f32[136,640]{1,0:T(8,128)}, /*index...) custom-call(s32[1,4]{1,0:T(1,128)} %starts.3, ...), custom_call_target="tpu_custom_call" | custom-call | flops 4000000000 | bytes 1000000 | tf_op jit(solution)/shard_map/states/pallas_call | solution.py:474
  7.1 3.0 %collective-permute-start = (f32[136,640]{1,0:T(8,128)}, f32[136,640]{1,0:T(8,128)S(1)}, u32[]{:S(2)}, u32[]{:S(2)}) collective-permute-start(f32[136,640]{1,0:T(8,128)} %get-tuple-element.53), channel_id=1, source_target_pairs={{0,1},{1,0},{2,3},{3,2},{4,5},{5,4},{6,7},{7,6},{8,9},{9,8},{10,11... | collective-permute-start | bytes 1044488 | tf_op jit(solution)/shard_map/ppermute | solution.py:431
  10.1 1.5 %collective-permute-start.1 = (f32[136,640]{1,0:T(8,128)}, f32[136,640]{1,0:T(8,128)S(1)}, u32[]{:S(2)}, u32[]{:S(2)}) collective-permute-start(f32[136,640]{1,0:T(8,128)} %get-tuple-element.54), channel_id=1, source_target_pairs={{0,2},{1,3},{2,0},{3,1},{4,6},{5,7},{6,4},{7,5},{8,10},{9,11},{10,... | collective-permute-start | bytes 1044488 | tf_op jit(solution)/shard_map/ppermute | solution.py:431
  11.6 2.0 %collective-permute-start.3 = (f32[136,640]{1,0:T(8,128)}, f32[136,640]{1,0:T(8,128)S(1)}, u32[]{:S(2)}, u32[]{:S(2)}) collective-permute-start(f32[136,640]{1,0:T(8,128)} %get-tuple-element.60), channel_id=1, source_target_pairs={{0,4},{1,5},{2,6},{3,7},{4,0},{5,1},{6,2},{7,3},{8,12},{9,13},{10,... | collective-permute-start | bytes 1044488 | tf_op jit(solution)/shard_map/ppermute | solution.py:431
  13.7 1.4 %collective-permute-start.4 = (f32[136,640]{1,0:T(8,128)}, f32[136,640]{1,0:T(8,128)S(1)}, u32[]{:S(2)}, u32[]{:S(2)}) collective-permute-start(f32[136,640]{1,0:T(8,128)} %get-tuple-element.61), channel_id=1, source_target_pairs={{0,5},{1,4},{2,7},{3,6},{4,1},{5,0},{6,3},{7,2},{8,13},{9,12},{10,... | collective-permute-start | bytes 1044488 | tf_op jit(solution)/shard_map/ppermute | solution.py:431
  15.0 4.2 %collective-permute-done.refs_0_.refs_1_ = f32[136,640]{1,0:T(8,128)S(1)} collective-permute-done((f32[136,640]{1,0:T(8,128)}, f32[136,640]{1,0:T(8,128)S(1)}, u32[]{:S(2)}, u32[]{:S(2)}) %collective-permute-start) | collective-permute-done | bytes 348192 | tf_op jit(solution)/shard_map/ppermute | solution.py:431
  19.3 3.1 %collective-permute-start.5 = (f32[136,640]{1,0:T(8,128)}, f32[136,640]{1,0:T(8,128)S(1)}, u32[]{:S(2)}, u32[]{:S(2)}) collective-permute-start(f32[136,640]{1,0:T(8,128)} %get-tuple-element.62), channel_id=1, source_target_pairs={{0,6},{1,7},{2,4},{3,5},{4,2},{5,3},{6,0},{7,1},{8,14},{9,15},{10,... | collective-permute-start | bytes 1044488 | tf_op jit(solution)/shard_map/ppermute | solution.py:431
  22.4 1.8 %collective-permute-start.6 = (f32[136,640]{1,0:T(8,128)}, f32[136,640]{1,0:T(8,128)S(1)}, u32[]{:S(2)}, u32[]{:S(2)}) collective-permute-start(f32[136,640]{1,0:T(8,128)} %get-tuple-element.63), channel_id=1, source_target_pairs={{0,7},{1,6},{2,5},{3,4},{4,3},{5,2},{6,1},{7,0},{8,15},{9,14},{10,... | collective-permute-start | bytes 1044488 | tf_op jit(solution)/shard_map/ppermute | solution.py:431
  27.5 15.9 %inner.1 = (f32[256,2560]{1,0:T(8,128)S(1)}, f32[256,2560]{1,0:T(8,128)S(1)}, f32[1,2560]{1,0:T(1,128)S(1)}, f32[256,128]{1,0:T(8,128)S(1)}, f32[256,128]{1,0:T(...) custom-call(s32[1,4]{1,0:T(1,128)S(1)} %copy-done.12, ...), custom_call_target="tpu_custom_call" | custom-call | flops 10000000000 | bytes 1000000 | tf_op jit(solution)/shard_map/inner/pallas_call | solution.py:487
  43.5 4.6 %collective-permute-done.6.refs_7_ = f32[136,640]{1,0:T(8,128)S(1)} collective-permute-done((f32[136,640]{1,0:T(8,128)}, f32[136,640]{1,0:T(8,128)S(1)}, u32[]{:S(2)}, u32[]{:S(2)}) %collective-permute-start.6) | collective-permute-done | bytes 348192 | tf_op jit(solution)/shard_map/ppermute | solution.py:431
  48.5 2.7 %collective-permute-start.7 = (f32[72,640]{1,0:T(8,128)S(1)}, f32[72,640]{1,0:T(8,128)S(1)}, u32[]{:S(2)}, u32[]{:S(2)}) collective-permute-start(f32[72,640]{1,0:T(8,128)S(1)} %get-tuple-element.65), channel_id=1, source_target_pairs={{0,8},{1,9},{2,10},{3,11},{4,12},{5,13},{6,14},{7,15},{8,0},{9,1},... | collective-permute-start | bytes 552968 | tf_op jit(solution)/shard_map/ppermute | solution.py:431
  51.2 6.8 %collective-permute-done.7.refs_8_ = f32[72,640]{1,0:T(8,128)S(1)} collective-permute-done((f32[72,640]{1,0:T(8,128)S(1)}, f32[72,640]{1,0:T(8,128)S(1)}, u32[]{:S(2)}, u32[]{:S(2)}) %collective-permute-start.7) | collective-permute-done | bytes 184352 | tf_op jit(solution)/shard_map/ppermute | solution.py:431
  58.7 0.9 collective-permute-start.8
  59.5 1.0 collective-permute-start.9
  60.5 1.7 %collective-permute-start.10 = (f32[128,640]{1,0:T(8,128)S(1)}, f32[128,640]{1,0:T(8,128)S(1)}, u32[]{:S(2)}, u32[]{:S(2)}) collective-permute-start(f32[128,640]{1,0:T(8,128)S(1)} %get-tuple-element.70), channel_id=1, source_target_pairs={{0,3},{1,2},{2,1},{3,0},{4,7},{5,6},{6,5},{7,4},{8,11},{9,10},{10,... | collective-permute-start | bytes 983048 | tf_op jit(solution)/shard_map/ppermute | solution.py:431
  62.9 1.6 %collective-permute-start.12 = (f32[128,640]{1,0:T(8,128)S(1)}, f32[128,640]{1,0:T(8,128)S(1)}, u32[]{:S(2)}, u32[]{:S(2)}) collective-permute-start(f32[128,640]{1,0:T(8,128)S(1)} %get-tuple-element.72), channel_id=1, source_target_pairs={{0,5},{1,4},{2,7},{3,6},{4,1},{5,0},{6,3},{7,2},{8,13},{9,12},{10,... | collective-permute-start | bytes 983048 | tf_op jit(solution)/shard_map/ppermute | solution.py:431
  64.5 7.0 %collective-permute-done.8.refs_1_ = f32[128,640]{1,0:T(8,128)S(1)} collective-permute-done((f32[128,640]{1,0:T(8,128)S(1)}, f32[128,640]{1,0:T(8,128)S(1)}, u32[]{:S(2)}, u32[]{:S(2)}) %collective-permute-start.8) | collective-permute-done | bytes 327712 | tf_op jit(solution)/shard_map/ppermute | solution.py:431
  71.5 2.7 %collective-permute-start.14 = (f32[128,640]{1,0:T(8,128)S(1)}, f32[128,640]{1,0:T(8,128)S(1)}, u32[]{:S(2)}, u32[]{:S(2)}) collective-permute-start(f32[128,640]{1,0:T(8,128)S(1)} %get-tuple-element.74), channel_id=1, source_target_pairs={{0,7},{1,6},{2,5},{3,4},{4,3},{5,2},{6,1},{7,0},{8,15},{9,14},{10,... | collective-permute-start | bytes 983048 | tf_op jit(solution)/shard_map/ppermute | solution.py:431
  74.3 8.5 %collective-permute-done.10.refs_3_ = f32[128,640]{1,0:T(8,128)S(1)} collective-permute-done((f32[128,640]{1,0:T(8,128)S(1)}, f32[128,640]{1,0:T(8,128)S(1)}, u32[]{:S(2)}, u32[]{:S(2)}) %collective-permute-start.10) | collective-permute-done | bytes 327712 | tf_op jit(solution)/shard_map/ppermute | solution.py:431
  82.8 4.7 %collective-permute-done.13.refs_6_ = f32[128,640]{1,0:T(8,128)S(1)} collective-permute-done((f32[128,640]{1,0:T(8,128)S(1)}, f32[128,640]{1,0:T(8,128)S(1)}, u32[]{:S(2)}, u32[]{:S(2)}) %collective-permute-start.13) | collective-permute-done | bytes 327712 | tf_op jit(solution)/shard_map/ppermute | solution.py:431
  87.5 5.3 %collective-permute-done.14.refs_7_ = f32[128,640]{1,0:T(8,128)S(1)} collective-permute-done((f32[128,640]{1,0:T(8,128)S(1)}, f32[128,640]{1,0:T(8,128)S(1)}, u32[]{:S(2)}, u32[]{:S(2)}) %collective-permute-start.14) | collective-permute-done | bytes 327712 | tf_op jit(solution)/shard_map/ppermute | solution.py:431
  92.9 8.4 %finish.1 = (bf16[256,2560]{1,0:T(8,128)(2,1)}, bf16[256,2560]{1,0:T(8,128)(2,1)}, f32[40,256]{1,0:T(8,128)}, f32[32,1,128]{2,1,0:T(1,128)}) custom-call(f32[40,256]{1,0:T(8,128)S(1)} %bitcast.26, f32[1,40]{1,0:T(1,128)S(1)} %bitcast.28, f32[1,40]{1,0:T(1,128)S(1)} %bitcast.30, f32[1,40]{1,0:T(1,128)S(1)} %bitcast.31, bf16[256,128]{1,0:T(8,128)(2,1)S(1)} %copy-done.26, ...), custom_call_target="tpu_custom_call" | custom-call | flops 8000000000 | bytes 1000000 | tf_op jit(solution)/shard_map/finish/pallas_call | solution.py:528
  101.3 4.6 %all-to-all-start = ((f32[32,1,128]{2,1,0:T(1,128)}), f32[32,1,128]{2,1,0:T(1,128)S(1)}, u32[]{:S(2)}, u32[]{:S(2)}) async-start(f32[32,1,128]{2,1,0:T(1,128)} %get-tuple-element.85), calls=%async_computation | async-start | bytes 32768 | tf_op jit(solution)/shard_map/all_to_all | solution.py:555
  105.9 6.5 %keys.1 = (bf16[256,128]{1,0:T(8,128)(2,1)}, bf16[256,128]{1,0:T(8,128)(2,1)}) custom-call(f32[256,128]{1,0:T(8,128)} %copy-done.24, f32[256,128]{1,0:T(8,128)} %copy-done.25, bf16[256,2560]{1,0:T(8,128)(2,1)} %copy-done.20, bf16[256,2560]{1,0:T(8,128)(2,1)} %copy-done.21, bf16[256,2560]{1,0:T(8,128)(2,1)} %copy-done.22, bf16[256,2560]{1,0:T(8,128)(2,1)} %copy-done.23, ...), custom_call_target="tpu_custom_call" | custom-call | flops 6000000000 | bytes 1000000 | tf_op jit(solution)/shard_map/keys/pallas_call | solution.py:544
  (80 shorter events, 6.4 us)
Async XLA Ops:
  7.1 12.2 %collective-permute-start = (f32[136,640]{1,0:T(8,128)}, f32[136,640]{1,0:T(8,128)S(1)}, u32[]{:S(2)}, u32[]{:S(2)}) collective-permute-start(f32[136,640]{1,0:T(8,128)} %get-tuple-element.53), channel_id=1, source_target_pairs={{0,1},{1,0},{2,3},{3,2},{4,5},{5,4},{6,7},{7,6},{8,9},{9,8},{10,11... | collective-permute-start | bytes 1044488 | tf_op jit(solution)/shard_map/ppermute | solution.py:431
  10.1 12.3 %collective-permute-start.1 = (f32[136,640]{1,0:T(8,128)}, f32[136,640]{1,0:T(8,128)S(1)}, u32[]{:S(2)}, u32[]{:S(2)}) collective-permute-start(f32[136,640]{1,0:T(8,128)} %get-tuple-element.54), channel_id=1, source_target_pairs={{0,2},{1,3},{2,0},{3,1},{4,6},{5,7},{6,4},{7,5},{8,10},{9,11},{10,... | collective-permute-start | bytes 1044488 | tf_op jit(solution)/shard_map/ppermute | solution.py:431
  11.6 31.9 %collective-permute-start.2 = (f32[136,640]{1,0:T(8,128)}, f32[136,640]{1,0:T(8,128)S(1)}, u32[]{:S(2)}, u32[]{:S(2)}) collective-permute-start(f32[136,640]{1,0:T(8,128)} %get-tuple-element.59), channel_id=1, source_target_pairs={{0,3},{1,2},{2,1},{3,0},{4,7},{5,6},{6,5},{7,4},{8,11},{9,10},{10,... | collective-permute-start | bytes 1044488 | tf_op jit(solution)/shard_map/ppermute | solution.py:431
  11.6 31.8 %collective-permute-start.3 = (f32[136,640]{1,0:T(8,128)}, f32[136,640]{1,0:T(8,128)S(1)}, u32[]{:S(2)}, u32[]{:S(2)}) collective-permute-start(f32[136,640]{1,0:T(8,128)} %get-tuple-element.60), channel_id=1, source_target_pairs={{0,4},{1,5},{2,6},{3,7},{4,0},{5,1},{6,2},{7,3},{8,12},{9,13},{10,... | collective-permute-start | bytes 1044488 | tf_op jit(solution)/shard_map/ppermute | solution.py:431
  13.7 29.8 %collective-permute-start.4 = (f32[136,640]{1,0:T(8,128)}, f32[136,640]{1,0:T(8,128)S(1)}, u32[]{:S(2)}, u32[]{:S(2)}) collective-permute-start(f32[136,640]{1,0:T(8,128)} %get-tuple-element.61), channel_id=1, source_target_pairs={{0,5},{1,4},{2,7},{3,6},{4,1},{5,0},{6,3},{7,2},{8,13},{9,12},{10,... | collective-permute-start | bytes 1044488 | tf_op jit(solution)/shard_map/ppermute | solution.py:431
  19.3 24.2 %collective-permute-start.5 = (f32[136,640]{1,0:T(8,128)}, f32[136,640]{1,0:T(8,128)S(1)}, u32[]{:S(2)}, u32[]{:S(2)}) collective-permute-start(f32[136,640]{1,0:T(8,128)} %get-tuple-element.62), channel_id=1, source_target_pairs={{0,6},{1,7},{2,4},{3,5},{4,2},{5,3},{6,0},{7,1},{8,14},{9,15},{10,... | collective-permute-start | bytes 1044488 | tf_op jit(solution)/shard_map/ppermute | solution.py:431
  22.4 25.7 %collective-permute-start.6 = (f32[136,640]{1,0:T(8,128)}, f32[136,640]{1,0:T(8,128)S(1)}, u32[]{:S(2)}, u32[]{:S(2)}) collective-permute-start(f32[136,640]{1,0:T(8,128)} %get-tuple-element.63), channel_id=1, source_target_pairs={{0,7},{1,6},{2,5},{3,4},{4,3},{5,2},{6,1},{7,0},{8,15},{9,14},{10,... | collective-permute-start | bytes 1044488 | tf_op jit(solution)/shard_map/ppermute | solution.py:431
  48.5 9.5 %collective-permute-start.7 = (f32[72,640]{1,0:T(8,128)S(1)}, f32[72,640]{1,0:T(8,128)S(1)}, u32[]{:S(2)}, u32[]{:S(2)}) collective-permute-start(f32[72,640]{1,0:T(8,128)S(1)} %get-tuple-element.65), channel_id=1, source_target_pairs={{0,8},{1,9},{2,10},{3,11},{4,12},{5,13},{6,14},{7,15},{8,0},{9,1},... | collective-permute-start | bytes 552968 | tf_op jit(solution)/shard_map/ppermute | solution.py:431
  58.0 34.8 %copy-start.11 = (f32[1,40,256]{2,1,0:T(8,128)S(1)}, f32[1,40,256]{2,1,0:T(8,128)}, u32[]{:S(2)}) copy-start(f32[1,40,256]{2,1,0:T(8,128)} %param.13) | copy-start | bytes 122884
  58.0 34.8 %copy-start.13 = (f32[40]{0:T(128)S(1)}, f32[40]{0:T(128)}, u32[]{:S(2)}) copy-start(f32[40]{0:T(128)} %param.14) | copy-start | bytes 484
  58.0 34.8 %copy-start.14 = (f32[40]{0:T(128)S(1)}, f32[40]{0:T(128)}, u32[]{:S(2)}) copy-start(f32[40]{0:T(128)} %param.15) | copy-start | bytes 484
  58.0 34.8 %copy-start.15 = (f32[40]{0:T(128)S(1)}, f32[40]{0:T(128)}, u32[]{:S(2)}) copy-start(f32[40]{0:T(128)} %param.16) | copy-start | bytes 484
  58.0 34.8 %copy-start.17 = (bf16[128,2560]{1,0:T(8,128)(2,1)S(1)}, bf16[128,2560]{1,0:T(8,128)(2,1)}, u32[]{:S(2)}) copy-start(bf16[128,2560]{1,0:T(8,128)(2,1)} %constant.4.clone.spread_ref) | copy-start | bytes 1966084
  58.0 34.8 %copy-start.29 = (f32[40,256]{1,0:T(8,128)S(1)}, f32[40,256]{1,0:T(8,128)}, u32[]{:S(2)}) copy-start(f32[40,256]{1,0:T(8,128)} %get-tuple-element.49.stride_ref) | copy-start | bytes 122884
  58.0 34.8 %copy-start.30 = (f32[40,256]{1,0:T(8,128)S(1)}, f32[40,256]{1,0:T(8,128)}, u32[]{:S(2)}) copy-start(f32[40,256]{1,0:T(8,128)} %get-tuple-element.50.log_ref) | copy-start | bytes 122884
  58.7 42.6 %copy-start.19 = (f32[128,640]{1,0:T(8,128)}, f32[128,640]{1,0:T(8,128)S(1)}, u32[]{:S(2)}) copy-start(f32[128,640]{1,0:T(8,128)S(1)} %get-tuple-element.67.refs_0_) | copy-start | bytes 983044
  58.7 12.8 %collective-permute-start.8 = (f32[128,640]{1,0:T(8,128)S(1)}, f32[128,640]{1,0:T(8,128)S(1)}, u32[]{:S(2)}, u32[]{:S(2)}) collective-permute-start(f32[128,640]{1,0:T(8,128)S(1)} %get-tuple-element.68), channel_id=1, source_target_pairs={{0,1},{1,0},{2,3},{3,2},{4,5},{5,4},{6,7},{7,6},{8,9},{9,8},{10,11... | collective-permute-start | bytes 983048 | tf_op jit(solution)/shard_map/ppermute | solution.py:431
  59.5 12.0 %collective-permute-start.9 = (f32[128,640]{1,0:T(8,128)S(1)}, f32[128,640]{1,0:T(8,128)S(1)}, u32[]{:S(2)}, u32[]{:S(2)}) collective-permute-start(f32[128,640]{1,0:T(8,128)S(1)} %get-tuple-element.69), channel_id=1, source_target_pairs={{0,2},{1,3},{2,0},{3,1},{4,6},{5,7},{6,4},{7,5},{8,10},{9,11},{10,... | collective-permute-start | bytes 983048 | tf_op jit(solution)/shard_map/ppermute | solution.py:431
  60.5 22.3 %collective-permute-start.10 = (f32[128,640]{1,0:T(8,128)S(1)}, f32[128,640]{1,0:T(8,128)S(1)}, u32[]{:S(2)}, u32[]{:S(2)}) collective-permute-start(f32[128,640]{1,0:T(8,128)S(1)} %get-tuple-element.70), channel_id=1, source_target_pairs={{0,3},{1,2},{2,1},{3,0},{4,7},{5,6},{6,5},{7,4},{8,11},{9,10},{10,... | collective-permute-start | bytes 983048 | tf_op jit(solution)/shard_map/ppermute | solution.py:431
  62.2 20.6 %collective-permute-start.11 = (f32[128,640]{1,0:T(8,128)S(1)}, f32[128,640]{1,0:T(8,128)S(1)}, u32[]{:S(2)}, u32[]{:S(2)}) collective-permute-start(f32[128,640]{1,0:T(8,128)S(1)} %get-tuple-element.71), channel_id=1, source_target_pairs={{0,4},{1,5},{2,6},{3,7},{4,0},{5,1},{6,2},{7,3},{8,12},{9,13},{10,... | collective-permute-start | bytes 983048 | tf_op jit(solution)/shard_map/ppermute | solution.py:431
  62.9 19.9 %collective-permute-start.12 = (f32[128,640]{1,0:T(8,128)S(1)}, f32[128,640]{1,0:T(8,128)S(1)}, u32[]{:S(2)}, u32[]{:S(2)}) collective-permute-start(f32[128,640]{1,0:T(8,128)S(1)} %get-tuple-element.72), channel_id=1, source_target_pairs={{0,5},{1,4},{2,7},{3,6},{4,1},{5,0},{6,3},{7,2},{8,13},{9,12},{10,... | collective-permute-start | bytes 983048 | tf_op jit(solution)/shard_map/ppermute | solution.py:431
  71.5 16.0 %collective-permute-start.13 = (f32[128,640]{1,0:T(8,128)S(1)}, f32[128,640]{1,0:T(8,128)S(1)}, u32[]{:S(2)}, u32[]{:S(2)}) collective-permute-start(f32[128,640]{1,0:T(8,128)S(1)} %get-tuple-element.73), channel_id=1, source_target_pairs={{0,6},{1,7},{2,4},{3,5},{4,2},{5,3},{6,0},{7,1},{8,14},{9,15},{10,... | collective-permute-start | bytes 983048 | tf_op jit(solution)/shard_map/ppermute | solution.py:431
  71.5 21.3 %collective-permute-start.14 = (f32[128,640]{1,0:T(8,128)S(1)}, f32[128,640]{1,0:T(8,128)S(1)}, u32[]{:S(2)}, u32[]{:S(2)}) collective-permute-start(f32[128,640]{1,0:T(8,128)S(1)} %get-tuple-element.74), channel_id=1, source_target_pairs={{0,7},{1,6},{2,5},{3,4},{4,3},{5,2},{6,1},{7,0},{8,15},{9,14},{10,... | collective-permute-start | bytes 983048 | tf_op jit(solution)/shard_map/ppermute | solution.py:431
  101.3 11.7 %all-to-all-start = ((f32[32,1,128]{2,1,0:T(1,128)}), f32[32,1,128]{2,1,0:T(1,128)S(1)}, u32[]{:S(2)}, u32[]{:S(2)}) async-start(f32[32,1,128]{2,1,0:T(1,128)} %get-tuple-element.85), calls=%async_computation | async-start | bytes 32768 | tf_op jit(solution)/shard_map/all_to_all | solution.py:555
  (24 other events, 332.3 us)

commit v8 on v7

--- a/solution.py
+++ b/solution.py
@@ -20,7 +20,10 @@
 VMEM = pl.BlockSpec(memory_space=pltpu.VMEM)
 SMEM = pl.BlockSpec(memory_space=pltpu.SMEM)
 ANY = pl.BlockSpec(memory_space=pl.ANY)
-INNER_AFTER = 2
+WIDE_PARTS = 7
+AFTER = 2
+CUM, WEIGHT, FACTOR = 0, 1, 2
+STRIDE, LOG = 1, 2
 
 
 def iota(shape, axis):
@@ -95,8 +98,8 @@
 
 
 def states_kernel(starts, logits, bias, decay, spread_ref, features, writes, cotangent, reads, *refs):
-    sends = refs[:GROUP]
-    weight_cols, factor_cols, cum_cols, cum_rows, stride_out, log_out, scratch = refs[GROUP:]
+    sends, back_sends = refs[:GROUP], refs[GROUP : 2 * GROUP]
+    cols_out, rows_out, scratch = refs[2 * GROUP :]
     heads, length = logits.shape
     state = writes.shape[1]
     width = features.shape[1] // QUARTERS
@@ -134,25 +137,29 @@
         high, low = split2(cotangent[:, cols].astype(F32) * wide)
         return matmul(read_t, high) + matmul(read_t, low)
 
-    share_out(own, back_quarter, [send.at[part + 8 :] for send in sends], scratch)
+    share_out(own, back_quarter, back_sends, scratch)
     for distance, send in enumerate(sends):
-        send[part : part + 8] = keeps[distance % QUARTERS]
-    weight_cols[...] = weight_stack
-    factor_cols[...] = factor_stack
-    cum_cols[...] = stacked_columns(cum * LOG2E)
-    cum_rows[...] = cum * LOG2E - jnp.log2(stride)
-    stride_out[...] = stride
-    log_out[...] = log_decay
+        send[part:] = keeps[distance % QUARTERS]
+    cols_out[CUM] = stacked_columns(cum * LOG2E)
+    cols_out[WEIGHT] = weight_stack
+    cols_out[FACTOR] = factor_stack
+    rows_out[CUM] = cum * LOG2E - jnp.log2(stride)
+    rows_out[STRIDE] = stride
+    rows_out[LOG] = log_decay
 
 
 def inner_kernel(
-    starts, cum_cols, cum_rows, features, cotangent, writes, reads, weight_cols, factor_cols, spread_ref, *refs
+    offset, last, starts, cols_ref, rows_ref, features, cotangent, writes, reads, spread_ref, *refs
 ):
-    refs = refs[INNER_AFTER:]
-    inside, feature_part, skip_part, write_part, read_part, write_high, write_low, read_high, read_low = refs[:9]
-    scores_ref, mask_ref, grad_ref = refs[9:]
+    if offset:
+        before, refs = refs[0], refs[1 + WIDE_PARTS + AFTER :]
+    else:
+        refs = refs[AFTER:]
+    inside, feature_part, skip_part, write_high, write_low, read_high, read_low = refs[:WIDE_PARTS]
+    results = refs[WIDE_PARTS:-3]
+    scores_ref, mask_ref, grad_ref = refs[-3:]
     length, width = features.shape
-    heads = cum_rows.shape[0]
+    heads = rows_ref.shape[1]
     here = heads // QUARTERS
     head_dim = width // here
     pair = 2 * head_dim
@@ -166,10 +173,10 @@
         causal = iota((length, length), 0) >= iota((length, length), 1)
         mask_ref[...] = jnp.where((segment_row == segment_col) & causal, 0.0, FAR)
         scores_ref[...] = matmul_nt(reads[...], writes[...])
-        grad_ref[...] = jnp.zeros_like(grad_ref)
-
-    write_high[...], write_low[...] = split2(matmul(weight_cols[...], spread_ref[...]) * features[...].astype(F32))
-    read_high[...], read_low[...] = split2(matmul(factor_cols[...], spread_ref[...]) * cotangent[...].astype(F32))
+        grad_ref[...] = before[...] if offset else jnp.zeros_like(grad_ref)
+
+    write_high[...], write_low[...] = split2(matmul(cols_ref[WEIGHT], spread_ref[...]) * features[...].astype(F32))
+    read_high[...], read_low[...] = split2(matmul(cols_ref[FACTOR], spread_ref[...]) * cotangent[...].astype(F32))
 
     def one_pair(at, carry):
         cols = pl.ds(pl.multiple_of(at * pair, LANES), pair)
@@ -178,11 +185,11 @@
         grad_f32 = grad.astype(F32)
         grad_t = grad_f32.T.astype(BF16)
         skip_part[:, cols] = jnp.sum(grad_f32 * feature.astype(F32), axis=0, keepdims=True)
-        head = step * here + at * 2
+        head = (offset + step) * here + at * 2
         lane = iota((LANES, 2 * LANES), 0)
         wanted = head + lax.div(iota((LANES, 2 * LANES), 1), LANES)
         pick = (lane == wanted) | (lane == wanted + heads) | (lane == wanted + 2 * heads)
-        upper = matmul(cum_cols[...], jnp.where(pick, 1.0, 0.0).astype(BF16))
+        upper = matmul(cols_ref[CUM], jnp.where(pick, 1.0, 0.0).astype(BF16))
         second = iota((LANES, pair), 1) >= head_dim
         back = [None, None]
         for block in range(length // LANES):
@@ -191,12 +198,12 @@
             values = []
             for side in range(2):
                 high_row = jnp.concatenate([upper[rows, side * LANES : (side + 1) * LANES]] * (block + 1), axis=1)
-                low_row = cum_rows[pl.ds(head + side, 1), :][:, 0:reach]
+                low_row = rows_ref[CUM, pl.ds(head + side, 1), :][:, 0:reach]
                 weight = jnp.exp2(high_row - low_row + mask_ref[rows, 0:reach])
-                high, low = split2(weight * scores_ref[rows, 0:reach])
-                values.append(matmul(high, feature[0:reach]) + matmul(low, feature[0:reach]))
+                pieces = split2(weight * scores_ref[rows, 0:reach])
+                values.append(matmul(jnp.concatenate(pieces, axis=1), jnp.concatenate([feature[0:reach]] * 2, axis=0)))
                 grad_rows = grad_t[side * head_dim : (side + 1) * head_dim, rows]
-                found = matmul(grad_rows, high) + matmul(grad_rows, low)
+                found = matmul(jnp.concatenate([grad_rows] * 2, axis=1), jnp.concatenate(pieces, axis=0))
                 if block:
                     found = jnp.concatenate([found[:, : reach - LANES] + back[side], found[:, reach - LANES :]], axis=1)
                 back[side] = found
@@ -208,27 +215,33 @@
 
     lax.fori_loop(0, here // 2, one_pair, 0)
 
-    @pl.when(step == QUARTERS - 1)
+    @pl.when(step == pl.num_programs(0) - 1)
     def _():
         score_grad = grad_ref[...]
-        high, low = split2(score_grad)
-        read_part[...] = matmul(high, writes[...]) + matmul(low, writes[...])
-        high, low = split2(score_grad.T)
-        write_part[...] = matmul(high, reads[...]) + matmul(low, reads[...])
-
-
-def in_order(refs, scratch, back=False):
+        if last:
+            write_part, read_part = results
+            high, low = split2(score_grad)
+            read_part[...] = matmul(high, writes[...]) + matmul(low, writes[...])
+            high, low = split2(score_grad.T)
+            write_part[...] = matmul(high, reads[...]) + matmul(low, reads[...])
+        else:
+            results[0][...] = score_grad
+
+
+def in_order(refs, scratch):
     own = group_place()
-    rows = scratch.shape[1]
     for distance, ref in enumerate(refs):
-        first = ref.shape[0] - rows if back else 0
-        scratch[own ^ distance] = ref[first : first + rows]
+        scratch[own ^ distance] = ref[...]
+
+
+def hold_kernel(*refs):
+    count = len(refs) // 2
+    for value, out in zip(refs[:count], refs[count + 1 :]):
+        out[...] = value[...]
 
 
 def group_kernel(part, *refs):
-    keeps, came, back_came = refs[-3:]
-    sums = refs[GROUP + 1 : -3]
-    up, down = sums[0], sums[-1]
+    up, keeps, came = refs[-3:]
     in_order(refs[:GROUP], came)
     total = came[0, 0:part]
     keep = came[0, part:]
@@ -239,16 +252,22 @@
     up[part:] = keep
     for j in range(GROUP):
         keeps[j : j + 1] = came[j, part : part + 1]
-    in_order(refs[:GROUP], back_came, back=True)
+
+
+def back_group_kernel(part, two, *refs):
+    up, keeps = refs[GROUP : GROUP + 2]
+    out, came = refs[-2:]
+    in_order(refs[:GROUP], came)
+    out[part:] = up[part:]
 
     def downward():
-        total = back_came[GROUP - 1]
+        total = came[GROUP - 1]
         for j in reversed(range(GROUP - 1)):
-            total = total * keeps[j : j + 1] + back_came[j]
-        down[0:part] = total
-        down[part:] = keep
-
-    if len(sums) == 1:
+            total = total * keeps[j : j + 1] + came[j]
+        out[0:part] = total
+
+    if two:
+        out[0:part] = up[0:part]
         pl.when(lax.axis_index("ctx") >= GROUP)(downward)
     else:
         downward()
@@ -269,10 +288,11 @@
 
 
 def spread_kernel(part, count, back_count, *refs):
-    ups, downs = refs[GROUP : GROUP + count], refs[GROUP + count : GROUP + count + back_count]
-    keeps = refs[GROUP + count + back_count]
-    outs = refs[GROUP + count + back_count + 1 : -3]
-    came, back_came, give = refs[-3:]
+    first = 2 * GROUP
+    ups, downs = refs[first : first + count], refs[first + count : first + count + back_count]
+    keeps = refs[first + count + back_count]
+    outs = refs[first + count + back_count + 2 : -4]
+    came, back_came, give, back_give = refs[-4:]
     in_order(refs[:GROUP], came)
     if downs:
         entering, returning = arrived(part, ups)[0], arrived(part, downs)[0]
@@ -282,18 +302,19 @@
         returning = jnp.where(upper, 0.0, ups[0][0:part])
     total = entering
     for j in range(GROUP):
-        give[j, 0:part] = total
+        give[j] = total
         if j < GROUP - 1:
             total = total * keeps[j : j + 1] + came[j, 0:part]
-    in_order(refs[:GROUP], back_came, back=True)
+    in_order(refs[GROUP : 2 * GROUP], back_came)
     total = returning
     for j in reversed(range(GROUP)):
-        give[j, part:] = total
+        back_give[j] = total
         if j > 0:
             total = total * keeps[j : j + 1] + back_came[j]
     own = group_place()
-    for distance, out in enumerate(outs):
-        out[...] = give[own ^ distance]
+    for distance in range(GROUP):
+        outs[distance][...] = give[own ^ distance]
+        outs[GROUP + distance][...] = back_give[own ^ distance]
 
 
 def head_sums(ref, value, spread):
@@ -306,17 +327,37 @@
     return matmul(stack[0:16], spread)[0:1]
 
 
-def quarter_rows(have, step, back):
-    part = have.shape[1] // 2
-    return jnp.concatenate([have[half * QUARTERS + step, back * part : (back + 1) * part] for half in range(HALVES)], axis=0)
-
-
-def finish_kernel(
-    logits, bias, decay, skip, weight_cols, factor_cols, stride_ref, log_ref, spread_ref,
-    features, cotangent, writes, reads, inside, feature_part, skip_part, *refs,
+def quarter_rows(have, step):
+    return jnp.concatenate([have[half * QUARTERS + step] for half in range(HALVES)], axis=0)
+
+
+def finish_kernel(skip, cols_ref, spread_ref, features, cotangent, reads, inside, *refs):
+    mixed, rows, kept, have = refs[GROUP + 1 :]
+    length = reads.shape[0]
+    heads = skip.shape[1]
+    step = pl.program_id(0)
+
+    @pl.when(step == 0)
+    def _():
+        rows[...] = jnp.zeros_like(rows)
+        in_order(refs[:GROUP], have)
+
+    spread = spread_ref[...]
+    factor = matmul(cols_ref[FACTOR], spread)
+    entering = quarter_rows(have, step)
+    kept[...] = entering * factor[length - 1 :]
+    stack = jnp.concatenate(split2(entering), axis=0)
+    total = inside[...] + factor * matmul(jnp.concatenate([reads[...]] * 2, axis=1), stack)
+    mixed[...] = (total + wide_skip(skip, heads, spread) * features[...].astype(F32)).astype(BF16)
+    head_sums(rows, cotangent[...].astype(F32) * total, spread)
+
+
+def back_finish_kernel(
+    logits, bias, decay, skip, cols_ref, rows_ref, spread_ref,
+    features, cotangent, writes, feature_part, skip_part, row_ref, kept, *refs,
 ):
     haves = refs[:GROUP]
-    mixed, feature_grad, step_grad, sums, row_acc, col_acc, last_acc, skip_acc, have = refs[GROUP:]
+    feature_grad, step_grad, sums, col_acc, last_acc, skip_acc, have = refs[GROUP:]
     heads, length = logits.shape
     state = writes.shape[1]
     width = features.shape[1]
@@ -324,37 +365,31 @@
 
     @pl.when(step == 0)
     def _():
-        for ref in (row_acc, col_acc, last_acc, skip_acc):
+        for ref in (col_acc, last_acc, skip_acc):
             ref[...] = jnp.zeros_like(ref)
         in_order(haves, have)
 
     spread = spread_ref[...]
-    skips = wide_skip(skip, heads, spread)
+    weight = matmul(cols_ref[WEIGHT], spread)
     feature = features[...].astype(F32)
-    grad = cotangent[...].astype(F32)
-    factor = matmul(factor_cols[...], spread)
-    entering = quarter_rows(have, step, 0)
-    stack = jnp.concatenate(split2(entering), axis=0)
-    total = inside[...] + factor * matmul(jnp.concatenate([reads[...]] * 2, axis=1), stack)
-    mixed[...] = (total + skips * feature).astype(BF16)
-    head_sums(row_acc, grad * total, spread)
-    returning = quarter_rows(have, step, 1)
+    returning = quarter_rows(have, step)
     stack = jnp.concatenate(split2(returning), axis=0)
-    carried = matmul(weight_cols[...], spread) * matmul(jnp.concatenate([writes[...]] * 2, axis=1), stack)
+    writes2 = jnp.concatenate([writes[...]] * 2, axis=1)
+    carried = weight * matmul(writes2, stack)
     total = feature_part[...] + carried
-    feature_grad[...] = (total + skips * grad).astype(BF16)
+    feature_grad[...] = (total + wide_skip(skip, heads, spread) * cotangent[...].astype(F32)).astype(BF16)
     head_sums(col_acc, feature * total, spread)
-    leaving = jnp.sum((returning * entering).reshape(state // 8, 8, width), axis=0) * factor[length - 1 :]
+    leaving = jnp.sum((returning * kept[...]).reshape(state // 8, 8, width), axis=0)
     leaving = leaving + jnp.sum((feature * carried).reshape(length // 8, 8, width), axis=0)
     head_sums(last_acc, leaving, spread)
     head_sums(skip_acc, jnp.broadcast_to(skip_part[...], (8, width)), spread)
 
     @pl.when(step == QUARTERS - 1)
     def _():
-        rows = row_acc[...].T[:heads]
+        rows = row_ref[...].T[:heads]
         cols = col_acc[...].T[:heads]
         last = column(jnp.sum(last_acc[...], axis=0, keepdims=True))[:heads]
-        stride = stride_ref[...]
+        stride = rows_ref[STRIDE]
         gap_grad = rows - cols + jnp.where(iota((heads, length), 1) == length - 1, last, 0.0)
         onward = jnp.where(iota((length, length), 0) >= iota((length, length), 1), 1.0, 0.0).astype(BF16)
         parts = matmul(jnp.concatenate(split3(gap_grad), axis=0), onward)
@@ -364,7 +399,7 @@
         step_value = (cols / stride + rate * log_grad) * slope
         step_grad[...] = step_value
         bias_sum = jnp.sum(step_value, axis=1, keepdims=True)
-        decay_sum = jnp.sum(log_grad * log_ref[...], axis=1, keepdims=True)
+        decay_sum = jnp.sum(log_grad * rows_ref[LOG], axis=1, keepdims=True)
         skip_sum = column(skip_acc[0:1])[:heads]
         spare = jnp.zeros((LANES - 3 * heads, 1), F32)
         table = jnp.concatenate([bias_sum, decay_sum, skip_sum, spare], axis=0)
@@ -374,7 +409,7 @@
 
 
 def keys_kernel(write_part, read_part, write_high, write_low, read_high, read_low, *refs):
-    write_grad, read_grad, write_acc, read_acc, have = refs[GROUP + 1 :]
+    write_grad, read_grad, write_acc, read_acc, have, back_have = refs[2 * GROUP + 1 :]
     state = write_part.shape[1]
     step = pl.program_id(0)
 
@@ -383,9 +418,13 @@
         write_acc[...] = jnp.zeros_like(write_acc)
         read_acc[...] = jnp.zeros_like(read_acc)
         in_order(refs[:GROUP], have)
-
-    for back, high, low, acc in ((0, read_high, read_low, read_acc), (1, write_high, write_low, write_acc)):
-        stack = jnp.concatenate(split2(quarter_rows(have, step, back)), axis=0)
+        in_order(refs[GROUP : 2 * GROUP], back_have)
+
+    for states, high, low, acc in (
+        (have, read_high, read_low, read_acc),
+        (back_have, write_high, write_low, write_acc),
+    ):
+        stack = jnp.concatenate(split2(quarter_rows(states, step)), axis=0)
         acc[...] += matmul_nt(high[...], stack) + matmul_nt(low[...], stack)
 
     @pl.when(step == QUARTERS - 1)
@@ -455,7 +494,6 @@
     def quarter_of(rows, offset=0):
         return pl.BlockSpec((rows, width), lambda step: (0, step + offset))
 
-    stack = struct((length, LANES), BF16)
     small = struct((heads, length))
     result = struct((length, wide), BF16)
     tokens_result = struct((length, state), BF16)
@@ -463,95 +501,143 @@
     tokens = all_of(length, state)
     columns = all_of(length, LANES)
     by_heads = all_of(heads, length)
+    all_cols, all_rows = all_of(3, length, LANES), all_of(3, heads, length)
     row = all_of(1, heads)
     by_quarter = quarter_of(length)
     spread_quarter = quarter_of(LANES)
     shares = pltpu.VMEM((GROUP, part, width), F32)
     long_shares = pltpu.VMEM((GROUP, part + 8, width), F32)
-    both_shares = pltpu.VMEM((GROUP, 2 * part, width), F32)
-
-    both = struct((2 * part + 8, width))
+
+    share = struct((part, width))
     out = call(
         states_kernel,
         "states",
-        [both] * GROUP + [stack] * 3 + [small] * 3,
+        [group_sum] * GROUP + [share] * GROUP + [struct((3, length, LANES), BF16), struct((3, heads, length))],
         [SMEM] + [VMEM] * 8,
         4,
         60,
         scratch_shapes=[pltpu.VMEM((state, width), F32)],
     )(doc_starts, logits, bias, decay, spread, features, writes, cotangent, reads)
     came = swap(out[:GROUP])
-    weight_cols, factor_cols, cum_cols, cum_rows, stride, log_decay = out[GROUP:]
+    back_sends = out[GROUP : 2 * GROUP]
+    cols, head_rows = out[2 * GROUP :]
 
     wide_part, wide_piece = struct((length, wide)), struct((length, wide), BF16)
-    inside, feature_part, skip_part, write_part, read_part, *pieces = call(
-        inner_kernel,
-        "inner",
-        [wide_part] * 2 + [struct((1, wide))] + [struct((length, state))] * 2 + [wide_piece] * 4,
-        [SMEM, columns, by_heads, by_quarter, by_quarter, tokens, tokens, columns, columns, spread_quarter]
-        + [ANY] * INNER_AFTER,
-        10,
-        24,
-        grid=(QUARTERS,),
-        out_specs=[by_quarter, by_quarter, quarter_of(1), tokens, tokens] + [by_quarter] * 4,
-        scratch_shapes=[pltpu.VMEM((length, length), F32)] * 3,
-    )(
-        doc_starts, cum_cols, cum_rows, features, cotangent, writes, reads, weight_cols, factor_cols, spread,
-        *[came[d] for d in DISTANCES[:INNER_AFTER]],
+    wide_parts = [wide_part] * 2 + [struct((1, wide))] + [wide_piece] * 4
+    inner_args = (
+        doc_starts, cols, head_rows, features, cotangent, writes, reads, spread
     )
-    two = blocks == 2 * GROUP
-    *sums, keeps = call(
+
+    square = all_of(length, length)
+    token_part = struct((length, state))
+
+    def inner(offset, count, begun, after):
+        mine = quarter_of(length, offset)
+        last = offset + count == QUARTERS
+        n_args = len(inner_args) + 1
+        return call(
+            functools.partial(inner_kernel, offset, last),
+            "inner_" + str(offset),
+            wide_parts + ([token_part] * 2 if last else [struct((length, length))]),
+            [SMEM, all_cols, all_rows, mine, mine, tokens, tokens, quarter_of(LANES, offset)]
+            + ([square] + [ANY] * WIDE_PARTS if offset else [])
+            + [ANY] * AFTER,
+            5 * count,
+            24,
+            grid=(count,),
+            out_specs=[mine, mine, quarter_of(1, offset)] + [mine] * 4 + ([tokens] * 2 if last else [square]),
+            scratch_shapes=[pltpu.VMEM((length, length), F32)] * 3,
+            input_output_aliases={n_args + at: at for at in range(WIDE_PARTS)} if offset else {},
+        )(*inner_args, *begun, *after)
+
+    def hold(values, distances, until):
+        chosen = [values[d] for d in distances]
+        count = len(chosen)
+        held = call(hold_kernel, "hold", [share] * count, [VMEM] * count + [ANY], 1, 12)(*chosen, until)
+        return dict(zip(distances, held))
+
+    *begun, score_grad = inner(0, 1, [], [came[1], came[2]])
+    early = hold(back_sends, (1, 2, 3), score_grad)
+    back_came = [back_sends[0]] + [exchange(early[d], d) for d in (1, 2, 3)]
+    up, keeps = call(
         functools.partial(group_kernel, part),
         "group",
-        [group_sum] * (1 if two else 2) + [struct((GROUP, width))],
+        [group_sum, struct((GROUP, width))],
         [VMEM] * GROUP + [ANY],
         2,
         12,
-        scratch_shapes=[long_shares, shares],
-    )(*came, write_part)
+        scratch_shapes=[long_shares],
+    )(*came, score_grad)
+    *begun, score_grad = inner(1, 1, [score_grad, *begun], [up, back_came[1]])
+    late = hold(back_sends, (4, 5, 6, 7), score_grad)
+    back_came += [exchange(late[d], d) for d in (4, 5, 6, 7)]
+    two = blocks == 2 * GROUP
+    (cross,) = call(
+        functools.partial(back_group_kernel, part, two),
+        "back_group",
+        [group_sum],
+        [VMEM] * (GROUP + 2) + [ANY],
+        2,
+        12,
+        scratch_shapes=[shares],
+    )(*back_came, up, keeps, score_grad)
     if two:
-        ups, downs = [exchange(sums[0], GROUP)], []
+        ups, downs = [exchange(cross, GROUP)], []
     else:
-        ups, downs = scan(sums[0], 1), scan(sums[1], -1)
+        ups, downs = scan(up, 1), scan(cross, -1)
+    *done, write_part, read_part = inner(2, QUARTERS - 2, [score_grad, *begun], [cross] * AFTER)
+    inside, feature_part, skip_part, *pieces = done
     give = call(
         functools.partial(spread_kernel, part, len(ups), len(downs)),
         "spread",
-        [struct((2 * part, width))] * GROUP,
-        [VMEM] * (GROUP + len(ups) + len(downs) + 1),
+        [share] * 2 * GROUP,
+        [VMEM] * (2 * GROUP + len(ups) + len(downs) + 1) + [ANY],
         2,
         16,
-        scratch_shapes=[long_shares, shares, both_shares],
-    )(*came, *ups, *downs, keeps)
-    have = swap(give)
+        scratch_shapes=[long_shares, shares, shares, shares],
+    )(*came, *back_came, *ups, *downs, keeps, write_part)
+    have, back_have = swap(give[:GROUP]), swap(give[GROUP:])
     devices = blocks * members
-    whole_shares = [all_of(2 * part, width)] * GROUP
-    mixed, feature_grad, step_grad, sums = call(
+    whole_shares = [all_of(part, width)] * GROUP
+    mixed, rows, kept = call(
         finish_kernel,
         "finish",
-        [result, result, small, struct((devices, 1, LANES))],
-        [by_heads, row, row, row, columns, columns, by_heads, by_heads, spread_quarter]
-        + [by_quarter, by_quarter, tokens, tokens, by_quarter, by_quarter, quarter_of(1)]
+        [result, struct((length, LANES)), struct((state, wide))],
+        [row, all_cols, spread_quarter, by_quarter, by_quarter, tokens, by_quarter] + whole_shares + [ANY],
+        8,
+        24,
+        grid=(QUARTERS,),
+        out_specs=[by_quarter, columns, quarter_of(state)],
+        scratch_shapes=[shares],
+    )(skip, cols, spread, features, cotangent, reads, inside, *have, back_have[DISTANCES[1]])
+    feature_grad, step_grad, sums = call(
+        back_finish_kernel,
+        "back_finish",
+        [result, small, struct((devices, 1, LANES))],
+        [by_heads, row, row, row, all_cols, all_rows, spread_quarter]
+        + [by_quarter, by_quarter, tokens, by_quarter]
+        + [quarter_of(1), columns, quarter_of(state)]
         + whole_shares,
         8,
         24,
         grid=(QUARTERS,),
-        out_specs=[by_quarter, by_quarter, by_heads, all_of(devices, 1, LANES)],
-        scratch_shapes=[pltpu.VMEM((length, LANES), F32)] * 2 + [pltpu.VMEM((8, LANES), F32)] * 2 + [both_shares],
+        out_specs=[by_quarter, by_heads, all_of(devices, 1, LANES)],
+        scratch_shapes=[pltpu.VMEM((length, LANES), F32)] + [pltpu.VMEM((8, LANES), F32)] * 2 + [shares],
     )(
-        logits, bias, decay, skip, weight_cols, factor_cols, stride, log_decay, spread,
-        features, cotangent, writes, reads, inside, feature_part, skip_part, *have,
+        logits, bias, decay, skip, cols, head_rows, spread, features, cotangent, writes,
+        feature_part, skip_part, rows, kept, *back_have,
     )
     write_grad, read_grad = call(
         keys_kernel,
         "keys",
         [tokens_result] * 2,
-        [tokens] * 2 + [by_quarter] * 4 + whole_shares + [ANY],
+        [tokens] * 2 + [by_quarter] * 4 + whole_shares * 2 + [ANY],
         6,
         60,
         grid=(QUARTERS,),
         out_specs=[tokens] * 2,
-        scratch_shapes=[pltpu.VMEM((length, 2 * state), F32)] * 2 + [both_shares],
-    )(write_part, read_part, *pieces, *have, step_grad)
+        scratch_shapes=[pltpu.VMEM((length, 2 * state), F32)] * 2 + [shares] * 2,
+    )(write_part, read_part, *pieces, *have, *back_have, step_grad)
     sums = jnp.sum(lax.all_to_all(sums, ("dp", "ctx"), 0, 0), axis=(0, 1))
     return (
         mixed[None],

time: 114 us -> 122 us (1.070)
  starting transfers between devices: 28.6 us -> 44.7 us
  waiting for transfers between devices: 41.9 us -> 28.9 us
  local copies, waits for them, and re-layouts: 4 us -> 6.23 us
  Pallas kernels: 38.1 us -> 40.2 us
    ppermute x15 -> x29, starting transfers between devices: 24.1 us -> 42.2 us  [exchange(): lax.ppermute(value, 'ctx', [(k, k ^ distance) for k in range(blocks)])]
    ppermute x15 -> x29, waiting for transfers between devices: 41.3 us -> 28.3 us  [exchange(): lax.ppermute(value, 'ctx', [(k, k ^ distance) for k in range(blocks)])]
    unnamed x64 -> x96, local copies, waits for them, and re-layouts: 3.41 us -> 5.63 us
    pallas_call x4 -> x10, Pallas kernels: 31 us -> 33.1 us  [the longest x3 15.6 us: inner(): call(functools.partial(inner_kernel, offset, last), 'inner_' + str(offset...]
    all_to_all x1, starting transfers between devices: 4.55 us -> 2.56 us  [local(): sums = jnp.sum(lax.all_to_all(sums, ('dp', 'ctx'), 0, 0), axis=(0, 1))]
  transfers between devices with their start and end apart: 16 -> 30, of which waited for: 8 -> 12; matrix products, arithmetic and copies ran while one was open for 0% -> 0% of each run, Pallas kernels for 20% -> 22%
where the time goes in v8:
time: 122 us; the launch traced here: 121 us
  starting transfers between devices  44.7 us (37%)
  Pallas kernels  40.2 us (33%)
  waiting for transfers between devices  28.9 us (24%)
  local copies, waits for them, and re-layouts  6.23 us (5%)
    ppermute x29, starting transfers between devices, exchange(): lax.ppermute(value, 'ctx', [(k, k ^ distance) for k in range(blocks)])  42.2 us
    ppermute x29, waiting for transfers between devices, exchange(): lax.ppermute(value, 'ctx', [(k, k ^ distance) for k in range(blocks)])  28.3 us
    pallas_call x3, Pallas kernels, inner(): call(functools.partial(inner_kernel, offset, last), 'inner_' + str(offset...  15.6 us
    pallas_call x1, Pallas kernels, local(): call(keys_kernel, 'keys', [tokens_result] * 2, [tokens] * 2 + [by_quarter...  6.51 us
    pallas_call x1, Pallas kernels, local(): call(states_kernel, 'states', [group_sum] * GROUP + [share] * GROUP + [st...  6.44 us
    pallas_call x1, Pallas kernels, local(): call(back_finish_kernel, 'back_finish', [result, small, struct((devices,...  6.03 us
    unnamed x96, local copies, waits for them, and re-layouts  5.63 us
    pallas_call x1, Pallas kernels, local(): call(finish_kernel, 'finish', [result, struct((length, LANES)), struct((s...  4.42 us
  transfers between devices with their start and end apart: 30, of which 12 were waited for; matrix products, arithmetic and copies ran while one was open for 0% of the time, Pallas kernels for 22%

profile of v8, /device:TPU:0, one launch (start us, length us, event | category | flops | bytes accessed | tf_op | source)
XLA Modules:
  0.0 121.3 jit_solution(7931228011222365592)
XLA Ops:
  0.7 6.4 %states.1 = (f32[72,640]{1,0:T(8,128)}, f32[72,640]{1,0:T(8,128)}, f32[72,640]{1,0:T(8,128)}, f32[72,640]{1,0:T(8,128)}, f32[72,640]{1,0:T(8,128)}, /*index=5*/f...) custom-call(s32[1,4]{1,0:T(1,128)} %starts.7, ...), custom_call_target="tpu_custom_call" | custom-call | flops 4000000000 | bytes 1000000 | tf_op jit(solution)/shard_map/states/pallas_call | solution.py:512
  7.1 3.0 %collective-permute-start = (f32[72,640]{1,0:T(8,128)}, f32[72,640]{1,0:T(8,128)S(1)}, u32[]{:S(2)}, u32[]{:S(2)}) collective-permute-start(f32[72,640]{1,0:T(8,128)} %get-tuple-element.86), channel_id=1, source_target_pairs={{0,1},{1,0},{2,3},{3,2},{4,5},{5,4},{6,7},{7,6},{8,9},{9,8},{10,11... | collective-permute-start | bytes 552968 | tf_op jit(solution)/shard_map/ppermute | solution.py:470
  11.7 2.0 %collective-permute-start.3 = (f32[72,640]{1,0:T(8,128)}, f32[72,640]{1,0:T(8,128)S(1)}, u32[]{:S(2)}, u32[]{:S(2)}) collective-permute-start(f32[72,640]{1,0:T(8,128)} %get-tuple-element.98), channel_id=1, source_target_pairs={{0,4},{1,5},{2,6},{3,7},{4,0},{5,1},{6,2},{7,3},{8,12},{9,13},{10,... | collective-permute-start | bytes 552968 | tf_op jit(solution)/shard_map/ppermute | solution.py:470
  15.8 3.1 %collective-permute-start.5 = (f32[72,640]{1,0:T(8,128)}, f32[72,640]{1,0:T(8,128)S(1)}, u32[]{:S(2)}, u32[]{:S(2)}) collective-permute-start(f32[72,640]{1,0:T(8,128)} %get-tuple-element.100), channel_id=1, source_target_pairs={{0,6},{1,7},{2,4},{3,5},{4,2},{5,3},{6,0},{7,1},{8,14},{9,15},{10,... | collective-permute-start | bytes 552968 | tf_op jit(solution)/shard_map/ppermute | solution.py:470
  22.4 3.9 %inner_0.1 = (f32[256,2560]{1,0:T(8,128)S(1)}, f32[256,2560]{1,0:T(8,128)S(1)}, f32[1,2560]{1,0:T(1,128)S(1)}, bf16[256,2560]{1,0:T(8,128)(2,1)S(1)}, bf16[256,2...) custom-call(s32[1,4]{1,0:T(1,128)S(1)} %copy-done.21, ...), custom_call_target="tpu_custom_call" | custom-call | flops 5000000000 | bytes 1000000 | tf_op jit(solution)/shard_map/inner_0/pallas_call | solution.py:538
  26.4 2.8 %collective-permute-start.7 = (f32[64,640]{1,0:T(8,128)S(1)}, f32[64,640]{1,0:T(8,128)S(1)}, u32[]{:S(2)}, u32[]{:S(2)}) collective-permute-start(f32[64,640]{1,0:T(8,128)S(1)} %get-tuple-element.106), channel_id=1, source_target_pairs={{0,1},{1,0},{2,3},{3,2},{4,5},{5,4},{6,7},{7,6},{8,9},{9,8},{10,11... | collective-permute-start | bytes 491528 | tf_op jit(solution)/shard_map/ppermute | solution.py:470
  32.0 2.3 %collective-permute-done.7.refs_9_.refs_1_ = f32[64,640]{1,0:T(8,128)S(1)} collective-permute-done((f32[64,640]{1,0:T(8,128)S(1)}, f32[64,640]{1,0:T(8,128)S(1)}, u32[]{:S(2)}, u32[]{:S(2)}) %collective-permute-start.7) | collective-permute-done | bytes 163872 | tf_op jit(solution)/shard_map/ppermute | solution.py:470
  34.4 3.9 %inner_1.1 = (f32[256,2560]{1,0:T(8,128)S(1)}, f32[256,2560]{1,0:T(8,128)S(1)}, f32[1,2560]{1,0:T(1,128)S(1)}, bf16[256,2560]{1,0:T(8,128)(2,1)S(1)}, bf16[256,2...) custom-call(s32[1,4]{1,0:T(1,128)S(1)} %copy-done.21, ...), custom_call_target="tpu_custom_call", output_to_operand_aliasing={{0}: (9, {}), {1}: (10, {}), {2}: (11, {}), {3}: (12, {}), ... | custom-call | flops 5000000000 | bytes 1000000 | tf_op jit(solution)/shard_map/inner_1/pallas_call | solution.py:538
  45.6 3.5 %collective-permute-done.11.refs_5_.refs_13_ = f32[64,640]{1,0:T(8,128)S(1)} collective-permute-done((f32[64,640]{1,0:T(8,128)S(1)}, f32[64,640]{1,0:T(8,128)S(1)}, u32[]{:S(2)}, u32[]{:S(2)}) %collective-permute-start.11) | collective-permute-done | bytes 163872 | tf_op jit(solution)/shard_map/ppermute | solution.py:470
  49.1 2.5 %collective-permute-done.12.refs_6_.refs_14_ = f32[64,640]{1,0:T(8,128)S(1)} collective-permute-done((f32[64,640]{1,0:T(8,128)S(1)}, f32[64,640]{1,0:T(8,128)S(1)}, u32[]{:S(2)}, u32[]{:S(2)}) %collective-permute-start.12) | collective-permute-done | bytes 163872 | tf_op jit(solution)/shard_map/ppermute | solution.py:470
  51.6 2.0 %collective-permute-done.13.refs_7_.refs_15_ = f32[64,640]{1,0:T(8,128)S(1)} collective-permute-done((f32[64,640]{1,0:T(8,128)S(1)}, f32[64,640]{1,0:T(8,128)S(1)}, u32[]{:S(2)}, u32[]{:S(2)}) %collective-permute-start.13) | collective-permute-done | bytes 163872 | tf_op jit(solution)/shard_map/ppermute | solution.py:470
  53.9 3.2 %collective-permute-start.14 = (f32[72,640]{1,0:T(8,128)S(1)}, f32[72,640]{1,0:T(8,128)S(1)}, u32[]{:S(2)}, u32[]{:S(2)}) collective-permute-start(f32[72,640]{1,0:T(8,128)S(1)} %back_group.1.refs_8_.refs_9_), channel_id=1, source_target_pairs={{0,8},{1,9},{2,10},{3,11},{4,12},{5,13},{6,14},{7,15},{8,0},{9,1},... | collective-permute-start | bytes 552968 | tf_op jit(solution)/shard_map/ppermute | solution.py:470
  57.1 7.8 %inner_2.1 = (f32[256,2560]{1,0:T(8,128)S(1)}, f32[256,2560]{1,0:T(8,128)S(1)}, f32[1,2560]{1,0:T(1,128)S(1)}, bf16[256,2560]{1,0:T(8,128)(2,1)S(1)}, bf16[256,2...) custom-call(s32[1,4]{1,0:T(1,128)S(1)} %copy-done.21, ...), custom_call_target="tpu_custom_call", output_to_operand_aliasing={{0}: (9, {}), {1}: (10, {}), {2}: (11, {}), {3}: (12, {}), ... | custom-call | flops 10000000000 | bytes 1000000 | tf_op jit(solution)/shard_map/inner_2/pallas_call | solution.py:538
  69.3 1.9 %collective-permute-start.15 = (f32[64,640]{1,0:T(8,128)S(1)}, f32[64,640]{1,0:T(8,128)S(1)}, u32[]{:S(2)}, u32[]{:S(2)}) collective-permute-start(f32[64,640]{1,0:T(8,128)S(1)} %get-tuple-element.130), channel_id=1, source_target_pairs={{0,1},{1,0},{2,3},{3,2},{4,5},{5,4},{6,7},{7,6},{8,9},{9,8},{10,11... | collective-permute-start | bytes 491528 | tf_op jit(solution)/shard_map/ppermute | solution.py:470
  73.6 2.5 %collective-permute-start.19 = (f32[64,640]{1,0:T(8,128)S(1)}, f32[64,640]{1,0:T(8,128)S(1)}, u32[]{:S(2)}, u32[]{:S(2)}) collective-permute-start(f32[64,640]{1,0:T(8,128)S(1)} %get-tuple-element.134), channel_id=1, source_target_pairs={{0,5},{1,4},{2,7},{3,6},{4,1},{5,0},{6,3},{7,2},{8,13},{9,12},{10,... | collective-permute-start | bytes 491528 | tf_op jit(solution)/shard_map/ppermute | solution.py:470
  77.2 7.1 %collective-permute-done.16.refs_2_ = f32[64,640]{1,0:T(8,128)S(1)} collective-permute-done((f32[64,640]{1,0:T(8,128)S(1)}, f32[64,640]{1,0:T(8,128)S(1)}, u32[]{:S(2)}, u32[]{:S(2)}) %collective-permute-start.16) | collective-permute-done | bytes 163872 | tf_op jit(solution)/shard_map/ppermute | solution.py:470
  84.4 2.2 %collective-permute-start.23 = (f32[64,640]{1,0:T(8,128)S(1)}, f32[64,640]{1,0:T(8,128)S(1)}, u32[]{:S(2)}, u32[]{:S(2)}) collective-permute-start(f32[64,640]{1,0:T(8,128)S(1)} %get-tuple-element.144), channel_id=1, source_target_pairs={{0,1},{1,0},{2,3},{3,2},{4,5},{5,4},{6,7},{7,6},{8,9},{9,8},{10,11... | collective-permute-start | bytes 491528 | tf_op jit(solution)/shard_map/ppermute | solution.py:470
  89.4 4.2 %collective-permute-done.21.refs_7_ = f32[64,640]{1,0:T(8,128)S(1)} collective-permute-done((f32[64,640]{1,0:T(8,128)S(1)}, f32[64,640]{1,0:T(8,128)S(1)}, u32[]{:S(2)}, u32[]{:S(2)}) %collective-permute-start.21) | collective-permute-done | bytes 163872 | tf_op jit(solution)/shard_map/ppermute | solution.py:470
  93.6 3.1 %collective-permute-done.22.refs_8_.refs_2_.refs_10_ = f32[64,640]{1,0:T(8,128)S(1)} collective-permute-done((f32[64,640]{1,0:T(8,128)S(1)}, f32[64,640]{1,0:T(8,128)S(1)}, u32[]{:S(2)}, u32[]{:S(2)}) %collective-permute-start.22) | collective-permute-done | bytes 163872 | tf_op jit(solution)/shard_map/ppermute | solution.py:470
  96.8 3.1 %collective-permute-start.28 = (f32[64,640]{1,0:T(8,128)S(1)}, f32[64,640]{1,0:T(8,128)S(1)}, u32[]{:S(2)}, u32[]{:S(2)}) collective-permute-start(f32[64,640]{1,0:T(8,128)S(1)} %get-tuple-element.149), channel_id=1, source_target_pairs={{0,7},{1,6},{2,5},{3,4},{4,3},{5,2},{6,1},{7,0},{8,15},{9,14},{10,... | collective-permute-start | bytes 491528 | tf_op jit(solution)/shard_map/ppermute | solution.py:470
  99.9 4.4 %finish.1 = (bf16[256,2560]{1,0:T(8,128)(2,1)}, f32[256,128]{1,0:T(8,128)S(1)}, f32[128,2560]{1,0:T(8,128)S(1)}) custom-call(f32[1,40]{1,0:T(1,128)S(1)} %bitcast.37, bf16[3,256,128]{2,1,0:T(8,128)(2,1)S(1)} %copy-done.39, bf16[128,2560]{1,0:T(8,128)(2,1)S(1)} %copy-done.26, bf16[256,2560]{1,0:T(8,128)(2,1)S(1)} %bitcast.17, bf16[256,2560]{1,0:T(8,128)(2,1)S(1)} %bitcast.23, ...), custom_call_target="tpu_custom_call" | custom-call | flops 8000000000 | bytes 1000000 | tf_op jit(solution)/shard_map/finish/pallas_call | solution.py:602
  104.9 6.0 %back_finish.1 = (bf16[256,2560]{1,0:T(8,128)(2,1)}, f32[40,256]{1,0:T(8,128)}, f32[32,1,128]{2,1,0:T(1,128)}) custom-call(f32[40,256]{1,0:T(8,128)S(1)} %bitcast.36, f32[1,40]{1,0:T(1,128)S(1)} %bitcast.40, f32[1,40]{1,0:T(1,128)S(1)} %bitcast.42, f32[1,40]{1,0:T(1,128)S(1)} %bitcast.38, bf16[3,256,128]{2,1,0:T(8,128)(2,1)S(1)} %copy-done.39, ...), custom_call_target="tpu_custom_call" | custom-call | flops 8000000000 | bytes 1000000 | tf_op jit(solution)/shard_map/back_finish/pallas_call | solution.py:613
  111.0 2.6 %all-to-all-start = ((f32[32,1,128]{2,1,0:T(1,128)}), f32[32,1,128]{2,1,0:T(1,128)S(1)}, u32[]{:S(2)}, u32[]{:S(2)}) async-start(f32[32,1,128]{2,1,0:T(1,128)} %get-tuple-element.159), calls=%async_computation | async-start | bytes 32768 | tf_op jit(solution)/shard_map/all_to_all | solution.py:641
  113.5 6.5 %keys.1 = (bf16[256,128]{1,0:T(8,128)(2,1)}, bf16[256,128]{1,0:T(8,128)(2,1)}) custom-call(f32[256,128]{1,0:T(8,128)} %copy-done.46, f32[256,128]{1,0:T(8,128)} %copy-done.47, bf16[256,2560]{1,0:T(8,128)(2,1)} %copy-done.27, bf16[256,2560]{1,0:T(8,128)(2,1)} %copy-done.28, bf16[256,2560]{1,0:T(8,128)(2,1)} %copy-done.29, bf16[256,2560]{1,0:T(8,128)(2,1)} %copy-done.30, ...), custom_call_target="tpu_custom_call" | custom-call | flops 6000000000 | bytes 1000000 | tf_op jit(solution)/shard_map/keys/pallas_call | solution.py:630
  (146 shorter events, 29.8 us)
Async XLA Ops:
  10.1 8.8 %collective-permute-start.1 = (f32[72,640]{1,0:T(8,128)}, f32[72,640]{1,0:T(8,128)S(1)}, u32[]{:S(2)}, u32[]{:S(2)}) collective-permute-start(f32[72,640]{1,0:T(8,128)} %get-tuple-element.87), channel_id=1, source_target_pairs={{0,2},{1,3},{2,0},{3,1},{4,6},{5,7},{6,4},{7,5},{8,10},{9,11},{10,... | collective-permute-start | bytes 552968 | tf_op jit(solution)/shard_map/ppermute | solution.py:470
  11.7 14.7 %collective-permute-start.2 = (f32[72,640]{1,0:T(8,128)}, f32[72,640]{1,0:T(8,128)S(1)}, u32[]{:S(2)}, u32[]{:S(2)}) collective-permute-start(f32[72,640]{1,0:T(8,128)} %get-tuple-element.97), channel_id=1, source_target_pairs={{0,3},{1,2},{2,1},{3,0},{4,7},{5,6},{6,5},{7,4},{8,11},{9,10},{10,... | collective-permute-start | bytes 552968 | tf_op jit(solution)/shard_map/ppermute | solution.py:470
  11.7 17.5 %collective-permute-start.3 = (f32[72,640]{1,0:T(8,128)}, f32[72,640]{1,0:T(8,128)S(1)}, u32[]{:S(2)}, u32[]{:S(2)}) collective-permute-start(f32[72,640]{1,0:T(8,128)} %get-tuple-element.98), channel_id=1, source_target_pairs={{0,4},{1,5},{2,6},{3,7},{4,0},{5,1},{6,2},{7,3},{8,12},{9,13},{10,... | collective-permute-start | bytes 552968 | tf_op jit(solution)/shard_map/ppermute | solution.py:470
  13.7 15.5 %collective-permute-start.4 = (f32[72,640]{1,0:T(8,128)}, f32[72,640]{1,0:T(8,128)S(1)}, u32[]{:S(2)}, u32[]{:S(2)}) collective-permute-start(f32[72,640]{1,0:T(8,128)} %get-tuple-element.99), channel_id=1, source_target_pairs={{0,5},{1,4},{2,7},{3,6},{4,1},{5,0},{6,3},{7,2},{8,13},{9,12},{10,... | collective-permute-start | bytes 552968 | tf_op jit(solution)/shard_map/ppermute | solution.py:470
  15.8 15.0 %collective-permute-start.5 = (f32[72,640]{1,0:T(8,128)}, f32[72,640]{1,0:T(8,128)S(1)}, u32[]{:S(2)}, u32[]{:S(2)}) collective-permute-start(f32[72,640]{1,0:T(8,128)} %get-tuple-element.100), channel_id=1, source_target_pairs={{0,6},{1,7},{2,4},{3,5},{4,2},{5,3},{6,0},{7,1},{8,14},{9,15},{10,... | collective-permute-start | bytes 552968 | tf_op jit(solution)/shard_map/ppermute | solution.py:470
  18.9 12.8 %collective-permute-start.6 = (f32[72,640]{1,0:T(8,128)}, f32[72,640]{1,0:T(8,128)S(1)}, u32[]{:S(2)}, u32[]{:S(2)}) collective-permute-start(f32[72,640]{1,0:T(8,128)} %get-tuple-element.101), channel_id=1, source_target_pairs={{0,7},{1,6},{2,5},{3,4},{4,3},{5,2},{6,1},{7,0},{8,15},{9,14},{10,... | collective-permute-start | bytes 552968 | tf_op jit(solution)/shard_map/ppermute | solution.py:470
  29.2 13.7 %collective-permute-start.8 = (f32[64,640]{1,0:T(8,128)S(1)}, f32[64,640]{1,0:T(8,128)S(1)}, u32[]{:S(2)}, u32[]{:S(2)}) collective-permute-start(f32[64,640]{1,0:T(8,128)S(1)} %get-tuple-element.116), channel_id=1, source_target_pairs={{0,2},{1,3},{2,0},{3,1},{4,6},{5,7},{6,4},{7,5},{8,10},{9,11},{10,... | collective-permute-start | bytes 491528 | tf_op jit(solution)/shard_map/ppermute | solution.py:470
  29.2 15.1 %collective-permute-start.9 = (f32[64,640]{1,0:T(8,128)S(1)}, f32[64,640]{1,0:T(8,128)S(1)}, u32[]{:S(2)}, u32[]{:S(2)}) collective-permute-start(f32[64,640]{1,0:T(8,128)S(1)} %get-tuple-element.117), channel_id=1, source_target_pairs={{0,3},{1,2},{2,1},{3,0},{4,7},{5,6},{6,5},{7,4},{8,11},{9,10},{10,... | collective-permute-start | bytes 491528 | tf_op jit(solution)/shard_map/ppermute | solution.py:470
  40.0 9.1 %collective-permute-start.11 = (f32[64,640]{1,0:T(8,128)S(1)}, f32[64,640]{1,0:T(8,128)S(1)}, u32[]{:S(2)}, u32[]{:S(2)}) collective-permute-start(f32[64,640]{1,0:T(8,128)S(1)} %get-tuple-element.123), channel_id=1, source_target_pairs={{0,5},{1,4},{2,7},{3,6},{4,1},{5,0},{6,3},{7,2},{8,13},{9,12},{10,... | collective-permute-start | bytes 491528 | tf_op jit(solution)/shard_map/ppermute | solution.py:470
  41.7 9.9 %collective-permute-start.12 = (f32[64,640]{1,0:T(8,128)S(1)}, f32[64,640]{1,0:T(8,128)S(1)}, u32[]{:S(2)}, u32[]{:S(2)}) collective-permute-start(f32[64,640]{1,0:T(8,128)S(1)} %get-tuple-element.124), channel_id=1, source_target_pairs={{0,6},{1,7},{2,4},{3,5},{4,2},{5,3},{6,0},{7,1},{8,14},{9,15},{10,... | collective-permute-start | bytes 491528 | tf_op jit(solution)/shard_map/ppermute | solution.py:470
  42.9 10.7 %collective-permute-start.13 = (f32[64,640]{1,0:T(8,128)S(1)}, f32[64,640]{1,0:T(8,128)S(1)}, u32[]{:S(2)}, u32[]{:S(2)}) collective-permute-start(f32[64,640]{1,0:T(8,128)S(1)} %get-tuple-element.125), channel_id=1, source_target_pairs={{0,7},{1,6},{2,5},{3,4},{4,3},{5,2},{6,1},{7,0},{8,15},{9,14},{10,... | collective-permute-start | bytes 491528 | tf_op jit(solution)/shard_map/ppermute | solution.py:470
  53.9 13.8 %collective-permute-start.14 = (f32[72,640]{1,0:T(8,128)S(1)}, f32[72,640]{1,0:T(8,128)S(1)}, u32[]{:S(2)}, u32[]{:S(2)}) collective-permute-start(f32[72,640]{1,0:T(8,128)S(1)} %back_group.1.refs_8_.refs_9_), channel_id=1, source_target_pairs={{0,8},{1,9},{2,10},{3,11},{4,12},{5,13},{6,14},{7,15},{8,0},{9,1},... | collective-permute-start | bytes 552968 | tf_op jit(solution)/shard_map/ppermute | solution.py:470
  71.2 13.1 %collective-permute-start.16 = (f32[64,640]{1,0:T(8,128)S(1)}, f32[64,640]{1,0:T(8,128)S(1)}, u32[]{:S(2)}, u32[]{:S(2)}) collective-permute-start(f32[64,640]{1,0:T(8,128)S(1)} %get-tuple-element.131), channel_id=1, source_target_pairs={{0,2},{1,3},{2,0},{3,1},{4,6},{5,7},{6,4},{7,5},{8,10},{9,11},{10,... | collective-permute-start | bytes 491528 | tf_op jit(solution)/shard_map/ppermute | solution.py:470
  71.6 12.8 %collective-permute-start.17 = (f32[64,640]{1,0:T(8,128)S(1)}, f32[64,640]{1,0:T(8,128)S(1)}, u32[]{:S(2)}, u32[]{:S(2)}) collective-permute-start(f32[64,640]{1,0:T(8,128)S(1)} %get-tuple-element.132), channel_id=1, source_target_pairs={{0,3},{1,2},{2,1},{3,0},{4,7},{5,6},{6,5},{7,4},{8,11},{9,10},{10,... | collective-permute-start | bytes 491528 | tf_op jit(solution)/shard_map/ppermute | solution.py:470
  72.7 11.7 %collective-permute-start.18 = (f32[64,640]{1,0:T(8,128)S(1)}, f32[64,640]{1,0:T(8,128)S(1)}, u32[]{:S(2)}, u32[]{:S(2)}) collective-permute-start(f32[64,640]{1,0:T(8,128)S(1)} %get-tuple-element.133), channel_id=1, source_target_pairs={{0,4},{1,5},{2,6},{3,7},{4,0},{5,1},{6,2},{7,3},{8,12},{9,13},{10,... | collective-permute-start | bytes 491528 | tf_op jit(solution)/shard_map/ppermute | solution.py:470
  73.6 13.1 %collective-permute-start.19 = (f32[64,640]{1,0:T(8,128)S(1)}, f32[64,640]{1,0:T(8,128)S(1)}, u32[]{:S(2)}, u32[]{:S(2)}) collective-permute-start(f32[64,640]{1,0:T(8,128)S(1)} %get-tuple-element.134), channel_id=1, source_target_pairs={{0,5},{1,4},{2,7},{3,6},{4,1},{5,0},{6,3},{7,2},{8,13},{9,12},{10,... | collective-permute-start | bytes 491528 | tf_op jit(solution)/shard_map/ppermute | solution.py:470
  76.2 11.7 %collective-permute-start.20 = (f32[64,640]{1,0:T(8,128)S(1)}, f32[64,640]{1,0:T(8,128)S(1)}, u32[]{:S(2)}, u32[]{:S(2)}) collective-permute-start(f32[64,640]{1,0:T(8,128)S(1)} %get-tuple-element.135), channel_id=1, source_target_pairs={{0,6},{1,7},{2,4},{3,5},{4,2},{5,3},{6,0},{7,1},{8,14},{9,15},{10,... | collective-permute-start | bytes 491528 | tf_op jit(solution)/shard_map/ppermute | solution.py:470
  84.3 9.3 %collective-permute-start.21 = (f32[64,640]{1,0:T(8,128)S(1)}, f32[64,640]{1,0:T(8,128)S(1)}, u32[]{:S(2)}, u32[]{:S(2)}) collective-permute-start(f32[64,640]{1,0:T(8,128)S(1)} %get-tuple-element.136), channel_id=1, source_target_pairs={{0,7},{1,6},{2,5},{3,4},{4,3},{5,2},{6,1},{7,0},{8,15},{9,14},{10,... | collective-permute-start | bytes 491528 | tf_op jit(solution)/shard_map/ppermute | solution.py:470
  84.3 12.4 %collective-permute-start.22 = (f32[64,640]{1,0:T(8,128)S(1)}, f32[64,640]{1,0:T(8,128)S(1)}, u32[]{:S(2)}, u32[]{:S(2)}) collective-permute-start(f32[64,640]{1,0:T(8,128)S(1)} %get-tuple-element.137), channel_id=1, source_target_pairs={{0,2},{1,3},{2,0},{3,1},{4,6},{5,7},{6,4},{7,5},{8,10},{9,11},{10,... | collective-permute-start | bytes 491528 | tf_op jit(solution)/shard_map/ppermute | solution.py:470
  84.4 12.3 %collective-permute-start.23 = (f32[64,640]{1,0:T(8,128)S(1)}, f32[64,640]{1,0:T(8,128)S(1)}, u32[]{:S(2)}, u32[]{:S(2)}) collective-permute-start(f32[64,640]{1,0:T(8,128)S(1)} %get-tuple-element.144), channel_id=1, source_target_pairs={{0,1},{1,0},{2,3},{3,2},{4,5},{5,4},{6,7},{7,6},{8,9},{9,8},{10,11... | collective-permute-start | bytes 491528 | tf_op jit(solution)/shard_map/ppermute | solution.py:470
  86.7 17.7 %collective-permute-start.24 = (f32[64,640]{1,0:T(8,128)S(1)}, f32[64,640]{1,0:T(8,128)S(1)}, u32[]{:S(2)}, u32[]{:S(2)}) collective-permute-start(f32[64,640]{1,0:T(8,128)S(1)} %get-tuple-element.145), channel_id=1, source_target_pairs={{0,3},{1,2},{2,1},{3,0},{4,7},{5,6},{6,5},{7,4},{8,11},{9,10},{10,... | collective-permute-start | bytes 491528 | tf_op jit(solution)/shard_map/ppermute | solution.py:470
  87.9 16.5 %collective-permute-start.25 = (f32[64,640]{1,0:T(8,128)S(1)}, f32[64,640]{1,0:T(8,128)S(1)}, u32[]{:S(2)}, u32[]{:S(2)}) collective-permute-start(f32[64,640]{1,0:T(8,128)S(1)} %get-tuple-element.146), channel_id=1, source_target_pairs={{0,4},{1,5},{2,6},{3,7},{4,0},{5,1},{6,2},{7,3},{8,12},{9,13},{10,... | collective-permute-start | bytes 491528 | tf_op jit(solution)/shard_map/ppermute | solution.py:470
  93.6 10.8 %collective-permute-start.26 = (f32[64,640]{1,0:T(8,128)S(1)}, f32[64,640]{1,0:T(8,128)S(1)}, u32[]{:S(2)}, u32[]{:S(2)}) collective-permute-start(f32[64,640]{1,0:T(8,128)S(1)} %get-tuple-element.147), channel_id=1, source_target_pairs={{0,5},{1,4},{2,7},{3,6},{4,1},{5,0},{6,3},{7,2},{8,13},{9,12},{10,... | collective-permute-start | bytes 491528 | tf_op jit(solution)/shard_map/ppermute | solution.py:470
  111.0 9.7 %all-to-all-start = ((f32[32,1,128]{2,1,0:T(1,128)}), f32[32,1,128]{2,1,0:T(1,128)S(1)}, u32[]{:S(2)}, u32[]{:S(2)}) async-start(f32[32,1,128]{2,1,0:T(1,128)} %get-tuple-element.159), calls=%async_computation | async-start | bytes 32768 | tf_op jit(solution)/shard_map/all_to_all | solution.py:641
  (54 other events, 596.6 us)

commit v9 on v8

--- a/solution.py
+++ b/solution.py
@@ -13,7 +13,7 @@
 QUARTERS = 4
 HALVES = 2
 GROUP = QUARTERS * HALVES
-DISTANCES = (1, 2, 3, 4, 5, 6, 7)
+DISTANCES = (7, 1, 6, 2, 5, 3, 4)
 LANES = 128
 LOG2E = 1.4426950408889634
 FAR = -1e30
@@ -98,8 +98,8 @@
 
 
 def states_kernel(starts, logits, bias, decay, spread_ref, features, writes, cotangent, reads, *refs):
-    sends, back_sends = refs[:GROUP], refs[GROUP : 2 * GROUP]
-    cols_out, rows_out, scratch = refs[2 * GROUP :]
+    sends = refs[:GROUP]
+    cols_out, rows_out, scratch = refs[GROUP:]
     heads, length = logits.shape
     state = writes.shape[1]
     width = features.shape[1] // QUARTERS
@@ -137,9 +137,9 @@
         high, low = split2(cotangent[:, cols].astype(F32) * wide)
         return matmul(read_t, high) + matmul(read_t, low)
 
-    share_out(own, back_quarter, back_sends, scratch)
+    share_out(own, back_quarter, [send.at[part + 8 :] for send in sends], scratch)
     for distance, send in enumerate(sends):
-        send[part:] = keeps[distance % QUARTERS]
+        send[part : part + 8] = keeps[distance % QUARTERS]
     cols_out[CUM] = stacked_columns(cum * LOG2E)
     cols_out[WEIGHT] = weight_stack
     cols_out[FACTOR] = factor_stack
@@ -149,14 +149,11 @@
 
 
 def inner_kernel(
-    offset, last, starts, cols_ref, rows_ref, features, cotangent, writes, reads, spread_ref, *refs
+    starts, cols_ref, rows_ref, features, cotangent, writes, reads, spread_ref, *refs
 ):
-    if offset:
-        before, refs = refs[0], refs[1 + WIDE_PARTS + AFTER :]
-    else:
-        refs = refs[AFTER:]
+    refs = refs[AFTER:]
     inside, feature_part, skip_part, write_high, write_low, read_high, read_low = refs[:WIDE_PARTS]
-    results = refs[WIDE_PARTS:-3]
+    write_part, read_part = refs[WIDE_PARTS:-3]
     scores_ref, mask_ref, grad_ref = refs[-3:]
     length, width = features.shape
     heads = rows_ref.shape[1]
@@ -173,7 +170,7 @@
         causal = iota((length, length), 0) >= iota((length, length), 1)
         mask_ref[...] = jnp.where((segment_row == segment_col) & causal, 0.0, FAR)
         scores_ref[...] = matmul_nt(reads[...], writes[...])
-        grad_ref[...] = before[...] if offset else jnp.zeros_like(grad_ref)
+        grad_ref[...] = jnp.zeros_like(grad_ref)
 
     write_high[...], write_low[...] = split2(matmul(cols_ref[WEIGHT], spread_ref[...]) * features[...].astype(F32))
     read_high[...], read_low[...] = split2(matmul(cols_ref[FACTOR], spread_ref[...]) * cotangent[...].astype(F32))
@@ -185,7 +182,7 @@
         grad_f32 = grad.astype(F32)
         grad_t = grad_f32.T.astype(BF16)
         skip_part[:, cols] = jnp.sum(grad_f32 * feature.astype(F32), axis=0, keepdims=True)
-        head = (offset + step) * here + at * 2
+        head = step * here + at * 2
         lane = iota((LANES, 2 * LANES), 0)
         wanted = head + lax.div(iota((LANES, 2 * LANES), 1), LANES)
         pick = (lane == wanted) | (lane == wanted + heads) | (lane == wanted + 2 * heads)
@@ -215,33 +212,27 @@
 
     lax.fori_loop(0, here // 2, one_pair, 0)
 
-    @pl.when(step == pl.num_programs(0) - 1)
+    @pl.when(step == QUARTERS - 1)
     def _():
         score_grad = grad_ref[...]
-        if last:
-            write_part, read_part = results
-            high, low = split2(score_grad)
-            read_part[...] = matmul(high, writes[...]) + matmul(low, writes[...])
-            high, low = split2(score_grad.T)
-            write_part[...] = matmul(high, reads[...]) + matmul(low, reads[...])
-        else:
-            results[0][...] = score_grad
-
-
-def in_order(refs, scratch):
+        high, low = split2(score_grad)
+        read_part[...] = matmul(high, writes[...]) + matmul(low, writes[...])
+        high, low = split2(score_grad.T)
+        write_part[...] = matmul(high, reads[...]) + matmul(low, reads[...])
+
+
+def in_order(refs, scratch, back=False):
     own = group_place()
+    rows = scratch.shape[1]
     for distance, ref in enumerate(refs):
-        scratch[own ^ distance] = ref[...]
-
-
-def hold_kernel(*refs):
-    count = len(refs) // 2
-    for value, out in zip(refs[:count], refs[count + 1 :]):
-        out[...] = value[...]
+        first = ref.shape[0] - rows if back else 0
+        scratch[own ^ distance] = ref[first : first + rows]
 
 
 def group_kernel(part, *refs):
-    up, keeps, came = refs[-3:]
+    keeps, came, back_came = refs[-3:]
+    sums = refs[GROUP + 1 : -3]
+    up, down = sums[0], sums[-1]
     in_order(refs[:GROUP], came)
     total = came[0, 0:part]
     keep = came[0, part:]
@@ -252,22 +243,16 @@
     up[part:] = keep
     for j in range(GROUP):
         keeps[j : j + 1] = came[j, part : part + 1]
-
-
-def back_group_kernel(part, two, *refs):
-    up, keeps = refs[GROUP : GROUP + 2]
-    out, came = refs[-2:]
-    in_order(refs[:GROUP], came)
-    out[part:] = up[part:]
+    in_order(refs[:GROUP], back_came, back=True)
 
     def downward():
-        total = came[GROUP - 1]
+        total = back_came[GROUP - 1]
         for j in reversed(range(GROUP - 1)):
-            total = total * keeps[j : j + 1] + came[j]
-        out[0:part] = total
-
-    if two:
-        out[0:part] = up[0:part]
+            total = total * keeps[j : j + 1] + back_came[j]
+        down[0:part] = total
+        down[part:] = keep
+
+    if len(sums) == 1:
         pl.when(lax.axis_index("ctx") >= GROUP)(downward)
     else:
         downward()
@@ -288,7 +273,7 @@
 
 
 def spread_kernel(part, count, back_count, *refs):
-    first = 2 * GROUP
+    first = GROUP
     ups, downs = refs[first : first + count], refs[first + count : first + count + back_count]
     keeps = refs[first + count + back_count]
     outs = refs[first + count + back_count + 2 : -4]
@@ -305,7 +290,7 @@
         give[j] = total
         if j < GROUP - 1:
             total = total * keeps[j : j + 1] + came[j, 0:part]
-    in_order(refs[GROUP : 2 * GROUP], back_came)
+    in_order(refs[:GROUP], back_came, back=True)
     total = returning
     for j in reversed(range(GROUP)):
         back_give[j] = total
@@ -512,90 +497,55 @@
     out = call(
         states_kernel,
         "states",
-        [group_sum] * GROUP + [share] * GROUP + [struct((3, length, LANES), BF16), struct((3, heads, length))],
+        [struct((2 * part + 8, width))] * GROUP + [struct((3, length, LANES), BF16), struct((3, heads, length))],
         [SMEM] + [VMEM] * 8,
         4,
         60,
         scratch_shapes=[pltpu.VMEM((state, width), F32)],
     )(doc_starts, logits, bias, decay, spread, features, writes, cotangent, reads)
     came = swap(out[:GROUP])
-    back_sends = out[GROUP : 2 * GROUP]
-    cols, head_rows = out[2 * GROUP :]
+    cols, head_rows = out[GROUP:]
 
     wide_part, wide_piece = struct((length, wide)), struct((length, wide), BF16)
     wide_parts = [wide_part] * 2 + [struct((1, wide))] + [wide_piece] * 4
-    inner_args = (
-        doc_starts, cols, head_rows, features, cotangent, writes, reads, spread
+    token_part = struct((length, state))
+    inside, feature_part, skip_part, *pieces, write_part, read_part = call(
+        inner_kernel,
+        "inner",
+        wide_parts + [token_part] * 2,
+        [SMEM, all_cols, all_rows, by_quarter, by_quarter, tokens, tokens, spread_quarter] + [ANY] * AFTER,
+        10,
+        24,
+        grid=(QUARTERS,),
+        out_specs=[by_quarter, by_quarter, quarter_of(1)] + [by_quarter] * 4 + [tokens] * 2,
+        scratch_shapes=[pltpu.VMEM((length, length), F32)] * 3,
+    )(
+        doc_starts, cols, head_rows, features, cotangent, writes, reads, spread,
+        *[came[d] for d in DISTANCES[1 : 1 + AFTER]],
     )
-
-    square = all_of(length, length)
-    token_part = struct((length, state))
-
-    def inner(offset, count, begun, after):
-        mine = quarter_of(length, offset)
-        last = offset + count == QUARTERS
-        n_args = len(inner_args) + 1
-        return call(
-            functools.partial(inner_kernel, offset, last),
-            "inner_" + str(offset),
-            wide_parts + ([token_part] * 2 if last else [struct((length, length))]),
-            [SMEM, all_cols, all_rows, mine, mine, tokens, tokens, quarter_of(LANES, offset)]
-            + ([square] + [ANY] * WIDE_PARTS if offset else [])
-            + [ANY] * AFTER,
-            5 * count,
-            24,
-            grid=(count,),
-            out_specs=[mine, mine, quarter_of(1, offset)] + [mine] * 4 + ([tokens] * 2 if last else [square]),
-            scratch_shapes=[pltpu.VMEM((length, length), F32)] * 3,
-            input_output_aliases={n_args + at: at for at in range(WIDE_PARTS)} if offset else {},
-        )(*inner_args, *begun, *after)
-
-    def hold(values, distances, until):
-        chosen = [values[d] for d in distances]
-        count = len(chosen)
-        held = call(hold_kernel, "hold", [share] * count, [VMEM] * count + [ANY], 1, 12)(*chosen, until)
-        return dict(zip(distances, held))
-
-    *begun, score_grad = inner(0, 1, [], [came[1], came[2]])
-    early = hold(back_sends, (1, 2, 3), score_grad)
-    back_came = [back_sends[0]] + [exchange(early[d], d) for d in (1, 2, 3)]
-    up, keeps = call(
+    two = blocks == 2 * GROUP
+    *group_sums, keeps = call(
         functools.partial(group_kernel, part),
         "group",
-        [group_sum, struct((GROUP, width))],
+        [group_sum] * (1 if two else 2) + [struct((GROUP, width))],
         [VMEM] * GROUP + [ANY],
         2,
         12,
-        scratch_shapes=[long_shares],
-    )(*came, score_grad)
-    *begun, score_grad = inner(1, 1, [score_grad, *begun], [up, back_came[1]])
-    late = hold(back_sends, (4, 5, 6, 7), score_grad)
-    back_came += [exchange(late[d], d) for d in (4, 5, 6, 7)]
-    two = blocks == 2 * GROUP
-    (cross,) = call(
-        functools.partial(back_group_kernel, part, two),
-        "back_group",
-        [group_sum],
-        [VMEM] * (GROUP + 2) + [ANY],
-        2,
-        12,
-        scratch_shapes=[shares],
-    )(*back_came, up, keeps, score_grad)
+        scratch_shapes=[long_shares, shares],
+    )(*came, write_part)
     if two:
-        ups, downs = [exchange(cross, GROUP)], []
+        ups, downs = [exchange(group_sums[0], GROUP)], []
     else:
-        ups, downs = scan(up, 1), scan(cross, -1)
-    *done, write_part, read_part = inner(2, QUARTERS - 2, [score_grad, *begun], [cross] * AFTER)
-    inside, feature_part, skip_part, *pieces = done
+        ups, downs = scan(group_sums[0], 1), scan(group_sums[1], -1)
     give = call(
         functools.partial(spread_kernel, part, len(ups), len(downs)),
         "spread",
         [share] * 2 * GROUP,
-        [VMEM] * (2 * GROUP + len(ups) + len(downs) + 1) + [ANY],
+        [VMEM] * (GROUP + len(ups) + len(downs) + 1) + [ANY],
         2,
         16,
         scratch_shapes=[long_shares, shares, shares, shares],
-    )(*came, *back_came, *ups, *downs, keeps, write_part)
+    )(*came, *ups, *downs, keeps, write_part)
     have, back_have = swap(give[:GROUP]), swap(give[GROUP:])
     devices = blocks * members
     whole_shares = [all_of(part, width)] * GROUP

time: 122 us -> 110 us (0.902)
  waiting for transfers between devices: 28.9 us -> 21.1 us
  local copies, waits for them, and re-layouts: 6.23 us -> 3.55 us
    ppermute x29 -> x22, waiting for transfers between devices: 28.3 us -> 20.5 us  [exchange(): lax.ppermute(value, 'ctx', [(k, k ^ distance) for k in range(blocks)])]
    all_to_all x1, starting transfers between devices: 2.56 us -> 6.64 us  [local(): sums = jnp.sum(lax.all_to_all(sums, ('dp', 'ctx'), 0, 0), axis=(0, 1))]
    ppermute x29 -> x22, starting transfers between devices: 42.2 us -> 38.3 us  [exchange(): lax.ppermute(value, 'ctx', [(k, k ^ distance) for k in range(blocks)])]
    unnamed x96 -> x80, local copies, waits for them, and re-layouts: 5.63 us -> 2.95 us
    pallas_call x8 -> x3, Pallas kernels: 22.6 us -> 21.5 us  [the longest x1 14.7 us: local(): call(inner_kernel, 'inner', wide_parts + [token_part] * 2, [SMEM, all_col...]
  transfers between devices with their start and end apart: 30 -> 23, of which waited for: 12 -> 12; matrix products, arithmetic and copies ran while one was open for 0% -> 0% of each run, Pallas kernels for 22% -> 23%
where the time goes in v9:
time: 110 us
  starting transfers between devices  44.9 us (41%)
  Pallas kernels  39.1 us (36%)
  waiting for transfers between devices  21.1 us (19%)
  local copies, waits for them, and re-layouts  3.55 us (3%)
  between operations  1.1 us (1%)
    ppermute x22, starting transfers between devices, exchange(): lax.ppermute(value, 'ctx', [(k, k ^ distance) for k in range(blocks)])  38.3 us
    ppermute x22, waiting for transfers between devices, exchange(): lax.ppermute(value, 'ctx', [(k, k ^ distance) for k in range(blocks)])  20.5 us
    pallas_call x1, Pallas kernels, local(): call(inner_kernel, 'inner', wide_parts + [token_part] * 2, [SMEM, all_col...  14.7 us
    all_to_all x1, starting transfers between devices, local(): sums = jnp.sum(lax.all_to_all(sums, ('dp', 'ctx'), 0, 0), axis=(0, 1))  6.64 us
    pallas_call x1, Pallas kernels, local(): call(keys_kernel, 'keys', [tokens_result] * 2, [tokens] * 2 + [by_quarter...  6.51 us
    pallas_call x1, Pallas kernels, local(): call(states_kernel, 'states', [struct((2 * part + 8, width))] * GROUP + [...  6.49 us
    pallas_call x1, Pallas kernels, local(): call(back_finish_kernel, 'back_finish', [result, small, struct((devices,...  6.06 us
    pallas_call x1, Pallas kernels, local(): call(finish_kernel, 'finish', [result, struct((length, LANES)), struct((s...  4.44 us
  transfers between devices with their start and end apart: 23, of which 12 were waited for; matrix products, arithmetic and copies ran while one was open for 0% of the time, Pallas kernels for 23%

profile of v9, /device:TPU:0, one launch (start us, length us, event | category | flops | bytes accessed | tf_op | source)
XLA Modules:
  0.0 109.8 jit_solution(10542298893635554172)
XLA Ops:
  0.7 6.5 %states.1 = (f32[136,640]{1,0:T(8,128)}, f32[136,640]{1,0:T(8,128)}, f32[136,640]{1,0:T(8,128)}, f32[136,640]{1,0:T(8,128)}, f32[136,640]{1,0:T(8,128)}, /*index...) custom-call(s32[1,4]{1,0:T(1,128)} %starts.3, ...), custom_call_target="tpu_custom_call" | custom-call | flops 4000000000 | bytes 1000000 | tf_op jit(solution)/shard_map/states/pallas_call | solution.py:497
  7.2 2.9 %collective-permute-start = (f32[136,640]{1,0:T(8,128)}, f32[136,640]{1,0:T(8,128)S(1)}, u32[]{:S(2)}, u32[]{:S(2)}) collective-permute-start(f32[136,640]{1,0:T(8,128)} %get-tuple-element.55), channel_id=1, source_target_pairs={{0,1},{1,0},{2,3},{3,2},{4,5},{5,4},{6,7},{7,6},{8,9},{9,8},{10,11... | collective-permute-start | bytes 1044488 | tf_op jit(solution)/shard_map/ppermute | solution.py:455
  10.1 2.5 %collective-permute-start.1 = (f32[136,640]{1,0:T(8,128)}, f32[136,640]{1,0:T(8,128)S(1)}, u32[]{:S(2)}, u32[]{:S(2)}) collective-permute-start(f32[136,640]{1,0:T(8,128)} %get-tuple-element.56), channel_id=1, source_target_pairs={{0,6},{1,7},{2,4},{3,5},{4,2},{5,3},{6,0},{7,1},{8,14},{9,15},{10,... | collective-permute-start | bytes 1044488 | tf_op jit(solution)/shard_map/ppermute | solution.py:455
  13.2 1.5 %collective-permute-start.3 = (f32[136,640]{1,0:T(8,128)}, f32[136,640]{1,0:T(8,128)S(1)}, u32[]{:S(2)}, u32[]{:S(2)}) collective-permute-start(f32[136,640]{1,0:T(8,128)} %get-tuple-element.60), channel_id=1, source_target_pairs={{0,3},{1,2},{2,1},{3,0},{4,7},{5,6},{6,5},{7,4},{8,11},{9,10},{10,... | collective-permute-start | bytes 1044488 | tf_op jit(solution)/shard_map/ppermute | solution.py:455
  15.1 4.2 %collective-permute-done.refs_0_.refs_1_ = f32[136,640]{1,0:T(8,128)S(1)} collective-permute-done((f32[136,640]{1,0:T(8,128)}, f32[136,640]{1,0:T(8,128)S(1)}, u32[]{:S(2)}, u32[]{:S(2)}) %collective-permute-start) | collective-permute-done | bytes 348192 | tf_op jit(solution)/shard_map/ppermute | solution.py:455
  19.3 3.1 %collective-permute-start.5 = (f32[136,640]{1,0:T(8,128)}, f32[136,640]{1,0:T(8,128)S(1)}, u32[]{:S(2)}, u32[]{:S(2)}) collective-permute-start(f32[136,640]{1,0:T(8,128)} %get-tuple-element.62), channel_id=1, source_target_pairs={{0,5},{1,4},{2,7},{3,6},{4,1},{5,0},{6,3},{7,2},{8,13},{9,12},{10,... | collective-permute-start | bytes 1044488 | tf_op jit(solution)/shard_map/ppermute | solution.py:455
  23.1 2.5 %collective-permute-start.6 = (f32[136,640]{1,0:T(8,128)}, f32[136,640]{1,0:T(8,128)S(1)}, u32[]{:S(2)}, u32[]{:S(2)}) collective-permute-start(f32[136,640]{1,0:T(8,128)} %get-tuple-element.63), channel_id=1, source_target_pairs={{0,7},{1,6},{2,5},{3,4},{4,3},{5,2},{6,1},{7,0},{8,15},{9,14},{10,... | collective-permute-start | bytes 1044488 | tf_op jit(solution)/shard_map/ppermute | solution.py:455
  27.5 14.7 %inner.1 = (f32[256,2560]{1,0:T(8,128)S(1)}, f32[256,2560]{1,0:T(8,128)S(1)}, f32[1,2560]{1,0:T(1,128)S(1)}, bf16[256,2560]{1,0:T(8,128)(2,1)S(1)}, bf16[256,256...) custom-call(s32[1,4]{1,0:T(1,128)S(1)} %copy-done.21, ...), custom_call_target="tpu_custom_call" | custom-call | flops 10000000000 | bytes 1000000 | tf_op jit(solution)/shard_map/inner/pallas_call | solution.py:512
  44.6 2.6 %collective-permute-start.7 = (f32[72,640]{1,0:T(8,128)S(1)}, f32[72,640]{1,0:T(8,128)S(1)}, u32[]{:S(2)}, u32[]{:S(2)}) collective-permute-start(f32[72,640]{1,0:T(8,128)S(1)} %get-tuple-element.65), channel_id=1, source_target_pairs={{0,8},{1,9},{2,10},{3,11},{4,12},{5,13},{6,14},{7,15},{8,0},{9,1},... | collective-permute-start | bytes 552968 | tf_op jit(solution)/shard_map/ppermute | solution.py:455
  47.2 6.8 %collective-permute-done.7.refs_8_ = f32[72,640]{1,0:T(8,128)S(1)} collective-permute-done((f32[72,640]{1,0:T(8,128)S(1)}, f32[72,640]{1,0:T(8,128)S(1)}, u32[]{:S(2)}, u32[]{:S(2)}) %collective-permute-start.7) | collective-permute-done | bytes 184352 | tf_op jit(solution)/shard_map/ppermute | solution.py:455
  56.0 2.0 %collective-permute-start.9 = (f32[64,640]{1,0:T(8,128)S(1)}, f32[64,640]{1,0:T(8,128)S(1)}, u32[]{:S(2)}, u32[]{:S(2)}) collective-permute-start(f32[64,640]{1,0:T(8,128)S(1)} %get-tuple-element.69), channel_id=1, source_target_pairs={{0,2},{1,3},{2,0},{3,1},{4,6},{5,7},{6,4},{7,5},{8,10},{9,11},{10,... | collective-permute-start | bytes 491528 | tf_op jit(solution)/shard_map/ppermute | solution.py:455
  58.7 2.3 %collective-permute-start.12 = (f32[64,640]{1,0:T(8,128)S(1)}, f32[64,640]{1,0:T(8,128)S(1)}, u32[]{:S(2)}, u32[]{:S(2)}) collective-permute-start(f32[64,640]{1,0:T(8,128)S(1)} %get-tuple-element.72), channel_id=1, source_target_pairs={{0,5},{1,4},{2,7},{3,6},{4,1},{5,0},{6,3},{7,2},{8,13},{9,12},{10,... | collective-permute-start | bytes 491528 | tf_op jit(solution)/shard_map/ppermute | solution.py:455
  61.5 1.5 %collective-permute-start.13 = (f32[64,640]{1,0:T(8,128)S(1)}, f32[64,640]{1,0:T(8,128)S(1)}, u32[]{:S(2)}, u32[]{:S(2)}) collective-permute-start(f32[64,640]{1,0:T(8,128)S(1)} %get-tuple-element.73), channel_id=1, source_target_pairs={{0,6},{1,7},{2,4},{3,5},{4,2},{5,3},{6,0},{7,1},{8,14},{9,15},{10,... | collective-permute-start | bytes 491528 | tf_op jit(solution)/shard_map/ppermute | solution.py:455
  63.3 2.9 %collective-permute-start.14 = (f32[64,640]{1,0:T(8,128)S(1)}, f32[64,640]{1,0:T(8,128)S(1)}, u32[]{:S(2)}, u32[]{:S(2)}) collective-permute-start(f32[64,640]{1,0:T(8,128)S(1)} %get-tuple-element.74), channel_id=1, source_target_pairs={{0,7},{1,6},{2,5},{3,4},{4,3},{5,2},{6,1},{7,0},{8,15},{9,14},{10,... | collective-permute-start | bytes 491528 | tf_op jit(solution)/shard_map/ppermute | solution.py:455
  66.4 3.0 %collective-permute-start.15 = (f32[64,640]{1,0:T(8,128)S(1)}, f32[64,640]{1,0:T(8,128)S(1)}, u32[]{:S(2)}, u32[]{:S(2)}) collective-permute-start(f32[64,640]{1,0:T(8,128)S(1)} %get-tuple-element.75), channel_id=1, source_target_pairs={{0,1},{1,0},{2,3},{3,2},{4,5},{5,4},{6,7},{7,6},{8,9},{9,8},{10,11... | collective-permute-start | bytes 491528 | tf_op jit(solution)/shard_map/ppermute | solution.py:455
  69.7 1.4 %collective-permute-start.17 = (f32[64,640]{1,0:T(8,128)S(1)}, f32[64,640]{1,0:T(8,128)S(1)}, u32[]{:S(2)}, u32[]{:S(2)}) collective-permute-start(f32[64,640]{1,0:T(8,128)S(1)} %get-tuple-element.83), channel_id=1, source_target_pairs={{0,3},{1,2},{2,1},{3,0},{4,7},{5,6},{6,5},{7,4},{8,11},{9,10},{10,... | collective-permute-start | bytes 491528 | tf_op jit(solution)/shard_map/ppermute | solution.py:455
  71.1 1.9 %collective-permute-done.13.refs_6_ = f32[64,640]{1,0:T(8,128)S(1)} collective-permute-done((f32[64,640]{1,0:T(8,128)S(1)}, f32[64,640]{1,0:T(8,128)S(1)}, u32[]{:S(2)}, u32[]{:S(2)}) %collective-permute-start.13) | collective-permute-done | bytes 163872 | tf_op jit(solution)/shard_map/ppermute | solution.py:455
  73.0 1.5 %collective-permute-start.18 = (f32[64,640]{1,0:T(8,128)S(1)}, f32[64,640]{1,0:T(8,128)S(1)}, u32[]{:S(2)}, u32[]{:S(2)}) collective-permute-start(f32[64,640]{1,0:T(8,128)S(1)} %get-tuple-element.84), channel_id=1, source_target_pairs={{0,4},{1,5},{2,6},{3,7},{4,0},{5,1},{6,2},{7,3},{8,12},{9,13},{10,... | collective-permute-start | bytes 491528 | tf_op jit(solution)/shard_map/ppermute | solution.py:455
  74.5 3.6 %collective-permute-done.14.refs_7_ = f32[64,640]{1,0:T(8,128)S(1)} collective-permute-done((f32[64,640]{1,0:T(8,128)S(1)}, f32[64,640]{1,0:T(8,128)S(1)}, u32[]{:S(2)}, u32[]{:S(2)}) %collective-permute-start.14) | collective-permute-done | bytes 163872 | tf_op jit(solution)/shard_map/ppermute | solution.py:455
  79.2 4.5 %collective-permute-start.21 = (f32[64,640]{1,0:T(8,128)S(1)}, f32[64,640]{1,0:T(8,128)S(1)}, u32[]{:S(2)}, u32[]{:S(2)}) collective-permute-start(f32[64,640]{1,0:T(8,128)S(1)} %get-tuple-element.87), channel_id=1, source_target_pairs={{0,7},{1,6},{2,5},{3,4},{4,3},{5,2},{6,1},{7,0},{8,15},{9,14},{10,... | collective-permute-start | bytes 491528 | tf_op jit(solution)/shard_map/ppermute | solution.py:455
  83.8 4.4 %finish.1 = (bf16[256,2560]{1,0:T(8,128)(2,1)}, f32[256,128]{1,0:T(8,128)S(1)}, f32[128,2560]{1,0:T(8,128)S(1)}) custom-call(f32[1,40]{1,0:T(1,128)S(1)} %bitcast.29, bf16[3,256,128]{2,1,0:T(8,128)(2,1)S(1)} %copy-done.36, bf16[128,2560]{1,0:T(8,128)(2,1)S(1)} %copy-done.26, bf16[256,2560]{1,0:T(8,128)(2,1)S(1)} %bitcast.15, bf16[256,2560]{1,0:T(8,128)(2,1)S(1)} %bitcast.19, ...), custom_call_target="tpu_custom_call" | custom-call | flops 8000000000 | bytes 1000000 | tf_op jit(solution)/shard_map/finish/pallas_call | solution.py:552
  89.3 6.1 %back_finish.1 = (bf16[256,2560]{1,0:T(8,128)(2,1)}, f32[40,256]{1,0:T(8,128)}, f32[32,1,128]{2,1,0:T(1,128)}) custom-call(f32[40,256]{1,0:T(8,128)S(1)} %bitcast.28, f32[1,40]{1,0:T(1,128)S(1)} %bitcast.32, f32[1,40]{1,0:T(1,128)S(1)} %bitcast.34, f32[1,40]{1,0:T(1,128)S(1)} %bitcast.30, bf16[3,256,128]{2,1,0:T(8,128)(2,1)S(1)} %copy-done.36, ...), custom_call_target="tpu_custom_call" | custom-call | flops 8000000000 | bytes 1000000 | tf_op jit(solution)/shard_map/back_finish/pallas_call | solution.py:563
  95.4 6.6 %all-to-all-start = ((f32[32,1,128]{2,1,0:T(1,128)}), f32[32,1,128]{2,1,0:T(1,128)S(1)}, u32[]{:S(2)}, u32[]{:S(2)}) async-start(f32[32,1,128]{2,1,0:T(1,128)} %get-tuple-element.97), calls=%async_computation | async-start | bytes 32768 | tf_op jit(solution)/shard_map/all_to_all | solution.py:591
  102.0 6.5 %keys.1 = (bf16[256,128]{1,0:T(8,128)(2,1)}, bf16[256,128]{1,0:T(8,128)(2,1)}) custom-call(f32[256,128]{1,0:T(8,128)} %copy-done.30, f32[256,128]{1,0:T(8,128)} %copy-done.39, bf16[256,2560]{1,0:T(8,128)(2,1)} %copy-done.31, bf16[256,2560]{1,0:T(8,128)(2,1)} %copy-done.32, bf16[256,2560]{1,0:T(8,128)(2,1)} %copy-done.33, bf16[256,2560]{1,0:T(8,128)(2,1)} %copy-done.34, ...), custom_call_target="tpu_custom_call" | custom-call | flops 6000000000 | bytes 1000000 | tf_op jit(solution)/shard_map/keys/pallas_call | solution.py:580
  (111 shorter events, 13.2 us)
Async XLA Ops:
  7.2 12.1 %collective-permute-start = (f32[136,640]{1,0:T(8,128)}, f32[136,640]{1,0:T(8,128)S(1)}, u32[]{:S(2)}, u32[]{:S(2)}) collective-permute-start(f32[136,640]{1,0:T(8,128)} %get-tuple-element.55), channel_id=1, source_target_pairs={{0,1},{1,0},{2,3},{3,2},{4,5},{5,4},{6,7},{7,6},{8,9},{9,8},{10,11... | collective-permute-start | bytes 1044488 | tf_op jit(solution)/shard_map/ppermute | solution.py:455
  10.1 13.0 %collective-permute-start.1 = (f32[136,640]{1,0:T(8,128)}, f32[136,640]{1,0:T(8,128)S(1)}, u32[]{:S(2)}, u32[]{:S(2)}) collective-permute-start(f32[136,640]{1,0:T(8,128)} %get-tuple-element.56), channel_id=1, source_target_pairs={{0,6},{1,7},{2,4},{3,5},{4,2},{5,3},{6,0},{7,1},{8,14},{9,15},{10,... | collective-permute-start | bytes 1044488 | tf_op jit(solution)/shard_map/ppermute | solution.py:455
  12.7 29.6 %collective-permute-start.2 = (f32[136,640]{1,0:T(8,128)}, f32[136,640]{1,0:T(8,128)S(1)}, u32[]{:S(2)}, u32[]{:S(2)}) collective-permute-start(f32[136,640]{1,0:T(8,128)} %get-tuple-element.59), channel_id=1, source_target_pairs={{0,2},{1,3},{2,0},{3,1},{4,6},{5,7},{6,4},{7,5},{8,10},{9,11},{10,... | collective-permute-start | bytes 1044488 | tf_op jit(solution)/shard_map/ppermute | solution.py:455
  13.2 30.1 %collective-permute-start.3 = (f32[136,640]{1,0:T(8,128)}, f32[136,640]{1,0:T(8,128)S(1)}, u32[]{:S(2)}, u32[]{:S(2)}) collective-permute-start(f32[136,640]{1,0:T(8,128)} %get-tuple-element.60), channel_id=1, source_target_pairs={{0,3},{1,2},{2,1},{3,0},{4,7},{5,6},{6,5},{7,4},{8,11},{9,10},{10,... | collective-permute-start | bytes 1044488 | tf_op jit(solution)/shard_map/ppermute | solution.py:455
  14.7 28.6 %collective-permute-start.4 = (f32[136,640]{1,0:T(8,128)}, f32[136,640]{1,0:T(8,128)S(1)}, u32[]{:S(2)}, u32[]{:S(2)}) collective-permute-start(f32[136,640]{1,0:T(8,128)} %get-tuple-element.61), channel_id=1, source_target_pairs={{0,4},{1,5},{2,6},{3,7},{4,0},{5,1},{6,2},{7,3},{8,12},{9,13},{10,... | collective-permute-start | bytes 1044488 | tf_op jit(solution)/shard_map/ppermute | solution.py:455
  19.3 24.0 %collective-permute-start.5 = (f32[136,640]{1,0:T(8,128)}, f32[136,640]{1,0:T(8,128)S(1)}, u32[]{:S(2)}, u32[]{:S(2)}) collective-permute-start(f32[136,640]{1,0:T(8,128)} %get-tuple-element.62), channel_id=1, source_target_pairs={{0,5},{1,4},{2,7},{3,6},{4,1},{5,0},{6,3},{7,2},{8,13},{9,12},{10,... | collective-permute-start | bytes 1044488 | tf_op jit(solution)/shard_map/ppermute | solution.py:455
  23.1 20.2 %collective-permute-start.6 = (f32[136,640]{1,0:T(8,128)}, f32[136,640]{1,0:T(8,128)S(1)}, u32[]{:S(2)}, u32[]{:S(2)}) collective-permute-start(f32[136,640]{1,0:T(8,128)} %get-tuple-element.63), channel_id=1, source_target_pairs={{0,7},{1,6},{2,5},{3,4},{4,3},{5,2},{6,1},{7,0},{8,15},{9,14},{10,... | collective-permute-start | bytes 1044488 | tf_op jit(solution)/shard_map/ppermute | solution.py:455
  44.6 9.4 %collective-permute-start.7 = (f32[72,640]{1,0:T(8,128)S(1)}, f32[72,640]{1,0:T(8,128)S(1)}, u32[]{:S(2)}, u32[]{:S(2)}) collective-permute-start(f32[72,640]{1,0:T(8,128)S(1)} %get-tuple-element.65), channel_id=1, source_target_pairs={{0,8},{1,9},{2,10},{3,11},{4,12},{5,13},{6,14},{7,15},{8,0},{9,1},... | collective-permute-start | bytes 552968 | tf_op jit(solution)/shard_map/ppermute | solution.py:455
  54.6 34.6 %copy-start.29 = (f32[64,640]{1,0:T(8,128)}, f32[64,640]{1,0:T(8,128)S(1)}, u32[]{:S(2)}) copy-start(f32[64,640]{1,0:T(8,128)S(1)} %get-tuple-element.81.refs_0_.refs_8_) | copy-start | bytes 491524
  54.6 6.9 %collective-permute-start.8 = (f32[64,640]{1,0:T(8,128)S(1)}, f32[64,640]{1,0:T(8,128)S(1)}, u32[]{:S(2)}, u32[]{:S(2)}) collective-permute-start(f32[64,640]{1,0:T(8,128)S(1)} %get-tuple-element.68), channel_id=1, source_target_pairs={{0,1},{1,0},{2,3},{3,2},{4,5},{5,4},{6,7},{7,6},{8,9},{9,8},{10,11... | collective-permute-start | bytes 491528 | tf_op jit(solution)/shard_map/ppermute | solution.py:455
  56.0 7.3 %collective-permute-start.9 = (f32[64,640]{1,0:T(8,128)S(1)}, f32[64,640]{1,0:T(8,128)S(1)}, u32[]{:S(2)}, u32[]{:S(2)}) collective-permute-start(f32[64,640]{1,0:T(8,128)S(1)} %get-tuple-element.69), channel_id=1, source_target_pairs={{0,2},{1,3},{2,0},{3,1},{4,6},{5,7},{6,4},{7,5},{8,10},{9,11},{10,... | collective-permute-start | bytes 491528 | tf_op jit(solution)/shard_map/ppermute | solution.py:455
  58.0 8.4 %collective-permute-start.10 = (f32[64,640]{1,0:T(8,128)S(1)}, f32[64,640]{1,0:T(8,128)S(1)}, u32[]{:S(2)}, u32[]{:S(2)}) collective-permute-start(f32[64,640]{1,0:T(8,128)S(1)} %get-tuple-element.70), channel_id=1, source_target_pairs={{0,3},{1,2},{2,1},{3,0},{4,7},{5,6},{6,5},{7,4},{8,11},{9,10},{10,... | collective-permute-start | bytes 491528 | tf_op jit(solution)/shard_map/ppermute | solution.py:455
  58.2 11.1 %collective-permute-start.11 = (f32[64,640]{1,0:T(8,128)S(1)}, f32[64,640]{1,0:T(8,128)S(1)}, u32[]{:S(2)}, u32[]{:S(2)}) collective-permute-start(f32[64,640]{1,0:T(8,128)S(1)} %get-tuple-element.71), channel_id=1, source_target_pairs={{0,4},{1,5},{2,6},{3,7},{4,0},{5,1},{6,2},{7,3},{8,12},{9,13},{10,... | collective-permute-start | bytes 491528 | tf_op jit(solution)/shard_map/ppermute | solution.py:455
  58.7 11.0 %collective-permute-start.12 = (f32[64,640]{1,0:T(8,128)S(1)}, f32[64,640]{1,0:T(8,128)S(1)}, u32[]{:S(2)}, u32[]{:S(2)}) collective-permute-start(f32[64,640]{1,0:T(8,128)S(1)} %get-tuple-element.72), channel_id=1, source_target_pairs={{0,5},{1,4},{2,7},{3,6},{4,1},{5,0},{6,3},{7,2},{8,13},{9,12},{10,... | collective-permute-start | bytes 491528 | tf_op jit(solution)/shard_map/ppermute | solution.py:455
  61.5 11.5 %collective-permute-start.13 = (f32[64,640]{1,0:T(8,128)S(1)}, f32[64,640]{1,0:T(8,128)S(1)}, u32[]{:S(2)}, u32[]{:S(2)}) collective-permute-start(f32[64,640]{1,0:T(8,128)S(1)} %get-tuple-element.73), channel_id=1, source_target_pairs={{0,6},{1,7},{2,4},{3,5},{4,2},{5,3},{6,0},{7,1},{8,14},{9,15},{10,... | collective-permute-start | bytes 491528 | tf_op jit(solution)/shard_map/ppermute | solution.py:455
  63.3 14.8 %collective-permute-start.14 = (f32[64,640]{1,0:T(8,128)S(1)}, f32[64,640]{1,0:T(8,128)S(1)}, u32[]{:S(2)}, u32[]{:S(2)}) collective-permute-start(f32[64,640]{1,0:T(8,128)S(1)} %get-tuple-element.74), channel_id=1, source_target_pairs={{0,7},{1,6},{2,5},{3,4},{4,3},{5,2},{6,1},{7,0},{8,15},{9,14},{10,... | collective-permute-start | bytes 491528 | tf_op jit(solution)/shard_map/ppermute | solution.py:455
  66.4 11.9 %collective-permute-start.15 = (f32[64,640]{1,0:T(8,128)S(1)}, f32[64,640]{1,0:T(8,128)S(1)}, u32[]{:S(2)}, u32[]{:S(2)}) collective-permute-start(f32[64,640]{1,0:T(8,128)S(1)} %get-tuple-element.75), channel_id=1, source_target_pairs={{0,1},{1,0},{2,3},{3,2},{4,5},{5,4},{6,7},{7,6},{8,9},{9,8},{10,11... | collective-permute-start | bytes 491528 | tf_op jit(solution)/shard_map/ppermute | solution.py:455
  69.3 9.9 %collective-permute-start.16 = (f32[64,640]{1,0:T(8,128)S(1)}, f32[64,640]{1,0:T(8,128)S(1)}, u32[]{:S(2)}, u32[]{:S(2)}) collective-permute-start(f32[64,640]{1,0:T(8,128)S(1)} %get-tuple-element.82), channel_id=1, source_target_pairs={{0,2},{1,3},{2,0},{3,1},{4,6},{5,7},{6,4},{7,5},{8,10},{9,11},{10,... | collective-permute-start | bytes 491528 | tf_op jit(solution)/shard_map/ppermute | solution.py:455
  69.7 18.6 %collective-permute-start.17 = (f32[64,640]{1,0:T(8,128)S(1)}, f32[64,640]{1,0:T(8,128)S(1)}, u32[]{:S(2)}, u32[]{:S(2)}) collective-permute-start(f32[64,640]{1,0:T(8,128)S(1)} %get-tuple-element.83), channel_id=1, source_target_pairs={{0,3},{1,2},{2,1},{3,0},{4,7},{5,6},{6,5},{7,4},{8,11},{9,10},{10,... | collective-permute-start | bytes 491528 | tf_op jit(solution)/shard_map/ppermute | solution.py:455
  73.0 15.3 %collective-permute-start.18 = (f32[64,640]{1,0:T(8,128)S(1)}, f32[64,640]{1,0:T(8,128)S(1)}, u32[]{:S(2)}, u32[]{:S(2)}) collective-permute-start(f32[64,640]{1,0:T(8,128)S(1)} %get-tuple-element.84), channel_id=1, source_target_pairs={{0,4},{1,5},{2,6},{3,7},{4,0},{5,1},{6,2},{7,3},{8,12},{9,13},{10,... | collective-permute-start | bytes 491528 | tf_op jit(solution)/shard_map/ppermute | solution.py:455
  78.1 10.2 %collective-permute-start.19 = (f32[64,640]{1,0:T(8,128)S(1)}, f32[64,640]{1,0:T(8,128)S(1)}, u32[]{:S(2)}, u32[]{:S(2)}) collective-permute-start(f32[64,640]{1,0:T(8,128)S(1)} %get-tuple-element.85), channel_id=1, source_target_pairs={{0,5},{1,4},{2,7},{3,6},{4,1},{5,0},{6,3},{7,2},{8,13},{9,12},{10,... | collective-permute-start | bytes 491528 | tf_op jit(solution)/shard_map/ppermute | solution.py:455
  78.2 10.1 %collective-permute-start.20 = (f32[64,640]{1,0:T(8,128)S(1)}, f32[64,640]{1,0:T(8,128)S(1)}, u32[]{:S(2)}, u32[]{:S(2)}) collective-permute-start(f32[64,640]{1,0:T(8,128)S(1)} %get-tuple-element.86), channel_id=1, source_target_pairs={{0,6},{1,7},{2,4},{3,5},{4,2},{5,3},{6,0},{7,1},{8,14},{9,15},{10,... | collective-permute-start | bytes 491528 | tf_op jit(solution)/shard_map/ppermute | solution.py:455
  79.2 10.0 %collective-permute-start.21 = (f32[64,640]{1,0:T(8,128)S(1)}, f32[64,640]{1,0:T(8,128)S(1)}, u32[]{:S(2)}, u32[]{:S(2)}) collective-permute-start(f32[64,640]{1,0:T(8,128)S(1)} %get-tuple-element.87), channel_id=1, source_target_pairs={{0,7},{1,6},{2,5},{3,4},{4,3},{5,2},{6,1},{7,0},{8,15},{9,14},{10,... | collective-permute-start | bytes 491528 | tf_op jit(solution)/shard_map/ppermute | solution.py:455
  95.4 13.8 %all-to-all-start = ((f32[32,1,128]{2,1,0:T(1,128)}), f32[32,1,128]{2,1,0:T(1,128)S(1)}, u32[]{:S(2)}, u32[]{:S(2)}) async-start(f32[32,1,128]{2,1,0:T(1,128)} %get-tuple-element.97), calls=%async_computation | async-start | bytes 32768 | tf_op jit(solution)/shard_map/all_to_all | solution.py:591
  (39 other events, 560.4 us)

commit v10 on v9

--- a/solution.py
+++ b/solution.py
@@ -13,14 +13,15 @@
 QUARTERS = 4
 HALVES = 2
 GROUP = QUARTERS * HALVES
-DISTANCES = (7, 1, 6, 2, 5, 3, 4)
+DISTANCES = (1, 2, 3, 4, 5, 6, 7)
+ARRIVALS = (0, *DISTANCES)
 LANES = 128
 LOG2E = 1.4426950408889634
 FAR = -1e30
 VMEM = pl.BlockSpec(memory_space=pltpu.VMEM)
 SMEM = pl.BlockSpec(memory_space=pltpu.SMEM)
 ANY = pl.BlockSpec(memory_space=pl.ANY)
-WIDE_PARTS = 7
+WIDE_PARTS = 8
 AFTER = 2
 CUM, WEIGHT, FACTOR = 0, 1, 2
 STRIDE, LOG = 1, 2
@@ -149,11 +150,14 @@
 
 
 def inner_kernel(
-    starts, cols_ref, rows_ref, features, cotangent, writes, reads, spread_ref, *refs
+    offset, last, starts, cols_ref, rows_ref, features, cotangent, writes, reads, skip, spread_ref, *refs
 ):
-    refs = refs[AFTER:]
-    inside, feature_part, skip_part, write_high, write_low, read_high, read_low = refs[:WIDE_PARTS]
-    write_part, read_part = refs[WIDE_PARTS:-3]
+    if offset:
+        before, refs = refs[0], refs[1 + WIDE_PARTS + AFTER :]
+    else:
+        refs = refs[AFTER:]
+    inside, feature_part, skip_part, skip_wide, write_high, write_low, read_high, read_low = refs[:WIDE_PARTS]
+    results = refs[WIDE_PARTS:-3]
     scores_ref, mask_ref, grad_ref = refs[-3:]
     length, width = features.shape
     heads = rows_ref.shape[1]
@@ -170,8 +174,9 @@
         causal = iota((length, length), 0) >= iota((length, length), 1)
         mask_ref[...] = jnp.where((segment_row == segment_col) & causal, 0.0, FAR)
         scores_ref[...] = matmul_nt(reads[...], writes[...])
-        grad_ref[...] = jnp.zeros_like(grad_ref)
-
+        grad_ref[...] = before[...] if offset else jnp.zeros_like(grad_ref)
+
+    skip_wide[...] = wide_skip(skip, heads, spread_ref[...])
     write_high[...], write_low[...] = split2(matmul(cols_ref[WEIGHT], spread_ref[...]) * features[...].astype(F32))
     read_high[...], read_low[...] = split2(matmul(cols_ref[FACTOR], spread_ref[...]) * cotangent[...].astype(F32))
 
@@ -182,7 +187,7 @@
         grad_f32 = grad.astype(F32)
         grad_t = grad_f32.T.astype(BF16)
         skip_part[:, cols] = jnp.sum(grad_f32 * feature.astype(F32), axis=0, keepdims=True)
-        head = step * here + at * 2
+        head = (offset + step) * here + at * 2
         lane = iota((LANES, 2 * LANES), 0)
         wanted = head + lax.div(iota((LANES, 2 * LANES), 1), LANES)
         pick = (lane == wanted) | (lane == wanted + heads) | (lane == wanted + 2 * heads)
@@ -212,19 +217,23 @@
 
     lax.fori_loop(0, here // 2, one_pair, 0)
 
-    @pl.when(step == QUARTERS - 1)
+    @pl.when(step == pl.num_programs(0) - 1)
     def _():
         score_grad = grad_ref[...]
-        high, low = split2(score_grad)
-        read_part[...] = matmul(high, writes[...]) + matmul(low, writes[...])
-        high, low = split2(score_grad.T)
-        write_part[...] = matmul(high, reads[...]) + matmul(low, reads[...])
+        if last:
+            write_part, read_part = results
+            high, low = split2(score_grad)
+            read_part[...] = matmul(high, writes[...]) + matmul(low, writes[...])
+            high, low = split2(score_grad.T)
+            write_part[...] = matmul(high, reads[...]) + matmul(low, reads[...])
+        else:
+            results[0][...] = score_grad
 
 
 def in_order(refs, scratch, back=False):
     own = group_place()
     rows = scratch.shape[1]
-    for distance, ref in enumerate(refs):
+    for distance, ref in zip(ARRIVALS, refs):
         first = ref.shape[0] - rows if back else 0
         scratch[own ^ distance] = ref[first : first + rows]
 
@@ -272,34 +281,63 @@
     refs[-1][part:] = own[part:] * keep
 
 
-def spread_kernel(part, count, back_count, *refs):
-    first = GROUP
-    ups, downs = refs[first : first + count], refs[first + count : first + count + back_count]
-    keeps = refs[first + count + back_count]
-    outs = refs[first + count + back_count + 2 : -4]
-    came, back_came, give, back_give = refs[-4:]
-    in_order(refs[:GROUP], came)
-    if downs:
-        entering, returning = arrived(part, ups)[0], arrived(part, downs)[0]
+def in_upper():
+    return lax.axis_index("ctx") >= GROUP
+
+
+def spread_kernel(part, two, second, *refs):
+    keeps = refs[GROUP]
+    arrivals = refs[GROUP + 1 : -3 - GROUP]
+    outs = refs[-3 - GROUP : -3]
+    came, back_came, give = refs[-3:]
+
+    def start():
+        return arrived(part, arrivals)[0] if arrivals else jnp.zeros(give.shape[1:], F32)
+
+    def forward():
+        in_order(refs[:GROUP], came)
+        total = start()
+        for j in range(GROUP):
+            give[j] = total
+            if j < GROUP - 1:
+                total = total * keeps[j : j + 1] + came[j, 0:part]
+
+    def backward():
+        in_order(refs[:GROUP], back_came, back=True)
+        total = start()
+        for j in reversed(range(GROUP)):
+            give[j] = total
+            if j > 0:
+                total = total * keeps[j : j + 1] + back_came[j]
+
+    if two:
+        upper = in_upper()
+        pl.when(upper == second)(forward)
+        pl.when(upper != second)(backward)
     else:
-        upper = jnp.full((1, 1), lax.axis_index("ctx")) >= GROUP
-        entering = jnp.where(upper, ups[0][0:part], 0.0)
-        returning = jnp.where(upper, 0.0, ups[0][0:part])
-    total = entering
-    for j in range(GROUP):
-        give[j] = total
-        if j < GROUP - 1:
-            total = total * keeps[j : j + 1] + came[j, 0:part]
-    in_order(refs[:GROUP], back_came, back=True)
-    total = returning
-    for j in reversed(range(GROUP)):
-        back_give[j] = total
-        if j > 0:
-            total = total * keeps[j : j + 1] + back_came[j]
+        (backward if second else forward)()
     own = group_place()
-    for distance in range(GROUP):
-        outs[distance][...] = give[own ^ distance]
-        outs[GROUP + distance][...] = back_give[own ^ distance]
+    for distance, out in enumerate(outs):
+        out[...] = give[own ^ distance]
+
+
+def both_sets(two, refs, have, back_have):
+    sets = refs[:GROUP], refs[GROUP : 2 * GROUP]
+
+    def straight():
+        in_order(sets[0], have)
+        in_order(sets[1], back_have)
+
+    def crossed():
+        in_order(sets[1], have)
+        in_order(sets[0], back_have)
+
+    if two:
+        upper = in_upper()
+        pl.when(upper)(crossed)
+        pl.when(jnp.logical_not(upper))(straight)
+    else:
+        straight()
 
 
 def head_sums(ref, value, spread):
@@ -316,33 +354,18 @@
     return jnp.concatenate([have[half * QUARTERS + step] for half in range(HALVES)], axis=0)
 
 
-def finish_kernel(skip, cols_ref, spread_ref, features, cotangent, reads, inside, *refs):
-    mixed, rows, kept, have = refs[GROUP + 1 :]
-    length = reads.shape[0]
-    heads = skip.shape[1]
-    step = pl.program_id(0)
-
-    @pl.when(step == 0)
-    def _():
-        rows[...] = jnp.zeros_like(rows)
-        in_order(refs[:GROUP], have)
-
-    spread = spread_ref[...]
-    factor = matmul(cols_ref[FACTOR], spread)
-    entering = quarter_rows(have, step)
-    kept[...] = entering * factor[length - 1 :]
-    stack = jnp.concatenate(split2(entering), axis=0)
-    total = inside[...] + factor * matmul(jnp.concatenate([reads[...]] * 2, axis=1), stack)
-    mixed[...] = (total + wide_skip(skip, heads, spread) * features[...].astype(F32)).astype(BF16)
-    head_sums(rows, cotangent[...].astype(F32) * total, spread)
-
-
-def back_finish_kernel(
-    logits, bias, decay, skip, cols_ref, rows_ref, spread_ref,
-    features, cotangent, writes, feature_part, skip_part, row_ref, kept, *refs,
+def summed_onward(value):
+    count, length = value.shape
+    onward = jnp.where(iota((length, length), 0) >= iota((length, length), 1), 1.0, 0.0).astype(BF16)
+    parts = matmul(jnp.concatenate(split3(value), axis=0), onward)
+    return parts[:count] + parts[count : 2 * count] + parts[2 * count :]
+
+
+def finish_kernel(
+    two, logits, bias, decay, cols_ref, rows_ref, spread_ref, features, cotangent, writes, reads,
+    inside, feature_part, skip_part, skip_wide, *refs,
 ):
-    haves = refs[:GROUP]
-    feature_grad, step_grad, sums, col_acc, last_acc, skip_acc, have = refs[GROUP:]
+    mixed, feature_grad, step_grad, sums, row_acc, col_acc, last_acc, skip_acc, have, back_have = refs[2 * GROUP :]
     heads, length = logits.shape
     state = writes.shape[1]
     width = features.shape[1]
@@ -350,38 +373,37 @@
 
     @pl.when(step == 0)
     def _():
-        for ref in (col_acc, last_acc, skip_acc):
+        for ref in (row_acc, col_acc, last_acc, skip_acc):
             ref[...] = jnp.zeros_like(ref)
-        in_order(haves, have)
+        both_sets(two, refs, have, back_have)
 
     spread = spread_ref[...]
-    weight = matmul(cols_ref[WEIGHT], spread)
     feature = features[...].astype(F32)
-    returning = quarter_rows(have, step)
+    grad = cotangent[...].astype(F32)
+    factor = matmul(cols_ref[FACTOR], spread)
+    entering = quarter_rows(have, step)
+    stack = jnp.concatenate(split2(entering), axis=0)
+    total = inside[...] + factor * matmul(jnp.concatenate([reads[...]] * 2, axis=1), stack)
+    mixed[...] = (total + skip_wide[...] * feature).astype(BF16)
+    head_sums(row_acc, grad * total, spread)
+    returning = quarter_rows(back_have, step)
     stack = jnp.concatenate(split2(returning), axis=0)
-    writes2 = jnp.concatenate([writes[...]] * 2, axis=1)
-    carried = weight * matmul(writes2, stack)
+    carried = matmul(cols_ref[WEIGHT], spread) * matmul(jnp.concatenate([writes[...]] * 2, axis=1), stack)
     total = feature_part[...] + carried
-    feature_grad[...] = (total + wide_skip(skip, heads, spread) * cotangent[...].astype(F32)).astype(BF16)
+    feature_grad[...] = (total + skip_wide[...] * grad).astype(BF16)
     head_sums(col_acc, feature * total, spread)
-    leaving = jnp.sum((returning * kept[...]).reshape(state // 8, 8, width), axis=0)
+    leaving = jnp.sum((returning * entering).reshape(state // 8, 8, width), axis=0) * factor[length - 1 :]
     leaving = leaving + jnp.sum((feature * carried).reshape(length // 8, 8, width), axis=0)
     head_sums(last_acc, leaving, spread)
     head_sums(skip_acc, jnp.broadcast_to(skip_part[...], (8, width)), spread)
 
     @pl.when(step == QUARTERS - 1)
     def _():
-        rows = row_ref[...].T[:heads]
         cols = col_acc[...].T[:heads]
         last = column(jnp.sum(last_acc[...], axis=0, keepdims=True))[:heads]
-        stride = rows_ref[STRIDE]
-        gap_grad = rows - cols + jnp.where(iota((heads, length), 1) == length - 1, last, 0.0)
-        onward = jnp.where(iota((length, length), 0) >= iota((length, length), 1), 1.0, 0.0).astype(BF16)
-        parts = matmul(jnp.concatenate(split3(gap_grad), axis=0), onward)
-        log_grad = parts[:heads] + parts[heads : 2 * heads] + parts[2 * heads :]
-        rate = column(-jnp.exp(decay[...]))
+        log_grad = last + summed_onward(row_acc[...].T[:heads] - cols)
         slope = 1.0 / (1.0 + jnp.exp(-(logits[...] + column(bias[...]))))
-        step_value = (cols / stride + rate * log_grad) * slope
+        step_value = (cols / rows_ref[STRIDE] + column(-jnp.exp(decay[...])) * log_grad) * slope
         step_grad[...] = step_value
         bias_sum = jnp.sum(step_value, axis=1, keepdims=True)
         decay_sum = jnp.sum(log_grad * rows_ref[LOG], axis=1, keepdims=True)
@@ -393,7 +415,7 @@
         sums[...] = jnp.broadcast_to(table[None], sums.shape)
 
 
-def keys_kernel(write_part, read_part, write_high, write_low, read_high, read_low, *refs):
+def keys_kernel(two, write_part, read_part, write_high, write_low, read_high, read_low, *refs):
     write_grad, read_grad, write_acc, read_acc, have, back_have = refs[2 * GROUP + 1 :]
     state = write_part.shape[1]
     step = pl.program_id(0)
@@ -402,8 +424,7 @@
     def _():
         write_acc[...] = jnp.zeros_like(write_acc)
         read_acc[...] = jnp.zeros_like(read_acc)
-        in_order(refs[:GROUP], have)
-        in_order(refs[GROUP : 2 * GROUP], back_have)
+        both_sets(two, refs, have, back_have)
 
     for states, high, low, acc in (
         (have, read_high, read_low, read_acc),
@@ -455,8 +476,7 @@
         return lax.ppermute(value, "ctx", [(k, k ^ distance) for k in range(blocks)])
 
     def swap(values):
-        came = {d: exchange(values[d], d) for d in DISTANCES}
-        return [came.get(d, values[0]) for d in range(GROUP)]
+        return [values[0]] + [exchange(values[d], d) for d in DISTANCES]
 
     def shift(value, distance):
         pairs = [(k, k + distance) for k in range(blocks) if 0 <= k + distance < blocks]
@@ -507,21 +527,32 @@
     cols, head_rows = out[GROUP:]
 
     wide_part, wide_piece = struct((length, wide)), struct((length, wide), BF16)
-    wide_parts = [wide_part] * 2 + [struct((1, wide))] + [wide_piece] * 4
+    wide_parts = [wide_part] * 2 + [struct((1, wide))] * 2 + [wide_piece] * 4
     token_part = struct((length, state))
-    inside, feature_part, skip_part, *pieces, write_part, read_part = call(
-        inner_kernel,
-        "inner",
-        wide_parts + [token_part] * 2,
-        [SMEM, all_cols, all_rows, by_quarter, by_quarter, tokens, tokens, spread_quarter] + [ANY] * AFTER,
-        10,
-        24,
-        grid=(QUARTERS,),
-        out_specs=[by_quarter, by_quarter, quarter_of(1)] + [by_quarter] * 4 + [tokens] * 2,
-        scratch_shapes=[pltpu.VMEM((length, length), F32)] * 3,
-    )(
-        doc_starts, cols, head_rows, features, cotangent, writes, reads, spread,
-        *[came[d] for d in DISTANCES[1 : 1 + AFTER]],
+    square = all_of(length, length)
+    inner_args = (doc_starts, cols, head_rows, features, cotangent, writes, reads, skip, spread)
+
+    def inner(offset, count, begun, after):
+        mine, thin = quarter_of(length, offset), quarter_of(1, offset)
+        last = offset + count == QUARTERS
+        n_args = len(inner_args) + 1
+        return call(
+            functools.partial(inner_kernel, offset, last),
+            "inner_" + str(offset),
+            wide_parts + ([token_part] * 2 if last else [struct((length, length))]),
+            [SMEM, all_cols, all_rows, mine, mine, tokens, tokens, row, quarter_of(LANES, offset)]
+            + ([square] + [ANY] * WIDE_PARTS if offset else [])
+            + [ANY] * AFTER,
+            5 * count,
+            24,
+            grid=(count,),
+            out_specs=[mine, mine, thin, thin] + [mine] * 4 + ([tokens] * 2 if last else [square]),
+            scratch_shapes=[pltpu.VMEM((length, length), F32)] * 3,
+            input_output_aliases={n_args + at: at for at in range(WIDE_PARTS)} if offset else {},
+        )(*inner_args, *begun, *after)
+
+    inside, feature_part, skip_part, skip_wide, *pieces, write_part, read_part = inner(
+        0, QUARTERS, [], came[1 : 1 + AFTER]
     )
     two = blocks == 2 * GROUP
     *group_sums, keeps = call(
@@ -534,51 +565,45 @@
         scratch_shapes=[long_shares, shares],
     )(*came, write_part)
     if two:
-        ups, downs = [exchange(group_sums[0], GROUP)], []
+        near, far = [], [exchange(group_sums[0], GROUP)]
     else:
-        ups, downs = scan(group_sums[0], 1), scan(group_sums[1], -1)
-    give = call(
-        functools.partial(spread_kernel, part, len(ups), len(downs)),
-        "spread",
-        [share] * 2 * GROUP,
-        [VMEM] * (GROUP + len(ups) + len(downs) + 1) + [ANY],
-        2,
-        16,
-        scratch_shapes=[long_shares, shares, shares, shares],
-    )(*came, *ups, *downs, keeps, write_part)
-    have, back_have = swap(give[:GROUP]), swap(give[GROUP:])
+        near, far = scan(group_sums[0], 1), scan(group_sums[1], -1)
+
+    def give_back(second, arrivals):
+        return swap(
+            call(
+                functools.partial(spread_kernel, part, two, second),
+                "spread",
+                [share] * GROUP,
+                [VMEM] * (GROUP + 1 + len(arrivals)),
+                2,
+                12,
+                scratch_shapes=[long_shares, shares, shares],
+            )(*came, keeps, *arrivals)
+        )
+
+    sets = [*give_back(False, near), *give_back(True, far)]
     devices = blocks * members
     whole_shares = [all_of(part, width)] * GROUP
-    mixed, rows, kept = call(
-        finish_kernel,
+    mixed, feature_grad, step_grad, sums = call(
+        functools.partial(finish_kernel, two),
         "finish",
-        [result, struct((length, LANES)), struct((state, wide))],
-        [row, all_cols, spread_quarter, by_quarter, by_quarter, tokens, by_quarter] + whole_shares + [ANY],
+        [result, result, small, struct((devices, 1, LANES))],
+        [by_heads, row, row, all_cols, all_rows, spread_quarter, by_quarter, by_quarter, tokens, tokens]
+        + [by_quarter] * 2
+        + [quarter_of(1)] * 2
+        + whole_shares * 2,
         8,
         24,
         grid=(QUARTERS,),
-        out_specs=[by_quarter, columns, quarter_of(state)],
-        scratch_shapes=[shares],
-    )(skip, cols, spread, features, cotangent, reads, inside, *have, back_have[DISTANCES[1]])
-    feature_grad, step_grad, sums = call(
-        back_finish_kernel,
-        "back_finish",
-        [result, small, struct((devices, 1, LANES))],
-        [by_heads, row, row, row, all_cols, all_rows, spread_quarter]
-        + [by_quarter, by_quarter, tokens, by_quarter]
-        + [quarter_of(1), columns, quarter_of(state)]
-        + whole_shares,
-        8,
-        24,
-        grid=(QUARTERS,),
-        out_specs=[by_quarter, by_heads, all_of(devices, 1, LANES)],
-        scratch_shapes=[pltpu.VMEM((length, LANES), F32)] + [pltpu.VMEM((8, LANES), F32)] * 2 + [shares],
+        out_specs=[by_quarter, by_quarter, by_heads, all_of(devices, 1, LANES)],
+        scratch_shapes=[pltpu.VMEM((length, LANES), F32)] * 2 + [pltpu.VMEM((8, LANES), F32)] * 2 + [shares] * 2,
     )(
-        logits, bias, decay, skip, cols, head_rows, spread, features, cotangent, writes,
-        feature_part, skip_part, rows, kept, *back_have,
+        logits, bias, decay, cols, head_rows, spread, features, cotangent, writes, reads,
+        inside, feature_part, skip_part, skip_wide, *sets,
     )
     write_grad, read_grad = call(
-        keys_kernel,
+        functools.partial(keys_kernel, two),
         "keys",
         [tokens_result] * 2,
         [tokens] * 2 + [by_quarter] * 4 + whole_shares * 2 + [ANY],
@@ -587,7 +612,7 @@
         grid=(QUARTERS,),
         out_specs=[tokens] * 2,
         scratch_shapes=[pltpu.VMEM((length, 2 * state), F32)] * 2 + [shares] * 2,
-    )(write_part, read_part, *pieces, *have, *back_have, step_grad)
+    )(write_part, read_part, *pieces, *sets, step_grad)
     sums = jnp.sum(lax.all_to_all(sums, ("dp", "ctx"), 0, 0), axis=(0, 1))
     return (
         mixed[None],

time: 110 us -> 107 us (0.973)
  starting transfers between devices: 44.9 us -> 40.5 us
  waiting for transfers between devices: 21.1 us -> 25.4 us
  Pallas kernels: 39.1 us -> 36.7 us
    ppermute x22, waiting for transfers between devices: 20.5 us -> 24.8 us  [exchange(): lax.ppermute(value, 'ctx', [(k, k ^ distance) for k in range(blocks)])]
    pallas_call x5, Pallas kernels: 32.3 us -> 30 us  [the longest x1 15.2 us: inner(): call(functools.partial(inner_kernel, offset, last), 'inner_' + str(offset...]
    all_to_all x1, starting transfers between devices: 6.64 us -> 4.39 us  [local(): sums = jnp.sum(lax.all_to_all(sums, ('dp', 'ctx'), 0, 0), axis=(0, 1))]
    ppermute x22, starting transfers between devices: 38.3 us -> 36.1 us  [exchange(): lax.ppermute(value, 'ctx', [(k, k ^ distance) for k in range(blocks)])]
    unnamed x80 -> x78, local copies, waits for them, and re-layouts: 2.95 us -> 1.98 us
  transfers between devices with their start and end apart: 23 -> 23, of which waited for: 12 -> 12; matrix products, arithmetic and copies ran while one was open for 0% -> 0% of each run, Pallas kernels for 23% -> 21%
where the time goes in v10:
time: 107 us; the launch traced here: 106 us
  starting transfers between devices  40.5 us (38%)
  Pallas kernels  36.7 us (34%)
  waiting for transfers between devices  25.4 us (24%)
  local copies, waits for them, and re-layouts  2.57 us (2%)
  between operations  1.15 us (1%)
    ppermute x22, starting transfers between devices, exchange(): lax.ppermute(value, 'ctx', [(k, k ^ distance) for k in range(blocks)])  36.1 us
    ppermute x22, waiting for transfers between devices, exchange(): lax.ppermute(value, 'ctx', [(k, k ^ distance) for k in range(blocks)])  24.8 us
    pallas_call x1, Pallas kernels, inner(): call(functools.partial(inner_kernel, offset, last), 'inner_' + str(offset...  15.2 us
    pallas_call x1, Pallas kernels, local(): call(functools.partial(finish_kernel, two), 'finish', [result, result, sm...  7.67 us
    pallas_call x1, Pallas kernels, local(): call(functools.partial(keys_kernel, two), 'keys', [tokens_result] * 2, [t...  6.51 us
    pallas_call x1, Pallas kernels, local(): call(states_kernel, 'states', [struct((2 * part + 8, width))] * GROUP + [...  6.46 us
    all_to_all x1, starting transfers between devices, local(): sums = jnp.sum(lax.all_to_all(sums, ('dp', 'ctx'), 0, 0), axis=(0, 1))  4.39 us
  transfers between devices with their start and end apart: 23, of which 12 were waited for; matrix products, arithmetic and copies ran while one was open for 0% of the time, Pallas kernels for 21%

profile of v10, /device:TPU:0, one launch (start us, length us, event | category | flops | bytes accessed | tf_op | source)
XLA Modules:
  0.0 106.4 jit_solution(6229284982167123355)
XLA Ops:
  0.7 6.5 %states.1 = (f32[136,640]{1,0:T(8,128)}, f32[136,640]{1,0:T(8,128)}, f32[136,640]{1,0:T(8,128)}, f32[136,640]{1,0:T(8,128)}, f32[136,640]{1,0:T(8,128)}, /*index...) custom-call(s32[1,4]{1,0:T(1,128)} %starts.3, ...), custom_call_target="tpu_custom_call" | custom-call | flops 4000000000 | bytes 1000000 | tf_op jit(solution)/shard_map/states/pallas_call | solution.py:517
  7.2 2.9 %collective-permute-start = (f32[136,640]{1,0:T(8,128)}, f32[136,640]{1,0:T(8,128)S(1)}, u32[]{:S(2)}, u32[]{:S(2)}) collective-permute-start(f32[136,640]{1,0:T(8,128)} %get-tuple-element.54), channel_id=1, source_target_pairs={{0,1},{1,0},{2,3},{3,2},{4,5},{5,4},{6,7},{7,6},{8,9},{9,8},{10,11... | collective-permute-start | bytes 1044488 | tf_op jit(solution)/shard_map/ppermute | solution.py:476
  10.1 1.5 %collective-permute-start.1 = (f32[136,640]{1,0:T(8,128)}, f32[136,640]{1,0:T(8,128)S(1)}, u32[]{:S(2)}, u32[]{:S(2)}) collective-permute-start(f32[136,640]{1,0:T(8,128)} %get-tuple-element.55), channel_id=1, source_target_pairs={{0,2},{1,3},{2,0},{3,1},{4,6},{5,7},{6,4},{7,5},{8,10},{9,11},{10,... | collective-permute-start | bytes 1044488 | tf_op jit(solution)/shard_map/ppermute | solution.py:476
  11.7 2.0 %collective-permute-start.3 = (f32[136,640]{1,0:T(8,128)}, f32[136,640]{1,0:T(8,128)S(1)}, u32[]{:S(2)}, u32[]{:S(2)}) collective-permute-start(f32[136,640]{1,0:T(8,128)} %get-tuple-element.62), channel_id=1, source_target_pairs={{0,4},{1,5},{2,6},{3,7},{4,0},{5,1},{6,2},{7,3},{8,12},{9,13},{10,... | collective-permute-start | bytes 1044488 | tf_op jit(solution)/shard_map/ppermute | solution.py:476
  15.1 4.2 %collective-permute-done.refs_0_.refs_1_ = f32[136,640]{1,0:T(8,128)S(1)} collective-permute-done((f32[136,640]{1,0:T(8,128)}, f32[136,640]{1,0:T(8,128)S(1)}, u32[]{:S(2)}, u32[]{:S(2)}) %collective-permute-start) | collective-permute-done | bytes 348192 | tf_op jit(solution)/shard_map/ppermute | solution.py:476
  19.3 3.1 %collective-permute-start.5 = (f32[136,640]{1,0:T(8,128)}, f32[136,640]{1,0:T(8,128)S(1)}, u32[]{:S(2)}, u32[]{:S(2)}) collective-permute-start(f32[136,640]{1,0:T(8,128)} %get-tuple-element.64), channel_id=1, source_target_pairs={{0,6},{1,7},{2,4},{3,5},{4,2},{5,3},{6,0},{7,1},{8,14},{9,15},{10,... | collective-permute-start | bytes 1044488 | tf_op jit(solution)/shard_map/ppermute | solution.py:476
  22.4 1.8 %collective-permute-start.6 = (f32[136,640]{1,0:T(8,128)}, f32[136,640]{1,0:T(8,128)S(1)}, u32[]{:S(2)}, u32[]{:S(2)}) collective-permute-start(f32[136,640]{1,0:T(8,128)} %get-tuple-element.65), channel_id=1, source_target_pairs={{0,7},{1,6},{2,5},{3,4},{4,3},{5,2},{6,1},{7,0},{8,15},{9,14},{10,... | collective-permute-start | bytes 1044488 | tf_op jit(solution)/shard_map/ppermute | solution.py:476
  26.0 15.2 %inner_0.1 = (f32[256,2560]{1,0:T(8,128)S(1)}, f32[256,2560]{1,0:T(8,128)S(1)}, f32[1,2560]{1,0:T(1,128)S(1)}, f32[1,2560]{1,0:T(1,128)S(1)}, bf16[256,2560]{1,0...) custom-call(s32[1,4]{1,0:T(1,128)S(1)} %copy-done.21, ...), custom_call_target="tpu_custom_call" | custom-call | flops 20000000000 | bytes 1000000 | tf_op jit(solution)/shard_map/inner_0/pallas_call | solution.py:539
  41.5 6.6 %collective-permute-done.6.refs_7_ = f32[136,640]{1,0:T(8,128)S(1)} collective-permute-done((f32[136,640]{1,0:T(8,128)}, f32[136,640]{1,0:T(8,128)S(1)}, u32[]{:S(2)}, u32[]{:S(2)}) %collective-permute-start.6) | collective-permute-done | bytes 348192 | tf_op jit(solution)/shard_map/ppermute | solution.py:476
  48.4 2.8 %collective-permute-start.14 = (f32[72,640]{1,0:T(8,128)S(1)}, f32[72,640]{1,0:T(8,128)S(1)}, u32[]{:S(2)}, u32[]{:S(2)}) collective-permute-start(f32[72,640]{1,0:T(8,128)S(1)} %get-tuple-element.76), channel_id=1, source_target_pairs={{0,8},{1,9},{2,10},{3,11},{4,12},{5,13},{6,14},{7,15},{8,0},{9,1},... | collective-permute-start | bytes 552968 | tf_op jit(solution)/shard_map/ppermute | solution.py:476
  53.0 2.1 %collective-permute-start.9 = (f32[64,640]{1,0:T(8,128)S(1)}, f32[64,640]{1,0:T(8,128)S(1)}, u32[]{:S(2)}, u32[]{:S(2)}) collective-permute-start(f32[64,640]{1,0:T(8,128)S(1)} %get-tuple-element.71), channel_id=1, source_target_pairs={{0,3},{1,2},{2,1},{3,0},{4,7},{5,6},{6,5},{7,4},{8,11},{9,10},{10,... | collective-permute-start | bytes 491528 | tf_op jit(solution)/shard_map/ppermute | solution.py:476
  55.1 1.5 %collective-permute-start.10 = (f32[64,640]{1,0:T(8,128)S(1)}, f32[64,640]{1,0:T(8,128)S(1)}, u32[]{:S(2)}, u32[]{:S(2)}) collective-permute-start(f32[64,640]{1,0:T(8,128)S(1)} %get-tuple-element.72), channel_id=1, source_target_pairs={{0,4},{1,5},{2,6},{3,7},{4,0},{5,1},{6,2},{7,3},{8,12},{9,13},{10,... | collective-permute-start | bytes 491528 | tf_op jit(solution)/shard_map/ppermute | solution.py:476
  59.4 1.9 %collective-permute-start.12 = (f32[64,640]{1,0:T(8,128)S(1)}, f32[64,640]{1,0:T(8,128)S(1)}, u32[]{:S(2)}, u32[]{:S(2)}) collective-permute-start(f32[64,640]{1,0:T(8,128)S(1)} %get-tuple-element.74), channel_id=1, source_target_pairs={{0,6},{1,7},{2,4},{3,5},{4,2},{5,3},{6,0},{7,1},{8,14},{9,15},{10,... | collective-permute-start | bytes 491528 | tf_op jit(solution)/shard_map/ppermute | solution.py:476
  61.3 1.8 %collective-permute-start.13 = (f32[64,640]{1,0:T(8,128)S(1)}, f32[64,640]{1,0:T(8,128)S(1)}, u32[]{:S(2)}, u32[]{:S(2)}) collective-permute-start(f32[64,640]{1,0:T(8,128)S(1)} %get-tuple-element.75), channel_id=1, source_target_pairs={{0,7},{1,6},{2,5},{3,4},{4,3},{5,2},{6,1},{7,0},{8,15},{9,14},{10,... | collective-permute-start | bytes 491528 | tf_op jit(solution)/shard_map/ppermute | solution.py:476
  64.4 2.0 %collective-permute-done.11.refs_5_ = f32[64,640]{1,0:T(8,128)S(1)} collective-permute-done((f32[64,640]{1,0:T(8,128)S(1)}, f32[64,640]{1,0:T(8,128)S(1)}, u32[]{:S(2)}, u32[]{:S(2)}) %collective-permute-start.11) | collective-permute-done | bytes 163872 | tf_op jit(solution)/shard_map/ppermute | solution.py:476
  67.6 1.9 %collective-permute-done.12.refs_6_ = f32[64,640]{1,0:T(8,128)S(1)} collective-permute-done((f32[64,640]{1,0:T(8,128)S(1)}, f32[64,640]{1,0:T(8,128)S(1)}, u32[]{:S(2)}, u32[]{:S(2)}) %collective-permute-start.12) | collective-permute-done | bytes 163872 | tf_op jit(solution)/shard_map/ppermute | solution.py:476
  72.2 2.3 %collective-permute-start.19 = (f32[64,640]{1,0:T(8,128)S(1)}, f32[64,640]{1,0:T(8,128)S(1)}, u32[]{:S(2)}, u32[]{:S(2)}) collective-permute-start(f32[64,640]{1,0:T(8,128)S(1)} %get-tuple-element.82), channel_id=1, source_target_pairs={{0,5},{1,4},{2,7},{3,6},{4,1},{5,0},{6,3},{7,2},{8,13},{9,12},{10,... | collective-permute-start | bytes 491528 | tf_op jit(solution)/shard_map/ppermute | solution.py:476
  74.6 1.9 %collective-permute-start.20 = (f32[64,640]{1,0:T(8,128)S(1)}, f32[64,640]{1,0:T(8,128)S(1)}, u32[]{:S(2)}, u32[]{:S(2)}) collective-permute-start(f32[64,640]{1,0:T(8,128)S(1)} %get-tuple-element.83), channel_id=1, source_target_pairs={{0,6},{1,7},{2,4},{3,5},{4,2},{5,3},{6,0},{7,1},{8,14},{9,15},{10,... | collective-permute-start | bytes 491528 | tf_op jit(solution)/shard_map/ppermute | solution.py:476
  76.6 2.7 %collective-permute-start.21 = (f32[64,640]{1,0:T(8,128)S(1)}, f32[64,640]{1,0:T(8,128)S(1)}, u32[]{:S(2)}, u32[]{:S(2)}) collective-permute-start(f32[64,640]{1,0:T(8,128)S(1)} %get-tuple-element.84), channel_id=1, source_target_pairs={{0,7},{1,6},{2,5},{3,4},{4,3},{5,2},{6,1},{7,0},{8,15},{9,14},{10,... | collective-permute-start | bytes 491528 | tf_op jit(solution)/shard_map/ppermute | solution.py:476
  80.2 4.0 %collective-permute-done.20.refs_14_ = f32[64,640]{1,0:T(8,128)S(1)} collective-permute-done((f32[64,640]{1,0:T(8,128)S(1)}, f32[64,640]{1,0:T(8,128)S(1)}, u32[]{:S(2)}, u32[]{:S(2)}) %collective-permute-start.20) | collective-permute-done | bytes 163872 | tf_op jit(solution)/shard_map/ppermute | solution.py:476
  84.2 2.1 %collective-permute-done.21.refs_15_ = f32[64,640]{1,0:T(8,128)S(1)} collective-permute-done((f32[64,640]{1,0:T(8,128)S(1)}, f32[64,640]{1,0:T(8,128)S(1)}, u32[]{:S(2)}, u32[]{:S(2)}) %collective-permute-start.21) | collective-permute-done | bytes 163872 | tf_op jit(solution)/shard_map/ppermute | solution.py:476
  86.4 7.7 %finish.1 = (bf16[256,2560]{1,0:T(8,128)(2,1)}, bf16[256,2560]{1,0:T(8,128)(2,1)}, f32[40,256]{1,0:T(8,128)}, f32[32,1,128]{2,1,0:T(1,128)}) custom-call(f32[40,256]{1,0:T(8,128)S(1)} %bitcast.26, f32[1,40]{1,0:T(1,128)S(1)} %bitcast.29, f32[1,40]{1,0:T(1,128)S(1)} %bitcast.31, bf16[3,256,128]{2,1,0:T(8,128)(2,1)S(1)} %copy-done.35, ...), custom_call_target="tpu_custom_call" | custom-call | flops 8000000000 | bytes 1000000 | tf_op jit(solution)/shard_map/finish/pallas_call | solution.py:588
  94.2 4.4 %all-to-all-start = ((f32[32,1,128]{2,1,0:T(1,128)}), f32[32,1,128]{2,1,0:T(1,128)S(1)}, u32[]{:S(2)}, u32[]{:S(2)}) async-start(f32[32,1,128]{2,1,0:T(1,128)} %get-tuple-element.95), calls=%async_computation | async-start | bytes 32768 | tf_op jit(solution)/shard_map/all_to_all | solution.py:616
  98.6 6.5 %keys.1 = (bf16[256,128]{1,0:T(8,128)(2,1)}, bf16[256,128]{1,0:T(8,128)(2,1)}) custom-call(f32[256,128]{1,0:T(8,128)} %copy-done.34, f32[256,128]{1,0:T(8,128)} %copy-done.38, bf16[256,2560]{1,0:T(8,128)(2,1)} %copy-done.30, bf16[256,2560]{1,0:T(8,128)(2,1)} %copy-done.31, bf16[256,2560]{1,0:T(8,128)(2,1)} %copy-done.32, bf16[256,2560]{1,0:T(8,128)(2,1)} %copy-done.33, ...), custom_call_target="tpu_custom_call" | custom-call | flops 6000000000 | bytes 1000000 | tf_op jit(solution)/shard_map/keys/pallas_call | solution.py:605
  (109 shorter events, 15.8 us)
Async XLA Ops:
  7.2 12.1 %collective-permute-start = (f32[136,640]{1,0:T(8,128)}, f32[136,640]{1,0:T(8,128)S(1)}, u32[]{:S(2)}, u32[]{:S(2)}) collective-permute-start(f32[136,640]{1,0:T(8,128)} %get-tuple-element.54), channel_id=1, source_target_pairs={{0,1},{1,0},{2,3},{3,2},{4,5},{5,4},{6,7},{7,6},{8,9},{9,8},{10,11... | collective-permute-start | bytes 1044488 | tf_op jit(solution)/shard_map/ppermute | solution.py:476
  10.1 12.3 %collective-permute-start.1 = (f32[136,640]{1,0:T(8,128)}, f32[136,640]{1,0:T(8,128)S(1)}, u32[]{:S(2)}, u32[]{:S(2)}) collective-permute-start(f32[136,640]{1,0:T(8,128)} %get-tuple-element.55), channel_id=1, source_target_pairs={{0,2},{1,3},{2,0},{3,1},{4,6},{5,7},{6,4},{7,5},{8,10},{9,11},{10,... | collective-permute-start | bytes 1044488 | tf_op jit(solution)/shard_map/ppermute | solution.py:476
  11.6 29.7 %collective-permute-start.2 = (f32[136,640]{1,0:T(8,128)}, f32[136,640]{1,0:T(8,128)S(1)}, u32[]{:S(2)}, u32[]{:S(2)}) collective-permute-start(f32[136,640]{1,0:T(8,128)} %get-tuple-element.61), channel_id=1, source_target_pairs={{0,3},{1,2},{2,1},{3,0},{4,7},{5,6},{6,5},{7,4},{8,11},{9,10},{10,... | collective-permute-start | bytes 1044488 | tf_op jit(solution)/shard_map/ppermute | solution.py:476
  11.7 29.7 %collective-permute-start.3 = (f32[136,640]{1,0:T(8,128)}, f32[136,640]{1,0:T(8,128)S(1)}, u32[]{:S(2)}, u32[]{:S(2)}) collective-permute-start(f32[136,640]{1,0:T(8,128)} %get-tuple-element.62), channel_id=1, source_target_pairs={{0,4},{1,5},{2,6},{3,7},{4,0},{5,1},{6,2},{7,3},{8,12},{9,13},{10,... | collective-permute-start | bytes 1044488 | tf_op jit(solution)/shard_map/ppermute | solution.py:476
  13.7 27.6 %collective-permute-start.4 = (f32[136,640]{1,0:T(8,128)}, f32[136,640]{1,0:T(8,128)S(1)}, u32[]{:S(2)}, u32[]{:S(2)}) collective-permute-start(f32[136,640]{1,0:T(8,128)} %get-tuple-element.63), channel_id=1, source_target_pairs={{0,5},{1,4},{2,7},{3,6},{4,1},{5,0},{6,3},{7,2},{8,13},{9,12},{10,... | collective-permute-start | bytes 1044488 | tf_op jit(solution)/shard_map/ppermute | solution.py:476
  19.3 22.2 %collective-permute-start.5 = (f32[136,640]{1,0:T(8,128)}, f32[136,640]{1,0:T(8,128)S(1)}, u32[]{:S(2)}, u32[]{:S(2)}) collective-permute-start(f32[136,640]{1,0:T(8,128)} %get-tuple-element.64), channel_id=1, source_target_pairs={{0,6},{1,7},{2,4},{3,5},{4,2},{5,3},{6,0},{7,1},{8,14},{9,15},{10,... | collective-permute-start | bytes 1044488 | tf_op jit(solution)/shard_map/ppermute | solution.py:476
  22.4 25.7 %collective-permute-start.6 = (f32[136,640]{1,0:T(8,128)}, f32[136,640]{1,0:T(8,128)S(1)}, u32[]{:S(2)}, u32[]{:S(2)}) collective-permute-start(f32[136,640]{1,0:T(8,128)} %get-tuple-element.65), channel_id=1, source_target_pairs={{0,7},{1,6},{2,5},{3,4},{4,3},{5,2},{6,1},{7,0},{8,15},{9,14},{10,... | collective-permute-start | bytes 1044488 | tf_op jit(solution)/shard_map/ppermute | solution.py:476
  48.4 9.7 %collective-permute-start.14 = (f32[72,640]{1,0:T(8,128)S(1)}, f32[72,640]{1,0:T(8,128)S(1)}, u32[]{:S(2)}, u32[]{:S(2)}) collective-permute-start(f32[72,640]{1,0:T(8,128)S(1)} %get-tuple-element.76), channel_id=1, source_target_pairs={{0,8},{1,9},{2,10},{3,11},{4,12},{5,13},{6,14},{7,15},{8,0},{9,1},... | collective-permute-start | bytes 552968 | tf_op jit(solution)/shard_map/ppermute | solution.py:476
  51.5 34.8 %copy-start.29 = (f32[64,640]{1,0:T(8,128)}, f32[64,640]{1,0:T(8,128)S(1)}, u32[]{:S(2)}) copy-start(f32[64,640]{1,0:T(8,128)S(1)} %get-tuple-element.68.refs_0_) | copy-start | bytes 491524
  51.5 7.9 %collective-permute-start.7 = (f32[64,640]{1,0:T(8,128)S(1)}, f32[64,640]{1,0:T(8,128)S(1)}, u32[]{:S(2)}, u32[]{:S(2)}) collective-permute-start(f32[64,640]{1,0:T(8,128)S(1)} %get-tuple-element.69), channel_id=1, source_target_pairs={{0,1},{1,0},{2,3},{3,2},{4,5},{5,4},{6,7},{7,6},{8,9},{9,8},{10,11... | collective-permute-start | bytes 491528 | tf_op jit(solution)/shard_map/ppermute | solution.py:476
  52.5 8.8 %collective-permute-start.8 = (f32[64,640]{1,0:T(8,128)S(1)}, f32[64,640]{1,0:T(8,128)S(1)}, u32[]{:S(2)}, u32[]{:S(2)}) collective-permute-start(f32[64,640]{1,0:T(8,128)S(1)} %get-tuple-element.70), channel_id=1, source_target_pairs={{0,2},{1,3},{2,0},{3,1},{4,6},{5,7},{6,4},{7,5},{8,10},{9,11},{10,... | collective-permute-start | bytes 491528 | tf_op jit(solution)/shard_map/ppermute | solution.py:476
  53.0 10.1 %collective-permute-start.9 = (f32[64,640]{1,0:T(8,128)S(1)}, f32[64,640]{1,0:T(8,128)S(1)}, u32[]{:S(2)}, u32[]{:S(2)}) collective-permute-start(f32[64,640]{1,0:T(8,128)S(1)} %get-tuple-element.71), channel_id=1, source_target_pairs={{0,3},{1,2},{2,1},{3,0},{4,7},{5,6},{6,5},{7,4},{8,11},{9,10},{10,... | collective-permute-start | bytes 491528 | tf_op jit(solution)/shard_map/ppermute | solution.py:476
  55.1 8.8 %collective-permute-start.10 = (f32[64,640]{1,0:T(8,128)S(1)}, f32[64,640]{1,0:T(8,128)S(1)}, u32[]{:S(2)}, u32[]{:S(2)}) collective-permute-start(f32[64,640]{1,0:T(8,128)S(1)} %get-tuple-element.72), channel_id=1, source_target_pairs={{0,4},{1,5},{2,6},{3,7},{4,0},{5,1},{6,2},{7,3},{8,12},{9,13},{10,... | collective-permute-start | bytes 491528 | tf_op jit(solution)/shard_map/ppermute | solution.py:476
  58.2 8.2 %collective-permute-start.11 = (f32[64,640]{1,0:T(8,128)S(1)}, f32[64,640]{1,0:T(8,128)S(1)}, u32[]{:S(2)}, u32[]{:S(2)}) collective-permute-start(f32[64,640]{1,0:T(8,128)S(1)} %get-tuple-element.73), channel_id=1, source_target_pairs={{0,5},{1,4},{2,7},{3,6},{4,1},{5,0},{6,3},{7,2},{8,13},{9,12},{10,... | collective-permute-start | bytes 491528 | tf_op jit(solution)/shard_map/ppermute | solution.py:476
  59.4 10.1 %collective-permute-start.12 = (f32[64,640]{1,0:T(8,128)S(1)}, f32[64,640]{1,0:T(8,128)S(1)}, u32[]{:S(2)}, u32[]{:S(2)}) collective-permute-start(f32[64,640]{1,0:T(8,128)S(1)} %get-tuple-element.74), channel_id=1, source_target_pairs={{0,6},{1,7},{2,4},{3,5},{4,2},{5,3},{6,0},{7,1},{8,14},{9,15},{10,... | collective-permute-start | bytes 491528 | tf_op jit(solution)/shard_map/ppermute | solution.py:476
  61.3 10.9 %collective-permute-start.13 = (f32[64,640]{1,0:T(8,128)S(1)}, f32[64,640]{1,0:T(8,128)S(1)}, u32[]{:S(2)}, u32[]{:S(2)}) collective-permute-start(f32[64,640]{1,0:T(8,128)S(1)} %get-tuple-element.75), channel_id=1, source_target_pairs={{0,7},{1,6},{2,5},{3,4},{4,3},{5,2},{6,1},{7,0},{8,15},{9,14},{10,... | collective-permute-start | bytes 491528 | tf_op jit(solution)/shard_map/ppermute | solution.py:476
  63.1 11.4 %collective-permute-start.15 = (f32[64,640]{1,0:T(8,128)S(1)}, f32[64,640]{1,0:T(8,128)S(1)}, u32[]{:S(2)}, u32[]{:S(2)}) collective-permute-start(f32[64,640]{1,0:T(8,128)S(1)} %get-tuple-element.78), channel_id=1, source_target_pairs={{0,1},{1,0},{2,3},{3,2},{4,5},{5,4},{6,7},{7,6},{8,9},{9,8},{10,11... | collective-permute-start | bytes 491528 | tf_op jit(solution)/shard_map/ppermute | solution.py:476
  63.9 12.7 %collective-permute-start.16 = (f32[64,640]{1,0:T(8,128)S(1)}, f32[64,640]{1,0:T(8,128)S(1)}, u32[]{:S(2)}, u32[]{:S(2)}) collective-permute-start(f32[64,640]{1,0:T(8,128)S(1)} %get-tuple-element.79), channel_id=1, source_target_pairs={{0,2},{1,3},{2,0},{3,1},{4,6},{5,7},{6,4},{7,5},{8,10},{9,11},{10,... | collective-permute-start | bytes 491528 | tf_op jit(solution)/shard_map/ppermute | solution.py:476
  66.4 12.9 %collective-permute-start.17 = (f32[64,640]{1,0:T(8,128)S(1)}, f32[64,640]{1,0:T(8,128)S(1)}, u32[]{:S(2)}, u32[]{:S(2)}) collective-permute-start(f32[64,640]{1,0:T(8,128)S(1)} %get-tuple-element.80), channel_id=1, source_target_pairs={{0,3},{1,2},{2,1},{3,0},{4,7},{5,6},{6,5},{7,4},{8,11},{9,10},{10,... | collective-permute-start | bytes 491528 | tf_op jit(solution)/shard_map/ppermute | solution.py:476
  69.5 9.8 %collective-permute-start.18 = (f32[64,640]{1,0:T(8,128)S(1)}, f32[64,640]{1,0:T(8,128)S(1)}, u32[]{:S(2)}, u32[]{:S(2)}) collective-permute-start(f32[64,640]{1,0:T(8,128)S(1)} %get-tuple-element.81), channel_id=1, source_target_pairs={{0,4},{1,5},{2,6},{3,7},{4,0},{5,1},{6,2},{7,3},{8,12},{9,13},{10,... | collective-permute-start | bytes 491528 | tf_op jit(solution)/shard_map/ppermute | solution.py:476
  72.2 8.0 %collective-permute-start.19 = (f32[64,640]{1,0:T(8,128)S(1)}, f32[64,640]{1,0:T(8,128)S(1)}, u32[]{:S(2)}, u32[]{:S(2)}) collective-permute-start(f32[64,640]{1,0:T(8,128)S(1)} %get-tuple-element.82), channel_id=1, source_target_pairs={{0,5},{1,4},{2,7},{3,6},{4,1},{5,0},{6,3},{7,2},{8,13},{9,12},{10,... | collective-permute-start | bytes 491528 | tf_op jit(solution)/shard_map/ppermute | solution.py:476
  74.6 9.7 %collective-permute-start.20 = (f32[64,640]{1,0:T(8,128)S(1)}, f32[64,640]{1,0:T(8,128)S(1)}, u32[]{:S(2)}, u32[]{:S(2)}) collective-permute-start(f32[64,640]{1,0:T(8,128)S(1)} %get-tuple-element.83), channel_id=1, source_target_pairs={{0,6},{1,7},{2,4},{3,5},{4,2},{5,3},{6,0},{7,1},{8,14},{9,15},{10,... | collective-permute-start | bytes 491528 | tf_op jit(solution)/shard_map/ppermute | solution.py:476
  76.6 9.7 %collective-permute-start.21 = (f32[64,640]{1,0:T(8,128)S(1)}, f32[64,640]{1,0:T(8,128)S(1)}, u32[]{:S(2)}, u32[]{:S(2)}) collective-permute-start(f32[64,640]{1,0:T(8,128)S(1)} %get-tuple-element.84), channel_id=1, source_target_pairs={{0,7},{1,6},{2,5},{3,4},{4,3},{5,2},{6,1},{7,0},{8,15},{9,14},{10,... | collective-permute-start | bytes 491528 | tf_op jit(solution)/shard_map/ppermute | solution.py:476
  94.2 11.5 %all-to-all-start = ((f32[32,1,128]{2,1,0:T(1,128)}), f32[32,1,128]{2,1,0:T(1,128)S(1)}, u32[]{:S(2)}, u32[]{:S(2)}) async-start(f32[32,1,128]{2,1,0:T(1,128)} %get-tuple-element.95), calls=%async_computation | async-start | bytes 32768 | tf_op jit(solution)/shard_map/all_to_all | solution.py:616
  (38 other events, 764.9 us)

commit v11 on v10

--- a/solution.py
+++ b/solution.py
@@ -552,7 +552,7 @@
         )(*inner_args, *begun, *after)
 
     inside, feature_part, skip_part, skip_wide, *pieces, write_part, read_part = inner(
-        0, QUARTERS, [], came[1 : 1 + AFTER]
+        0, QUARTERS, [], [came[1], came[6]]
     )
     two = blocks == 2 * GROUP
     *group_sums, keeps = call(

time: 107 us -> 105 us (0.981)
  waiting for transfers between devices: 25.4 us -> 21 us
  local copies, waits for them, and re-layouts: 2.57 us -> 4.14 us
  starting transfers between devices: 40.5 us -> 41.9 us
    ppermute x22, waiting for transfers between devices: 24.8 us -> 20.4 us  [exchange(): lax.ppermute(value, 'ctx', [(k, k ^ distance) for k in range(blocks)])]
    unnamed x78, local copies, waits for them, and re-layouts: 1.98 us -> 3.55 us
    all_to_all x1, starting transfers between devices: 4.39 us -> 5.54 us  [local(): sums = jnp.sum(lax.all_to_all(sums, ('dp', 'ctx'), 0, 0), axis=(0, 1))]
where the time goes in v11:
time: 105 us
  starting transfers between devices  41.9 us (40%)
  Pallas kernels  36.7 us (35%)
  waiting for transfers between devices  21 us (20%)
  local copies, waits for them, and re-layouts  4.14 us (4%)
  between operations  1.1 us (1%)
    ppermute x22, starting transfers between devices, exchange(): lax.ppermute(value, 'ctx', [(k, k ^ distance) for k in range(blocks)])  36.4 us
    ppermute x22, waiting for transfers between devices, exchange(): lax.ppermute(value, 'ctx', [(k, k ^ distance) for k in range(blocks)])  20.4 us
    pallas_call x1, Pallas kernels, inner(): call(functools.partial(inner_kernel, offset, last), 'inner_' + str(offset...  15.2 us
    pallas_call x1, Pallas kernels, local(): call(functools.partial(finish_kernel, two), 'finish', [result, result, sm...  7.67 us
    pallas_call x1, Pallas kernels, local(): call(functools.partial(keys_kernel, two), 'keys', [tokens_result] * 2, [t...  6.51 us
    pallas_call x1, Pallas kernels, local(): call(states_kernel, 'states', [struct((2 * part + 8, width))] * GROUP + [...  6.46 us
    all_to_all x1, starting transfers between devices, local(): sums = jnp.sum(lax.all_to_all(sums, ('dp', 'ctx'), 0, 0), axis=(0, 1))  5.54 us
    unnamed x78, local copies, waits for them, and re-layouts  3.55 us
  transfers between devices with their start and end apart: 23, of which 12 were waited for; matrix products, arithmetic and copies ran while one was open for 0% of the time, Pallas kernels for 21%

profile of v11, /device:TPU:0, one launch (start us, length us, event | category | flops | bytes accessed | tf_op | source)
XLA Modules:
  0.0 104.9 jit_solution(5739090025428846194)
XLA Ops:
  0.7 6.5 %states.1 = (f32[136,640]{1,0:T(8,128)}, f32[136,640]{1,0:T(8,128)}, f32[136,640]{1,0:T(8,128)}, f32[136,640]{1,0:T(8,128)}, f32[136,640]{1,0:T(8,128)}, /*index...) custom-call(s32[1,4]{1,0:T(1,128)} %starts.3, ...), custom_call_target="tpu_custom_call" | custom-call | flops 4000000000 | bytes 1000000 | tf_op jit(solution)/shard_map/states/pallas_call | solution.py:517
  7.2 2.9 %collective-permute-start = (f32[136,640]{1,0:T(8,128)}, f32[136,640]{1,0:T(8,128)S(1)}, u32[]{:S(2)}, u32[]{:S(2)}) collective-permute-start(f32[136,640]{1,0:T(8,128)} %get-tuple-element.54), channel_id=1, source_target_pairs={{0,1},{1,0},{2,3},{3,2},{4,5},{5,4},{6,7},{7,6},{8,9},{9,8},{10,11... | collective-permute-start | bytes 1044488 | tf_op jit(solution)/shard_map/ppermute | solution.py:476
  10.1 2.5 %collective-permute-start.1 = (f32[136,640]{1,0:T(8,128)}, f32[136,640]{1,0:T(8,128)S(1)}, u32[]{:S(2)}, u32[]{:S(2)}) collective-permute-start(f32[136,640]{1,0:T(8,128)} %get-tuple-element.55), channel_id=1, source_target_pairs={{0,6},{1,7},{2,4},{3,5},{4,2},{5,3},{6,0},{7,1},{8,14},{9,15},{10,... | collective-permute-start | bytes 1044488 | tf_op jit(solution)/shard_map/ppermute | solution.py:476
  13.2 1.5 %collective-permute-start.3 = (f32[136,640]{1,0:T(8,128)}, f32[136,640]{1,0:T(8,128)S(1)}, u32[]{:S(2)}, u32[]{:S(2)}) collective-permute-start(f32[136,640]{1,0:T(8,128)} %get-tuple-element.62), channel_id=1, source_target_pairs={{0,3},{1,2},{2,1},{3,0},{4,7},{5,6},{6,5},{7,4},{8,11},{9,10},{10,... | collective-permute-start | bytes 1044488 | tf_op jit(solution)/shard_map/ppermute | solution.py:476
  15.1 4.2 %collective-permute-done.refs_0_.refs_1_ = f32[136,640]{1,0:T(8,128)S(1)} collective-permute-done((f32[136,640]{1,0:T(8,128)}, f32[136,640]{1,0:T(8,128)S(1)}, u32[]{:S(2)}, u32[]{:S(2)}) %collective-permute-start) | collective-permute-done | bytes 348192 | tf_op jit(solution)/shard_map/ppermute | solution.py:476
  19.3 3.1 %collective-permute-start.5 = (f32[136,640]{1,0:T(8,128)}, f32[136,640]{1,0:T(8,128)S(1)}, u32[]{:S(2)}, u32[]{:S(2)}) collective-permute-start(f32[136,640]{1,0:T(8,128)} %get-tuple-element.64), channel_id=1, source_target_pairs={{0,5},{1,4},{2,7},{3,6},{4,1},{5,0},{6,3},{7,2},{8,13},{9,12},{10,... | collective-permute-start | bytes 1044488 | tf_op jit(solution)/shard_map/ppermute | solution.py:476
  23.1 2.5 %collective-permute-start.6 = (f32[136,640]{1,0:T(8,128)}, f32[136,640]{1,0:T(8,128)S(1)}, u32[]{:S(2)}, u32[]{:S(2)}) collective-permute-start(f32[136,640]{1,0:T(8,128)} %get-tuple-element.65), channel_id=1, source_target_pairs={{0,7},{1,6},{2,5},{3,4},{4,3},{5,2},{6,1},{7,0},{8,15},{9,14},{10,... | collective-permute-start | bytes 1044488 | tf_op jit(solution)/shard_map/ppermute | solution.py:476
  27.5 15.2 %inner_0.1 = (f32[256,2560]{1,0:T(8,128)S(1)}, f32[256,2560]{1,0:T(8,128)S(1)}, f32[1,2560]{1,0:T(1,128)S(1)}, f32[1,2560]{1,0:T(1,128)S(1)}, bf16[256,2560]{1,0...) custom-call(s32[1,4]{1,0:T(1,128)S(1)} %copy-done.21, ...), custom_call_target="tpu_custom_call" | custom-call | flops 20000000000 | bytes 1000000 | tf_op jit(solution)/shard_map/inner_0/pallas_call | solution.py:539
  45.2 2.6 %collective-permute-start.14 = (f32[72,640]{1,0:T(8,128)S(1)}, f32[72,640]{1,0:T(8,128)S(1)}, u32[]{:S(2)}, u32[]{:S(2)}) collective-permute-start(f32[72,640]{1,0:T(8,128)S(1)} %get-tuple-element.76), channel_id=1, source_target_pairs={{0,8},{1,9},{2,10},{3,11},{4,12},{5,13},{6,14},{7,15},{8,0},{9,1},... | collective-permute-start | bytes 552968 | tf_op jit(solution)/shard_map/ppermute | solution.py:476
  48.1 2.2 %collective-permute-start.7 = (f32[64,640]{1,0:T(8,128)S(1)}, f32[64,640]{1,0:T(8,128)S(1)}, u32[]{:S(2)}, u32[]{:S(2)}) collective-permute-start(f32[64,640]{1,0:T(8,128)S(1)} %get-tuple-element.69), channel_id=1, source_target_pairs={{0,1},{1,0},{2,3},{3,2},{4,5},{5,4},{6,7},{7,6},{8,9},{9,8},{10,11... | collective-permute-start | bytes 491528 | tf_op jit(solution)/shard_map/ppermute | solution.py:476
  50.3 1.5 %collective-permute-start.9 = (f32[64,640]{1,0:T(8,128)S(1)}, f32[64,640]{1,0:T(8,128)S(1)}, u32[]{:S(2)}, u32[]{:S(2)}) collective-permute-start(f32[64,640]{1,0:T(8,128)S(1)} %get-tuple-element.71), channel_id=1, source_target_pairs={{0,3},{1,2},{2,1},{3,0},{4,7},{5,6},{6,5},{7,4},{8,11},{9,10},{10,... | collective-permute-start | bytes 491528 | tf_op jit(solution)/shard_map/ppermute | solution.py:476
  52.3 1.8 %collective-permute-done.14.refs_9_ = f32[72,640]{1,0:T(8,128)S(1)} collective-permute-done((f32[72,640]{1,0:T(8,128)S(1)}, f32[72,640]{1,0:T(8,128)S(1)}, u32[]{:S(2)}, u32[]{:S(2)}) %collective-permute-start.14) | collective-permute-done | bytes 184352 | tf_op jit(solution)/shard_map/ppermute | solution.py:476
  55.8 2.9 %collective-permute-start.12 = (f32[64,640]{1,0:T(8,128)S(1)}, f32[64,640]{1,0:T(8,128)S(1)}, u32[]{:S(2)}, u32[]{:S(2)}) collective-permute-start(f32[64,640]{1,0:T(8,128)S(1)} %get-tuple-element.74), channel_id=1, source_target_pairs={{0,6},{1,7},{2,4},{3,5},{4,2},{5,3},{6,0},{7,1},{8,14},{9,15},{10,... | collective-permute-start | bytes 491528 | tf_op jit(solution)/shard_map/ppermute | solution.py:476
  58.9 1.5 %collective-permute-start.15 = (f32[64,640]{1,0:T(8,128)S(1)}, f32[64,640]{1,0:T(8,128)S(1)}, u32[]{:S(2)}, u32[]{:S(2)}) collective-permute-start(f32[64,640]{1,0:T(8,128)S(1)} %get-tuple-element.78), channel_id=1, source_target_pairs={{0,1},{1,0},{2,3},{3,2},{4,5},{5,4},{6,7},{7,6},{8,9},{9,8},{10,11... | collective-permute-start | bytes 491528 | tf_op jit(solution)/shard_map/ppermute | solution.py:476
  60.3 2.0 %collective-permute-start.16 = (f32[64,640]{1,0:T(8,128)S(1)}, f32[64,640]{1,0:T(8,128)S(1)}, u32[]{:S(2)}, u32[]{:S(2)}) collective-permute-start(f32[64,640]{1,0:T(8,128)S(1)} %get-tuple-element.79), channel_id=1, source_target_pairs={{0,2},{1,3},{2,0},{3,1},{4,6},{5,7},{6,4},{7,5},{8,10},{9,11},{10,... | collective-permute-start | bytes 491528 | tf_op jit(solution)/shard_map/ppermute | solution.py:476
  63.2 1.9 %collective-permute-start.17 = (f32[64,640]{1,0:T(8,128)S(1)}, f32[64,640]{1,0:T(8,128)S(1)}, u32[]{:S(2)}, u32[]{:S(2)}) collective-permute-start(f32[64,640]{1,0:T(8,128)S(1)} %get-tuple-element.80), channel_id=1, source_target_pairs={{0,3},{1,2},{2,1},{3,0},{4,7},{5,6},{6,5},{7,4},{8,11},{9,10},{10,... | collective-permute-start | bytes 491528 | tf_op jit(solution)/shard_map/ppermute | solution.py:476
  65.0 2.3 %collective-permute-done.12.refs_6_ = f32[64,640]{1,0:T(8,128)S(1)} collective-permute-done((f32[64,640]{1,0:T(8,128)S(1)}, f32[64,640]{1,0:T(8,128)S(1)}, u32[]{:S(2)}, u32[]{:S(2)}) %collective-permute-start.12) | collective-permute-done | bytes 163872 | tf_op jit(solution)/shard_map/ppermute | solution.py:476
  68.3 2.5 %collective-permute-done.13.refs_7_ = f32[64,640]{1,0:T(8,128)S(1)} collective-permute-done((f32[64,640]{1,0:T(8,128)S(1)}, f32[64,640]{1,0:T(8,128)S(1)}, u32[]{:S(2)}, u32[]{:S(2)}) %collective-permute-start.13) | collective-permute-done | bytes 163872 | tf_op jit(solution)/shard_map/ppermute | solution.py:476
  73.6 3.4 %collective-permute-start.21 = (f32[64,640]{1,0:T(8,128)S(1)}, f32[64,640]{1,0:T(8,128)S(1)}, u32[]{:S(2)}, u32[]{:S(2)}) collective-permute-start(f32[64,640]{1,0:T(8,128)S(1)} %get-tuple-element.84), channel_id=1, source_target_pairs={{0,7},{1,6},{2,5},{3,4},{4,3},{5,2},{6,1},{7,0},{8,15},{9,14},{10,... | collective-permute-start | bytes 491528 | tf_op jit(solution)/shard_map/ppermute | solution.py:476
  78.1 3.0 %collective-permute-done.20.refs_14_ = f32[64,640]{1,0:T(8,128)S(1)} collective-permute-done((f32[64,640]{1,0:T(8,128)S(1)}, f32[64,640]{1,0:T(8,128)S(1)}, u32[]{:S(2)}, u32[]{:S(2)}) %collective-permute-start.20) | collective-permute-done | bytes 163872 | tf_op jit(solution)/shard_map/ppermute | solution.py:476
  81.1 2.7 %collective-permute-done.21.refs_15_ = f32[64,640]{1,0:T(8,128)S(1)} collective-permute-done((f32[64,640]{1,0:T(8,128)S(1)}, f32[64,640]{1,0:T(8,128)S(1)}, u32[]{:S(2)}, u32[]{:S(2)}) %collective-permute-start.21) | collective-permute-done | bytes 163872 | tf_op jit(solution)/shard_map/ppermute | solution.py:476
  83.8 7.7 %finish.1 = (bf16[256,2560]{1,0:T(8,128)(2,1)}, bf16[256,2560]{1,0:T(8,128)(2,1)}, f32[40,256]{1,0:T(8,128)}, f32[32,1,128]{2,1,0:T(1,128)}) custom-call(f32[40,256]{1,0:T(8,128)S(1)} %bitcast.26, f32[1,40]{1,0:T(1,128)S(1)} %bitcast.29, f32[1,40]{1,0:T(1,128)S(1)} %bitcast.31, bf16[3,256,128]{2,1,0:T(8,128)(2,1)S(1)} %copy-done.35, ...), custom_call_target="tpu_custom_call" | custom-call | flops 8000000000 | bytes 1000000 | tf_op jit(solution)/shard_map/finish/pallas_call | solution.py:588
  91.6 5.5 %all-to-all-start = ((f32[32,1,128]{2,1,0:T(1,128)}), f32[32,1,128]{2,1,0:T(1,128)S(1)}, u32[]{:S(2)}, u32[]{:S(2)}) async-start(f32[32,1,128]{2,1,0:T(1,128)} %get-tuple-element.95), calls=%async_computation | async-start | bytes 32768 | tf_op jit(solution)/shard_map/all_to_all | solution.py:616
  97.2 6.5 %keys.1 = (bf16[256,128]{1,0:T(8,128)(2,1)}, bf16[256,128]{1,0:T(8,128)(2,1)}) custom-call(f32[256,128]{1,0:T(8,128)} %copy-done.34, f32[256,128]{1,0:T(8,128)} %copy-done.38, bf16[256,2560]{1,0:T(8,128)(2,1)} %copy-done.30, bf16[256,2560]{1,0:T(8,128)(2,1)} %copy-done.31, bf16[256,2560]{1,0:T(8,128)(2,1)} %copy-done.32, bf16[256,2560]{1,0:T(8,128)(2,1)} %copy-done.33, ...), custom_call_target="tpu_custom_call" | custom-call | flops 6000000000 | bytes 1000000 | tf_op jit(solution)/shard_map/keys/pallas_call | solution.py:605
  (109 shorter events, 15.6 us)
Async XLA Ops:
  7.2 12.1 %collective-permute-start = (f32[136,640]{1,0:T(8,128)}, f32[136,640]{1,0:T(8,128)S(1)}, u32[]{:S(2)}, u32[]{:S(2)}) collective-permute-start(f32[136,640]{1,0:T(8,128)} %get-tuple-element.54), channel_id=1, source_target_pairs={{0,1},{1,0},{2,3},{3,2},{4,5},{5,4},{6,7},{7,6},{8,9},{9,8},{10,11... | collective-permute-start | bytes 1044488 | tf_op jit(solution)/shard_map/ppermute | solution.py:476
  10.1 13.0 %collective-permute-start.1 = (f32[136,640]{1,0:T(8,128)}, f32[136,640]{1,0:T(8,128)S(1)}, u32[]{:S(2)}, u32[]{:S(2)}) collective-permute-start(f32[136,640]{1,0:T(8,128)} %get-tuple-element.55), channel_id=1, source_target_pairs={{0,6},{1,7},{2,4},{3,5},{4,2},{5,3},{6,0},{7,1},{8,14},{9,15},{10,... | collective-permute-start | bytes 1044488 | tf_op jit(solution)/shard_map/ppermute | solution.py:476
  12.6 30.1 %collective-permute-start.2 = (f32[136,640]{1,0:T(8,128)}, f32[136,640]{1,0:T(8,128)S(1)}, u32[]{:S(2)}, u32[]{:S(2)}) collective-permute-start(f32[136,640]{1,0:T(8,128)} %get-tuple-element.61), channel_id=1, source_target_pairs={{0,2},{1,3},{2,0},{3,1},{4,6},{5,7},{6,4},{7,5},{8,10},{9,11},{10,... | collective-permute-start | bytes 1044488 | tf_op jit(solution)/shard_map/ppermute | solution.py:476
  13.2 30.1 %collective-permute-start.3 = (f32[136,640]{1,0:T(8,128)}, f32[136,640]{1,0:T(8,128)S(1)}, u32[]{:S(2)}, u32[]{:S(2)}) collective-permute-start(f32[136,640]{1,0:T(8,128)} %get-tuple-element.62), channel_id=1, source_target_pairs={{0,3},{1,2},{2,1},{3,0},{4,7},{5,6},{6,5},{7,4},{8,11},{9,10},{10,... | collective-permute-start | bytes 1044488 | tf_op jit(solution)/shard_map/ppermute | solution.py:476
  14.6 28.6 %collective-permute-start.4 = (f32[136,640]{1,0:T(8,128)}, f32[136,640]{1,0:T(8,128)S(1)}, u32[]{:S(2)}, u32[]{:S(2)}) collective-permute-start(f32[136,640]{1,0:T(8,128)} %get-tuple-element.63), channel_id=1, source_target_pairs={{0,4},{1,5},{2,6},{3,7},{4,0},{5,1},{6,2},{7,3},{8,12},{9,13},{10,... | collective-permute-start | bytes 1044488 | tf_op jit(solution)/shard_map/ppermute | solution.py:476
  19.3 24.0 %collective-permute-start.5 = (f32[136,640]{1,0:T(8,128)}, f32[136,640]{1,0:T(8,128)S(1)}, u32[]{:S(2)}, u32[]{:S(2)}) collective-permute-start(f32[136,640]{1,0:T(8,128)} %get-tuple-element.64), channel_id=1, source_target_pairs={{0,5},{1,4},{2,7},{3,6},{4,1},{5,0},{6,3},{7,2},{8,13},{9,12},{10,... | collective-permute-start | bytes 1044488 | tf_op jit(solution)/shard_map/ppermute | solution.py:476
  23.1 20.2 %collective-permute-start.6 = (f32[136,640]{1,0:T(8,128)}, f32[136,640]{1,0:T(8,128)S(1)}, u32[]{:S(2)}, u32[]{:S(2)}) collective-permute-start(f32[136,640]{1,0:T(8,128)} %get-tuple-element.65), channel_id=1, source_target_pairs={{0,7},{1,6},{2,5},{3,4},{4,3},{5,2},{6,1},{7,0},{8,15},{9,14},{10,... | collective-permute-start | bytes 1044488 | tf_op jit(solution)/shard_map/ppermute | solution.py:476
  45.2 8.9 %collective-permute-start.14 = (f32[72,640]{1,0:T(8,128)S(1)}, f32[72,640]{1,0:T(8,128)S(1)}, u32[]{:S(2)}, u32[]{:S(2)}) collective-permute-start(f32[72,640]{1,0:T(8,128)S(1)} %get-tuple-element.76), channel_id=1, source_target_pairs={{0,8},{1,9},{2,10},{3,11},{4,12},{5,13},{6,14},{7,15},{8,0},{9,1},... | collective-permute-start | bytes 552968 | tf_op jit(solution)/shard_map/ppermute | solution.py:476
  48.1 7.7 %collective-permute-start.7 = (f32[64,640]{1,0:T(8,128)S(1)}, f32[64,640]{1,0:T(8,128)S(1)}, u32[]{:S(2)}, u32[]{:S(2)}) collective-permute-start(f32[64,640]{1,0:T(8,128)S(1)} %get-tuple-element.69), channel_id=1, source_target_pairs={{0,1},{1,0},{2,3},{3,2},{4,5},{5,4},{6,7},{7,6},{8,9},{9,8},{10,11... | collective-permute-start | bytes 491528 | tf_op jit(solution)/shard_map/ppermute | solution.py:476
  50.3 8.5 %collective-permute-start.8 = (f32[64,640]{1,0:T(8,128)S(1)}, f32[64,640]{1,0:T(8,128)S(1)}, u32[]{:S(2)}, u32[]{:S(2)}) collective-permute-start(f32[64,640]{1,0:T(8,128)S(1)} %get-tuple-element.70), channel_id=1, source_target_pairs={{0,2},{1,3},{2,0},{3,1},{4,6},{5,7},{6,4},{7,5},{8,10},{9,11},{10,... | collective-permute-start | bytes 491528 | tf_op jit(solution)/shard_map/ppermute | solution.py:476
  50.3 8.6 %collective-permute-start.9 = (f32[64,640]{1,0:T(8,128)S(1)}, f32[64,640]{1,0:T(8,128)S(1)}, u32[]{:S(2)}, u32[]{:S(2)}) collective-permute-start(f32[64,640]{1,0:T(8,128)S(1)} %get-tuple-element.71), channel_id=1, source_target_pairs={{0,3},{1,2},{2,1},{3,0},{4,7},{5,6},{6,5},{7,4},{8,11},{9,10},{10,... | collective-permute-start | bytes 491528 | tf_op jit(solution)/shard_map/ppermute | solution.py:476
  51.8 8.5 %collective-permute-start.10 = (f32[64,640]{1,0:T(8,128)S(1)}, f32[64,640]{1,0:T(8,128)S(1)}, u32[]{:S(2)}, u32[]{:S(2)}) collective-permute-start(f32[64,640]{1,0:T(8,128)S(1)} %get-tuple-element.72), channel_id=1, source_target_pairs={{0,4},{1,5},{2,6},{3,7},{4,0},{5,1},{6,2},{7,3},{8,12},{9,13},{10,... | collective-permute-start | bytes 491528 | tf_op jit(solution)/shard_map/ppermute | solution.py:476
  54.1 9.0 %collective-permute-start.11 = (f32[64,640]{1,0:T(8,128)S(1)}, f32[64,640]{1,0:T(8,128)S(1)}, u32[]{:S(2)}, u32[]{:S(2)}) collective-permute-start(f32[64,640]{1,0:T(8,128)S(1)} %get-tuple-element.73), channel_id=1, source_target_pairs={{0,5},{1,4},{2,7},{3,6},{4,1},{5,0},{6,3},{7,2},{8,13},{9,12},{10,... | collective-permute-start | bytes 491528 | tf_op jit(solution)/shard_map/ppermute | solution.py:476
  55.8 35.7 %copy-start.28 = (f32[64,640]{1,0:T(8,128)}, f32[64,640]{1,0:T(8,128)S(1)}, u32[]{:S(2)}) copy-start(f32[64,640]{1,0:T(8,128)S(1)} %get-tuple-element.77.refs_8_) | copy-start | bytes 491524
  55.8 11.5 %collective-permute-start.12 = (f32[64,640]{1,0:T(8,128)S(1)}, f32[64,640]{1,0:T(8,128)S(1)}, u32[]{:S(2)}, u32[]{:S(2)}) collective-permute-start(f32[64,640]{1,0:T(8,128)S(1)} %get-tuple-element.74), channel_id=1, source_target_pairs={{0,6},{1,7},{2,4},{3,5},{4,2},{5,3},{6,0},{7,1},{8,14},{9,15},{10,... | collective-permute-start | bytes 491528 | tf_op jit(solution)/shard_map/ppermute | solution.py:476
  58.8 12.0 %collective-permute-start.13 = (f32[64,640]{1,0:T(8,128)S(1)}, f32[64,640]{1,0:T(8,128)S(1)}, u32[]{:S(2)}, u32[]{:S(2)}) collective-permute-start(f32[64,640]{1,0:T(8,128)S(1)} %get-tuple-element.75), channel_id=1, source_target_pairs={{0,7},{1,6},{2,5},{3,4},{4,3},{5,2},{6,1},{7,0},{8,15},{9,14},{10,... | collective-permute-start | bytes 491528 | tf_op jit(solution)/shard_map/ppermute | solution.py:476
  58.9 13.2 %collective-permute-start.15 = (f32[64,640]{1,0:T(8,128)S(1)}, f32[64,640]{1,0:T(8,128)S(1)}, u32[]{:S(2)}, u32[]{:S(2)}) collective-permute-start(f32[64,640]{1,0:T(8,128)S(1)} %get-tuple-element.78), channel_id=1, source_target_pairs={{0,1},{1,0},{2,3},{3,2},{4,5},{5,4},{6,7},{7,6},{8,9},{9,8},{10,11... | collective-permute-start | bytes 491528 | tf_op jit(solution)/shard_map/ppermute | solution.py:476
  60.3 13.3 %collective-permute-start.16 = (f32[64,640]{1,0:T(8,128)S(1)}, f32[64,640]{1,0:T(8,128)S(1)}, u32[]{:S(2)}, u32[]{:S(2)}) collective-permute-start(f32[64,640]{1,0:T(8,128)S(1)} %get-tuple-element.79), channel_id=1, source_target_pairs={{0,2},{1,3},{2,0},{3,1},{4,6},{5,7},{6,4},{7,5},{8,10},{9,11},{10,... | collective-permute-start | bytes 491528 | tf_op jit(solution)/shard_map/ppermute | solution.py:476
  63.2 13.9 %collective-permute-start.17 = (f32[64,640]{1,0:T(8,128)S(1)}, f32[64,640]{1,0:T(8,128)S(1)}, u32[]{:S(2)}, u32[]{:S(2)}) collective-permute-start(f32[64,640]{1,0:T(8,128)S(1)} %get-tuple-element.80), channel_id=1, source_target_pairs={{0,3},{1,2},{2,1},{3,0},{4,7},{5,6},{6,5},{7,4},{8,11},{9,10},{10,... | collective-permute-start | bytes 491528 | tf_op jit(solution)/shard_map/ppermute | solution.py:476
  67.3 9.7 %collective-permute-start.18 = (f32[64,640]{1,0:T(8,128)S(1)}, f32[64,640]{1,0:T(8,128)S(1)}, u32[]{:S(2)}, u32[]{:S(2)}) collective-permute-start(f32[64,640]{1,0:T(8,128)S(1)} %get-tuple-element.81), channel_id=1, source_target_pairs={{0,4},{1,5},{2,6},{3,7},{4,0},{5,1},{6,2},{7,3},{8,12},{9,13},{10,... | collective-permute-start | bytes 491528 | tf_op jit(solution)/shard_map/ppermute | solution.py:476
  70.8 7.3 %collective-permute-start.19 = (f32[64,640]{1,0:T(8,128)S(1)}, f32[64,640]{1,0:T(8,128)S(1)}, u32[]{:S(2)}, u32[]{:S(2)}) collective-permute-start(f32[64,640]{1,0:T(8,128)S(1)} %get-tuple-element.82), channel_id=1, source_target_pairs={{0,5},{1,4},{2,7},{3,6},{4,1},{5,0},{6,3},{7,2},{8,13},{9,12},{10,... | collective-permute-start | bytes 491528 | tf_op jit(solution)/shard_map/ppermute | solution.py:476
  72.0 9.1 %collective-permute-start.20 = (f32[64,640]{1,0:T(8,128)S(1)}, f32[64,640]{1,0:T(8,128)S(1)}, u32[]{:S(2)}, u32[]{:S(2)}) collective-permute-start(f32[64,640]{1,0:T(8,128)S(1)} %get-tuple-element.83), channel_id=1, source_target_pairs={{0,6},{1,7},{2,4},{3,5},{4,2},{5,3},{6,0},{7,1},{8,14},{9,15},{10,... | collective-permute-start | bytes 491528 | tf_op jit(solution)/shard_map/ppermute | solution.py:476
  73.6 10.1 %collective-permute-start.21 = (f32[64,640]{1,0:T(8,128)S(1)}, f32[64,640]{1,0:T(8,128)S(1)}, u32[]{:S(2)}, u32[]{:S(2)}) collective-permute-start(f32[64,640]{1,0:T(8,128)S(1)} %get-tuple-element.84), channel_id=1, source_target_pairs={{0,7},{1,6},{2,5},{3,4},{4,3},{5,2},{6,1},{7,0},{8,15},{9,14},{10,... | collective-permute-start | bytes 491528 | tf_op jit(solution)/shard_map/ppermute | solution.py:476
  91.6 12.7 %all-to-all-start = ((f32[32,1,128]{2,1,0:T(1,128)}), f32[32,1,128]{2,1,0:T(1,128)S(1)}, u32[]{:S(2)}, u32[]{:S(2)}) async-start(f32[32,1,128]{2,1,0:T(1,128)} %get-tuple-element.95), calls=%async_computation | async-start | bytes 32768 | tf_op jit(solution)/shard_map/all_to_all | solution.py:616
  (38 other events, 751.5 us)

commit v12 on v11

--- a/solution.py
+++ b/solution.py
@@ -21,7 +21,7 @@
 VMEM = pl.BlockSpec(memory_space=pltpu.VMEM)
 SMEM = pl.BlockSpec(memory_space=pltpu.SMEM)
 ANY = pl.BlockSpec(memory_space=pl.ANY)
-WIDE_PARTS = 8
+WIDE_PARTS = 4
 AFTER = 2
 CUM, WEIGHT, FACTOR = 0, 1, 2
 STRIDE, LOG = 1, 2
@@ -156,7 +156,7 @@
         before, refs = refs[0], refs[1 + WIDE_PARTS + AFTER :]
     else:
         refs = refs[AFTER:]
-    inside, feature_part, skip_part, skip_wide, write_high, write_low, read_high, read_low = refs[:WIDE_PARTS]
+    inside, feature_part, skip_part, skip_wide = refs[:WIDE_PARTS]
     results = refs[WIDE_PARTS:-3]
     scores_ref, mask_ref, grad_ref = refs[-3:]
     length, width = features.shape
@@ -177,9 +177,6 @@
         grad_ref[...] = before[...] if offset else jnp.zeros_like(grad_ref)
 
     skip_wide[...] = wide_skip(skip, heads, spread_ref[...])
-    write_high[...], write_low[...] = split2(matmul(cols_ref[WEIGHT], spread_ref[...]) * features[...].astype(F32))
-    read_high[...], read_low[...] = split2(matmul(cols_ref[FACTOR], spread_ref[...]) * cotangent[...].astype(F32))
-
     def one_pair(at, carry):
         cols = pl.ds(pl.multiple_of(at * pair, LANES), pair)
         feature = features[:, cols]
@@ -415,7 +412,7 @@
         sums[...] = jnp.broadcast_to(table[None], sums.shape)
 
 
-def keys_kernel(two, write_part, read_part, write_high, write_low, read_high, read_low, *refs):
+def keys_kernel(two, write_part, read_part, cols_ref, spread_ref, features, cotangent, *refs):
     write_grad, read_grad, write_acc, read_acc, have, back_have = refs[2 * GROUP + 1 :]
     state = write_part.shape[1]
     step = pl.program_id(0)
@@ -426,12 +423,13 @@
         read_acc[...] = jnp.zeros_like(read_acc)
         both_sets(two, refs, have, back_have)
 
-    for states, high, low, acc in (
-        (have, read_high, read_low, read_acc),
-        (back_have, write_high, write_low, write_acc),
+    for states, scale, wide, acc in (
+        (have, FACTOR, cotangent, read_acc),
+        (back_have, WEIGHT, features, write_acc),
     ):
         stack = jnp.concatenate(split2(quarter_rows(states, step)), axis=0)
-        acc[...] += matmul_nt(high[...], stack) + matmul_nt(low[...], stack)
+        high, low = split2(matmul(cols_ref[scale], spread_ref[...]) * wide[...].astype(F32))
+        acc[...] += matmul_nt(high, stack) + matmul_nt(low, stack)
 
     @pl.when(step == QUARTERS - 1)
     def _():
@@ -526,8 +524,7 @@
     came = swap(out[:GROUP])
     cols, head_rows = out[GROUP:]
 
-    wide_part, wide_piece = struct((length, wide)), struct((length, wide), BF16)
-    wide_parts = [wide_part] * 2 + [struct((1, wide))] * 2 + [wide_piece] * 4
+    wide_parts = [struct((length, wide))] * 2 + [struct((1, wide))] * 2
     token_part = struct((length, state))
     square = all_of(length, length)
     inner_args = (doc_starts, cols, head_rows, features, cotangent, writes, reads, skip, spread)
@@ -546,12 +543,12 @@
             5 * count,
             24,
             grid=(count,),
-            out_specs=[mine, mine, thin, thin] + [mine] * 4 + ([tokens] * 2 if last else [square]),
+            out_specs=[mine, mine, thin, thin] + ([tokens] * 2 if last else [square]),
             scratch_shapes=[pltpu.VMEM((length, length), F32)] * 3,
             input_output_aliases={n_args + at: at for at in range(WIDE_PARTS)} if offset else {},
         )(*inner_args, *begun, *after)
 
-    inside, feature_part, skip_part, skip_wide, *pieces, write_part, read_part = inner(
+    inside, feature_part, skip_part, skip_wide, write_part, read_part = inner(
         0, QUARTERS, [], [came[1], came[6]]
     )
     two = blocks == 2 * GROUP
@@ -606,13 +603,13 @@
         functools.partial(keys_kernel, two),
         "keys",
         [tokens_result] * 2,
-        [tokens] * 2 + [by_quarter] * 4 + whole_shares * 2 + [ANY],
+        [tokens] * 2 + [all_cols, spread_quarter] + [by_quarter] * 2 + whole_shares * 2 + [ANY],
         6,
         60,
         grid=(QUARTERS,),
         out_specs=[tokens] * 2,
         scratch_shapes=[pltpu.VMEM((length, 2 * state), F32)] * 2 + [shares] * 2,
-    )(write_part, read_part, *pieces, *sets, step_grad)
+    )(write_part, read_part, cols, spread, features, cotangent, *sets, step_grad)
     sums = jnp.sum(lax.all_to_all(sums, ("dp", "ctx"), 0, 0), axis=(0, 1))
     return (
         mixed[None],

time: 105 us -> 106 us (level)
  waiting for transfers between devices: 21 us -> 23.6 us
  local copies, waits for them, and re-layouts: 4.14 us -> 2.54 us
    ppermute x22, waiting for transfers between devices: 20.4 us -> 23.6 us  [exchange(): lax.ppermute(value, 'ctx', [(k, k ^ distance) for k in range(blocks)])]
    unnamed x78 -> x66, local copies, waits for them, and re-layouts: 3.55 us -> 1.95 us
    pallas_call x1, Pallas kernels: 15.2 us -> 13.7 us  [inner(): call(functools.partial(inner_kernel, offset, last), 'inner_' + str(offset...]
    pallas_call x1, Pallas kernels: 6.51 us -> 7.7 us  [local(): call(functools.partial(keys_kernel, two), 'keys', [tokens_result] * 2, [t...]
  transfers between devices with their start and end apart: 23 -> 23, of which waited for: 12 -> 10; matrix products, arithmetic and copies ran while one was open for 0% -> 0% of each run, Pallas kernels for 21% -> 21%
where the time goes in v12:
time: 106 us; the launch traced here: 105 us
  starting transfers between devices  41.8 us (39%)
  Pallas kernels  36.4 us (34%)
  waiting for transfers between devices  23.6 us (22%)
  local copies, waits for them, and re-layouts  2.54 us (2%)
    ppermute x22, starting transfers between devices, exchange(): lax.ppermute(value, 'ctx', [(k, k ^ distance) for k in range(blocks)])  36.3 us
    ppermute x22, waiting for transfers between devices, exchange(): lax.ppermute(value, 'ctx', [(k, k ^ distance) for k in range(blocks)])  23.6 us
    pallas_call x1, Pallas kernels, inner(): call(functools.partial(inner_kernel, offset, last), 'inner_' + str(offset...  13.7 us
    pallas_call x1, Pallas kernels, local(): call(functools.partial(keys_kernel, two), 'keys', [tokens_result] * 2, [t...  7.7 us
    pallas_call x1, Pallas kernels, local(): call(functools.partial(finish_kernel, two), 'finish', [result, result, sm...  7.64 us
    pallas_call x1, Pallas kernels, local(): call(states_kernel, 'states', [struct((2 * part + 8, width))] * GROUP + [...  6.47 us
    all_to_all x1, starting transfers between devices, local(): sums = jnp.sum(lax.all_to_all(sums, ('dp', 'ctx'), 0, 0), axis=(0, 1))  5.46 us
  transfers between devices with their start and end apart: 23, of which 10 were waited for; matrix products, arithmetic and copies ran while one was open for 0% of the time, Pallas kernels for 21%

profile of v12, /device:TPU:0, one launch (start us, length us, event | category | flops | bytes accessed | tf_op | source)
XLA Modules:
  0.0 105.5 jit_solution(17149868633672819719)
XLA Ops:
  0.7 6.5 %states.1 = (f32[136,640]{1,0:T(8,128)}, f32[136,640]{1,0:T(8,128)}, f32[136,640]{1,0:T(8,128)}, f32[136,640]{1,0:T(8,128)}, f32[136,640]{1,0:T(8,128)}, /*index...) custom-call(s32[1,4]{1,0:T(1,128)} %starts.3, ...), custom_call_target="tpu_custom_call" | custom-call | flops 4000000000 | bytes 1000000 | tf_op jit(solution)/shard_map/states/pallas_call | solution.py:515
  7.2 3.0 %collective-permute-start = (f32[136,640]{1,0:T(8,128)}, f32[136,640]{1,0:T(8,128)S(1)}, u32[]{:S(2)}, u32[]{:S(2)}) collective-permute-start(f32[136,640]{1,0:T(8,128)} %get-tuple-element.50), channel_id=1, source_target_pairs={{0,1},{1,0},{2,3},{3,2},{4,5},{5,4},{6,7},{7,6},{8,9},{9,8},{10,11... | collective-permute-start | bytes 1044488 | tf_op jit(solution)/shard_map/ppermute | solution.py:474
  10.1 2.5 %collective-permute-start.1 = (f32[136,640]{1,0:T(8,128)}, f32[136,640]{1,0:T(8,128)S(1)}, u32[]{:S(2)}, u32[]{:S(2)}) collective-permute-start(f32[136,640]{1,0:T(8,128)} %get-tuple-element.51), channel_id=1, source_target_pairs={{0,6},{1,7},{2,4},{3,5},{4,2},{5,3},{6,0},{7,1},{8,14},{9,15},{10,... | collective-permute-start | bytes 1044488 | tf_op jit(solution)/shard_map/ppermute | solution.py:474
  15.1 4.2 %collective-permute-done.refs_0_.refs_1_ = f32[136,640]{1,0:T(8,128)S(1)} collective-permute-done((f32[136,640]{1,0:T(8,128)}, f32[136,640]{1,0:T(8,128)S(1)}, u32[]{:S(2)}, u32[]{:S(2)}) %collective-permute-start) | collective-permute-done | bytes 348192 | tf_op jit(solution)/shard_map/ppermute | solution.py:474
  19.3 3.1 %collective-permute-start.5 = (f32[136,640]{1,0:T(8,128)}, f32[136,640]{1,0:T(8,128)S(1)}, u32[]{:S(2)}, u32[]{:S(2)}) collective-permute-start(f32[136,640]{1,0:T(8,128)} %get-tuple-element.60), channel_id=1, source_target_pairs={{0,5},{1,4},{2,7},{3,6},{4,1},{5,0},{6,3},{7,2},{8,13},{9,12},{10,... | collective-permute-start | bytes 1044488 | tf_op jit(solution)/shard_map/ppermute | solution.py:474
  23.1 2.5 %collective-permute-start.6 = (f32[136,640]{1,0:T(8,128)}, f32[136,640]{1,0:T(8,128)S(1)}, u32[]{:S(2)}, u32[]{:S(2)}) collective-permute-start(f32[136,640]{1,0:T(8,128)} %get-tuple-element.61), channel_id=1, source_target_pairs={{0,7},{1,6},{2,5},{3,4},{4,3},{5,2},{6,1},{7,0},{8,15},{9,14},{10,... | collective-permute-start | bytes 1044488 | tf_op jit(solution)/shard_map/ppermute | solution.py:474
  27.5 13.7 %inner_0.1 = (f32[256,2560]{1,0:T(8,128)S(1)}, f32[256,2560]{1,0:T(8,128)S(1)}, f32[1,2560]{1,0:T(1,128)S(1)}, f32[1,2560]{1,0:T(1,128)S(1)}, f32[256,128]{1,0:T(8,128)S(1)}, /*index=5*/f32[256,128]{1,0:T(8,128)S(1)}) custom-call(s32[1,4]{1,0:T(1,128)S(1)} %copy-done.19, bf16[3,256,128]{2,1,0:T(8,128)(2,1)S(1)} %copy-done.29, f32[3,40,256]{2,1,0:T(8,128)S(1)} %copy-done.31, ...), custom_call_target="tpu_custom_call" | custom-call | flops 20000000000 | bytes 1000000 | tf_op jit(solution)/shard_map/inner_0/pallas_call | solution.py:536
  41.2 2.0 %collective-permute-done.3.refs_3_ = f32[136,640]{1,0:T(8,128)S(1)} collective-permute-done((f32[136,640]{1,0:T(8,128)}, f32[136,640]{1,0:T(8,128)S(1)}, u32[]{:S(2)}, u32[]{:S(2)}) %collective-permute-start.3) | collective-permute-done | bytes 348192 | tf_op jit(solution)/shard_map/ppermute | solution.py:474
  43.6 2.7 %collective-permute-start.14 = (f32[72,640]{1,0:T(8,128)S(1)}, f32[72,640]{1,0:T(8,128)S(1)}, u32[]{:S(2)}, u32[]{:S(2)}) collective-permute-start(f32[72,640]{1,0:T(8,128)S(1)} %get-tuple-element.72), channel_id=1, source_target_pairs={{0,8},{1,9},{2,10},{3,11},{4,12},{5,13},{6,14},{7,15},{8,0},{9,1},... | collective-permute-start | bytes 552968 | tf_op jit(solution)/shard_map/ppermute | solution.py:474
  48.2 2.0 %collective-permute-start.8 = (f32[64,640]{1,0:T(8,128)S(1)}, f32[64,640]{1,0:T(8,128)S(1)}, u32[]{:S(2)}, u32[]{:S(2)}) collective-permute-start(f32[64,640]{1,0:T(8,128)S(1)} %get-tuple-element.66), channel_id=1, source_target_pairs={{0,2},{1,3},{2,0},{3,1},{4,6},{5,7},{6,4},{7,5},{8,10},{9,11},{10,... | collective-permute-start | bytes 491528 | tf_op jit(solution)/shard_map/ppermute | solution.py:474
  51.8 2.3 %collective-permute-done.14.refs_9_ = f32[72,640]{1,0:T(8,128)S(1)} collective-permute-done((f32[72,640]{1,0:T(8,128)S(1)}, f32[72,640]{1,0:T(8,128)S(1)}, u32[]{:S(2)}, u32[]{:S(2)}) %collective-permute-start.14) | collective-permute-done | bytes 184352 | tf_op jit(solution)/shard_map/ppermute | solution.py:474
  55.8 2.9 %collective-permute-start.12 = (f32[64,640]{1,0:T(8,128)S(1)}, f32[64,640]{1,0:T(8,128)S(1)}, u32[]{:S(2)}, u32[]{:S(2)}) collective-permute-start(f32[64,640]{1,0:T(8,128)S(1)} %get-tuple-element.70), channel_id=1, source_target_pairs={{0,6},{1,7},{2,4},{3,5},{4,2},{5,3},{6,0},{7,1},{8,14},{9,15},{10,... | collective-permute-start | bytes 491528 | tf_op jit(solution)/shard_map/ppermute | solution.py:474
  58.8 1.8 %collective-permute-start.15 = (f32[64,640]{1,0:T(8,128)S(1)}, f32[64,640]{1,0:T(8,128)S(1)}, u32[]{:S(2)}, u32[]{:S(2)}) collective-permute-start(f32[64,640]{1,0:T(8,128)S(1)} %get-tuple-element.74), channel_id=1, source_target_pairs={{0,1},{1,0},{2,3},{3,2},{4,5},{5,4},{6,7},{7,6},{8,9},{9,8},{10,11... | collective-permute-start | bytes 491528 | tf_op jit(solution)/shard_map/ppermute | solution.py:474
  60.6 1.7 %collective-permute-start.16 = (f32[64,640]{1,0:T(8,128)S(1)}, f32[64,640]{1,0:T(8,128)S(1)}, u32[]{:S(2)}, u32[]{:S(2)}) collective-permute-start(f32[64,640]{1,0:T(8,128)S(1)} %get-tuple-element.75), channel_id=1, source_target_pairs={{0,2},{1,3},{2,0},{3,1},{4,6},{5,7},{6,4},{7,5},{8,10},{9,11},{10,... | collective-permute-start | bytes 491528 | tf_op jit(solution)/shard_map/ppermute | solution.py:474
  62.3 2.7 %collective-permute-start.17 = (f32[64,640]{1,0:T(8,128)S(1)}, f32[64,640]{1,0:T(8,128)S(1)}, u32[]{:S(2)}, u32[]{:S(2)}) collective-permute-start(f32[64,640]{1,0:T(8,128)S(1)} %get-tuple-element.76), channel_id=1, source_target_pairs={{0,3},{1,2},{2,1},{3,0},{4,7},{5,6},{6,5},{7,4},{8,11},{9,10},{10,... | collective-permute-start | bytes 491528 | tf_op jit(solution)/shard_map/ppermute | solution.py:474
  65.0 2.2 %collective-permute-done.12.refs_6_ = f32[64,640]{1,0:T(8,128)S(1)} collective-permute-done((f32[64,640]{1,0:T(8,128)S(1)}, f32[64,640]{1,0:T(8,128)S(1)}, u32[]{:S(2)}, u32[]{:S(2)}) %collective-permute-start.12) | collective-permute-done | bytes 163872 | tf_op jit(solution)/shard_map/ppermute | solution.py:474
  68.3 2.6 %collective-permute-done.13.refs_7_ = f32[64,640]{1,0:T(8,128)S(1)} collective-permute-done((f32[64,640]{1,0:T(8,128)S(1)}, f32[64,640]{1,0:T(8,128)S(1)}, u32[]{:S(2)}, u32[]{:S(2)}) %collective-permute-start.13) | collective-permute-done | bytes 163872 | tf_op jit(solution)/shard_map/ppermute | solution.py:474
  72.5 3.1 %collective-permute-done.16.refs_10_ = f32[64,640]{1,0:T(8,128)S(1)} collective-permute-done((f32[64,640]{1,0:T(8,128)S(1)}, f32[64,640]{1,0:T(8,128)S(1)}, u32[]{:S(2)}, u32[]{:S(2)}) %collective-permute-start.16) | collective-permute-done | bytes 163872 | tf_op jit(solution)/shard_map/ppermute | solution.py:474
  75.6 1.7 %collective-permute-start.21 = (f32[64,640]{1,0:T(8,128)S(1)}, f32[64,640]{1,0:T(8,128)S(1)}, u32[]{:S(2)}, u32[]{:S(2)}) collective-permute-start(f32[64,640]{1,0:T(8,128)S(1)} %get-tuple-element.80), channel_id=1, source_target_pairs={{0,7},{1,6},{2,5},{3,4},{4,3},{5,2},{6,1},{7,0},{8,15},{9,14},{10,... | collective-permute-start | bytes 491528 | tf_op jit(solution)/shard_map/ppermute | solution.py:474
  78.1 2.2 %collective-permute-done.20.refs_14_ = f32[64,640]{1,0:T(8,128)S(1)} collective-permute-done((f32[64,640]{1,0:T(8,128)S(1)}, f32[64,640]{1,0:T(8,128)S(1)}, u32[]{:S(2)}, u32[]{:S(2)}) %collective-permute-start.20) | collective-permute-done | bytes 163872 | tf_op jit(solution)/shard_map/ppermute | solution.py:474
  80.4 3.4 %collective-permute-done.21.refs_15_ = f32[64,640]{1,0:T(8,128)S(1)} collective-permute-done((f32[64,640]{1,0:T(8,128)S(1)}, f32[64,640]{1,0:T(8,128)S(1)}, u32[]{:S(2)}, u32[]{:S(2)}) %collective-permute-start.21) | collective-permute-done | bytes 163872 | tf_op jit(solution)/shard_map/ppermute | solution.py:474
  83.9 7.6 %finish.1 = (bf16[256,2560]{1,0:T(8,128)(2,1)}, bf16[256,2560]{1,0:T(8,128)(2,1)}, f32[40,256]{1,0:T(8,128)}, f32[32,1,128]{2,1,0:T(1,128)}) custom-call(f32[40,256]{1,0:T(8,128)S(1)} %bitcast.28, f32[1,40]{1,0:T(1,128)S(1)} %bitcast.31, f32[1,40]{1,0:T(1,128)S(1)} %bitcast.33, bf16[3,256,128]{2,1,0:T(8,128)(2,1)S(1)} %copy-done.30, ...), custom_call_target="tpu_custom_call" | custom-call | flops 8000000000 | bytes 1000000 | tf_op jit(solution)/shard_map/finish/pallas_call | solution.py:585
  91.6 5.5 %all-to-all-start = ((f32[32,1,128]{2,1,0:T(1,128)}), f32[32,1,128]{2,1,0:T(1,128)S(1)}, u32[]{:S(2)}, u32[]{:S(2)}) async-start(f32[32,1,128]{2,1,0:T(1,128)} %get-tuple-element.87), calls=%async_computation | async-start | bytes 32768 | tf_op jit(solution)/shard_map/all_to_all | solution.py:613
  97.1 7.7 %keys.1 = (bf16[256,128]{1,0:T(8,128)(2,1)}, bf16[256,128]{1,0:T(8,128)(2,1)}) custom-call(f32[256,128]{1,0:T(8,128)} %copy-done.28, f32[256,128]{1,0:T(8,128)} %copy-done.32, bf16[3,256,128]{2,1,0:T(8,128)(2,1)} %get-tuple-element.48.cols_ref, bf16[128,2560]{1,0:T(8,128)(2,1)} %constant.4.clone.spread_ref, bf16[256,2560]{1,0:T(8,128)(2,1)} %bitcast.14, ...), custom_call_target="tpu_custom_call" | custom-call | flops 6000000000 | bytes 1000000 | tf_op jit(solution)/shard_map/keys/pallas_call | solution.py:602
  (97 shorter events, 14.9 us)
Async XLA Ops:
  7.2 12.1 %collective-permute-start = (f32[136,640]{1,0:T(8,128)}, f32[136,640]{1,0:T(8,128)S(1)}, u32[]{:S(2)}, u32[]{:S(2)}) collective-permute-start(f32[136,640]{1,0:T(8,128)} %get-tuple-element.50), channel_id=1, source_target_pairs={{0,1},{1,0},{2,3},{3,2},{4,5},{5,4},{6,7},{7,6},{8,9},{9,8},{10,11... | collective-permute-start | bytes 1044488 | tf_op jit(solution)/shard_map/ppermute | solution.py:474
  10.1 13.0 %collective-permute-start.1 = (f32[136,640]{1,0:T(8,128)}, f32[136,640]{1,0:T(8,128)S(1)}, u32[]{:S(2)}, u32[]{:S(2)}) collective-permute-start(f32[136,640]{1,0:T(8,128)} %get-tuple-element.51), channel_id=1, source_target_pairs={{0,6},{1,7},{2,4},{3,5},{4,2},{5,3},{6,0},{7,1},{8,14},{9,15},{10,... | collective-permute-start | bytes 1044488 | tf_op jit(solution)/shard_map/ppermute | solution.py:474
  12.7 28.6 %collective-permute-start.2 = (f32[136,640]{1,0:T(8,128)}, f32[136,640]{1,0:T(8,128)S(1)}, u32[]{:S(2)}, u32[]{:S(2)}) collective-permute-start(f32[136,640]{1,0:T(8,128)} %get-tuple-element.57), channel_id=1, source_target_pairs={{0,2},{1,3},{2,0},{3,1},{4,6},{5,7},{6,4},{7,5},{8,10},{9,11},{10,... | collective-permute-start | bytes 1044488 | tf_op jit(solution)/shard_map/ppermute | solution.py:474
  13.2 30.1 %collective-permute-start.3 = (f32[136,640]{1,0:T(8,128)}, f32[136,640]{1,0:T(8,128)S(1)}, u32[]{:S(2)}, u32[]{:S(2)}) collective-permute-start(f32[136,640]{1,0:T(8,128)} %get-tuple-element.58), channel_id=1, source_target_pairs={{0,3},{1,2},{2,1},{3,0},{4,7},{5,6},{6,5},{7,4},{8,11},{9,10},{10,... | collective-permute-start | bytes 1044488 | tf_op jit(solution)/shard_map/ppermute | solution.py:474
  14.7 28.6 %collective-permute-start.4 = (f32[136,640]{1,0:T(8,128)}, f32[136,640]{1,0:T(8,128)S(1)}, u32[]{:S(2)}, u32[]{:S(2)}) collective-permute-start(f32[136,640]{1,0:T(8,128)} %get-tuple-element.59), channel_id=1, source_target_pairs={{0,4},{1,5},{2,6},{3,7},{4,0},{5,1},{6,2},{7,3},{8,12},{9,13},{10,... | collective-permute-start | bytes 1044488 | tf_op jit(solution)/shard_map/ppermute | solution.py:474
  19.3 24.0 %collective-permute-start.5 = (f32[136,640]{1,0:T(8,128)}, f32[136,640]{1,0:T(8,128)S(1)}, u32[]{:S(2)}, u32[]{:S(2)}) collective-permute-start(f32[136,640]{1,0:T(8,128)} %get-tuple-element.60), channel_id=1, source_target_pairs={{0,5},{1,4},{2,7},{3,6},{4,1},{5,0},{6,3},{7,2},{8,13},{9,12},{10,... | collective-permute-start | bytes 1044488 | tf_op jit(solution)/shard_map/ppermute | solution.py:474
  23.1 20.1 %collective-permute-start.6 = (f32[136,640]{1,0:T(8,128)}, f32[136,640]{1,0:T(8,128)S(1)}, u32[]{:S(2)}, u32[]{:S(2)}) collective-permute-start(f32[136,640]{1,0:T(8,128)} %get-tuple-element.61), channel_id=1, source_target_pairs={{0,7},{1,6},{2,5},{3,4},{4,3},{5,2},{6,1},{7,0},{8,15},{9,14},{10,... | collective-permute-start | bytes 1044488 | tf_op jit(solution)/shard_map/ppermute | solution.py:474
  43.6 10.4 %collective-permute-start.14 = (f32[72,640]{1,0:T(8,128)S(1)}, f32[72,640]{1,0:T(8,128)S(1)}, u32[]{:S(2)}, u32[]{:S(2)}) collective-permute-start(f32[72,640]{1,0:T(8,128)S(1)} %get-tuple-element.72), channel_id=1, source_target_pairs={{0,8},{1,9},{2,10},{3,11},{4,12},{5,13},{6,14},{7,15},{8,0},{9,1},... | collective-permute-start | bytes 552968 | tf_op jit(solution)/shard_map/ppermute | solution.py:474
  46.7 37.1 %copy-start.27 = (f32[64,640]{1,0:T(8,128)}, f32[64,640]{1,0:T(8,128)S(1)}, u32[]{:S(2)}) copy-start(f32[64,640]{1,0:T(8,128)S(1)} %get-tuple-element.64.refs_0_) | copy-start | bytes 491524
  46.7 9.1 %collective-permute-start.7 = (f32[64,640]{1,0:T(8,128)S(1)}, f32[64,640]{1,0:T(8,128)S(1)}, u32[]{:S(2)}, u32[]{:S(2)}) collective-permute-start(f32[64,640]{1,0:T(8,128)S(1)} %get-tuple-element.65), channel_id=1, source_target_pairs={{0,1},{1,0},{2,3},{3,2},{4,5},{5,4},{6,7},{7,6},{8,9},{9,8},{10,11... | collective-permute-start | bytes 491528 | tf_op jit(solution)/shard_map/ppermute | solution.py:474
  48.2 10.5 %collective-permute-start.8 = (f32[64,640]{1,0:T(8,128)S(1)}, f32[64,640]{1,0:T(8,128)S(1)}, u32[]{:S(2)}, u32[]{:S(2)}) collective-permute-start(f32[64,640]{1,0:T(8,128)S(1)} %get-tuple-element.66), channel_id=1, source_target_pairs={{0,2},{1,3},{2,0},{3,1},{4,6},{5,7},{6,4},{7,5},{8,10},{9,11},{10,... | collective-permute-start | bytes 491528 | tf_op jit(solution)/shard_map/ppermute | solution.py:474
  50.2 8.6 %collective-permute-start.9 = (f32[64,640]{1,0:T(8,128)S(1)}, f32[64,640]{1,0:T(8,128)S(1)}, u32[]{:S(2)}, u32[]{:S(2)}) collective-permute-start(f32[64,640]{1,0:T(8,128)S(1)} %get-tuple-element.67), channel_id=1, source_target_pairs={{0,3},{1,2},{2,1},{3,0},{4,7},{5,6},{6,5},{7,4},{8,11},{9,10},{10,... | collective-permute-start | bytes 491528 | tf_op jit(solution)/shard_map/ppermute | solution.py:474
  50.2 10.3 %collective-permute-start.10 = (f32[64,640]{1,0:T(8,128)S(1)}, f32[64,640]{1,0:T(8,128)S(1)}, u32[]{:S(2)}, u32[]{:S(2)}) collective-permute-start(f32[64,640]{1,0:T(8,128)S(1)} %get-tuple-element.68), channel_id=1, source_target_pairs={{0,4},{1,5},{2,6},{3,7},{4,0},{5,1},{6,2},{7,3},{8,12},{9,13},{10,... | collective-permute-start | bytes 491528 | tf_op jit(solution)/shard_map/ppermute | solution.py:474
  54.1 8.2 %collective-permute-start.11 = (f32[64,640]{1,0:T(8,128)S(1)}, f32[64,640]{1,0:T(8,128)S(1)}, u32[]{:S(2)}, u32[]{:S(2)}) collective-permute-start(f32[64,640]{1,0:T(8,128)S(1)} %get-tuple-element.69), channel_id=1, source_target_pairs={{0,5},{1,4},{2,7},{3,6},{4,1},{5,0},{6,3},{7,2},{8,13},{9,12},{10,... | collective-permute-start | bytes 491528 | tf_op jit(solution)/shard_map/ppermute | solution.py:474
  55.8 11.4 %collective-permute-start.12 = (f32[64,640]{1,0:T(8,128)S(1)}, f32[64,640]{1,0:T(8,128)S(1)}, u32[]{:S(2)}, u32[]{:S(2)}) collective-permute-start(f32[64,640]{1,0:T(8,128)S(1)} %get-tuple-element.70), channel_id=1, source_target_pairs={{0,6},{1,7},{2,4},{3,5},{4,2},{5,3},{6,0},{7,1},{8,14},{9,15},{10,... | collective-permute-start | bytes 491528 | tf_op jit(solution)/shard_map/ppermute | solution.py:474
  58.7 12.1 %collective-permute-start.13 = (f32[64,640]{1,0:T(8,128)S(1)}, f32[64,640]{1,0:T(8,128)S(1)}, u32[]{:S(2)}, u32[]{:S(2)}) collective-permute-start(f32[64,640]{1,0:T(8,128)S(1)} %get-tuple-element.71), channel_id=1, source_target_pairs={{0,7},{1,6},{2,5},{3,4},{4,3},{5,2},{6,1},{7,0},{8,15},{9,14},{10,... | collective-permute-start | bytes 491528 | tf_op jit(solution)/shard_map/ppermute | solution.py:474
  58.8 13.2 %collective-permute-start.15 = (f32[64,640]{1,0:T(8,128)S(1)}, f32[64,640]{1,0:T(8,128)S(1)}, u32[]{:S(2)}, u32[]{:S(2)}) collective-permute-start(f32[64,640]{1,0:T(8,128)S(1)} %get-tuple-element.74), channel_id=1, source_target_pairs={{0,1},{1,0},{2,3},{3,2},{4,5},{5,4},{6,7},{7,6},{8,9},{9,8},{10,11... | collective-permute-start | bytes 491528 | tf_op jit(solution)/shard_map/ppermute | solution.py:474
  60.6 15.0 %collective-permute-start.16 = (f32[64,640]{1,0:T(8,128)S(1)}, f32[64,640]{1,0:T(8,128)S(1)}, u32[]{:S(2)}, u32[]{:S(2)}) collective-permute-start(f32[64,640]{1,0:T(8,128)S(1)} %get-tuple-element.75), channel_id=1, source_target_pairs={{0,2},{1,3},{2,0},{3,1},{4,6},{5,7},{6,4},{7,5},{8,10},{9,11},{10,... | collective-permute-start | bytes 491528 | tf_op jit(solution)/shard_map/ppermute | solution.py:474
  62.3 15.0 %collective-permute-start.17 = (f32[64,640]{1,0:T(8,128)S(1)}, f32[64,640]{1,0:T(8,128)S(1)}, u32[]{:S(2)}, u32[]{:S(2)}) collective-permute-start(f32[64,640]{1,0:T(8,128)S(1)} %get-tuple-element.76), channel_id=1, source_target_pairs={{0,3},{1,2},{2,1},{3,0},{4,7},{5,6},{6,5},{7,4},{8,11},{9,10},{10,... | collective-permute-start | bytes 491528 | tf_op jit(solution)/shard_map/ppermute | solution.py:474
  67.2 10.1 %collective-permute-start.18 = (f32[64,640]{1,0:T(8,128)S(1)}, f32[64,640]{1,0:T(8,128)S(1)}, u32[]{:S(2)}, u32[]{:S(2)}) collective-permute-start(f32[64,640]{1,0:T(8,128)S(1)} %get-tuple-element.77), channel_id=1, source_target_pairs={{0,4},{1,5},{2,6},{3,7},{4,0},{5,1},{6,2},{7,3},{8,12},{9,13},{10,... | collective-permute-start | bytes 491528 | tf_op jit(solution)/shard_map/ppermute | solution.py:474
  70.8 7.3 %collective-permute-start.19 = (f32[64,640]{1,0:T(8,128)S(1)}, f32[64,640]{1,0:T(8,128)S(1)}, u32[]{:S(2)}, u32[]{:S(2)}) collective-permute-start(f32[64,640]{1,0:T(8,128)S(1)} %get-tuple-element.78), channel_id=1, source_target_pairs={{0,5},{1,4},{2,7},{3,6},{4,1},{5,0},{6,3},{7,2},{8,13},{9,12},{10,... | collective-permute-start | bytes 491528 | tf_op jit(solution)/shard_map/ppermute | solution.py:474
  72.0 8.4 %collective-permute-start.20 = (f32[64,640]{1,0:T(8,128)S(1)}, f32[64,640]{1,0:T(8,128)S(1)}, u32[]{:S(2)}, u32[]{:S(2)}) collective-permute-start(f32[64,640]{1,0:T(8,128)S(1)} %get-tuple-element.79), channel_id=1, source_target_pairs={{0,6},{1,7},{2,4},{3,5},{4,2},{5,3},{6,0},{7,1},{8,14},{9,15},{10,... | collective-permute-start | bytes 491528 | tf_op jit(solution)/shard_map/ppermute | solution.py:474
  75.6 8.2 %collective-permute-start.21 = (f32[64,640]{1,0:T(8,128)S(1)}, f32[64,640]{1,0:T(8,128)S(1)}, u32[]{:S(2)}, u32[]{:S(2)}) collective-permute-start(f32[64,640]{1,0:T(8,128)S(1)} %get-tuple-element.80), channel_id=1, source_target_pairs={{0,7},{1,6},{2,5},{3,4},{4,3},{5,2},{6,1},{7,0},{8,15},{9,14},{10,... | collective-permute-start | bytes 491528 | tf_op jit(solution)/shard_map/ppermute | solution.py:474
  91.6 13.2 %all-to-all-start = ((f32[32,1,128]{2,1,0:T(1,128)}), f32[32,1,128]{2,1,0:T(1,128)S(1)}, u32[]{:S(2)}, u32[]{:S(2)}) async-start(f32[32,1,128]{2,1,0:T(1,128)} %get-tuple-element.87), calls=%async_computation | async-start | bytes 32768 | tf_op jit(solution)/shard_map/all_to_all | solution.py:613
  (32 other events, 685.0 us)

commit v13 on v11

--- a/solution.py
+++ b/solution.py
@@ -13,7 +13,7 @@
 QUARTERS = 4
 HALVES = 2
 GROUP = QUARTERS * HALVES
-DISTANCES = (1, 2, 3, 4, 5, 6, 7)
+DISTANCES = (1, 6, 2, 5, 3, 4, 7)
 ARRIVALS = (0, *DISTANCES)
 LANES = 128
 LOG2E = 1.4426950408889634
@@ -552,7 +552,7 @@
         )(*inner_args, *begun, *after)
 
     inside, feature_part, skip_part, skip_wide, *pieces, write_part, read_part = inner(
-        0, QUARTERS, [], [came[1], came[6]]
+        0, QUARTERS, [], [came[1], came[2]]
     )
     two = blocks == 2 * GROUP
     *group_sums, keeps = call(

time: 105 us -> 102 us (0.971)
  waiting for transfers between devices: 21 us -> 18.1 us
    ppermute x22, waiting for transfers between devices: 20.4 us -> 17.5 us  [exchange(): lax.ppermute(value, 'ctx', [(k, k ^ distance) for k in range(blocks)])]
    all_to_all x1, starting transfers between devices: 5.54 us -> 4.4 us  [local(): sums = jnp.sum(lax.all_to_all(sums, ('dp', 'ctx'), 0, 0), axis=(0, 1))]
  transfers between devices with their start and end apart: 23 -> 23, of which waited for: 12 -> 12; matrix products, arithmetic and copies ran while one was open for 0% -> 0% of each run, Pallas kernels for 21% -> 22%
where the time goes in v13:
time: 102 us
  starting transfers between devices  41.6 us (41%)
  Pallas kernels  36.7 us (36%)
  waiting for transfers between devices  18.1 us (18%)
  local copies, waits for them, and re-layouts  4.02 us (4%)
  between operations  1.14 us (1%)
    ppermute x22, starting transfers between devices, exchange(): lax.ppermute(value, 'ctx', [(k, k ^ distance) for k in range(blocks)])  37.2 us
    ppermute x22, waiting for transfers between devices, exchange(): lax.ppermute(value, 'ctx', [(k, k ^ distance) for k in range(blocks)])  17.5 us
    pallas_call x1, Pallas kernels, inner(): call(functools.partial(inner_kernel, offset, last), 'inner_' + str(offset...  15.2 us
    pallas_call x1, Pallas kernels, local(): call(functools.partial(finish_kernel, two), 'finish', [result, result, sm...  7.67 us
    pallas_call x1, Pallas kernels, local(): call(functools.partial(keys_kernel, two), 'keys', [tokens_result] * 2, [t...  6.51 us
    pallas_call x1, Pallas kernels, local(): call(states_kernel, 'states', [struct((2 * part + 8, width))] * GROUP + [...  6.46 us
    all_to_all x1, starting transfers between devices, local(): sums = jnp.sum(lax.all_to_all(sums, ('dp', 'ctx'), 0, 0), axis=(0, 1))  4.4 us
    unnamed x78, local copies, waits for them, and re-layouts  3.43 us
  transfers between devices with their start and end apart: 23, of which 12 were waited for; matrix products, arithmetic and copies ran while one was open for 0% of the time, Pallas kernels for 22%

profile of v13, /device:TPU:0, one launch (start us, length us, event | category | flops | bytes accessed | tf_op | source)
XLA Modules:
  0.0 101.6 jit_solution(5878166627849077362)
XLA Ops:
  0.7 6.5 %states.1 = (f32[136,640]{1,0:T(8,128)}, f32[136,640]{1,0:T(8,128)}, f32[136,640]{1,0:T(8,128)}, f32[136,640]{1,0:T(8,128)}, f32[136,640]{1,0:T(8,128)}, /*index...) custom-call(s32[1,4]{1,0:T(1,128)} %starts.3, ...), custom_call_target="tpu_custom_call" | custom-call | flops 4000000000 | bytes 1000000 | tf_op jit(solution)/shard_map/states/pallas_call | solution.py:517
  7.2 2.9 %collective-permute-start = (f32[136,640]{1,0:T(8,128)}, f32[136,640]{1,0:T(8,128)S(1)}, u32[]{:S(2)}, u32[]{:S(2)}) collective-permute-start(f32[136,640]{1,0:T(8,128)} %get-tuple-element.54), channel_id=1, source_target_pairs={{0,1},{1,0},{2,3},{3,2},{4,5},{5,4},{6,7},{7,6},{8,9},{9,8},{10,11... | collective-permute-start | bytes 1044488 | tf_op jit(solution)/shard_map/ppermute | solution.py:476
  10.1 2.5 %collective-permute-start.1 = (f32[136,640]{1,0:T(8,128)}, f32[136,640]{1,0:T(8,128)S(1)}, u32[]{:S(2)}, u32[]{:S(2)}) collective-permute-start(f32[136,640]{1,0:T(8,128)} %get-tuple-element.55), channel_id=1, source_target_pairs={{0,6},{1,7},{2,4},{3,5},{4,2},{5,3},{6,0},{7,1},{8,14},{9,15},{10,... | collective-permute-start | bytes 1044488 | tf_op jit(solution)/shard_map/ppermute | solution.py:476
  13.2 2.8 %collective-permute-start.4 = (f32[136,640]{1,0:T(8,128)}, f32[136,640]{1,0:T(8,128)S(1)}, u32[]{:S(2)}, u32[]{:S(2)}) collective-permute-start(f32[136,640]{1,0:T(8,128)} %get-tuple-element.63), channel_id=1, source_target_pairs={{0,3},{1,2},{2,1},{3,0},{4,7},{5,6},{6,5},{7,4},{8,11},{9,10},{10,... | collective-permute-start | bytes 1044488 | tf_op jit(solution)/shard_map/ppermute | solution.py:476
  16.0 3.3 %collective-permute-done.refs_0_.refs_1_ = f32[136,640]{1,0:T(8,128)S(1)} collective-permute-done((f32[136,640]{1,0:T(8,128)}, f32[136,640]{1,0:T(8,128)S(1)}, u32[]{:S(2)}, u32[]{:S(2)}) %collective-permute-start) | collective-permute-done | bytes 348192 | tf_op jit(solution)/shard_map/ppermute | solution.py:476
  19.3 2.5 %collective-permute-start.5 = (f32[136,640]{1,0:T(8,128)}, f32[136,640]{1,0:T(8,128)S(1)}, u32[]{:S(2)}, u32[]{:S(2)}) collective-permute-start(f32[136,640]{1,0:T(8,128)} %get-tuple-element.64), channel_id=1, source_target_pairs={{0,4},{1,5},{2,6},{3,7},{4,0},{5,1},{6,2},{7,3},{8,12},{9,13},{10,... | collective-permute-start | bytes 1044488 | tf_op jit(solution)/shard_map/ppermute | solution.py:476
  22.3 3.1 %collective-permute-start.6 = (f32[136,640]{1,0:T(8,128)}, f32[136,640]{1,0:T(8,128)S(1)}, u32[]{:S(2)}, u32[]{:S(2)}) collective-permute-start(f32[136,640]{1,0:T(8,128)} %get-tuple-element.65), channel_id=1, source_target_pairs={{0,7},{1,6},{2,5},{3,4},{4,3},{5,2},{6,1},{7,0},{8,15},{9,14},{10,... | collective-permute-start | bytes 1044488 | tf_op jit(solution)/shard_map/ppermute | solution.py:476
  27.3 15.2 %inner_0.1 = (f32[256,2560]{1,0:T(8,128)S(1)}, f32[256,2560]{1,0:T(8,128)S(1)}, f32[1,2560]{1,0:T(1,128)S(1)}, f32[1,2560]{1,0:T(1,128)S(1)}, bf16[256,2560]{1,0...) custom-call(s32[1,4]{1,0:T(1,128)S(1)} %copy-done.21, ...), custom_call_target="tpu_custom_call" | custom-call | flops 20000000000 | bytes 1000000 | tf_op jit(solution)/shard_map/inner_0/pallas_call | solution.py:539
  45.0 2.6 %collective-permute-start.14 = (f32[72,640]{1,0:T(8,128)S(1)}, f32[72,640]{1,0:T(8,128)S(1)}, u32[]{:S(2)}, u32[]{:S(2)}) collective-permute-start(f32[72,640]{1,0:T(8,128)S(1)} %get-tuple-element.76), channel_id=1, source_target_pairs={{0,8},{1,9},{2,10},{3,11},{4,12},{5,13},{6,14},{7,15},{8,0},{9,1},... | collective-permute-start | bytes 552968 | tf_op jit(solution)/shard_map/ppermute | solution.py:476
  47.9 1.9 %collective-permute-start.7 = (f32[64,640]{1,0:T(8,128)S(1)}, f32[64,640]{1,0:T(8,128)S(1)}, u32[]{:S(2)}, u32[]{:S(2)}) collective-permute-start(f32[64,640]{1,0:T(8,128)S(1)} %get-tuple-element.69), channel_id=1, source_target_pairs={{0,1},{1,0},{2,3},{3,2},{4,5},{5,4},{6,7},{7,6},{8,9},{9,8},{10,11... | collective-permute-start | bytes 491528 | tf_op jit(solution)/shard_map/ppermute | solution.py:476
  49.8 1.5 %collective-permute-start.8 = (f32[64,640]{1,0:T(8,128)S(1)}, f32[64,640]{1,0:T(8,128)S(1)}, u32[]{:S(2)}, u32[]{:S(2)}) collective-permute-start(f32[64,640]{1,0:T(8,128)S(1)} %get-tuple-element.70), channel_id=1, source_target_pairs={{0,6},{1,7},{2,4},{3,5},{4,2},{5,3},{6,0},{7,1},{8,14},{9,15},{10,... | collective-permute-start | bytes 491528 | tf_op jit(solution)/shard_map/ppermute | solution.py:476
  51.7 1.2 %collective-permute-start.10 = (f32[64,640]{1,0:T(8,128)S(1)}, f32[64,640]{1,0:T(8,128)S(1)}, u32[]{:S(2)}, u32[]{:S(2)}) collective-permute-start(f32[64,640]{1,0:T(8,128)S(1)} %get-tuple-element.72), channel_id=1, source_target_pairs={{0,5},{1,4},{2,7},{3,6},{4,1},{5,0},{6,3},{7,2},{8,13},{9,12},{10,... | collective-permute-start | bytes 491528 | tf_op jit(solution)/shard_map/ppermute | solution.py:476
  53.8 3.1 %collective-permute-start.11 = (f32[64,640]{1,0:T(8,128)S(1)}, f32[64,640]{1,0:T(8,128)S(1)}, u32[]{:S(2)}, u32[]{:S(2)}) collective-permute-start(f32[64,640]{1,0:T(8,128)S(1)} %get-tuple-element.73), channel_id=1, source_target_pairs={{0,3},{1,2},{2,1},{3,0},{4,7},{5,6},{6,5},{7,4},{8,11},{9,10},{10,... | collective-permute-start | bytes 491528 | tf_op jit(solution)/shard_map/ppermute | solution.py:476
  58.6 1.3 %collective-permute-start.13 = (f32[64,640]{1,0:T(8,128)S(1)}, f32[64,640]{1,0:T(8,128)S(1)}, u32[]{:S(2)}, u32[]{:S(2)}) collective-permute-start(f32[64,640]{1,0:T(8,128)S(1)} %get-tuple-element.75), channel_id=1, source_target_pairs={{0,7},{1,6},{2,5},{3,4},{4,3},{5,2},{6,1},{7,0},{8,15},{9,14},{10,... | collective-permute-start | bytes 491528 | tf_op jit(solution)/shard_map/ppermute | solution.py:476
  60.9 2.1 %collective-permute-start.16 = (f32[64,640]{1,0:T(8,128)S(1)}, f32[64,640]{1,0:T(8,128)S(1)}, u32[]{:S(2)}, u32[]{:S(2)}) collective-permute-start(f32[64,640]{1,0:T(8,128)S(1)} %get-tuple-element.79), channel_id=1, source_target_pairs={{0,6},{1,7},{2,4},{3,5},{4,2},{5,3},{6,0},{7,1},{8,14},{9,15},{10,... | collective-permute-start | bytes 491528 | tf_op jit(solution)/shard_map/ppermute | solution.py:476
  63.0 1.8 %collective-permute-done.11.refs_5_ = f32[64,640]{1,0:T(8,128)S(1)} collective-permute-done((f32[64,640]{1,0:T(8,128)S(1)}, f32[64,640]{1,0:T(8,128)S(1)}, u32[]{:S(2)}, u32[]{:S(2)}) %collective-permute-start.11) | collective-permute-done | bytes 163872 | tf_op jit(solution)/shard_map/ppermute | solution.py:476
  64.8 4.1 %collective-permute-start.17 = (f32[64,640]{1,0:T(8,128)S(1)}, f32[64,640]{1,0:T(8,128)S(1)}, u32[]{:S(2)}, u32[]{:S(2)}) collective-permute-start(f32[64,640]{1,0:T(8,128)S(1)} %get-tuple-element.80), channel_id=1, source_target_pairs={{0,2},{1,3},{2,0},{3,1},{4,6},{5,7},{6,4},{7,5},{8,10},{9,11},{10,... | collective-permute-start | bytes 491528 | tf_op jit(solution)/shard_map/ppermute | solution.py:476
  69.4 1.9 %collective-permute-start.19 = (f32[64,640]{1,0:T(8,128)S(1)}, f32[64,640]{1,0:T(8,128)S(1)}, u32[]{:S(2)}, u32[]{:S(2)}) collective-permute-start(f32[64,640]{1,0:T(8,128)S(1)} %get-tuple-element.82), channel_id=1, source_target_pairs={{0,3},{1,2},{2,1},{3,0},{4,7},{5,6},{6,5},{7,4},{8,11},{9,10},{10,... | collective-permute-start | bytes 491528 | tf_op jit(solution)/shard_map/ppermute | solution.py:476
  72.5 1.3 %collective-permute-start.21 = (f32[64,640]{1,0:T(8,128)S(1)}, f32[64,640]{1,0:T(8,128)S(1)}, u32[]{:S(2)}, u32[]{:S(2)}) collective-permute-start(f32[64,640]{1,0:T(8,128)S(1)} %get-tuple-element.84), channel_id=1, source_target_pairs={{0,7},{1,6},{2,5},{3,4},{4,3},{5,2},{6,1},{7,0},{8,15},{9,14},{10,... | collective-permute-start | bytes 491528 | tf_op jit(solution)/shard_map/ppermute | solution.py:476
  73.8 4.8 %collective-permute-done.17.refs_11_ = f32[64,640]{1,0:T(8,128)S(1)} collective-permute-done((f32[64,640]{1,0:T(8,128)S(1)}, f32[64,640]{1,0:T(8,128)S(1)}, u32[]{:S(2)}, u32[]{:S(2)}) %collective-permute-start.17) | collective-permute-done | bytes 163872 | tf_op jit(solution)/shard_map/ppermute | solution.py:476
  78.6 3.0 %collective-permute-done.21.refs_15_ = f32[64,640]{1,0:T(8,128)S(1)} collective-permute-done((f32[64,640]{1,0:T(8,128)S(1)}, f32[64,640]{1,0:T(8,128)S(1)}, u32[]{:S(2)}, u32[]{:S(2)}) %collective-permute-start.21) | collective-permute-done | bytes 163872 | tf_op jit(solution)/shard_map/ppermute | solution.py:476
  81.7 7.7 %finish.1 = (bf16[256,2560]{1,0:T(8,128)(2,1)}, bf16[256,2560]{1,0:T(8,128)(2,1)}, f32[40,256]{1,0:T(8,128)}, f32[32,1,128]{2,1,0:T(1,128)}) custom-call(f32[40,256]{1,0:T(8,128)S(1)} %bitcast.26, f32[1,40]{1,0:T(1,128)S(1)} %bitcast.29, f32[1,40]{1,0:T(1,128)S(1)} %bitcast.31, bf16[3,256,128]{2,1,0:T(8,128)(2,1)S(1)} %copy-done.35, ...), custom_call_target="tpu_custom_call" | custom-call | flops 8000000000 | bytes 1000000 | tf_op jit(solution)/shard_map/finish/pallas_call | solution.py:588
  89.5 4.4 %all-to-all-start = ((f32[32,1,128]{2,1,0:T(1,128)}), f32[32,1,128]{2,1,0:T(1,128)S(1)}, u32[]{:S(2)}, u32[]{:S(2)}) async-start(f32[32,1,128]{2,1,0:T(1,128)} %get-tuple-element.95), calls=%async_computation | async-start | bytes 32768 | tf_op jit(solution)/shard_map/all_to_all | solution.py:616
  93.9 6.5 %keys.1 = (bf16[256,128]{1,0:T(8,128)(2,1)}, bf16[256,128]{1,0:T(8,128)(2,1)}) custom-call(f32[256,128]{1,0:T(8,128)} %copy-done.34, f32[256,128]{1,0:T(8,128)} %copy-done.38, bf16[256,2560]{1,0:T(8,128)(2,1)} %copy-done.30, bf16[256,2560]{1,0:T(8,128)(2,1)} %copy-done.31, bf16[256,2560]{1,0:T(8,128)(2,1)} %copy-done.32, bf16[256,2560]{1,0:T(8,128)(2,1)} %copy-done.33, ...), custom_call_target="tpu_custom_call" | custom-call | flops 6000000000 | bytes 1000000 | tf_op jit(solution)/shard_map/keys/pallas_call | solution.py:605
  (109 shorter events, 12.7 us)
Async XLA Ops:
  7.2 12.1 %collective-permute-start = (f32[136,640]{1,0:T(8,128)}, f32[136,640]{1,0:T(8,128)S(1)}, u32[]{:S(2)}, u32[]{:S(2)}) collective-permute-start(f32[136,640]{1,0:T(8,128)} %get-tuple-element.54), channel_id=1, source_target_pairs={{0,1},{1,0},{2,3},{3,2},{4,5},{5,4},{6,7},{7,6},{8,9},{9,8},{10,11... | collective-permute-start | bytes 1044488 | tf_op jit(solution)/shard_map/ppermute | solution.py:476
  10.1 12.2 %collective-permute-start.1 = (f32[136,640]{1,0:T(8,128)}, f32[136,640]{1,0:T(8,128)S(1)}, u32[]{:S(2)}, u32[]{:S(2)}) collective-permute-start(f32[136,640]{1,0:T(8,128)} %get-tuple-element.55), channel_id=1, source_target_pairs={{0,6},{1,7},{2,4},{3,5},{4,2},{5,3},{6,0},{7,1},{8,14},{9,15},{10,... | collective-permute-start | bytes 1044488 | tf_op jit(solution)/shard_map/ppermute | solution.py:476
  12.6 29.9 %collective-permute-start.2 = (f32[136,640]{1,0:T(8,128)}, f32[136,640]{1,0:T(8,128)S(1)}, u32[]{:S(2)}, u32[]{:S(2)}) collective-permute-start(f32[136,640]{1,0:T(8,128)} %get-tuple-element.61), channel_id=1, source_target_pairs={{0,2},{1,3},{2,0},{3,1},{4,6},{5,7},{6,4},{7,5},{8,10},{9,11},{10,... | collective-permute-start | bytes 1044488 | tf_op jit(solution)/shard_map/ppermute | solution.py:476
  13.2 29.4 %collective-permute-start.3 = (f32[136,640]{1,0:T(8,128)}, f32[136,640]{1,0:T(8,128)S(1)}, u32[]{:S(2)}, u32[]{:S(2)}) collective-permute-start(f32[136,640]{1,0:T(8,128)} %get-tuple-element.62), channel_id=1, source_target_pairs={{0,5},{1,4},{2,7},{3,6},{4,1},{5,0},{6,3},{7,2},{8,13},{9,12},{10,... | collective-permute-start | bytes 1044488 | tf_op jit(solution)/shard_map/ppermute | solution.py:476
  13.2 29.4 %collective-permute-start.4 = (f32[136,640]{1,0:T(8,128)}, f32[136,640]{1,0:T(8,128)S(1)}, u32[]{:S(2)}, u32[]{:S(2)}) collective-permute-start(f32[136,640]{1,0:T(8,128)} %get-tuple-element.63), channel_id=1, source_target_pairs={{0,3},{1,2},{2,1},{3,0},{4,7},{5,6},{6,5},{7,4},{8,11},{9,10},{10,... | collective-permute-start | bytes 1044488 | tf_op jit(solution)/shard_map/ppermute | solution.py:476
  19.3 23.3 %collective-permute-start.5 = (f32[136,640]{1,0:T(8,128)}, f32[136,640]{1,0:T(8,128)S(1)}, u32[]{:S(2)}, u32[]{:S(2)}) collective-permute-start(f32[136,640]{1,0:T(8,128)} %get-tuple-element.64), channel_id=1, source_target_pairs={{0,4},{1,5},{2,6},{3,7},{4,0},{5,1},{6,2},{7,3},{8,12},{9,13},{10,... | collective-permute-start | bytes 1044488 | tf_op jit(solution)/shard_map/ppermute | solution.py:476
  22.3 20.9 %collective-permute-start.6 = (f32[136,640]{1,0:T(8,128)}, f32[136,640]{1,0:T(8,128)S(1)}, u32[]{:S(2)}, u32[]{:S(2)}) collective-permute-start(f32[136,640]{1,0:T(8,128)} %get-tuple-element.65), channel_id=1, source_target_pairs={{0,7},{1,6},{2,5},{3,4},{4,3},{5,2},{6,1},{7,0},{8,15},{9,14},{10,... | collective-permute-start | bytes 1044488 | tf_op jit(solution)/shard_map/ppermute | solution.py:476
  45.0 8.7 %collective-permute-start.14 = (f32[72,640]{1,0:T(8,128)S(1)}, f32[72,640]{1,0:T(8,128)S(1)}, u32[]{:S(2)}, u32[]{:S(2)}) collective-permute-start(f32[72,640]{1,0:T(8,128)S(1)} %get-tuple-element.76), channel_id=1, source_target_pairs={{0,8},{1,9},{2,10},{3,11},{4,12},{5,13},{6,14},{7,15},{8,0},{9,1},... | collective-permute-start | bytes 552968 | tf_op jit(solution)/shard_map/ppermute | solution.py:476
  47.9 33.7 %copy-start.29 = (f32[64,640]{1,0:T(8,128)}, f32[64,640]{1,0:T(8,128)S(1)}, u32[]{:S(2)}) copy-start(f32[64,640]{1,0:T(8,128)S(1)} %get-tuple-element.68.refs_0_) | copy-start | bytes 491524
  47.9 9.3 %collective-permute-start.7 = (f32[64,640]{1,0:T(8,128)S(1)}, f32[64,640]{1,0:T(8,128)S(1)}, u32[]{:S(2)}, u32[]{:S(2)}) collective-permute-start(f32[64,640]{1,0:T(8,128)S(1)} %get-tuple-element.69), channel_id=1, source_target_pairs={{0,1},{1,0},{2,3},{3,2},{4,5},{5,4},{6,7},{7,6},{8,9},{9,8},{10,11... | collective-permute-start | bytes 491528 | tf_op jit(solution)/shard_map/ppermute | solution.py:476
  49.8 8.9 %collective-permute-start.8 = (f32[64,640]{1,0:T(8,128)S(1)}, f32[64,640]{1,0:T(8,128)S(1)}, u32[]{:S(2)}, u32[]{:S(2)}) collective-permute-start(f32[64,640]{1,0:T(8,128)S(1)} %get-tuple-element.70), channel_id=1, source_target_pairs={{0,6},{1,7},{2,4},{3,5},{4,2},{5,3},{6,0},{7,1},{8,14},{9,15},{10,... | collective-permute-start | bytes 491528 | tf_op jit(solution)/shard_map/ppermute | solution.py:476
  51.3 9.6 %collective-permute-start.9 = (f32[64,640]{1,0:T(8,128)S(1)}, f32[64,640]{1,0:T(8,128)S(1)}, u32[]{:S(2)}, u32[]{:S(2)}) collective-permute-start(f32[64,640]{1,0:T(8,128)S(1)} %get-tuple-element.71), channel_id=1, source_target_pairs={{0,2},{1,3},{2,0},{3,1},{4,6},{5,7},{6,4},{7,5},{8,10},{9,11},{10,... | collective-permute-start | bytes 491528 | tf_op jit(solution)/shard_map/ppermute | solution.py:476
  51.7 9.2 %collective-permute-start.10 = (f32[64,640]{1,0:T(8,128)S(1)}, f32[64,640]{1,0:T(8,128)S(1)}, u32[]{:S(2)}, u32[]{:S(2)}) collective-permute-start(f32[64,640]{1,0:T(8,128)S(1)} %get-tuple-element.72), channel_id=1, source_target_pairs={{0,5},{1,4},{2,7},{3,6},{4,1},{5,0},{6,3},{7,2},{8,13},{9,12},{10,... | collective-permute-start | bytes 491528 | tf_op jit(solution)/shard_map/ppermute | solution.py:476
  53.8 11.1 %collective-permute-start.11 = (f32[64,640]{1,0:T(8,128)S(1)}, f32[64,640]{1,0:T(8,128)S(1)}, u32[]{:S(2)}, u32[]{:S(2)}) collective-permute-start(f32[64,640]{1,0:T(8,128)S(1)} %get-tuple-element.73), channel_id=1, source_target_pairs={{0,3},{1,2},{2,1},{3,0},{4,7},{5,6},{6,5},{7,4},{8,11},{9,10},{10,... | collective-permute-start | bytes 491528 | tf_op jit(solution)/shard_map/ppermute | solution.py:476
  57.2 11.8 %collective-permute-start.12 = (f32[64,640]{1,0:T(8,128)S(1)}, f32[64,640]{1,0:T(8,128)S(1)}, u32[]{:S(2)}, u32[]{:S(2)}) collective-permute-start(f32[64,640]{1,0:T(8,128)S(1)} %get-tuple-element.74), channel_id=1, source_target_pairs={{0,4},{1,5},{2,6},{3,7},{4,0},{5,1},{6,2},{7,3},{8,12},{9,13},{10,... | collective-permute-start | bytes 491528 | tf_op jit(solution)/shard_map/ppermute | solution.py:476
  58.6 10.7 %collective-permute-start.13 = (f32[64,640]{1,0:T(8,128)S(1)}, f32[64,640]{1,0:T(8,128)S(1)}, u32[]{:S(2)}, u32[]{:S(2)}) collective-permute-start(f32[64,640]{1,0:T(8,128)S(1)} %get-tuple-element.75), channel_id=1, source_target_pairs={{0,7},{1,6},{2,5},{3,4},{4,3},{5,2},{6,1},{7,0},{8,15},{9,14},{10,... | collective-permute-start | bytes 491528 | tf_op jit(solution)/shard_map/ppermute | solution.py:476
  60.9 10.3 %collective-permute-start.15 = (f32[64,640]{1,0:T(8,128)S(1)}, f32[64,640]{1,0:T(8,128)S(1)}, u32[]{:S(2)}, u32[]{:S(2)}) collective-permute-start(f32[64,640]{1,0:T(8,128)S(1)} %get-tuple-element.78), channel_id=1, source_target_pairs={{0,1},{1,0},{2,3},{3,2},{4,5},{5,4},{6,7},{7,6},{8,9},{9,8},{10,11... | collective-permute-start | bytes 491528 | tf_op jit(solution)/shard_map/ppermute | solution.py:476
  60.9 11.6 %collective-permute-start.16 = (f32[64,640]{1,0:T(8,128)S(1)}, f32[64,640]{1,0:T(8,128)S(1)}, u32[]{:S(2)}, u32[]{:S(2)}) collective-permute-start(f32[64,640]{1,0:T(8,128)S(1)} %get-tuple-element.79), channel_id=1, source_target_pairs={{0,6},{1,7},{2,4},{3,5},{4,2},{5,3},{6,0},{7,1},{8,14},{9,15},{10,... | collective-permute-start | bytes 491528 | tf_op jit(solution)/shard_map/ppermute | solution.py:476
  64.8 13.7 %collective-permute-start.17 = (f32[64,640]{1,0:T(8,128)S(1)}, f32[64,640]{1,0:T(8,128)S(1)}, u32[]{:S(2)}, u32[]{:S(2)}) collective-permute-start(f32[64,640]{1,0:T(8,128)S(1)} %get-tuple-element.80), channel_id=1, source_target_pairs={{0,2},{1,3},{2,0},{3,1},{4,6},{5,7},{6,4},{7,5},{8,10},{9,11},{10,... | collective-permute-start | bytes 491528 | tf_op jit(solution)/shard_map/ppermute | solution.py:476
  69.0 9.6 %collective-permute-start.18 = (f32[64,640]{1,0:T(8,128)S(1)}, f32[64,640]{1,0:T(8,128)S(1)}, u32[]{:S(2)}, u32[]{:S(2)}) collective-permute-start(f32[64,640]{1,0:T(8,128)S(1)} %get-tuple-element.81), channel_id=1, source_target_pairs={{0,5},{1,4},{2,7},{3,6},{4,1},{5,0},{6,3},{7,2},{8,13},{9,12},{10,... | collective-permute-start | bytes 491528 | tf_op jit(solution)/shard_map/ppermute | solution.py:476
  69.4 9.2 %collective-permute-start.19 = (f32[64,640]{1,0:T(8,128)S(1)}, f32[64,640]{1,0:T(8,128)S(1)}, u32[]{:S(2)}, u32[]{:S(2)}) collective-permute-start(f32[64,640]{1,0:T(8,128)S(1)} %get-tuple-element.82), channel_id=1, source_target_pairs={{0,3},{1,2},{2,1},{3,0},{4,7},{5,6},{6,5},{7,4},{8,11},{9,10},{10,... | collective-permute-start | bytes 491528 | tf_op jit(solution)/shard_map/ppermute | solution.py:476
  71.3 7.3 %collective-permute-start.20 = (f32[64,640]{1,0:T(8,128)S(1)}, f32[64,640]{1,0:T(8,128)S(1)}, u32[]{:S(2)}, u32[]{:S(2)}) collective-permute-start(f32[64,640]{1,0:T(8,128)S(1)} %get-tuple-element.83), channel_id=1, source_target_pairs={{0,4},{1,5},{2,6},{3,7},{4,0},{5,1},{6,2},{7,3},{8,12},{9,13},{10,... | collective-permute-start | bytes 491528 | tf_op jit(solution)/shard_map/ppermute | solution.py:476
  72.5 9.1 %collective-permute-start.21 = (f32[64,640]{1,0:T(8,128)S(1)}, f32[64,640]{1,0:T(8,128)S(1)}, u32[]{:S(2)}, u32[]{:S(2)}) collective-permute-start(f32[64,640]{1,0:T(8,128)S(1)} %get-tuple-element.84), channel_id=1, source_target_pairs={{0,7},{1,6},{2,5},{3,4},{4,3},{5,2},{6,1},{7,0},{8,15},{9,14},{10,... | collective-permute-start | bytes 491528 | tf_op jit(solution)/shard_map/ppermute | solution.py:476
  89.5 11.5 %all-to-all-start = ((f32[32,1,128]{2,1,0:T(1,128)}), f32[32,1,128]{2,1,0:T(1,128)S(1)}, u32[]{:S(2)}, u32[]{:S(2)}) async-start(f32[32,1,128]{2,1,0:T(1,128)} %get-tuple-element.95), calls=%async_computation | async-start | bytes 32768 | tf_op jit(solution)/shard_map/all_to_all | solution.py:616
  (38 other events, 701.3 us)
